TPU v7x, 32 devices: a whole 2x2x4 slice. The times are simulated.
32 devices in a mesh: dp: 8 (over y, x, core), tensor: 4 (over z).
Axes of the slice: x: 2, y: 2, z: 4, core: 2. Of those that a mesh axis runs over, the one named last changes fastest.
Arguments:
- block_input: bfloat16 [8192, 1536], P(('dp', 'tensor')), may hold values from -6 to 6
- attn_gain: bfloat16 [1536], P('dp'), may hold values from 0.5 to 1.5
- w_query: bfloat16 [1536, 1536], P('dp', 'tensor'), may hold values from -0.15625 to 0.15625
- w_key: bfloat16 [1536, 1536], P('dp', 'tensor'), may hold values from -0.15625 to 0.15625
- w_value: bfloat16 [1536, 1536], P('dp', 'tensor'), may hold values from -0.15625 to 0.15625
- w_forget: bfloat16 [1536, 24], P(None, 'tensor'), may hold values from -0.15625 to 0.15625
- forget_bias: float32 [24], P('tensor'), may hold values from -1 to 7
- w_output: bfloat16 [1536, 1536], P('tensor', 'dp'), may hold values from -0.625 to 0.625
- mlp_gain: bfloat16 [1536], P('dp'), may hold values from 0.5 to 1.5
- w_gate: bfloat16 [1536, 4096], P('dp', 'tensor'), may hold values from -0.15625 to 0.15625
- w_up: bfloat16 [1536, 4096], P('dp', 'tensor'), may hold values from -0.15625 to 0.15625
- w_down: bfloat16 [4096, 1536], P('tensor', 'dp'), may hold values from -0.09375 to 0.09375
- segment_ids: int32 [8, 1024], P('dp'), may hold values from 0 to 3, never falling along the last dimension, each value on 1 to 512 neighbouring positions
- cotangent: bfloat16 [8192, 1536], P(('dp', 'tensor')), may hold values from -6 to 6
Outputs:
- output: bfloat16 [8192, 1536], P(('dp', 'tensor'))
- input_grad: float32 [8192, 1536], P(('dp', 'tensor'))
- grad_attn_gain: float32 [1536], P('dp')
- grad_w_query: float32 [1536, 1536], P('dp', 'tensor')
- grad_w_key: float32 [1536, 1536], P('dp', 'tensor')
- grad_w_value: float32 [1536, 1536], P('dp', 'tensor')
- grad_w_forget: float32 [1536, 24], P(None, 'tensor')
- grad_forget_bias: float32 [24], P('tensor')
- grad_w_output: float32 [1536, 1536], P('tensor', 'dp')
- grad_mlp_gain: float32 [1536], P('dp')
- grad_w_gate: float32 [1536, 4096], P('dp', 'tensor')
- grad_w_up: float32 [1536, 4096], P('dp', 'tensor')
- grad_w_down: float32 [4096, 1536], P('tensor', 'dp')
Inputs may be any that keep to these rules, and one draw needn't show every extreme that they name: Each row of segment_ids numbers the documents of one sequence in order, never falling; a document has 1 to 512 tokens, and the longest of a row has exactly 512.
All inputs are finite; a program needn't handle non-finite values.
Results may differ from a plain program's by a relative error of at most 0.018.
Values may be sent and summed in bfloat16 or wider, within the bound.
No kernel may reach another device: no remote copies, remote signals or barrier semaphores. Data moves between devices by JAX's collectives and lax.ppermute only.
A program may use at most 128 MiB of HBM per device.

v0:
```python
from functools import reduce

import jax
import jax.numpy as jnp
from jax import lax
from jax.sharding import PartitionSpec as P

HEAD_DIM = 64


EPS = 1e-06


def norm_rows(value, gain):
    scale = lax.rsqrt(jnp.mean(value * value, axis=-1, keepdims=True) + EPS)
    return (value * scale * gain, scale)


def norm_back(value, scale, gain, grad):
    weighted = grad * gain
    inner = jnp.mean(weighted * value, axis=-1, keepdims=True)
    return scale * weighted - value * (scale * scale * scale) * inner


def right_product(left, right):
    return jnp.dot(left, right, preferred_element_type=jnp.float32)


def back_terms(pairs):
    terms = [
        jnp.einsum("se,de->sd", grad, weight, preferred_element_type=jnp.float32)
        for grad, weight in pairs
    ]
    return reduce(jnp.add, terms)


def pair_scores(query_pair, key_pair, cum_pair, seg_row, start, block):
    length = key_pair.shape[0]
    raw = jnp.einsum("qhd,khd->hqk", query_pair, key_pair, preferred_element_type=jnp.float32)
    cum_rows = lax.dynamic_slice_in_dim(cum_pair, start, block, 1)
    scores = raw * 0.125 + cum_rows[:, :, None] - cum_pair[:, None, :]
    positions = start + jnp.arange(block, dtype=jnp.int32)
    columns = jnp.arange(length, dtype=jnp.int32)
    seg_rows = lax.dynamic_slice_in_dim(seg_row, start, block, 0)
    allowed = (columns[None, :] <= positions[:, None]) & (seg_rows[:, None] == seg_row[None, :])
    return jnp.where(allowed[None], scores, -jnp.inf)


def pair_inputs(index, blocks, block, query, keys, values, cumul):
    length = query.shape[0]
    span = 2 * HEAD_DIM
    group = index // blocks
    start = index % blocks * block
    column = group * span
    query_pair = lax.dynamic_slice(query, (start, column), (block, span)).reshape(
        block, 2, HEAD_DIM
    )
    key_pair = lax.dynamic_slice_in_dim(keys, column, span, 1).reshape(length, 2, HEAD_DIM)
    value_pair = lax.dynamic_slice_in_dim(values, column, span, 1).reshape(length, 2, HEAD_DIM)
    cum_pair = lax.dynamic_slice_in_dim(cumul, group * 2, 2, 0)
    return (group, start, column, query_pair, key_pair, value_pair, cum_pair)


def attend(query, keys, values, cumul, seg_row):
    length = query.shape[0]
    heads = query.shape[1] // HEAD_DIM
    block = min(512, length)
    blocks = length // block
    span = 2 * HEAD_DIM

    def step(index, carry):
        mixed, log_total = carry
        group, start, column, query_pair, key_pair, value_pair, cum_pair = pair_inputs(
            index, blocks, block, query, keys, values, cumul
        )
        scores = pair_scores(query_pair, key_pair, cum_pair, seg_row, start, block)
        top = jnp.max(scores, axis=-1, keepdims=True)
        expd = jnp.exp(scores - top)
        total = jnp.sum(expd, axis=-1, keepdims=True)
        probs = (expd / total).astype(jnp.bfloat16)
        out = jnp.einsum("hqk,khd->qhd", probs, value_pair, preferred_element_type=jnp.float32)
        mixed = lax.dynamic_update_slice(
            mixed, out.astype(jnp.bfloat16).reshape(block, span), (start, column)
        )
        log_total = lax.dynamic_update_slice(
            log_total, (top + jnp.log(total))[:, :, 0], (group * 2, start)
        )
        return (mixed, log_total)

    start_state = (jnp.zeros_like(query), jnp.zeros((heads, length), jnp.float32))
    return lax.fori_loop(0, heads // 2 * blocks, step, start_state)


def attend_back(query, keys, values, cumul, seg_row, log_total, grad_mixed):
    length = query.shape[0]
    heads = query.shape[1] // HEAD_DIM
    block = min(512, length)
    blocks = length // block
    span = 2 * HEAD_DIM

    def step(index, carry):
        grad_query, grad_keys, grad_values, grad_cum = carry
        group, start, column, query_pair, key_pair, value_pair, cum_pair = pair_inputs(
            index, blocks, block, query, keys, values, cumul
        )
        grad_pair = lax.dynamic_slice(grad_mixed, (start, column), (block, span)).reshape(
            block, 2, HEAD_DIM
        )
        scores = pair_scores(query_pair, key_pair, cum_pair, seg_row, start, block)
        lse_rows = lax.dynamic_slice(log_total, (group * 2, start), (2, block))
        probs = jnp.exp(scores - lse_rows[:, :, None])
        grad_probs = jnp.einsum(
            "qhd,khd->hqk", grad_pair, value_pair, preferred_element_type=jnp.float32
        )
        inner = jnp.sum(probs * grad_probs, axis=-1, keepdims=True)
        grad_scores = probs * (grad_probs - inner)
        rounded = grad_scores.astype(jnp.bfloat16)
        part_query = (
            jnp.einsum("hqk,khd->qhd", rounded, key_pair, preferred_element_type=jnp.float32)
            * 0.125
        )
        part_keys = (
            jnp.einsum("hqk,qhd->khd", rounded, query_pair, preferred_element_type=jnp.float32)
            * 0.125
        )
        part_values = jnp.einsum(
            "hqk,qhd->khd",
            probs.astype(jnp.bfloat16),
            grad_pair,
            preferred_element_type=jnp.float32,
        )
        grad_query = lax.dynamic_update_slice(
            grad_query, part_query.reshape(block, span), (start, column)
        )
        strip_keys = lax.dynamic_slice_in_dim(grad_keys, column, span, 1) + part_keys.reshape(
            length, span
        )
        grad_keys = lax.dynamic_update_slice_in_dim(grad_keys, strip_keys, column, 1)
        strip_values = lax.dynamic_slice_in_dim(grad_values, column, span, 1) + part_values.reshape(
            length, span
        )
        grad_values = lax.dynamic_update_slice_in_dim(grad_values, strip_values, column, 1)
        cum_cols = lax.dynamic_slice_in_dim(grad_cum, group * 2, 2, 0) - jnp.sum(
            grad_scores, axis=1
        )
        grad_cum = lax.dynamic_update_slice_in_dim(grad_cum, cum_cols, group * 2, 0)
        cum_rows = lax.dynamic_slice(grad_cum, (group * 2, start), (2, block)) + jnp.sum(
            grad_scores, axis=-1
        )
        grad_cum = lax.dynamic_update_slice(grad_cum, cum_rows, (group * 2, start))
        return (grad_query, grad_keys, grad_values, grad_cum)

    zeros_wide = jnp.zeros(query.shape, jnp.float32)
    start_state = (zeros_wide, zeros_wide, zeros_wide, jnp.zeros((heads, length), jnp.float32))
    return lax.fori_loop(0, heads // 2 * blocks, step, start_state)


def per_device(
    block_input,
    attn_gain,
    w_query,
    w_key,
    w_value,
    w_forget,
    forget_bias,
    w_output,
    mlp_gain,
    w_gate,
    w_up,
    w_down,
    segment_ids,
    cotangent,
):
    width = block_input.shape[1]
    heads = w_forget.shape[1]
    query_full, key_full, value_full, output_full, gain_one = (
        lax.all_gather(w_query, "dp", axis=0, tiled=True),
        lax.all_gather(w_key, "dp", axis=0, tiled=True),
        lax.all_gather(w_value, "dp", axis=0, tiled=True),
        lax.all_gather(w_output, "dp", axis=1, tiled=True),
        lax.all_gather(attn_gain, "dp", axis=0, tiled=True),
    )
    gate_full, up_full, down_full, gain_two = (
        lax.all_gather(w_gate, "dp", axis=0, tiled=True),
        lax.all_gather(w_up, "dp", axis=0, tiled=True),
        lax.all_gather(w_down, "dp", axis=1, tiled=True),
        lax.all_gather(mlp_gain, "dp", axis=0, tiled=True),
    )
    resid = block_input.astype(jnp.float32)
    normed, first_scale = norm_rows(resid, gain_one.astype(jnp.float32))
    normed_all = lax.all_gather(normed.astype(jnp.bfloat16), "tensor", axis=0, tiled=True)
    query = jnp.dot(normed_all, query_full, preferred_element_type=jnp.float32).astype(jnp.bfloat16)
    keys = jnp.dot(normed_all, key_full, preferred_element_type=jnp.float32).astype(jnp.bfloat16)
    values = jnp.dot(normed_all, value_full, preferred_element_type=jnp.float32).astype(
        jnp.bfloat16
    )
    forget_logit = jnp.dot(normed_all, w_forget, preferred_element_type=jnp.float32) + forget_bias
    cumul = jnp.cumsum(jax.nn.log_sigmoid(forget_logit), axis=0).T
    seg_row = segment_ids[0]
    mixed, log_total = attend(query, keys, values, cumul, seg_row)
    attn_out = lax.psum_scatter(
        right_product(mixed, output_full), "tensor", scatter_dimension=0, tiled=True
    )
    hidden_res = resid + attn_out
    second, second_scale = norm_rows(hidden_res, gain_two.astype(jnp.float32))
    second_all = lax.all_gather(second.astype(jnp.bfloat16), "tensor", axis=0, tiled=True)
    gate = jnp.dot(second_all, gate_full, preferred_element_type=jnp.float32)
    upper = jnp.dot(second_all, up_full, preferred_element_type=jnp.float32)
    sigma = jax.nn.sigmoid(gate)
    swish = gate * sigma
    hidden = (swish * upper).astype(jnp.bfloat16)
    mlp_out = lax.psum_scatter(
        right_product(hidden, down_full).astype(jnp.bfloat16),
        "tensor",
        scatter_dimension=0,
        tiled=True,
    ).astype(jnp.float32)
    output = (hidden_res + mlp_out).astype(jnp.bfloat16)
    (
        query_full,
        key_full,
        value_full,
        output_full,
        gain_one,
        gate_full,
        up_full,
        down_full,
        gain_two,
    ) = (
        lax.all_gather(w_query, "dp", axis=0, tiled=True),
        lax.all_gather(w_key, "dp", axis=0, tiled=True),
        lax.all_gather(w_value, "dp", axis=0, tiled=True),
        lax.all_gather(w_output, "dp", axis=1, tiled=True),
        lax.all_gather(attn_gain, "dp", axis=0, tiled=True),
        lax.all_gather(w_gate, "dp", axis=0, tiled=True),
        lax.all_gather(w_up, "dp", axis=0, tiled=True),
        lax.all_gather(w_down, "dp", axis=1, tiled=True),
        lax.all_gather(mlp_gain, "dp", axis=0, tiled=True),
    )
    grad_out = cotangent.astype(jnp.float32)
    grad_all = lax.all_gather(cotangent, "tensor", axis=0, tiled=True)
    grad_hidden = (
        jnp.einsum("sd,fd->sf", grad_all, down_full, preferred_element_type=jnp.float32)
        .astype(jnp.bfloat16)
        .astype(jnp.float32)
    )
    grad_gate = (grad_hidden * upper * sigma * (1.0 + gate * (1.0 - sigma))).astype(jnp.bfloat16)
    grad_up = (grad_hidden * swish).astype(jnp.bfloat16)
    grad_down_w = jnp.einsum("sf,sd->fd", hidden, grad_all, preferred_element_type=jnp.float32)
    grad_gate_w = jnp.einsum("sd,sf->df", second_all, grad_gate, preferred_element_type=jnp.float32)
    grad_up_w = jnp.einsum("sd,sf->df", second_all, grad_up, preferred_element_type=jnp.float32)
    grad_second = lax.psum_scatter(
        back_terms(((grad_gate, gate_full), (grad_up, up_full))).astype(jnp.bfloat16),
        "tensor",
        scatter_dimension=0,
        tiled=True,
    ).astype(jnp.float32)
    gain_two_f = gain_two.astype(jnp.float32)
    grad_res = grad_out + norm_back(hidden_res, second_scale, gain_two_f, grad_second)
    gain_two_part = jnp.sum(grad_second * hidden_res * second_scale, axis=0)
    mlp_shards = (
        lax.psum_scatter(
            grad_gate_w.astype(jnp.bfloat16), "dp", scatter_dimension=0, tiled=True
        ).astype(jnp.float32),
        lax.psum_scatter(
            grad_up_w.astype(jnp.bfloat16), "dp", scatter_dimension=0, tiled=True
        ).astype(jnp.float32),
        lax.psum_scatter(
            grad_down_w.astype(jnp.bfloat16), "dp", scatter_dimension=1, tiled=True
        ).astype(jnp.float32),
    )
    grad_branch = grad_res.astype(jnp.bfloat16)
    branch_all = lax.all_gather(grad_branch, "tensor", axis=0, tiled=True)
    grad_mixed = jnp.einsum(
        "sd,ed->se", branch_all, output_full, preferred_element_type=jnp.float32
    ).astype(jnp.bfloat16)
    grad_output_w = jnp.einsum("se,sd->ed", mixed, branch_all, preferred_element_type=jnp.float32)
    grad_query, grad_keys, grad_values, grad_cum = attend_back(
        query, keys, values, cumul, seg_row, log_total, grad_mixed
    )
    grad_logf = jnp.flip(jnp.cumsum(jnp.flip(grad_cum.T, 0), axis=0), 0)
    grad_logit = grad_logf * jax.nn.sigmoid(-forget_logit)
    grad_bias = jnp.sum(grad_logit, axis=0)
    logit_low = grad_logit.astype(jnp.bfloat16)
    query_low = grad_query.astype(jnp.bfloat16)
    keys_low = grad_keys.astype(jnp.bfloat16)
    values_low = grad_values.astype(jnp.bfloat16)
    grad_query_w = jnp.einsum(
        "sd,se->de", normed_all, query_low, preferred_element_type=jnp.float32
    )
    grad_key_w = jnp.einsum("sd,se->de", normed_all, keys_low, preferred_element_type=jnp.float32)
    grad_value_w = jnp.einsum(
        "sd,se->de", normed_all, values_low, preferred_element_type=jnp.float32
    )
    grad_forget_w = jnp.einsum(
        "sd,sh->dh", normed_all, logit_low, preferred_element_type=jnp.float32
    )
    grad_first = lax.psum_scatter(
        back_terms(
            (
                (query_low, query_full),
                (keys_low, key_full),
                (values_low, value_full),
                (logit_low, w_forget),
            )
        ).astype(jnp.bfloat16),
        "tensor",
        scatter_dimension=0,
        tiled=True,
    ).astype(jnp.float32)
    gain_one_f = gain_one.astype(jnp.float32)
    input_grad = grad_res + norm_back(resid, first_scale, gain_one_f, grad_first)
    gain_one_part = jnp.sum(grad_first * resid * first_scale, axis=0)
    attn_shards = (
        lax.psum_scatter(
            grad_query_w.astype(jnp.bfloat16), "dp", scatter_dimension=0, tiled=True
        ).astype(jnp.float32),
        lax.psum_scatter(
            grad_key_w.astype(jnp.bfloat16), "dp", scatter_dimension=0, tiled=True
        ).astype(jnp.float32),
        lax.psum_scatter(
            grad_value_w.astype(jnp.bfloat16), "dp", scatter_dimension=0, tiled=True
        ).astype(jnp.float32),
        lax.psum_scatter(
            grad_output_w.astype(jnp.bfloat16), "dp", scatter_dimension=1, tiled=True
        ).astype(jnp.float32),
    )
    tensor_index = lax.axis_index("tensor")
    all_heads = heads * lax.axis_size("tensor")
    forget_pad = lax.dynamic_update_slice(
        jnp.zeros((width, all_heads), jnp.float32), grad_forget_w, (0, tensor_index * heads)
    )
    bias_pad = lax.dynamic_update_slice(
        jnp.zeros((all_heads,), jnp.float32), grad_bias, (tensor_index * heads,)
    )
    summed = lax.psum((forget_pad, bias_pad, gain_one_part, gain_two_part), ("dp", "tensor"))
    share = width // lax.axis_size("dp")
    dp_start = lax.axis_index("dp") * share
    grad_forget_out = lax.dynamic_slice_in_dim(summed[0], tensor_index * heads, heads, 1)
    grad_bias_out = lax.dynamic_slice_in_dim(summed[1], tensor_index * heads, heads, 0)
    grad_gain_one = lax.dynamic_slice_in_dim(summed[2], dp_start, share, 0)
    grad_gain_two = lax.dynamic_slice_in_dim(summed[3], dp_start, share, 0)
    return (
        output,
        input_grad,
        grad_gain_one,
        attn_shards[0],
        attn_shards[1],
        attn_shards[2],
        grad_forget_out,
        grad_bias_out,
        attn_shards[3],
        grad_gain_two,
        mlp_shards[0],
        mlp_shards[1],
        mlp_shards[2],
    )


def solution(mesh):
    return jax.shard_map(
        per_device,
        mesh=mesh,
        in_specs=(
            P(("dp", "tensor"), None),
            P("dp"),
            P("dp", "tensor"),
            P("dp", "tensor"),
            P("dp", "tensor"),
            P(None, "tensor"),
            P("tensor"),
            P("tensor", "dp"),
            P("dp"),
            P("dp", "tensor"),
            P("dp", "tensor"),
            P("tensor", "dp"),
            P("dp", None),
            P(("dp", "tensor"), None),
        ),
        out_specs=(
            P(("dp", "tensor"), None),
            P(("dp", "tensor"), None),
            P("dp"),
            P("dp", "tensor"),
            P("dp", "tensor"),
            P("dp", "tensor"),
            P(None, "tensor"),
            P("tensor"),
            P("tensor", "dp"),
            P("dp"),
            P("dp", "tensor"),
            P("dp", "tensor"),
            P("tensor", "dp"),
        ),
        check_vma=False,
    )
```

profile of v0, /device:TPU:0, one launch (start us, length us, event | category | flops | bytes accessed | tf_op | source)
XLA Modules:
  0.0 1310.2 jit_solution(17133466086450550335)
XLA Ops:
  12.8 15.4 %all-reduce.3 = (bf16[1536]{0:T(1024)(128)(2,1)S(1)}, bf16[1536]{0:T(1024)(128)(2,1)S(1)}) all-reduce(bf16[1536]{0:T(1024)(128)(2,1)S(1)} %dynamic-update-slice, bf16[1536]{0:T(1024)(128)(2,1)S(1)} %dynamic-update-slice.1), channel_id=1, replica_groups=mesh['dp'=8,'tensor'=4] {'dp'}, use_global_device_ids=true, to_apply=%add | all-reduce | flops 3072 | bytes 12288
  33.9 60.3 %all-gather.12.cloned.1.call-done = bf16[1024,1536]{1,0:T(8,128)(2,1)} async-done(((bf16[256,1536]{1,0:T(8,128)(2,1)}), bf16[1024,1536]{1,0:T(8,128)(2,1)}) %all-gather.12.cloned.1.call-update) | async-done | bytes 3145744 | tf_op jit(solution)/shard_map/all_gather | solution.py:191
  94.2 2.9 convolution_add_fusion
  99.9 18.9 %all-gather.18.cloned.1.call-done = bf16[1536,384]{1,0:T(8,128)(2,1)} async-done(((bf16[192,384]{1,0:T(8,128)(2,1)}), bf16[1536,384]{1,0:T(8,128)(2,1)}) %all-gather.18.cloned.1.call-update) | async-done | bytes 1179664 | tf_op jit(solution)/shard_map/all_gather | solution.py:178
  118.8 3.9 convolution_convert_fusion.10
  125.0 19.8 %all-gather.16.cloned.1.call-done = bf16[1536,384]{1,0:T(8,128)(2,1)} async-done(((bf16[192,384]{1,0:T(8,128)(2,1)}), bf16[1536,384]{1,0:T(8,128)(2,1)}) %all-gather.16.cloned.1.call-update) | async-done | bytes 1179664 | tf_op jit(solution)/shard_map/all_gather | solution.py:177
  144.8 3.9 convolution_convert_fusion.11
  151.0 19.6 %all-gather.14.cloned.1.call-done = bf16[1536,384]{1,0:T(8,128)(2,1)} async-done(((bf16[192,384]{1,0:T(8,128)(2,1)}), bf16[1536,384]{1,0:T(8,128)(2,1)}) %all-gather.14.cloned.1.call-update) | async-done | bytes 1179664 | tf_op jit(solution)/shard_map/all_gather | solution.py:179
  170.6 3.9 convolution_convert_fusion.12
  176.1 59.4 %while.40 = (s32[]{:T(128)}, bf16[1024,384]{0,1:T(8,128)(2,1)S(1)}, f32[6,1024]{1,0:T(8,128)S(1)}, bf16[1024,384]{0,1:T(8,128)(2,1)S(1)}, s32[1024]{0:T(1024)S(1...) while((s32[]{:T(128)}, bf16[1024,384]{0,1:T(8,128)(2,1)S(1)}, ...), condition=%wide.region_6.7_spmd, body=%wide.region_3.6_spmd.sunk | while | flops 288947744 | bytes 17148404 | solution.py:91
  235.5 6.3 fusion.58
  244.4 108.4 %reduce-scatter.12.cloned.1.call-done = f32[256,1536]{1,0:T(8,128)} async-done(((f32[1024,1536]{1,0:T(8,128)}), f32[256,1536]{1,0:T(8,128)}) %reduce-scatter.12.cloned.1.call-update) | async-done | bytes 1572880 | tf_op jit(solution)/shard_map/reduce_scatter | solution.py:201
  356.4 62.0 %all-gather.30.cloned.1.call-done = bf16[1024,1536]{1,0:T(8,128)(2,1)} async-done(((bf16[256,1536]{1,0:T(8,128)(2,1)}), bf16[1024,1536]{1,0:T(8,128)(2,1)}) %all-gather.30.cloned.1.call-update) | async-done | bytes 3145744 | tf_op jit(solution)/shard_map/all_gather | solution.py:241
  418.4 32.9 %all-gather.28.cloned.1.call-done = bf16[1024,1536]{0,1:T(8,128)(2,1)} async-done(((bf16[1024,192]{0,1:T(8,128)(2,1)}), bf16[1024,1536]{0,1:T(8,128)(2,1)}) %all-gather.28.cloned.1.call-update) | async-done | bytes 3145744 | tf_op jit(solution)/shard_map/all_gather | solution.py:186
  451.3 7.6 convolution_convert_fusion.8
  458.9 26.6 %all-gather.24.cloned.1.call-done = bf16[1536,1024]{1,0:T(8,128)(2,1)} async-done(((bf16[192,1024]{1,0:T(8,128)(2,1)}), bf16[1536,1024]{1,0:T(8,128)(2,1)}) %all-gather.24.cloned.1.call-update) | async-done | bytes 3145744 | tf_op jit(solution)/shard_map/all_gather | solution.py:184
  485.5 65.5 %all-gather.22.cloned.1.call-done = bf16[1024,1536]{1,0:T(8,128)(2,1)} async-done(((bf16[256,1536]{1,0:T(8,128)(2,1)}), bf16[1024,1536]{1,0:T(8,128)(2,1)}) %all-gather.22.cloned.1.call-update) | async-done | bytes 3145744 | tf_op jit(solution)/shard_map/all_gather | solution.py:206
  551.1 8.2 fusion.59
  559.3 24.7 %all-gather.26.cloned.1.call-done = bf16[1536,1024]{1,0:T(8,128)(2,1)} async-done(((bf16[192,1024]{1,0:T(8,128)(2,1)}), bf16[1536,1024]{1,0:T(8,128)(2,1)}) %all-gather.26.cloned.1.call-update) | async-done | bytes 3145744 | tf_op jit(solution)/shard_map/all_gather | solution.py:185
  583.9 10.9 fusion.14
  594.8 3.5 fusion.60
  599.3 6.8 add_convert_fusion.1
  606.2 60.4 %reduce-scatter.16.cloned.1.call-done = bf16[256,1536]{1,0:T(8,128)(2,1)} async-done(((bf16[1024,1536]{1,0:T(8,128)(2,1)}), bf16[256,1536]{1,0:T(8,128)(2,1)}) %reduce-scatter.16.cloned.1.call-update) | async-done | bytes 786448 | tf_op jit(solution)/shard_map/reduce_scatter | solution.py:252
  671.4 9.0 convolution_convert_fusion.1
  680.5 7.7 convolution_convert_fusion.2
  689.4 7.7 convolution_convert_fusion
  697.2 37.8 %all-gather.32.cloned.1.call-done = bf16[1024,1536]{1,0:T(8,128)(2,1)} async-done(((bf16[256,1536]{1,0:T(8,128)(2,1)}), bf16[1024,1536]{1,0:T(8,128)(2,1)}) %all-gather.32.cloned.1.call-update) | async-done | bytes 3145744 | tf_op jit(solution)/shard_map/all_gather | solution.py:273
  735.0 4.5 convolution_convert_fusion.9
  741.1 91.9 %while.41 = (s32[]{:T(128)}, bf16[1024,384]{0,1:T(8,128)(2,1)}, f32[1024,384]{0,1:T(8,128)}, f32[1024,384]{0,1:T(8,128)S(1)}, f32[6,1024]{1,0:T(8,128)S(1)}, /*i...) while((s32[]{:T(128)}, bf16[1024,384]{0,1:T(8,128)(2,1)}, ...), condition=%wide.region_16.17_spmd, body=%wide.region_12.16_spmd.sunk | while | flops 686816768 | bytes 53156532 | solution.py:155
  752.3 3.4 dynamic_update_slice.101
  783.6 3.4 dynamic_update_slice.101
  799.6 2.8 dynamic_update_slice.101
  840.2 5.2 convolution_convert_fusion.4
  845.5 5.3 convolution_convert_fusion.7
  850.8 5.2 convolution_convert_fusion.6
  856.1 4.8 convolution_convert_fusion.5
  861.2 3.4 fusion.61
  868.5 2.9 add_convert_fusion
  871.4 7.7 convolution_convert_fusion.3
  885.5 124.8 %all-reduce.6.cloned.1.call-done = f32[1536,24]{0,1:T(8,128)} async-done(((f32[1536,24]{0,1:T(8,128)}), f32[1536,24]{0,1:T(8,128)}) %all-reduce.6.cloned.1.call-update) | async-done | bytes 147472 | tf_op jit(solution)/shard_map/psum | solution.py:336
  1011.8 40.7 %reduce-scatter.26.cloned.1.call-done = bf16[384,192]{0,1:T(8,128)(2,1)} async-done(((bf16[384,1536]{0,1:T(8,128)(2,1)}), bf16[384,192]{0,1:T(8,128)(2,1)}) %reduce-scatter.26.cloned.1.call-update) | async-done | bytes 147472 | tf_op jit(solution)/shard_map/reduce_scatter | solution.py:324
  1054.1 38.4 %reduce-scatter.20.cloned.1.call-done = bf16[192,384]{1,0:T(8,128)(2,1)} async-done(((bf16[1536,384]{1,0:T(8,128)(2,1)}), bf16[192,384]{1,0:T(8,128)(2,1)}) %reduce-scatter.20.cloned.1.call-update) | async-done | bytes 147472 | tf_op jit(solution)/shard_map/reduce_scatter | solution.py:315
  1094.1 38.6 %reduce-scatter.22.cloned.1.call-done = bf16[192,384]{1,0:T(8,128)(2,1)} async-done(((bf16[1536,384]{1,0:T(8,128)(2,1)}), bf16[192,384]{1,0:T(8,128)(2,1)}) %reduce-scatter.22.cloned.1.call-update) | async-done | bytes 147472 | tf_op jit(solution)/shard_map/reduce_scatter | solution.py:318
  1134.3 38.4 %reduce-scatter.24.cloned.1.call-done = bf16[192,384]{1,0:T(8,128)(2,1)} async-done(((bf16[1536,384]{1,0:T(8,128)(2,1)}), bf16[192,384]{1,0:T(8,128)(2,1)}) %reduce-scatter.24.cloned.1.call-update) | async-done | bytes 147472 | tf_op jit(solution)/shard_map/reduce_scatter | solution.py:321
  1174.4 61.0 %reduce-scatter.18.cloned.1.call-done = bf16[256,1536]{1,0:T(8,128)(2,1)} async-done(((bf16[1024,1536]{1,0:T(8,128)(2,1)}), bf16[256,1536]{1,0:T(8,128)(2,1)}) %reduce-scatter.18.cloned.1.call-update) | async-done | bytes 786448 | tf_op jit(solution)/shard_map/reduce_scatter | solution.py:298
  1237.1 45.5 %all-reduce.2 = (f32[1536]{0:T(1024)S(1)}, f32[24]{0:T(128)S(1)}, f32[1536]{0:T(1024)S(1)}) all-reduce(f32[1536]{0:T(1024)S(1)} %get-tuple-element.679, f32[24]{0:T(128)S(1)} %dynamic_update_slice.84, f32[1536]{0:T(1024)S(1)} %copy-done.25), channel_id=1, replica_groups=mesh['dp'=8,'tensor'=4] {'dp','tensor'}, use_global_device_ids=true, to_apply=%region_22.23 | all-reduce | flops 3096 | bytes 24768 | tf_op jit(solution)/shard_map/psum | solution.py:336
  1284.4 14.7 %reduce-scatter.14.cloned.1.call-done = bf16[256,1536]{1,0:T(8,128)(2,1)} async-done(((bf16[1024,1536]{1,0:T(8,128)(2,1)}), bf16[256,1536]{1,0:T(8,128)(2,1)}) %reduce-scatter.14.cloned.1.call-update) | async-done | bytes 786448 | tf_op jit(solution)/shard_map/reduce_scatter | solution.py:212
  1299.2 4.0 fusion.21
  (438 shorter events, 203.8 us)
Async XLA Ops:
  7.2 87.0 %copy-start = (bf16[1536,6]{0,1:T(8,128)(2,1)S(1)}, bf16[1536,6]{0,1:T(8,128)(2,1)}, u32[]{:S(2)}) copy-start(bf16[1536,6]{0,1:T(8,128)(2,1)} %param.23) | copy-start | bytes 55300
  7.2 87.0 %copy-start.35 = (f32[6]{0:T(128)S(1)}, f32[6]{0:T(128)}, u32[]{:S(2)}) copy-start(f32[6]{0:T(128)} %param.24) | copy-start | bytes 76
  7.2 87.0 %all-gather.12.cloned.1.call-start = ((), (), s32[]{:S(2)}) async-start(), calls=%async_computation.11 | async-start | bytes 3932160 | tf_op jit(solution)/shard_map/all_gather | solution.py:191
  9.2 24.6 %copy-start.28 = (f32[256]{0:T(256)}, f32[256]{0:T(256)S(1)}, u32[]{:S(2)}) copy-start(f32[256]{0:T(256)S(1)} %get-tuple-element.748) | copy-start | bytes 3076
  31.2 87.7 %all-gather.18.cloned.1.call-start = ((), (), s32[]{:S(2)}) async-start(), calls=%async_computation.14 | async-start | bytes 1327104 | tf_op jit(solution)/shard_map/all_gather | solution.py:178
  31.9 112.9 %all-gather.16.cloned.1.call-start = ((), (), s32[]{:S(2)}) async-start(), calls=%async_computation.13 | async-start | bytes 1327104 | tf_op jit(solution)/shard_map/all_gather | solution.py:177
  32.7 138.0 %all-gather.14.cloned.1.call-start = ((), (), s32[]{:S(2)}) async-start(), calls=%async_computation.12 | async-start | bytes 1327104 | tf_op jit(solution)/shard_map/all_gather | solution.py:179
  33.2 202.3 %all-gather.20.cloned.1.call-start = ((), (), s32[]{:S(2)}) async-start(), calls=%async_computation.15 | async-start | bytes 1327104 | tf_op jit(solution)/shard_map/all_gather | solution.py:180
  33.8 318.9 %reduce-scatter.12.cloned.1.call-start = ((), (), s32[]{:S(2)}) async-start(), calls=%async_computation.16 | async-start | bytes 7864320 | tf_op jit(solution)/shard_map/reduce_scatter | solution.py:201
  94.2 24.6 %copy-start.1 = (bf16[1024,1536]{1,0:T(8,128)(2,1)S(1)}, bf16[1024,1536]{1,0:T(8,128)(2,1)}, u32[]{:S(2)}) copy-start(bf16[1024,1536]{1,0:T(8,128)(2,1)} %all-gather.12.cloned.1.call-done) | copy-start | bytes 9437188
  151.0 25.1 %copy-start.14 = (s32[1,1024]{1,0:T(1,128)S(1)}, s32[1,1024]{1,0:T(1,128)}, u32[]{:S(2)}) copy-start(s32[1,1024]{1,0:T(1,128)} %param.30) | copy-start | bytes 12292
  235.5 6.3 copy-start.7
  241.8 110.9 %copy-start.5 = (bf16[256,1536]{1,0:T(8,128)(2,1)S(1)}, bf16[256,1536]{1,0:T(8,128)(2,1)}, u32[]{:S(2)}) copy-start(bf16[256,1536]{1,0:T(8,128)(2,1)} %param.18) | copy-start | bytes 2359300
  241.9 176.5 %all-gather.30.cloned.1.call-start = ((), (), s32[]{:S(2)}) async-start(), calls=%async_computation.22 | async-start | bytes 3932160 | tf_op jit(solution)/shard_map/all_gather | solution.py:241
  242.6 208.7 %all-gather.28.cloned.1.call-start = ((), (), s32[]{:S(2)}) async-start(), calls=%async_computation.20 | async-start | bytes 3538944 | tf_op jit(solution)/shard_map/all_gather | solution.py:186
  243.4 242.2 %all-gather.24.cloned.1.call-start = ((), (), s32[]{:S(2)}) async-start(), calls=%async_computation.18 | async-start | bytes 3538944 | tf_op jit(solution)/shard_map/all_gather | solution.py:184
  244.1 306.9 %all-gather.22.cloned.1.call-start = ((), (), s32[]{:S(2)}) async-start(), calls=%async_computation.17 | async-start | bytes 3932160 | tf_op jit(solution)/shard_map/all_gather | solution.py:206
  244.4 424.4 %copy-start.18 = (f32[1536]{0:T(1024)}, f32[1536]{0:T(1024)S(1)}, u32[]{:S(2)}) copy-start(f32[1536]{0:T(1024)S(1)} %convert_element_type.178) | copy-start | bytes 18436
  354.5 314.2 %copy-start.26 = (f32[256]{0:T(256)}, f32[256]{0:T(256)S(1)}, u32[]{:S(2)}) copy-start(f32[256]{0:T(256)S(1)} %get-tuple-element.750) | copy-start | bytes 3076
  354.5 314.2 %copy-start.30 = (f32[256]{0:T(256)}, f32[256]{0:T(256)S(1)}, u32[]{:S(2)}) copy-start(f32[256]{0:T(256)S(1)} %get-tuple-element.749) | copy-start | bytes 3076
  355.6 228.3 %all-gather.26.cloned.1.call-start = ((), (), s32[]{:S(2)}) async-start(), calls=%async_computation.19 | async-start | bytes 3538944 | tf_op jit(solution)/shard_map/all_gather | solution.py:185
  356.4 310.2 %reduce-scatter.16.cloned.1.call-start = ((), (), s32[]{:S(2)}) async-start(), calls=%async_computation.23 | async-start | bytes 3932160 | tf_op jit(solution)/shard_map/reduce_scatter | solution.py:252
  583.9 10.9 copy-start.36
  606.1 62.6 %copy-start.8 = (bf16[256,1536]{1,0:T(8,128)(2,1)S(1)}, bf16[256,1536]{1,0:T(8,128)(2,1)}, u32[]{:S(2)}) copy-start(bf16[256,1536]{1,0:T(8,128)(2,1)} %param.31) | copy-start | bytes 2359300
  606.1 128.9 %all-gather.32.cloned.1.call-start = ((), (), s32[]{:S(2)}) async-start(), calls=%async_computation.24 | async-start | bytes 3932160 | tf_op jit(solution)/shard_map/all_gather | solution.py:273
  668.7 11.7 copy-start.32
  671.3 207.8 %reduce-scatter.30.cloned.1.call-start = ((), (), s32[]{:S(2)}) async-start(), calls=%async_computation.32 | async-start | bytes 3538944 | tf_op jit(solution)/shard_map/reduce_scatter | solution.py:265
  680.4 200.9 %reduce-scatter.28.cloned.1.call-start = ((), (), s32[]{:S(2)}) async-start(), calls=%async_computation.31 | async-start | bytes 3538944 | tf_op jit(solution)/shard_map/reduce_scatter | solution.py:262
  688.2 195.1 %reduce-scatter.32.cloned.1.call-start = ((), (), s32[]{:S(2)}) async-start(), calls=%async_computation.33 | async-start | bytes 3538944 | tf_op jit(solution)/shard_map/reduce_scatter | solution.py:268
  697.1 37.9 %copy-start.13 = (bf16[384,1536]{0,1:T(8,128)(2,1)S(1)}, bf16[384,1536]{0,1:T(8,128)(2,1)}, u32[]{:S(2)}) copy-start(bf16[384,1536]{0,1:T(8,128)(2,1)} %all-gather.20.cloned.1.call-done) | copy-start | bytes 3538948
  697.2 313.1 %all-reduce.6.cloned.1.call-start = ((), (), s32[]{:S(2)}) async-start(), calls=%async_computation.29 | async-start | bytes 294912 | tf_op jit(solution)/shard_map/psum | solution.py:336
  741.1 95.2 %copy-start.17 = (f32[1024,6]{0,1:T(8,128)S(1)}, f32[1024,6]{0,1:T(8,128)}, u32[]{:S(2)}) copy-start(f32[1024,6]{0,1:T(8,128)} %copy-done.16) | copy-start | bytes 73732
  839.9 212.6 %reduce-scatter.26.cloned.1.call-start = ((), (), s32[]{:S(2)}) async-start(), calls=%async_computation.30 | async-start | bytes 1327104 | tf_op jit(solution)/shard_map/reduce_scatter | solution.py:324
  845.4 247.1 %reduce-scatter.20.cloned.1.call-start = ((), (), s32[]{:S(2)}) async-start(), calls=%async_computation.26 | async-start | bytes 1327104 | tf_op jit(solution)/shard_map/reduce_scatter | solution.py:315
  850.8 281.9 %reduce-scatter.22.cloned.1.call-start = ((), (), s32[]{:S(2)}) async-start(), calls=%async_computation.27 | async-start | bytes 1327104 | tf_op jit(solution)/shard_map/reduce_scatter | solution.py:318
  856.1 316.7 %reduce-scatter.24.cloned.1.call-start = ((), (), s32[]{:S(2)}) async-start(), calls=%async_computation.28 | async-start | bytes 1327104 | tf_op jit(solution)/shard_map/reduce_scatter | solution.py:321
  860.9 374.5 %reduce-scatter.18.cloned.1.call-start = ((), (), s32[]{:S(2)}) async-start(), calls=%async_computation.25 | async-start | bytes 3932160 | tf_op jit(solution)/shard_map/reduce_scatter | solution.py:298
  871.4 427.8 %reduce-scatter.14.cloned.1.call-start = ((), (), s32[]{:S(2)}) async-start(), calls=%async_computation.21 | async-start | bytes 3932160 | tf_op jit(solution)/shard_map/reduce_scatter | solution.py:212
  879.1 356.3 %copy-start.6 = (bf16[256,1536]{1,0:T(8,128)(2,1)S(1)}, bf16[256,1536]{1,0:T(8,128)(2,1)}, u32[]{:S(2)}) copy-start(bf16[256,1536]{1,0:T(8,128)(2,1)} %param.18) | copy-start | bytes 2359300
  879.1 356.3 %copy-start.21 = (f32[1536]{0:T(1024)S(1)}, f32[1536]{0:T(1024)}, u32[]{:S(2)}) copy-start(f32[1536]{0:T(1024)} %copy-done.20) | copy-start | bytes 18436
  879.1 356.3 %copy-start.29 = (f32[256]{0:T(256)S(1)}, f32[256]{0:T(256)}, u32[]{:S(2)}) copy-start(f32[256]{0:T(256)} %copy-done.28) | copy-start | bytes 3076
  881.2 355.8 %copy-start.25 = (f32[1536]{0:T(1024)S(1)}, f32[1536]{0:T(1024)}, u32[]{:S(2)}) copy-start(f32[1536]{0:T(1024)} %get-tuple-element.677) | copy-start | bytes 18436
  881.2 418.0 %copy-start.9 = (bf16[256,1536]{1,0:T(8,128)(2,1)S(1)}, bf16[256,1536]{1,0:T(8,128)(2,1)}, u32[]{:S(2)}) copy-start(bf16[256,1536]{1,0:T(8,128)(2,1)} %param.31) | copy-start | bytes 2359300
  881.2 418.0 %copy-start.19 = (f32[1536]{0:T(1024)S(1)}, f32[1536]{0:T(1024)}, u32[]{:S(2)}) copy-start(f32[1536]{0:T(1024)} %copy-done.18) | copy-start | bytes 18436
  881.2 418.0 %copy-start.27 = (f32[256]{0:T(256)S(1)}, f32[256]{0:T(256)}, u32[]{:S(2)}) copy-start(f32[256]{0:T(256)} %copy-done.26) | copy-start | bytes 3076
  881.2 418.0 %copy-start.31 = (f32[256]{0:T(256)S(1)}, f32[256]{0:T(256)}, u32[]{:S(2)}) copy-start(f32[256]{0:T(256)} %copy-done.30) | copy-start | bytes 3076
  881.2 418.0 %copy-start.33 = (f32[256]{0:T(256)S(1)}, f32[256]{0:T(256)}, u32[]{:S(2)}) copy-start(f32[256]{0:T(256)} %copy-done.32) | copy-start | bytes 3076
  881.2 418.0 %copy-start.34 = (f32[256]{0:T(256)S(1)}, f32[256]{0:T(256)}, u32[]{:S(2)}) copy-start(f32[256]{0:T(256)} %get-tuple-element.747) | copy-start | bytes 3076
  (41 other events, 115.7 us)
Sparse Core Ops, SparseCore 0:
  31.3 62.8 all-gather.11
  96.1 22.6 all-gather.17
  120.7 24.0 all-gather.15
  146.5 24.0 all-gather.13
  172.4 24.0 all-gather.19
  242.0 110.7 reduce-scatter.11
  354.3 64.0 all-gather.29
  420.3 30.9 all-gather.27
  453.2 32.3 all-gather.23
  487.5 63.4 all-gather.21
  552.9 30.9 all-gather.25
  606.3 60.2 reduce-scatter.15
  671.5 63.5 all-gather.31
  738.3 44.9 reduce-scatter.29
  786.8 46.2 reduce-scatter.27
  836.3 46.3 reduce-scatter.31
  889.6 120.6 all-reduce.5
  1013.7 38.7 reduce-scatter.25
  1055.7 36.7 reduce-scatter.19
  1095.9 36.7 reduce-scatter.21
  1135.9 36.7 reduce-scatter.23
  1175.2 60.2 reduce-scatter.17
  1237.9 61.3 reduce-scatter.13
where the time goes:
time: 1320 us; the launch traced here: 1310 us
  waiting for transfers between devices  899 us (68%)
  matrix products  175 us (13%)
  local copies, waits for them, and re-layouts  96.2 us (7%)
  blocking collectives  61 us (5%)
  other arithmetic  60.4 us (5%)
  between operations  15.6 us (1%)
    psum x1, waiting for transfers between devices, per_device(): lax.psum((forget_pad, bias_pad, gain_one_part, gain_two_part), ('dp', 'te...  125 us
    reduce_scatter x1, waiting for transfers between devices, per_device(): lax.psum_scatter(right_product(mixed, output_full), 'tensor', scatter_dim...  108 us
    all_gather x1, waiting for transfers between devices, per_device(): lax.all_gather(second.astype(jnp.bfloat16), 'tensor', axis=0, tiled=True)  65.5 us
    all_gather x1, waiting for transfers between devices, per_device(): grad_all = lax.all_gather(cotangent, 'tensor', axis=0, tiled=True)  62 us
    reduce_scatter x1, waiting for transfers between devices, per_device(): lax.psum_scatter(back_terms(((query_low, query_full), (keys_low, key_full...  61 us
    reduce_scatter x1, waiting for transfers between devices, per_device(): lax.psum_scatter(back_terms(((grad_gate, gate_full), (grad_up, up_full)))...  60.4 us
    all_gather x1, waiting for transfers between devices, per_device(): lax.all_gather(normed.astype(jnp.bfloat16), 'tensor', axis=0, tiled=True)  60.3 us
    psum x1, blocking collectives, per_device(): lax.psum((forget_pad, bias_pad, gain_one_part, gain_two_part), ('dp', 'te...  45.5 us
  transfers between devices with their start and end apart: 23, of which 19 were waited for; matrix products, arithmetic and copies ran while one was open for 21% of the time, Pallas kernels for 0%

commit v1 on v0

v1 whole, which is shorter than its diff:
```python
import functools

import jax
import jax.numpy as jnp
from jax import lax
from jax.experimental import pallas as pl
from jax.experimental.pallas import tpu as pltpu
from jax.sharding import PartitionSpec as P

HEAD = 64
PAIR = 2 * HEAD
EPS = 1e-06
F32 = jnp.float32
BF16 = jnp.bfloat16
NT = (((1,), (1,)), ((), ()))
TN = (((0,), (0,)), ((), ()))
AXES = ("dp", "tensor")


def nn(a, b):
    return jnp.dot(a, b, preferred_element_type=F32)


def nt(a, b):
    return lax.dot_general(a, b, NT, preferred_element_type=F32)


def tn(a, b):
    return lax.dot_general(a, b, TN, preferred_element_type=F32)


def send(value, move):
    tensor = lax.axis_size("tensor")
    pairs = []
    for d in range(lax.axis_size("dp")):
        for t in range(tensor):
            to = move(d, t)
            if to is not None:
                pairs.append((d * tensor + t, to[0] * tensor + to[1]))
    return lax.ppermute(value, AXES, pairs)


def to_home(d, t):
    return (d ^ 1, t ^ 2) if (d & 1) != (t >> 1) else (d, t)


def over_core(d, t):
    return (d ^ 1, t)


def over_z(d, t):
    return (d, t ^ 1)


def over_chip(bit):
    return lambda d, t: (d ^ (2 << bit), t)


def spread_one(d, t):
    return (d ^ 1, t) if d & 1 else (d ^ 1, t ^ 2)


def spread_two(d, t):
    return (d, t ^ 2) if d & 1 else None


def collect_one(d, t):
    return (d ^ 1, t ^ 2) if d & 1 else (d ^ 1, t)


def after(value, *others):
    return lax.optimization_barrier((value, *others))[0]


def gather_chips(even, odd, bits):
    evens, odds = {0: even}, {0: odd}
    for bit in range(bits):
        for at, piece in list(evens.items()):
            evens[at | (1 << bit)] = send(piece, over_chip(bit))
    for bit in reversed(range(bits)):
        for at, piece in list(odds.items()):
            odds[at | (1 << bit)] = send(piece, over_chip(bit))
    rows = []
    for at in range(1 << bits):
        rows += [evens[at], odds[at]]
    return jnp.concatenate(rows, axis=0)


def scatter_chips(blocks, order):
    blocks = dict(enumerate(blocks))
    for bit in order:
        kept = {}
        for at in sorted(blocks):
            if not at >> bit & 1:
                there = send(blocks[at | (1 << bit)], over_chip(bit))
                kept[at] = (blocks[at].astype(F32) + there.astype(F32)).astype(BF16)
        blocks = kept
    return blocks[0]


def gather_group(own):
    z = send(own, over_z)
    core = send(own, over_core)
    both = send(z, over_core)
    return own, core, z, both


def scatter_group(halves):
    far = halves(1)
    rows = far.shape[0] // 2
    far_in = send(far[rows:].astype(BF16), over_core)
    far_sum = (far[:rows] + far_in.astype(F32)).astype(BF16)
    far_got = send(far_sum, over_z)
    near = halves(0)
    near_in = send(near[rows:].astype(BF16), over_core)
    return near[:rows] + near_in.astype(F32) + far_got.astype(F32)


def block_of(pos_ref, at, size):
    return pl.ds(pl.multiple_of(pos_ref[at] * size, size), size)


def forward_kernel(quarter, pos_ref, qkv_ref, bias_ref, segr_ref, segc_ref, mixed_ref, lse_ref, cum_ref, cumr_ref):
    pair = pl.program_id(0)
    pairs = pl.num_programs(0)
    width = pairs * PAIR
    lane = lax.broadcasted_iota(jnp.int32, (quarter, PAIR), 1)
    count = segr_ref.shape[1] // quarter

    @pl.when(pair == 0)
    def _():
        rows = lax.broadcasted_iota(jnp.int32, (quarter, quarter), 0)
        cols = lax.broadcasted_iota(jnp.int32, (quarter, quarter), 1)
        lower = (cols <= rows).astype(F32)
        carry = jnp.zeros((1, PAIR), F32)
        for a in range(count):
            logit = qkv_ref[block_of(pos_ref, a, quarter), 3 * width : 3 * width + PAIR] + bias_ref[...]
            logsig = jnp.minimum(logit, 0.0) - jnp.log1p(jnp.exp(-jnp.abs(logit)))
            cum = jnp.dot(lower, logsig, precision=lax.Precision.HIGHEST, preferred_element_type=F32) + carry
            carry = cum[quarter - 1 :, :]
            cum_ref[a * quarter : (a + 1) * quarter, :] = cum
            cumr_ref[:, a * quarter : (a + 1) * quarter] = cum.T[: cumr_ref.shape[0], :]
        lse_ref[...] = jnp.zeros(lse_ref.shape, F32)

    def columns(part):
        return pl.ds(pl.multiple_of(part * width + pair * PAIR, PAIR), PAIR)

    diag_rows = lax.broadcasted_iota(jnp.int32, (quarter, quarter), 0)
    diag_cols = lax.broadcasted_iota(jnp.int32, (quarter, quarter), 1)
    for a in range(count):
        query = (qkv_ref[block_of(pos_ref, a, quarter), columns(0)].astype(BF16) * 0.125).astype(BF16)
        seg_q = segc_ref[a * quarter : (a + 1) * quarter, :]
        spans = range(max(0, a - 512 // quarter), a + 1)
        outs = []
        for h in range(2):
            head = pair * 2 + h
            mine = (lane >= HEAD) if h else (lane < HEAD)
            query_h = jnp.where(mine, query, jnp.zeros_like(query))
            scores = []
            for b in spans:
                keys = qkv_ref[block_of(pos_ref, b, quarter), columns(1)].astype(BF16)
                s = nt(query_h, keys) - cumr_ref[pl.ds(head, 1), b * quarter : (b + 1) * quarter]
                allowed = seg_q == segr_ref[:, b * quarter : (b + 1) * quarter]
                if a == b:
                    allowed &= diag_cols <= diag_rows
                scores.append(jnp.where(allowed, s, -jnp.inf))
            top = functools.reduce(jnp.maximum, [jnp.max(s, axis=1, keepdims=True) for s in scores])
            expd = [jnp.exp(s - top) for s in scores]
            total = functools.reduce(jnp.add, [jnp.sum(e, axis=1, keepdims=True) for e in expd])
            scale = 1.0 / total
            out = None
            for e, b in zip(expd, spans):
                values = qkv_ref[block_of(pos_ref, b, quarter), columns(2)].astype(BF16)
                part = nn((e * scale).astype(BF16), values)
                out = part if out is None else out + part
            outs.append(out)
            lse = top + jnp.log(total)
            at = pl.ds(a * quarter, quarter)
            lse_ref[at, :] = jnp.where(lane == head, lse, lse_ref[at, :])
        mixed_ref[block_of(pos_ref, a, quarter), columns(0)] = jnp.where(lane < HEAD, outs[0], outs[1]).astype(BF16)


def backward_kernel(
    quarter, pos_ref, qkv_ref, bias_ref, segr_ref, segc_ref, lse_ref, cum_ref, gmix_ref,
    grad_ref, gbias_ref, lser_ref, gcol_ref, grow_ref, gk_ref, gv_ref,
):
    pair = pl.program_id(0)
    pairs = pl.num_programs(0)
    width = pairs * PAIR
    lane = lax.broadcasted_iota(jnp.int32, (quarter, PAIR), 1)
    count = segr_ref.shape[1] // quarter
    rows8 = lser_ref.shape[0]

    @pl.when(pair == 0)
    def _():
        for a in range(count):
            at = slice(a * quarter, (a + 1) * quarter)
            lser_ref[:, at] = lse_ref[at, :].T[:rows8, :]
        gcol_ref[...] = jnp.zeros(gcol_ref.shape, F32)
        grow_ref[...] = jnp.zeros(grow_ref.shape, F32)

    def columns(part):
        return pl.ds(pl.multiple_of(part * width + pair * PAIR, PAIR), PAIR)

    diag_rows = lax.broadcasted_iota(jnp.int32, (quarter, quarter), 0)
    diag_cols = lax.broadcasted_iota(jnp.int32, (quarter, quarter), 1)
    gk_ref[...] = jnp.zeros(gk_ref.shape, F32)
    gv_ref[...] = jnp.zeros(gv_ref.shape, F32)
    for a in range(count):
        here = slice(a * quarter, (a + 1) * quarter)
        query = (qkv_ref[block_of(pos_ref, a, quarter), columns(0)].astype(BF16) * 0.125).astype(BF16)
        gout = gmix_ref[block_of(pos_ref, a, quarter), columns(0)]
        seg_q = segr_ref[:, here]
        spans = range(max(0, a - 512 // quarter), a + 1)
        grad_query = None
        for h in range(2):
            head = pair * 2 + h
            mine = (lane >= HEAD) if h else (lane < HEAD)
            query_h = jnp.where(mine, query, jnp.zeros_like(query))
            gout_h = jnp.where(mine, gout, jnp.zeros_like(gout))
            lse = lser_ref[pl.ds(head, 1), here]
            probs, gprobs = [], []
            inner = None
            for b in spans:
                there = slice(b * quarter, (b + 1) * quarter)
                keys = qkv_ref[block_of(pos_ref, b, quarter), columns(1)].astype(BF16)
                values = qkv_ref[block_of(pos_ref, b, quarter), columns(2)].astype(BF16)
                cum_k = jnp.sum(jnp.where(lane == head, cum_ref[there, :], 0.0), axis=1, keepdims=True)
                s = nt(keys, query_h) - cum_k
                allowed = segc_ref[there, :] == seg_q
                if a == b:
                    allowed &= diag_rows <= diag_cols
                p = jnp.where(allowed, jnp.exp(s - lse), 0.0)
                g = nt(values, gout_h)
                probs.append(p)
                gprobs.append(g)
                part = jnp.sum(p * g, axis=0, keepdims=True)
                inner = part if inner is None else inner + part
            row_sum = None
            for p, g, b in zip(probs, gprobs, spans):
                there = slice(b * quarter, (b + 1) * quarter)
                keys = (qkv_ref[block_of(pos_ref, b, quarter), columns(1)].astype(BF16) * 0.125).astype(BF16)
                keys_h = jnp.where(mine, keys, jnp.zeros_like(keys))
                gs = p * (g - inner)
                part = jnp.sum(gs, axis=0, keepdims=True)
                row_sum = part if row_sum is None else row_sum + part
                col_sum = jnp.sum(gs, axis=1, keepdims=True)
                gcol_ref[there, :] += jnp.where(lane == head, col_sum, 0.0)
                low = gs.astype(BF16)
                gk_ref[there, :] += nn(low, query_h)
                gv_ref[there, :] += nn(p.astype(BF16), gout_h)
                part = tn(low, keys_h)
                grad_query = part if grad_query is None else grad_query + part
            grow_ref[pl.ds(head, 1), here] = row_sum
        grad_ref[block_of(pos_ref, a, quarter), columns(0)] = grad_query.astype(BF16)
    for a in range(count):
        here = slice(a * quarter, (a + 1) * quarter)
        grad_ref[block_of(pos_ref, a, quarter), columns(1)] = gk_ref[here, :].astype(BF16)
        grad_ref[block_of(pos_ref, a, quarter), columns(2)] = gv_ref[here, :].astype(BF16)

    @pl.when(pair == pairs - 1)
    def _():
        upper = (diag_cols >= diag_rows).astype(F32)
        carry = jnp.zeros((1, PAIR), F32)
        bias = jnp.zeros((1, PAIR), F32)
        pad = jnp.zeros((PAIR - rows8, quarter), F32)
        for a in reversed(range(count)):
            here = slice(a * quarter, (a + 1) * quarter)
            logit = qkv_ref[block_of(pos_ref, a, quarter), 3 * width : 3 * width + PAIR] + bias_ref[...]
            grow = jnp.concatenate([grow_ref[:, here], pad], axis=0).T
            gcum = jnp.where(lane < 2 * pairs, grow - gcol_ref[here, :], 0.0)
            back = jnp.dot(upper, gcum, precision=lax.Precision.HIGHEST, preferred_element_type=F32) + carry
            carry = back[:1, :]
            glogit = back * (1.0 / (1.0 + jnp.exp(logit)))
            glogit = jnp.where(lane < 2 * pairs, glogit, 0.0)
            bias = bias + jnp.sum(glogit, axis=0, keepdims=True)
            grad_ref[block_of(pos_ref, a, quarter), 3 * width : 3 * width + PAIR] = glogit.astype(BF16)
        gbias_ref[...] = bias


def full_spec(shape):
    return pl.BlockSpec(shape, lambda *_: (0,) * len(shape))


def attend(pos, qkv, bias, seg_row, seg_col, quarter):
    length = qkv.shape[0]
    width = (qkv.shape[1] - PAIR) // 3
    pairs = width // PAIR
    return pl.pallas_call(
        functools.partial(forward_kernel, quarter),
        grid=(pairs,),
        out_shape=(
            jax.ShapeDtypeStruct((length, width), BF16),
            jax.ShapeDtypeStruct((length, PAIR), F32),
            jax.ShapeDtypeStruct((length, PAIR), F32),
        ),
        in_specs=[
            pl.BlockSpec(memory_space=pltpu.SMEM),
            full_spec(qkv.shape),
            full_spec(bias.shape),
            full_spec(seg_row.shape),
            full_spec(seg_col.shape),
        ],
        out_specs=(full_spec((length, width)), full_spec((length, PAIR)), full_spec((length, PAIR))),
        scratch_shapes=[pltpu.VMEM((8, length), F32)],
        compiler_params=pltpu.CompilerParams(vmem_limit_bytes=48 * 2**20, dimension_semantics=("arbitrary",)),
    )(pos, qkv, bias, seg_row, seg_col)


def attend_back(pos, qkv, bias, seg_row, seg_col, lse, cum, grad_mixed, quarter):
    length = qkv.shape[0]
    width = (qkv.shape[1] - PAIR) // 3
    pairs = width // PAIR
    return pl.pallas_call(
        functools.partial(backward_kernel, quarter),
        grid=(pairs,),
        out_shape=(
            jax.ShapeDtypeStruct(qkv.shape, BF16),
            jax.ShapeDtypeStruct((1, PAIR), F32),
        ),
        in_specs=[
            pl.BlockSpec(memory_space=pltpu.SMEM),
            full_spec(qkv.shape),
            full_spec(bias.shape),
            full_spec(seg_row.shape),
            full_spec(seg_col.shape),
            full_spec(lse.shape),
            full_spec(cum.shape),
            full_spec(grad_mixed.shape),
        ],
        out_specs=(full_spec(qkv.shape), full_spec((1, PAIR))),
        scratch_shapes=[
            pltpu.VMEM((8, length), F32),
            pltpu.VMEM((length, PAIR), F32),
            pltpu.VMEM((8, length), F32),
            pltpu.VMEM((length, PAIR), F32),
            pltpu.VMEM((length, PAIR), F32),
        ],
        compiler_params=pltpu.CompilerParams(vmem_limit_bytes=48 * 2**20, dimension_semantics=("arbitrary",)),
    )(pos, qkv, bias, seg_row, seg_col, lse, cum, grad_mixed)


def unit_rows(value):
    scale = lax.rsqrt(jnp.mean(value * value, axis=-1, keepdims=True) + EPS)
    return value * scale, scale


def unit_back(value, scale, weighted):
    inner = jnp.mean(weighted * value, axis=-1, keepdims=True)
    return scale * weighted - value * (scale * scale * scale) * inner


def per_device(
    block_input, attn_gain, w_query, w_key, w_value, w_forget, forget_bias, w_output,
    mlp_gain, w_gate, w_up, w_down, segment_ids, cotangent,
):
    width = block_input.shape[1]
    quarter = block_input.shape[0]
    heads = w_forget.shape[1]
    share = w_query.shape[0]
    chips = lax.axis_size("dp") // 2
    bits = chips.bit_length() - 1
    d = lax.axis_index("dp")
    t = lax.axis_index("tensor")
    core, chip = d & 1, d >> 1
    first = core == 0
    at_home = core == t >> 1
    wide = width // chips

    def reorder(rows):
        return jnp.concatenate(
            [lax.dynamic_slice_in_dim(rows, (chip ^ r) * wide, wide, 1) for r in range(chips)], axis=1
        )

    def spread(pack):
        one = send(pack, spread_one)
        two = send(pack, spread_two)
        even = jnp.where(first, pack, one)
        odd = jnp.where(first, one, two)
        return even, odd

    gain_one = attn_gain.astype(F32)[:, None]
    gain_two = mlp_gain.astype(F32)[:, None]
    forget_own = lax.dynamic_slice_in_dim(w_forget, d * share, share, 0)
    pack_one = jnp.concatenate(
        [
            (w_query.astype(F32) * gain_one).astype(BF16),
            (w_key.astype(F32) * gain_one).astype(BF16),
            (w_value.astype(F32) * gain_one).astype(BF16),
            (forget_own.astype(F32) * gain_one).astype(BF16),
            attn_gain[:, None],
            jnp.zeros((share, PAIR - heads - 1), BF16),
        ],
        axis=1,
    )
    even_one, odd_one = spread(pack_one)

    x_own = send(after(reorder(block_input), pack_one), to_home)
    x_blocks = gather_group(x_own)
    x_all = jnp.concatenate(x_blocks, axis=0)
    cot_own = send(after(reorder(cotangent), x_own), to_home)
    seg_other = send(segment_ids, over_core)
    seg_row = jnp.where(at_home, segment_ids, seg_other)
    seg_col = seg_row.reshape(-1, 1)
    bias_other = send(forget_bias, lambda d, t: (d, t ^ 2))
    bias = jnp.where(first, forget_bias, bias_other)
    bias = jnp.pad(bias, (0, PAIR - heads))[None, :]
    place = (t & 1) + 2 * core
    pos = jnp.stack([((a ^ place) >> 1) | (((a ^ place) & 1) << 1) for a in range(4)]).astype(jnp.int32)

    pack_two = jnp.concatenate([w_output.T, w_down.T], axis=1)
    even_two, odd_two = spread(after(pack_two, x_own))
    pack_three = jnp.concatenate(
        [(w_gate.astype(F32) * gain_two).astype(BF16), (w_up.astype(F32) * gain_two).astype(BF16)], axis=1
    )
    even_three, odd_three = spread(after(pack_three, even_two))

    full_one = gather_chips(even_one, odd_one, bits)
    full_two = gather_chips(after(even_two, full_one), after(odd_two, full_one), bits)
    full_three = gather_chips(after(even_three, full_two), after(odd_three, full_two), bits)
    inner_width = w_output.shape[0]
    wo_t, wd_t = full_two[:, :inner_width], full_two[:, inner_width:]
    hidden_width = w_gate.shape[1]

    x_hat = unit_rows(x_all.astype(F32))[0].astype(BF16)
    resid = x_own.astype(F32)
    first_scale = unit_rows(resid)[1]
    qkv = nn(x_hat, full_one)
    mixed, lse, cum = attend(pos, qkv, bias, seg_row, seg_col, quarter)

    def half(array, which):
        rows = array.shape[0] // 2
        return array[which * rows : (which + 1) * rows]

    hidden_res = resid + scatter_group(lambda which: nt(half(mixed, which), wo_t))
    second, second_scale = unit_rows(hidden_res)
    second_all = jnp.concatenate(gather_group(second.astype(BF16)), axis=0)
    cot_all = jnp.concatenate(gather_group(cot_own), axis=0)

    gate = nn(second_all, full_three[:, :hidden_width])
    upper = nn(second_all, full_three[:, hidden_width:])
    grad_hidden = nn(cot_all, wd_t).astype(BF16).astype(F32)
    sigma = jax.nn.sigmoid(gate)
    swish = gate * sigma
    hidden = (swish * upper).astype(BF16)
    grad_gate = (grad_hidden * upper * sigma * (1.0 + gate * (1.0 - sigma))).astype(BF16)
    grad_up = (grad_hidden * swish).astype(BF16)
    grad_both = jnp.concatenate([grad_gate, grad_up], axis=1)

    def second_part(which):
        return nt(half(grad_both, which), full_three)

    parts = {}

    def second_half(which):
        parts[which] = second_part(which)
        return parts[which]

    grad_second = scatter_group(second_half)
    gain_two_part = functools.reduce(
        jnp.add, [jnp.sum(half(second_all, w).astype(F32) * parts[w], axis=0) for w in (0, 1)]
    )
    grad_res = cot_own.astype(F32) + unit_back(hidden_res, second_scale, grad_second)
    branch_all = jnp.concatenate(gather_group(grad_res.astype(BF16)), axis=0)

    mlp_out = scatter_group(lambda which: nt(half(hidden, which), wd_t))
    out_home = (hidden_res + mlp_out).astype(BF16)
    output = reorder(send(out_home, to_home))

    def chip_grads(left, right):
        return [tn(left[:, r * wide : (r + 1) * wide], right).astype(BF16) for r in range(chips)]

    up_order, down_order = list(range(bits)), list(reversed(range(bits)))

    def finish(total):
        even, odd = total[:share], total[share:]
        one = send(jnp.where(first, odd, even), collect_one)
        two = send(odd, spread_two)
        return jnp.where(first, even, two).astype(F32) + one.astype(F32)

    split = hidden_width // 2
    gate_sum = finish(scatter_chips(chip_grads(second_all, grad_gate), up_order))
    up_sum = finish(scatter_chips(chip_grads(second_all, grad_up), down_order))
    down_sum = jnp.concatenate(
        [
            finish(scatter_chips(chip_grads(cot_all, hidden[:, :split]), up_order)),
            finish(scatter_chips(chip_grads(cot_all, hidden[:, split:]), down_order)),
        ],
        axis=1,
    )

    grad_mixed = nn(branch_all, wo_t).astype(BF16)
    output_sum = finish(scatter_chips(chip_grads(branch_all, mixed), up_order))
    grad_qkv, grad_bias = attend_back(pos, qkv, bias, seg_row, seg_col, lse, cum, grad_mixed, quarter)
    first_parts = {}

    def first_half(which):
        first_parts[which] = nt(half(grad_qkv, which), full_one)
        return first_parts[which]

    grad_first = scatter_group(first_half)
    gain_one_part = functools.reduce(
        jnp.add, [jnp.sum(half(x_hat, w).astype(F32) * first_parts[w], axis=0) for w in (0, 1)]
    )
    back_home = (grad_res + unit_back(resid, first_scale, grad_first)).astype(BF16)
    input_grad = reorder(send(back_home, to_home)).astype(F32)

    cut = qkv.shape[1] // 2
    qkv_sum = jnp.concatenate(
        [
            finish(scatter_chips(chip_grads(x_hat, grad_qkv[:, :cut]), up_order)),
            finish(scatter_chips(chip_grads(x_hat, grad_qkv[:, cut:]), down_order)),
        ],
        axis=1,
    )
    qkv_sum = qkv_sum * gain_one

    three = 3 * inner_width
    gain_row = full_one[:, three + heads].astype(F32)
    forget_part = tn(grad_qkv[:, three:], x_hat)[:heads] * gain_row[None, :]
    small = jnp.concatenate([forget_part, gain_one_part[None], gain_two_part[None]], axis=0)
    small = reorder(small)
    small = jnp.concatenate([small, jnp.pad(grad_bias[:, :PAIR], ((0, 0), (0, width - PAIR)))], axis=0)
    for bit in range(bits):
        small = small + send(small, over_chip(bit))
    one = send(small, collect_one)
    two = send(small, spread_two)
    small = jnp.where(first, small, two) + one
    grad_forget = small[:heads].T
    grad_bias_out = small[heads + 2, :heads]
    gains = small[heads : heads + 2]
    gains = gains + send(gains, over_z)
    gains = gains + send(gains, lambda d, t: (d, t ^ 2))
    gains = lax.dynamic_slice_in_dim(gains, d * share, share, 1)
    grad_gain_one = gains[0] / attn_gain.astype(F32)
    grad_gain_two = gains[1] / mlp_gain.astype(F32)

    return (
        output,
        input_grad,
        grad_gain_one,
        qkv_sum[:, :inner_width],
        qkv_sum[:, inner_width : 2 * inner_width],
        qkv_sum[:, 2 * inner_width : three],
        grad_forget,
        grad_bias_out,
        output_sum.T,
        grad_gain_two,
        gate_sum * gain_two,
        up_sum * gain_two,
        down_sum.T,
    )


def solution(mesh):
    return jax.shard_map(
        per_device,
        mesh=mesh,
        in_specs=(
            P(("dp", "tensor"), None),
            P("dp"),
            P("dp", "tensor"),
            P("dp", "tensor"),
            P("dp", "tensor"),
            P(None, "tensor"),
            P("tensor"),
            P("tensor", "dp"),
            P("dp"),
            P("dp", "tensor"),
            P("dp", "tensor"),
            P("tensor", "dp"),
            P("dp", None),
            P(("dp", "tensor"), None),
        ),
        out_specs=(
            P(("dp", "tensor"), None),
            P(("dp", "tensor"), None),
            P("dp"),
            P("dp", "tensor"),
            P("dp", "tensor"),
            P("dp", "tensor"),
            P(None, "tensor"),
            P("tensor"),
            P("tensor", "dp"),
            P("dp"),
            P("dp", "tensor"),
            P("dp", "tensor"),
            P("tensor", "dp"),
        ),
        check_vma=False,
    )
```

time: 1320 us -> 653 us (0.49)
  waiting for transfers between devices: 899 us -> 350 us
  starting transfers between devices: 1.77 us -> 110 us
  matrix products: 175 us -> 97.5 us
  local copies, waits for them, and re-layouts: 96.2 us -> 19.3 us
  blocking collectives: 61 us -> 0 us
  Pallas kernels: 0 us -> 36.7 us
  other arithmetic: 60.4 us -> 30.7 us
    reduce_scatter x11 -> x0, waiting for transfers between devices: 401 us -> none  [the longest x1 108 us: per_device(): lax.psum_scatter(right_product(mixed, output_full), 'tensor', scatter_dim...]
    all_gather x11 -> x0, waiting for transfers between devices: 368 us -> none  [the longest x1 65.5 us: per_device(): lax.all_gather(second.astype(jnp.bfloat16), 'tensor', axis=0, tiled=True)]
    ppermute x0 -> x95, waiting for transfers between devices: none -> 350 us  [send(): return lax.ppermute(value, AXES, pairs)]
    psum x1 -> x0, waiting for transfers between devices: 125 us -> none  [per_device(): lax.psum((forget_pad, bias_pad, gain_one_part, gain_two_part), ('dp', 'te...]
    ppermute x0 -> x95, starting transfers between devices: none -> 110 us  [send(): return lax.ppermute(value, AXES, pairs)]
    dot_general x66 -> x42, matrix products: 175 us -> 97.5 us  [the longest x29 36.5 us: tn(): return lax.dot_general(a, b, TN, preferred_element_type=F32)]
    psum x1 -> x0, blocking collectives: 45.5 us -> none  [per_device(): lax.psum((forget_pad, bias_pad, gain_one_part, gain_two_part), ('dp', 'te...]
    dynamic_slice x88 -> x4, local copies, waits for them, and re-layouts: 44.6 us -> 1.6 us  [reorder(): lax.dynamic_slice_in_dim(rows, (chip ^ r) * wide, wide, 1)]
  transfers between devices with their start and end apart: 23 -> 95, of which waited for: 19 -> 39; matrix products, arithmetic and copies ran while one was open for 21% -> 14% of each run, Pallas kernels for 0% -> 6%
where the time goes in v1:
time: 653 us; the launch traced here: 647 us
  waiting for transfers between devices  350 us (54%)
  starting transfers between devices  110 us (17%)
  matrix products  97.5 us (15%)
  Pallas kernels  36.7 us (6%)
  other arithmetic  30.7 us (5%)
  local copies, waits for them, and re-layouts  19.3 us (3%)
    ppermute x95, waiting for transfers between devices, send(): return lax.ppermute(value, AXES, pairs)  350 us
    ppermute x95, starting transfers between devices, send(): return lax.ppermute(value, AXES, pairs)  110 us
    dot_general x29, matrix products, tn(): return lax.dot_general(a, b, TN, preferred_element_type=F32)  36.5 us
    dot_general x5, matrix products, nn(): return jnp.dot(a, b, preferred_element_type=F32)  31.1 us
    dot_general x8, matrix products, nt(): return lax.dot_general(a, b, NT, preferred_element_type=F32)  30 us
    pallas_call x1, Pallas kernels, attend_back(): pl.pallas_call(functools.partial(backward_kernel, quarter), grid=(pairs,)...  21.1 us
    pallas_call x1, Pallas kernels, attend(): pl.pallas_call(functools.partial(forward_kernel, quarter), grid=(pairs,),...  15.6 us
  transfers between devices with their start and end apart: 95, of which 39 were waited for; matrix products, arithmetic and copies ran while one was open for 14% of the time, Pallas kernels for 6%

profile of v1, /device:TPU:0, one launch (start us, length us, event | category | flops | bytes accessed | tf_op | source)
XLA Modules:
  0.0 646.6 jit_solution(3703449351072791952)
XLA Ops:
  4.7 3.5 collective-permute-start.4
  13.7 4.0 collective-permute-start.12
  24.6 23.6 %collective-permute-done.12 = f32[6]{0:T(128)S(1)} collective-permute-done((f32[6]{0:T(128)S(1)}, f32[6]{0:T(128)S(1)}, u32[]{:S(2)}, u32[]{:S(2)}) %collective-permute-start.12) | collective-permute-done | bytes 56 | tf_op jit(solution)/shard_map/ppermute | solution.py:40
  51.0 10.7 %collective-permute-done.8 = bf16[192,1280]{1,0:T(8,128)(2,1)S(1)} collective-permute-done((bf16[192,1280]{1,0:T(8,128)(2,1)S(1)}, bf16[192,1280]{1,0:T(8,128)(2,1)S(1)}, u32[]{:S(2)}, u32[]{:S(2)}) %collective-permute-start.8) | collective-permute-done | bytes 491552 | tf_op jit(solution)/shard_map/ppermute | solution.py:40
  61.8 7.8 %collective-permute-done.9 = bf16[192,1280]{1,0:T(8,128)(2,1)S(1)} collective-permute-done((bf16[192,1280]{1,0:T(8,128)(2,1)S(1)}, bf16[192,1280]{1,0:T(8,128)(2,1)S(1)}, u32[]{:S(2)}, u32[]{:S(2)}) %collective-permute-start.9) | collective-permute-done | bytes 491552 | tf_op jit(solution)/shard_map/ppermute | solution.py:40
  71.7 6.7 %collective-permute-done.10 = bf16[192,1280]{1,0:T(8,128)(2,1)S(1)} collective-permute-done((bf16[192,1280]{1,0:T(8,128)(2,1)S(1)}, bf16[192,1280]{1,0:T(8,128)(2,1)S(1)}, u32[]{:S(2)}, u32[]{:S(2)}) %collective-permute-start.10) | collective-permute-done | bytes 491552 | tf_op jit(solution)/shard_map/ppermute | solution.py:40
  78.5 3.9 collective-permute-done.11
  91.0 4.6 collective-permute-done.16
  95.7 4.3 collective-permute-start.3
  101.8 5.3 collective-permute-done.17
  115.0 5.5 fusion.1
  120.5 6.0 fusion.162.qkv_ref
  126.5 15.6 %shard_map.237 = (bf16[1024,384]{1,0:T(8,128)(2,1)S(1)}, f32[1024,128]{1,0:T(8,128)S(1)}, f32[1024,128]{1,0:T(8,128)S(1)}) custom-call(s32[4]{0:T(128)S(1)} %pad_add_fusion.pos_ref, f32[1024,1280]{1,0:T(8,128)} %fusion.162.qkv_ref, f32[1,128]{1,0:T(1,128)S(1)} %pad_bitcast_fusion.bias_ref, s32[1,1024]{1,0:T(1,128)S(1)} %broadcast_select_fusion.13.segr_ref, ...), custom_call_target="tpu_custom_call" | custom-call | tf_op jit(solution)/shard_map/pallas_call | solution.py:289
  146.3 3.6 collective-permute-start.23
  157.3 9.0 %collective-permute-done.28 = bf16[192,2048]{1,0:T(8,128)(2,1)S(1)} collective-permute-done((bf16[192,2048]{1,0:T(8,128)(2,1)S(1)}, bf16[192,2048]{1,0:T(8,128)(2,1)S(1)}, u32[]{:S(2)}, u32[]{:S(2)}) %collective-permute-start.28) | collective-permute-done | bytes 786464 | tf_op jit(solution)/shard_map/ppermute | solution.py:40
  166.3 14.1 %collective-permute-start.24 = (bf16[256,1536]{1,0:T(8,128)(2,1)S(1)}, bf16[256,1536]{1,0:T(8,128)(2,1)S(1)}, u32[]{:S(2)}, u32[]{:S(2)}) collective-permute-start(bf16[256,1536]{1,0:T(8,128)(2,1)S(1)} %fusion.39), channel_id=1, source_target_pairs={{0,1},{1,0},{2,3},{3,2},{4,5},{5,4},{6,7},{7,6},{8,9},{9,8},{10,11... | collective-permute-start | bytes 2359304 | tf_op jit(solution)/shard_map/ppermute | solution.py:40
  180.6 11.0 %collective-permute-done.42 = bf16[256,1536]{1,0:T(8,128)(2,1)S(1)} collective-permute-done((bf16[256,1536]{1,0:T(8,128)(2,1)S(1)}, bf16[256,1536]{1,0:T(8,128)(2,1)S(1)}, u32[]{:S(2)}, u32[]{:S(2)}) %collective-permute-start.42) | collective-permute-done | bytes 786464 | tf_op jit(solution)/shard_map/ppermute | solution.py:40
  194.7 12.9 %collective-permute-done.24 = bf16[256,1536]{1,0:T(8,128)(2,1)S(1)} collective-permute-done((bf16[256,1536]{1,0:T(8,128)(2,1)S(1)}, bf16[256,1536]{1,0:T(8,128)(2,1)S(1)}, u32[]{:S(2)}, u32[]{:S(2)}) %collective-permute-start.24) | collective-permute-done | bytes 786464 | tf_op jit(solution)/shard_map/ppermute | solution.py:40
  213.0 17.6 %collective-permute-done.33 = bf16[192,2048]{1,0:T(8,128)(2,1)S(1)} collective-permute-done((bf16[192,2048]{1,0:T(8,128)(2,1)S(1)}, bf16[192,2048]{1,0:T(8,128)(2,1)S(1)}, u32[]{:S(2)}, u32[]{:S(2)}) %collective-permute-start.33) | collective-permute-done | bytes 786464 | tf_op jit(solution)/shard_map/ppermute | solution.py:40
  231.9 14.9 %collective-permute-done.34 = bf16[192,2048]{1,0:T(8,128)(2,1)S(1)} collective-permute-done((bf16[192,2048]{1,0:T(8,128)(2,1)S(1)}, bf16[192,2048]{1,0:T(8,128)(2,1)S(1)}, u32[]{:S(2)}, u32[]{:S(2)}) %collective-permute-start.34) | collective-permute-done | bytes 786464 | tf_op jit(solution)/shard_map/ppermute | solution.py:40
  248.8 5.6 fusion.9
  254.4 5.6 fusion.7
  260.0 10.0 %fusion.4 = (bf16[1024,1024]{0,1:T(8,128)(2,1)}, bf16[1024,1024]{0,1:T(8,128)(2,1)S(1)}, bf16[1024,1024]{0,1:T(8,128)(2,1)}) fusion(f32[1024,1024]{0,1:T(8,128)} %fusion.7, f32[1024,1024]{0,1:T(8,128)} %fusion.9, bf16[1024,1536]{1,0:T(8,128)(2,1)S(1)} %copy-done.16, bf16[1536,1408]{1,0:T(8,128)(2,1)} %constant_dynamic-update-slice_fusion.8), kind=kOutput, calls=%fused_computation.8 | convolution fusion | flops 3239051264 | bytes 20971520 | tf_op jit(solution)/shard_map/dot_general | solution.py:21
  289.9 3.7 fusion.15
  293.7 3.9 fusion.13
  299.9 6.7 %multiply_reduce_fusion.1 = (f32[1536]{0:T(1024)S(1)}, f32[512,1536]{1,0:T(8,128)S(1)}) fusion(bf16[256,1536]{1,0:T(8,128)(2,1)S(1)} %collective-permute-done.25, bf16[256,1536]{1,0:T(8,128)(2,1)S(1)} %multiply_convert_fusion.1, bf16[1536,2048]{1,0:T(8,128)(2,1)} %copy-done.19, bf16[1024,1024]{0,1:T(8,128)(2,1)S(1)} %copy-done.33, ...), kind=kOutput, calls=%fused_computation.23 | convolution fusion | flops 3230136832 | bytes 15210496 | tf_op jit(solution)/shard_map/dot_general | solution.py:25
  306.6 6.3 multiply_reduce_fusion
  330.5 7.7 %collective-permute-done.87 = bf16[384,512]{1,0:T(8,128)(2,1)S(1)} collective-permute-done((bf16[384,512]{1,0:T(8,128)(2,1)S(1)}, bf16[384,512]{1,0:T(8,128)(2,1)S(1)}, u32[]{:S(2)}, u32[]{:S(2)}) %collective-permute-start.87) | collective-permute-done | bytes 393248 | tf_op jit(solution)/shard_map/ppermute | solution.py:40
  340.0 22.4 %collective-permute-done.76 = bf16[384,1024]{1,0:T(8,128)(2,1)S(1)} collective-permute-done((bf16[384,1024]{1,0:T(8,128)(2,1)S(1)}, bf16[384,1024]{1,0:T(8,128)(2,1)S(1)}, u32[]{:S(2)}, u32[]{:S(2)}) %collective-permute-start.76) | collective-permute-done | bytes 786464 | tf_op jit(solution)/shard_map/ppermute | solution.py:40
  364.6 8.5 %collective-permute-done.92 = bf16[384,512]{1,0:T(8,128)(2,1)S(1)} collective-permute-done((bf16[384,512]{1,0:T(8,128)(2,1)S(1)}, bf16[384,512]{1,0:T(8,128)(2,1)S(1)}, u32[]{:S(2)}, u32[]{:S(2)}) %collective-permute-start.92) | collective-permute-done | bytes 393248 | tf_op jit(solution)/shard_map/ppermute | solution.py:40
  374.5 10.1 %collective-permute-done.46 = bf16[256,1536]{1,0:T(8,128)(2,1)S(1)} collective-permute-done((bf16[256,1536]{1,0:T(8,128)(2,1)S(1)}, bf16[256,1536]{1,0:T(8,128)(2,1)S(1)}, u32[]{:S(2)}, u32[]{:S(2)}) %collective-permute-start.46) | collective-permute-done | bytes 786464 | tf_op jit(solution)/shard_map/ppermute | solution.py:40
  387.1 14.8 %collective-permute-done.38 = bf16[256,1536]{1,0:T(8,128)(2,1)S(1)} collective-permute-done((bf16[256,1536]{1,0:T(8,128)(2,1)S(1)}, bf16[256,1536]{1,0:T(8,128)(2,1)S(1)}, u32[]{:S(2)}, u32[]{:S(2)}) %collective-permute-start.38) | collective-permute-done | bytes 786464 | tf_op jit(solution)/shard_map/ppermute | solution.py:40
  403.8 5.2 collective-permute-done.77
  411.9 7.9 %collective-permute-done.82 = bf16[384,1024]{1,0:T(8,128)(2,1)S(1)} collective-permute-done((bf16[384,1024]{1,0:T(8,128)(2,1)S(1)}, bf16[384,1024]{1,0:T(8,128)(2,1)S(1)}, u32[]{:S(2)}, u32[]{:S(2)}) %collective-permute-start.82) | collective-permute-done | bytes 786464 | tf_op jit(solution)/shard_map/ppermute | solution.py:40
  421.2 4.9 collective-permute-start.79
  426.1 32.5 %collective-permute-done.94 = bf16[192,512]{1,0:T(8,128)(2,1)S(1)} collective-permute-done((bf16[192,512]{1,0:T(8,128)(2,1)S(1)}, bf16[192,512]{1,0:T(8,128)(2,1)S(1)}, u32[]{:S(2)}, u32[]{:S(2)}) %collective-permute-start.94) | collective-permute-done | bytes 196640 | tf_op jit(solution)/shard_map/ppermute | solution.py:40
  463.5 11.4 %collective-permute-done.84 = bf16[192,1024]{1,0:T(8,128)(2,1)S(1)} collective-permute-done((bf16[192,1024]{1,0:T(8,128)(2,1)S(1)}, bf16[192,1024]{1,0:T(8,128)(2,1)S(1)}, u32[]{:S(2)}, u32[]{:S(2)}) %collective-permute-start.84) | collective-permute-done | bytes 393248 | tf_op jit(solution)/shard_map/ppermute | solution.py:40
  476.7 4.0 convolution_convert_fusion.gmix_ref
  480.7 21.1 %shard_map.238 = (bf16[1024,1280]{1,0:T(8,128)(2,1)S(1)}, f32[1,128]{1,0:T(1,128)S(1)}) custom-call(s32[4]{0:T(128)S(1)} %pad_add_fusion.pos_ref, f32[1024,1280]{1,0:T(8,128)} %fusion.162.qkv_ref, f32[1,128]{1,0:T(1,128)S(1)} %pad_bitcast_fusion.bias_ref, s32[1,1024]{1,0:T(1,128)S(1)} %broadcast_select_fusion.13.segr_ref, s32[1024,1]{1,0:T(8,128)S(1)} %copy.30.segc_ref, ...), custom_call_target="tpu_custom_call" | custom-call | tf_op jit(solution)/shard_map/pallas_call | solution.py:314
  512.6 3.1 collective-permute-done.54
  517.3 3.1 collective-permute-done.55
  530.5 4.1 collective-permute-done.59
  539.7 17.5 %collective-permute-done.61 = bf16[384,640]{1,0:T(8,128)(2,1)S(1)} collective-permute-done((bf16[384,640]{1,0:T(8,128)(2,1)S(1)}, bf16[384,640]{1,0:T(8,128)(2,1)S(1)}, u32[]{:S(2)}, u32[]{:S(2)}) %collective-permute-start.61) | collective-permute-done | bytes 491552 | tf_op jit(solution)/shard_map/ppermute | solution.py:40
  559.0 5.2 collective-permute-done.72
  573.9 19.2 %collective-permute-done.62 = bf16[384,640]{1,0:T(8,128)(2,1)S(1)} collective-permute-done((bf16[384,640]{1,0:T(8,128)(2,1)S(1)}, bf16[384,640]{1,0:T(8,128)(2,1)S(1)}, u32[]{:S(2)}, u32[]{:S(2)}) %collective-permute-start.62) | collective-permute-done | bytes 491552 | tf_op jit(solution)/shard_map/ppermute | solution.py:40
  597.7 7.2 %collective-permute-done.64 = bf16[192,640]{1,0:T(8,128)(2,1)S(1)} collective-permute-done((bf16[192,640]{1,0:T(8,128)(2,1)S(1)}, bf16[192,640]{1,0:T(8,128)(2,1)S(1)}, u32[]{:S(2)}, u32[]{:S(2)}) %collective-permute-start.64) | collective-permute-done | bytes 245792 | tf_op jit(solution)/shard_map/ppermute | solution.py:40
  604.9 13.1 %collective-permute-start.69 = (bf16[192,640]{1,0:T(8,128)(2,1)S(1)}, bf16[192,640]{1,0:T(8,128)(2,1)S(1)}, u32[]{:S(2)}, u32[]{:S(2)}) collective-permute-start(bf16[192,640]{1,0:T(8,128)(2,1)S(1)} %get-tuple-element.85), channel_id=1, source_target_pairs={{0,4},{1,5},{2,6},{3,7},{4,2},{5,3},{6,0},{7,1},{8,12},{9,13},{10,... | collective-permute-start | bytes 737288 | tf_op jit(solution)/shard_map/ppermute | solution.py:40
  620.2 22.6 %collective-permute-done.69 = bf16[192,640]{1,0:T(8,128)(2,1)S(1)} collective-permute-done((bf16[192,640]{1,0:T(8,128)(2,1)S(1)}, bf16[192,640]{1,0:T(8,128)(2,1)S(1)}, u32[]{:S(2)}, u32[]{:S(2)}) %collective-permute-start.69) | collective-permute-done | bytes 245792 | tf_op jit(solution)/shard_map/ppermute | solution.py:40
  (374 shorter events, 171.9 us)
Async XLA Ops:
  11.9 37.8 %collective-permute-start = (bf16[256,1536]{1,0:T(8,128)(2,1)}, bf16[256,1536]{1,0:T(8,128)(2,1)S(1)}, u32[]{:S(2)}, u32[]{:S(2)}) collective-permute-start(bf16[256,1536]{1,0:T(8,128)(2,1)} %pad_maximum_fusion.5), channel_id=1, source_target_pairs={{0,0},{1,1},{2,4},{3,5},{4,2},{5,3},{6,6},{7,7},{8,8},{9,9},{10,12... | collective-permute-start | bytes 2359304 | tf_op jit(solution)/shard_map/ppermute | solution.py:40
  13.7 34.5 %collective-permute-start.12 = (f32[6]{0:T(128)S(1)}, f32[6]{0:T(128)S(1)}, u32[]{:S(2)}, u32[]{:S(2)}) collective-permute-start(f32[6]{0:T(128)S(1)} %copy-done.26), channel_id=1, source_target_pairs={{0,2},{1,3},{2,0},{3,1},{4,6},{5,7},{6,4},{7,5},{8,10},{9,11},{10,... | collective-permute-start | bytes 80 | tf_op jit(solution)/shard_map/ppermute | solution.py:40
  17.7 64.8 %collective-permute-start.13 = (s32[1,1024]{1,0:T(1,128)S(1)}, s32[1,1024]{1,0:T(1,128)S(1)}, u32[]{:S(2)}, u32[]{:S(2)}) collective-permute-start(s32[1,1024]{1,0:T(1,128)S(1)} %copy-done.22), channel_id=1, source_target_pairs={{0,4},{1,5},{2,6},{3,7},{4,0},{5,1},{6,2},{7,3},{8,12},{9,13},{10,... | collective-permute-start | bytes 12296 | tf_op jit(solution)/shard_map/ppermute | solution.py:40
  22.3 28.0 %collective-permute-start.6 = (bf16[192,1280]{1,0:T(8,128)(2,1)S(1)}, bf16[192,1280]{1,0:T(8,128)(2,1)S(1)}, u32[]{:S(2)}, u32[]{:S(2)}) collective-permute-start(bf16[192,1280]{1,0:T(8,128)(2,1)S(1)} %get-tuple-element.50), channel_id=1, source_target_pairs={{0,8},{1,9},{2,10},{3,11},{4,12},{5,13},{6,14},{7,15},{8,0},{9,1},... | collective-permute-start | bytes 1474568 | tf_op jit(solution)/shard_map/ppermute | solution.py:40
  24.0 26.3 %collective-permute-start.7 = (bf16[192,1280]{1,0:T(8,128)(2,1)S(1)}, bf16[192,1280]{1,0:T(8,128)(2,1)S(1)}, u32[]{:S(2)}, u32[]{:S(2)}) collective-permute-start(bf16[192,1280]{1,0:T(8,128)(2,1)S(1)} %get-tuple-element.48), channel_id=1, source_target_pairs={{0,8},{1,9},{2,10},{3,11},{4,12},{5,13},{6,14},{7,15},{8,0},{9,1},... | collective-permute-start | bytes 1474568 | tf_op jit(solution)/shard_map/ppermute | solution.py:40
  61.7 28.1 %collective-permute-start.2 = (bf16[256,1536]{1,0:T(8,128)(2,1)S(1)}, bf16[256,1536]{1,0:T(8,128)(2,1)S(1)}, u32[]{:S(2)}, u32[]{:S(2)}) collective-permute-start(bf16[256,1536]{1,0:T(8,128)(2,1)S(1)} %collective-permute-done), channel_id=1, source_target_pairs={{0,1},{1,0},{2,3},{3,2},{4,5},{5,4},{6,7},{7,6},{8,9},{9,8},{10,11... | collective-permute-start | bytes 2359304 | tf_op jit(solution)/shard_map/ppermute | solution.py:40
  85.7 23.3 %collective-permute-start.18 = (bf16[192,1408]{1,0:T(8,128)(2,1)S(1)}, bf16[192,1408]{1,0:T(8,128)(2,1)S(1)}, u32[]{:S(2)}, u32[]{:S(2)}) collective-permute-start(bf16[192,1408]{1,0:T(8,128)(2,1)S(1)} %get-tuple-element.29), channel_id=1, source_target_pairs={{0,16},{1,17},{2,18},{3,19},{4,20},{5,21},{6,22},{7,23},{8,24},{9,... | collective-permute-start | bytes 1622024 | tf_op jit(solution)/shard_map/ppermute | solution.py:40
  86.6 23.8 %collective-permute-start.19 = (bf16[192,1408]{1,0:T(8,128)(2,1)S(1)}, bf16[192,1408]{1,0:T(8,128)(2,1)S(1)}, u32[]{:S(2)}, u32[]{:S(2)}) collective-permute-start(bf16[192,1408]{1,0:T(8,128)(2,1)S(1)} %get-tuple-element.30), channel_id=1, source_target_pairs={{0,16},{1,17},{2,18},{3,19},{4,20},{5,21},{6,22},{7,23},{8,24},{9,... | collective-permute-start | bytes 1622024 | tf_op jit(solution)/shard_map/ppermute | solution.py:40
  89.9 24.3 %collective-permute-start.1 = (bf16[256,1536]{1,0:T(8,128)(2,1)S(1)}, bf16[256,1536]{1,0:T(8,128)(2,1)S(1)}, u32[]{:S(2)}, u32[]{:S(2)}) collective-permute-start(bf16[256,1536]{1,0:T(8,128)(2,1)S(1)} %collective-permute-done), channel_id=1, source_target_pairs={{0,4},{1,5},{2,6},{3,7},{4,0},{5,1},{6,2},{7,3},{8,12},{9,13},{10,... | collective-permute-start | bytes 2359304 | tf_op jit(solution)/shard_map/ppermute | solution.py:40
  107.1 45.5 %collective-permute-start.40 = (bf16[256,1536]{1,0:T(8,128)(2,1)S(1)}, bf16[256,1536]{1,0:T(8,128)(2,1)S(1)}, u32[]{:S(2)}, u32[]{:S(2)}) collective-permute-start(bf16[256,1536]{1,0:T(8,128)(2,1)S(1)} %copy-done.7), channel_id=1, source_target_pairs={{0,0},{1,1},{2,4},{3,5},{4,2},{5,3},{6,6},{7,7},{8,8},{9,9},{10,12... | collective-permute-start | bytes 2359304 | tf_op jit(solution)/shard_map/ppermute | solution.py:40
  109.0 33.2 %collective-permute-start.20 = (bf16[192,1408]{1,0:T(8,128)(2,1)}, bf16[192,1408]{1,0:T(8,128)(2,1)S(1)}, u32[]{:S(2)}, u32[]{:S(2)}) collective-permute-start(bf16[192,1408]{1,0:T(8,128)(2,1)} %collective-permute-done.16), channel_id=1, source_target_pairs={{0,16},{1,17},{2,18},{3,19},{4,20},{5,21},{6,22},{7,23},{8,24},{9,... | collective-permute-start | bytes 1622024 | tf_op jit(solution)/shard_map/ppermute | solution.py:40
  110.4 32.6 %collective-permute-start.21 = (bf16[192,1408]{1,0:T(8,128)(2,1)S(1)}, bf16[192,1408]{1,0:T(8,128)(2,1)S(1)}, u32[]{:S(2)}, u32[]{:S(2)}) collective-permute-start(bf16[192,1408]{1,0:T(8,128)(2,1)S(1)} %collective-permute-done.19), channel_id=1, source_target_pairs={{0,8},{1,9},{2,10},{3,11},{4,12},{5,13},{6,14},{7,15},{8,0},{9,1},... | collective-permute-start | bytes 1622024 | tf_op jit(solution)/shard_map/ppermute | solution.py:40
  150.1 30.4 %collective-permute-start.29 = (bf16[192,2048]{1,0:T(8,128)(2,1)S(1)}, bf16[192,2048]{1,0:T(8,128)(2,1)S(1)}, u32[]{:S(2)}, u32[]{:S(2)}) collective-permute-start(bf16[192,2048]{1,0:T(8,128)(2,1)S(1)} %pad_maximum_fusion.6), channel_id=1, source_target_pairs={{4,6},{5,7},{6,4},{7,5},{12,14},{13,15},{14,12},{15,13},{20,22},{2... | collective-permute-start | bytes 2359304 | tf_op jit(solution)/shard_map/ppermute | solution.py:40
  152.7 38.9 %collective-permute-start.41 = (bf16[256,1536]{1,0:T(8,128)(2,1)S(1)}, bf16[256,1536]{1,0:T(8,128)(2,1)S(1)}, u32[]{:S(2)}, u32[]{:S(2)}) collective-permute-start(bf16[256,1536]{1,0:T(8,128)(2,1)S(1)} %collective-permute-done.40), channel_id=1, source_target_pairs={{0,4},{1,5},{2,6},{3,7},{4,0},{5,1},{6,2},{7,3},{8,12},{9,13},{10,... | collective-permute-start | bytes 2359304 | tf_op jit(solution)/shard_map/ppermute | solution.py:40
  154.5 37.2 %collective-permute-start.42 = (bf16[256,1536]{1,0:T(8,128)(2,1)S(1)}, bf16[256,1536]{1,0:T(8,128)(2,1)S(1)}, u32[]{:S(2)}, u32[]{:S(2)}) collective-permute-start(bf16[256,1536]{1,0:T(8,128)(2,1)S(1)} %collective-permute-done.40), channel_id=1, source_target_pairs={{0,1},{1,0},{2,3},{3,2},{4,5},{5,4},{6,7},{7,6},{8,9},{9,8},{10,11... | collective-permute-start | bytes 2359304 | tf_op jit(solution)/shard_map/ppermute | solution.py:40
  156.9 37.7 %collective-permute-start.22 = (bf16[256,1536]{1,0:T(8,128)(2,1)S(1)}, bf16[256,1536]{1,0:T(8,128)(2,1)S(1)}, u32[]{:S(2)}, u32[]{:S(2)}) collective-permute-start(bf16[256,1536]{1,0:T(8,128)(2,1)S(1)} %slice.603), channel_id=1, source_target_pairs={{0,4},{1,5},{2,6},{3,7},{4,0},{5,1},{6,2},{7,3},{8,12},{9,13},{10,... | collective-permute-start | bytes 2359304 | tf_op jit(solution)/shard_map/ppermute | solution.py:40
  166.3 41.3 %collective-permute-start.24 = (bf16[256,1536]{1,0:T(8,128)(2,1)S(1)}, bf16[256,1536]{1,0:T(8,128)(2,1)S(1)}, u32[]{:S(2)}, u32[]{:S(2)}) collective-permute-start(bf16[256,1536]{1,0:T(8,128)(2,1)S(1)} %fusion.39), channel_id=1, source_target_pairs={{0,1},{1,0},{2,3},{3,2},{4,5},{5,4},{6,7},{7,6},{8,9},{9,8},{10,11... | collective-permute-start | bytes 2359304 | tf_op jit(solution)/shard_map/ppermute | solution.py:40
  193.3 38.4 %collective-permute-start.32 = (bf16[192,2048]{1,0:T(8,128)(2,1)S(1)}, bf16[192,2048]{1,0:T(8,128)(2,1)S(1)}, u32[]{:S(2)}, u32[]{:S(2)}) collective-permute-start(bf16[192,2048]{1,0:T(8,128)(2,1)S(1)} %get-tuple-element.32), channel_id=1, source_target_pairs={{0,16},{1,17},{2,18},{3,19},{4,20},{5,21},{6,22},{7,23},{8,24},{9,... | collective-permute-start | bytes 2359304 | tf_op jit(solution)/shard_map/ppermute | solution.py:40
  194.6 36.5 %collective-permute-start.31 = (bf16[192,2048]{1,0:T(8,128)(2,1)S(1)}, bf16[192,2048]{1,0:T(8,128)(2,1)S(1)}, u32[]{:S(2)}, u32[]{:S(2)}) collective-permute-start(bf16[192,2048]{1,0:T(8,128)(2,1)S(1)} %get-tuple-element.33), channel_id=1, source_target_pairs={{0,8},{1,9},{2,10},{3,11},{4,12},{5,13},{6,14},{7,15},{8,0},{9,1},... | collective-permute-start | bytes 2359304 | tf_op jit(solution)/shard_map/ppermute | solution.py:40
  207.6 23.0 %collective-permute-start.33 = (bf16[192,2048]{1,0:T(8,128)(2,1)S(1)}, bf16[192,2048]{1,0:T(8,128)(2,1)S(1)}, u32[]{:S(2)}, u32[]{:S(2)}) collective-permute-start(bf16[192,2048]{1,0:T(8,128)(2,1)S(1)} %get-tuple-element.33), channel_id=1, source_target_pairs={{0,16},{1,17},{2,18},{3,19},{4,20},{5,21},{6,22},{7,23},{8,24},{9,... | collective-permute-start | bytes 2359304 | tf_op jit(solution)/shard_map/ppermute | solution.py:40
  212.1 34.6 %collective-permute-start.34 = (bf16[192,2048]{1,0:T(8,128)(2,1)S(1)}, bf16[192,2048]{1,0:T(8,128)(2,1)S(1)}, u32[]{:S(2)}, u32[]{:S(2)}) collective-permute-start(bf16[192,2048]{1,0:T(8,128)(2,1)S(1)} %collective-permute-done.30), channel_id=1, source_target_pairs={{0,16},{1,17},{2,18},{3,19},{4,20},{5,21},{6,22},{7,23},{8,24},{9,... | collective-permute-start | bytes 2359304 | tf_op jit(solution)/shard_map/ppermute | solution.py:40
  298.1 23.8 %collective-permute-start.91 = (bf16[384,512]{1,0:T(8,128)(2,1)}, bf16[384,512]{1,0:T(8,128)(2,1)}, u32[]{:S(2)}, u32[]{:S(2)}) collective-permute-start(bf16[384,512]{1,0:T(8,128)(2,1)} %convolution_convert_fusion.17), channel_id=1, source_target_pairs={{0,16},{1,17},{2,18},{3,19},{4,20},{5,21},{6,22},{7,23},{8,24},{9,... | collective-permute-start | bytes 1179656 | tf_op jit(solution)/shard_map/ppermute | solution.py:40
  299.8 24.0 %collective-permute-start.37 = (bf16[256,1536]{1,0:T(8,128)(2,1)S(1)}, bf16[256,1536]{1,0:T(8,128)(2,1)}, u32[]{:S(2)}, u32[]{:S(2)}) collective-permute-start(bf16[256,1536]{1,0:T(8,128)(2,1)S(1)} %slice.600), channel_id=1, source_target_pairs={{0,4},{1,5},{2,6},{3,7},{4,0},{5,1},{6,2},{7,3},{8,12},{9,13},{10,... | collective-permute-start | bytes 2359304 | tf_op jit(solution)/shard_map/ppermute | solution.py:40
  318.6 45.9 %collective-permute-start.90 = (bf16[384,512]{1,0:T(8,128)(2,1)S(1)}, bf16[384,512]{1,0:T(8,128)(2,1)S(1)}, u32[]{:S(2)}, u32[]{:S(2)}) collective-permute-start(bf16[384,512]{1,0:T(8,128)(2,1)S(1)} %convolution_convert_fusion.19), channel_id=1, source_target_pairs={{0,16},{1,17},{2,18},{3,19},{4,20},{5,21},{6,22},{7,23},{8,24},{9,... | collective-permute-start | bytes 1179656 | tf_op jit(solution)/shard_map/ppermute | solution.py:40
  319.7 84.0 %collective-permute-start.75 = (bf16[384,1024]{1,0:T(8,128)(2,1)}, bf16[384,1024]{1,0:T(8,128)(2,1)S(1)}, u32[]{:S(2)}, u32[]{:S(2)}) collective-permute-start(bf16[384,1024]{1,0:T(8,128)(2,1)} %convolution_convert_fusion.7), channel_id=1, source_target_pairs={{0,8},{1,9},{2,10},{3,11},{4,12},{5,13},{6,14},{7,15},{8,0},{9,1},... | collective-permute-start | bytes 2359304 | tf_op jit(solution)/shard_map/ppermute | solution.py:40
  329.2 33.3 %collective-permute-start.76 = (bf16[384,1024]{1,0:T(8,128)(2,1)S(1)}, bf16[384,1024]{1,0:T(8,128)(2,1)S(1)}, u32[]{:S(2)}, u32[]{:S(2)}) collective-permute-start(bf16[384,1024]{1,0:T(8,128)(2,1)S(1)} %copy-done.29), channel_id=1, source_target_pairs={{0,8},{1,9},{2,10},{3,11},{4,12},{5,13},{6,14},{7,15},{8,0},{9,1},... | collective-permute-start | bytes 2359304 | tf_op jit(solution)/shard_map/ppermute | solution.py:40
  338.2 25.9 %collective-permute-start.81 = (bf16[384,1024]{1,0:T(8,128)(2,1)S(1)}, bf16[384,1024]{1,0:T(8,128)(2,1)S(1)}, u32[]{:S(2)}, u32[]{:S(2)}) collective-permute-start(bf16[384,1024]{1,0:T(8,128)(2,1)S(1)} %copy-done.28), channel_id=1, source_target_pairs={{0,16},{1,17},{2,18},{3,19},{4,20},{5,21},{6,22},{7,23},{8,24},{9,... | collective-permute-start | bytes 2359304 | tf_op jit(solution)/shard_map/ppermute | solution.py:40
  339.7 34.1 %collective-permute-start.44 = (bf16[256,1536]{1,0:T(8,128)(2,1)S(1)}, bf16[256,1536]{1,0:T(8,128)(2,1)S(1)}, u32[]{:S(2)}, u32[]{:S(2)}) collective-permute-start(bf16[256,1536]{1,0:T(8,128)(2,1)S(1)} %slice.599), channel_id=1, source_target_pairs={{0,4},{1,5},{2,6},{3,7},{4,0},{5,1},{6,2},{7,3},{8,12},{9,13},{10,... | collective-permute-start | bytes 2359304 | tf_op jit(solution)/shard_map/ppermute | solution.py:40
  373.1 28.8 %collective-permute-start.38 = (bf16[256,1536]{1,0:T(8,128)(2,1)S(1)}, bf16[256,1536]{1,0:T(8,128)(2,1)S(1)}, u32[]{:S(2)}, u32[]{:S(2)}) collective-permute-start(bf16[256,1536]{1,0:T(8,128)(2,1)S(1)} %fusion.35), channel_id=1, source_target_pairs={{0,1},{1,0},{2,3},{3,2},{4,5},{5,4},{6,7},{7,6},{8,9},{9,8},{10,11... | collective-permute-start | bytes 2359304 | tf_op jit(solution)/shard_map/ppermute | solution.py:40
  373.8 37.4 %collective-permute-start.80 = (bf16[384,1024]{1,0:T(8,128)(2,1)S(1)}, bf16[384,1024]{1,0:T(8,128)(2,1)S(1)}, u32[]{:S(2)}, u32[]{:S(2)}) collective-permute-start(bf16[384,1024]{1,0:T(8,128)(2,1)S(1)} %copy-done.27), channel_id=1, source_target_pairs={{0,16},{1,17},{2,18},{3,19},{4,20},{5,21},{6,22},{7,23},{8,24},{9,... | collective-permute-start | bytes 2359304 | tf_op jit(solution)/shard_map/ppermute | solution.py:40
  384.6 36.3 %collective-permute-start.88 = (bf16[192,512]{1,0:T(8,128)(2,1)S(1)}, bf16[192,512]{1,0:T(8,128)(2,1)S(1)}, u32[]{:S(2)}, u32[]{:S(2)}) collective-permute-start(bf16[192,512]{1,0:T(8,128)(2,1)S(1)} %get-tuple-element.86), channel_id=1, source_target_pairs={{4,6},{5,7},{6,4},{7,5},{12,14},{13,15},{14,12},{15,13},{20,22},{2... | collective-permute-start | bytes 589832 | tf_op jit(solution)/shard_map/ppermute | solution.py:40
  386.2 22.8 %collective-permute-start.77 = (bf16[384,1024]{1,0:T(8,128)(2,1)S(1)}, bf16[384,1024]{1,0:T(8,128)(2,1)S(1)}, u32[]{:S(2)}, u32[]{:S(2)}) collective-permute-start(bf16[384,1024]{1,0:T(8,128)(2,1)S(1)} %add_convert_fusion.4), channel_id=1, source_target_pairs={{0,16},{1,17},{2,18},{3,19},{4,20},{5,21},{6,22},{7,23},{8,24},{9,... | collective-permute-start | bytes 2359304 | tf_op jit(solution)/shard_map/ppermute | solution.py:40
  409.0 51.0 %collective-permute-start.48 = (bf16[256,1536]{1,0:T(8,128)(2,1)S(1)}, bf16[256,1536]{1,0:T(8,128)(2,1)S(1)}, u32[]{:S(2)}, u32[]{:S(2)}) collective-permute-start(bf16[256,1536]{1,0:T(8,128)(2,1)S(1)} %get-tuple-element.43), channel_id=1, source_target_pairs={{0,1},{1,0},{2,3},{3,2},{4,5},{5,4},{6,7},{7,6},{8,9},{9,8},{10,11... | collective-permute-start | bytes 2359304 | tf_op jit(solution)/shard_map/ppermute | solution.py:40
  419.8 39.4 %collective-permute-start.78 = (bf16[192,1024]{1,0:T(8,128)(2,1)S(1)}, bf16[192,1024]{1,0:T(8,128)(2,1)S(1)}, u32[]{:S(2)}, u32[]{:S(2)}) collective-permute-start(bf16[192,1024]{1,0:T(8,128)(2,1)S(1)} %get-tuple-element.60), channel_id=1, source_target_pairs={{4,6},{5,7},{6,4},{7,5},{12,14},{13,15},{14,12},{15,13},{20,22},{2... | collective-permute-start | bytes 1179656 | tf_op jit(solution)/shard_map/ppermute | solution.py:40
  421.0 37.6 %collective-permute-start.94 = (bf16[192,512]{1,0:T(8,128)(2,1)S(1)}, bf16[192,512]{1,0:T(8,128)(2,1)S(1)}, u32[]{:S(2)}, u32[]{:S(2)}) collective-permute-start(bf16[192,512]{1,0:T(8,128)(2,1)S(1)} %get-tuple-element.89), channel_id=1, source_target_pairs={{0,4},{1,5},{2,6},{3,7},{4,2},{5,3},{6,0},{7,1},{8,12},{9,13},{10,... | collective-permute-start | bytes 589832 | tf_op jit(solution)/shard_map/ppermute | solution.py:40
  421.1 55.4 %collective-permute-start.47 = (bf16[256,1536]{1,0:T(8,128)(2,1)S(1)}, bf16[256,1536]{1,0:T(8,128)(2,1)S(1)}, u32[]{:S(2)}, u32[]{:S(2)}) collective-permute-start(bf16[256,1536]{1,0:T(8,128)(2,1)S(1)} %get-tuple-element.43), channel_id=1, source_target_pairs={{0,4},{1,5},{2,6},{3,7},{4,0},{5,1},{6,2},{7,3},{8,12},{9,13},{10,... | collective-permute-start | bytes 2359304 | tf_op jit(solution)/shard_map/ppermute | solution.py:40
  421.2 41.6 %collective-permute-start.79 = (bf16[192,1024]{1,0:T(8,128)(2,1)S(1)}, bf16[192,1024]{1,0:T(8,128)(2,1)S(1)}, u32[]{:S(2)}, u32[]{:S(2)}) collective-permute-start(bf16[192,1024]{1,0:T(8,128)(2,1)S(1)} %get-tuple-element.61), channel_id=1, source_target_pairs={{0,4},{1,5},{2,6},{3,7},{4,2},{5,3},{6,0},{7,1},{8,12},{9,13},{10,... | collective-permute-start | bytes 1179656 | tf_op jit(solution)/shard_map/ppermute | solution.py:40
  462.8 181.1 %collective-permute-start.39 = (bf16[256,1536]{1,0:T(8,128)(2,1)S(1)}, bf16[256,1536]{1,0:T(8,128)(2,1)S(1)}, u32[]{:S(2)}, u32[]{:S(2)}) collective-permute-start(bf16[256,1536]{1,0:T(8,128)(2,1)S(1)} %get-tuple-element.54), channel_id=1, source_target_pairs={{0,0},{1,1},{2,4},{3,5},{4,2},{5,3},{6,6},{7,7},{8,8},{9,9},{10,12... | collective-permute-start | bytes 2359304 | tf_op jit(solution)/shard_map/ppermute | solution.py:40
  521.9 37.1 %collective-permute-start.70 = (bf16[384,384]{1,0:T(8,128)(2,1)S(1)}, bf16[384,384]{1,0:T(8,128)(2,1)S(1)}, u32[]{:S(2)}, u32[]{:S(2)}) collective-permute-start(bf16[384,384]{1,0:T(8,128)(2,1)S(1)} %convolution_convert_fusion.27), channel_id=1, source_target_pairs={{0,8},{1,9},{2,10},{3,11},{4,12},{5,13},{6,14},{7,15},{8,0},{9,1},... | collective-permute-start | bytes 884744 | tf_op jit(solution)/shard_map/ppermute | solution.py:40
  524.0 49.8 %collective-permute-start.60 = (bf16[384,640]{1,0:T(8,128)(2,1)S(1)}, bf16[384,640]{1,0:T(8,128)(2,1)S(1)}, u32[]{:S(2)}, u32[]{:S(2)}) collective-permute-start(bf16[384,640]{1,0:T(8,128)(2,1)S(1)} %convolution_convert_fusion.15), channel_id=1, source_target_pairs={{0,8},{1,9},{2,10},{3,11},{4,12},{5,13},{6,14},{7,15},{8,0},{9,1},... | collective-permute-start | bytes 1474568 | tf_op jit(solution)/shard_map/ppermute | solution.py:40
  534.6 22.6 %collective-permute-start.61 = (bf16[384,640]{1,0:T(8,128)(2,1)S(1)}, bf16[384,640]{1,0:T(8,128)(2,1)S(1)}, u32[]{:S(2)}, u32[]{:S(2)}) collective-permute-start(bf16[384,640]{1,0:T(8,128)(2,1)S(1)} %convolution_convert_fusion.13), channel_id=1, source_target_pairs={{0,8},{1,9},{2,10},{3,11},{4,12},{5,13},{6,14},{7,15},{8,0},{9,1},... | collective-permute-start | bytes 1474568 | tf_op jit(solution)/shard_map/ppermute | solution.py:40
  538.2 27.4 %collective-permute-start.66 = (bf16[384,640]{1,0:T(8,128)(2,1)S(1)}, bf16[384,640]{1,0:T(8,128)(2,1)S(1)}, u32[]{:S(2)}, u32[]{:S(2)}) collective-permute-start(bf16[384,640]{1,0:T(8,128)(2,1)S(1)} %convolution_convert_fusion.9), channel_id=1, source_target_pairs={{0,16},{1,17},{2,18},{3,19},{4,20},{5,21},{6,22},{7,23},{8,24},{9,... | collective-permute-start | bytes 1474568 | tf_op jit(solution)/shard_map/ppermute | solution.py:40
  568.7 25.3 %collective-permute-start.65 = (bf16[384,640]{1,0:T(8,128)(2,1)S(1)}, bf16[384,640]{1,0:T(8,128)(2,1)S(1)}, u32[]{:S(2)}, u32[]{:S(2)}) collective-permute-start(bf16[384,640]{1,0:T(8,128)(2,1)S(1)} %convolution_convert_fusion.11), channel_id=1, source_target_pairs={{0,16},{1,17},{2,18},{3,19},{4,20},{5,21},{6,22},{7,23},{8,24},{9,... | collective-permute-start | bytes 1474568 | tf_op jit(solution)/shard_map/ppermute | solution.py:40
  571.9 46.2 %collective-permute-start.50 = (bf16[256,1536]{1,0:T(8,128)(2,1)S(1)}, bf16[256,1536]{1,0:T(8,128)(2,1)S(1)}, u32[]{:S(2)}, u32[]{:S(2)}) collective-permute-start(bf16[256,1536]{1,0:T(8,128)(2,1)S(1)} %slice.597), channel_id=1, source_target_pairs={{0,4},{1,5},{2,6},{3,7},{4,0},{5,1},{6,2},{7,3},{8,12},{9,13},{10,... | collective-permute-start | bytes 2359304 | tf_op jit(solution)/shard_map/ppermute | solution.py:40
  593.1 25.0 %collective-permute-start.52 = (bf16[256,1536]{1,0:T(8,128)(2,1)S(1)}, bf16[256,1536]{1,0:T(8,128)(2,1)S(1)}, u32[]{:S(2)}, u32[]{:S(2)}) collective-permute-start(bf16[256,1536]{1,0:T(8,128)(2,1)S(1)} %fusion.31), channel_id=1, source_target_pairs={{0,1},{1,0},{2,3},{3,2},{4,5},{5,4},{6,7},{7,6},{8,9},{9,8},{10,11... | collective-permute-start | bytes 2359304 | tf_op jit(solution)/shard_map/ppermute | solution.py:40
  597.0 23.2 %collective-permute-start.68 = (bf16[192,640]{1,0:T(8,128)(2,1)S(1)}, bf16[192,640]{1,0:T(8,128)(2,1)S(1)}, u32[]{:S(2)}, u32[]{:S(2)}) collective-permute-start(bf16[192,640]{1,0:T(8,128)(2,1)S(1)} %get-tuple-element.84), channel_id=1, source_target_pairs={{4,6},{5,7},{6,4},{7,5},{12,14},{13,15},{14,12},{15,13},{20,22},{2... | collective-permute-start | bytes 737288 | tf_op jit(solution)/shard_map/ppermute | solution.py:40
  604.9 37.8 %collective-permute-start.69 = (bf16[192,640]{1,0:T(8,128)(2,1)S(1)}, bf16[192,640]{1,0:T(8,128)(2,1)S(1)}, u32[]{:S(2)}, u32[]{:S(2)}) collective-permute-start(bf16[192,640]{1,0:T(8,128)(2,1)S(1)} %get-tuple-element.85), channel_id=1, source_target_pairs={{0,4},{1,5},{2,6},{3,7},{4,2},{5,3},{6,0},{7,1},{8,12},{9,13},{10,... | collective-permute-start | bytes 737288 | tf_op jit(solution)/shard_map/ppermute | solution.py:40
  619.4 24.5 %collective-permute-start.53 = (bf16[256,1536]{1,0:T(8,128)(2,1)S(1)}, bf16[256,1536]{1,0:T(8,128)(2,1)S(1)}, u32[]{:S(2)}, u32[]{:S(2)}) collective-permute-start(bf16[256,1536]{1,0:T(8,128)(2,1)S(1)} %fusion.29), channel_id=1, source_target_pairs={{0,0},{1,1},{2,4},{3,5},{4,2},{5,3},{6,6},{7,7},{8,8},{9,9},{10,12... | collective-permute-start | bytes 2359304 | tf_op jit(solution)/shard_map/ppermute | solution.py:40
  (82 other events, 1059.8 us)

commit v2 on v1

v2 whole, which is shorter than its diff:
```python
import functools

import jax
import jax.numpy as jnp
from jax import lax
from jax.experimental import pallas as pl
from jax.experimental.pallas import tpu as pltpu
from jax.sharding import PartitionSpec as P

HEAD = 64
PAIR = 2 * HEAD
EPS = 1e-06
F32 = jnp.float32
BF16 = jnp.bfloat16
NT = (((1,), (1,)), ((), ()))
TN = (((0,), (0,)), ((), ()))
AXES = ("dp", "tensor")


def nn(a, b):
    return jnp.dot(a, b, preferred_element_type=F32)


def nt(a, b):
    return lax.dot_general(a, b, NT, preferred_element_type=F32)


def tn(a, b):
    return lax.dot_general(a, b, TN, preferred_element_type=F32)


class Box:
    def __init__(self, v):
        self.v = v


def val(value):
    return value.v if isinstance(value, Box) else value


def boxes(tree):
    if isinstance(tree, Box):
        return [tree]
    assert isinstance(tree, (list, tuple)), type(tree)
    return [b for item in tree for b in boxes(item)]


def send(value, move):
    tensor = lax.axis_size("tensor")
    pairs = []
    for d in range(lax.axis_size("dp")):
        for t in range(tensor):
            to = move(d, t)
            if to is not None:
                pairs.append((d * tensor + t, to[0] * tensor + to[1]))
    return Box(lax.ppermute(val(value), AXES, pairs))


def to_home(d, t):
    return (d ^ 1, t ^ 2) if (d & 1) != (t >> 1) else (d, t)


def over_core(d, t):
    return (d ^ 1, t)


def over_z(d, t):
    return (d, t ^ 1)


def over_chip(bit):
    return lambda d, t: (d ^ (2 << bit), t)


def over_half(d, t):
    return (d, t ^ 2)


def over_core_half(d, t):
    return (d ^ 1, t ^ 2)


def hold(value, *others):
    held = boxes(others)
    result, new = lax.optimization_barrier((jax.tree.map(val, value, is_leaf=lambda x: isinstance(x, Box)), [b.v for b in held]))
    for b, v in zip(held, new):
        b.v = v
    if isinstance(value, Box):
        value.v = result
        return value
    return result


def meet(critical, *others):
    return hold(hold(critical), *others)


def rows_of(pieces):
    return jnp.concatenate([val(p) for p in pieces], axis=0)


def block_of(pos_ref, at, size):
    return pl.ds(pl.multiple_of(pos_ref[at] * size, size), size)


def lane_of(pair, h):
    return jnp.where(pair == 2, 2 + HEAD * h, HEAD * pair + h)


def pack_kernel(core_ref, query_ref, key_ref, value_ref, forget_ref, gain_ref, bias_ref, mine_ref, other_ref):
    share = gain_ref.shape[1]
    diagonal = lax.broadcasted_iota(jnp.int32, (share, share), 0) == lax.broadcasted_iota(jnp.int32, (share, share), 1)
    gain = jnp.sum(jnp.where(diagonal, gain_ref[...].astype(F32), 0.0), axis=1, keepdims=True)
    lane = lax.broadcasted_iota(jnp.int32, (share, PAIR), 1)
    low_lanes = lane < HEAD
    first = core_ref[0] == 0
    parts = [ref[...].astype(F32) * gain for ref in (query_ref, key_ref, value_ref)]
    forget = forget_ref[...].astype(F32) * gain
    bias = bias_ref[...]
    pieces = []
    for _ in range(3):
        piece = bias.astype(BF16).astype(F32)
        pieces.append(piece)
        bias = bias - piece
    halves = []
    for h in range(2):
        three = [p if h == 0 else pltpu.roll(p, p.shape[1] // 2, 1) for p in parts]
        tiles = [p[:, :PAIR] for p in three]
        lone = [p[:, PAIR : 2 * PAIR] for p in three]
        tiles.append(jnp.where(low_lanes, lone[0], pltpu.roll(lone[1], HEAD, 1)))
        rest = jnp.where(lane < HEAD + 3, pltpu.roll(forget, HEAD - 3 * h, 1), gain)
        for k, piece in enumerate(pieces):
            at = HEAD + 4 + 3 * k
            moved = jnp.broadcast_to(pltpu.roll(piece, at - 3 * h, 1), (share, PAIR))
            rest = jnp.where((lane >= at) & (lane < at + 3), moved, rest)
        rest = jnp.where(lane < HEAD + 13, rest, 0.0)
        tiles.append(jnp.where(low_lanes, lone[2], rest))
        halves.append(tiles)
    for k in range(5):
        at = slice(k * PAIR, (k + 1) * PAIR)
        mine_ref[:, at] = jnp.where(first, halves[0][k], halves[1][k]).astype(BF16)
        other_ref[:, at] = jnp.where(first, halves[1][k], halves[0][k]).astype(BF16)


def forward_kernel(
    quarter, pos_ref, x0_ref, x1_ref, x2_ref, x3_ref, wa_ref, wb_ref, bias_ref, segr_ref, segc_ref,
    mixed_ref, xhat_ref, qkv_ref, logit_ref, lse_ref, cum_ref, cumr_ref, rel_ref,
):
    pair = pl.program_id(0)
    width = 3 * PAIR
    lane = lax.broadcasted_iota(jnp.int32, (quarter, PAIR), 1)
    low_lanes = lane < HEAD
    count = segr_ref.shape[1] // quarter

    @pl.when(pair == 0)
    def _():
        for r, x_ref in enumerate((x0_ref, x1_ref, x2_ref, x3_ref)):
            at = slice(r * quarter, (r + 1) * quarter)
            x = x_ref[...].astype(F32)
            low = (x * lax.rsqrt(jnp.mean(x * x, axis=1, keepdims=True) + EPS)).astype(BF16)
            xhat_ref[at, :] = low
            near_all = nn(low, wa_ref[...])
            far_all = nn(low, wb_ref[...])

            def near(k):
                return near_all[:, k * PAIR : (k + 1) * PAIR]

            def far(k):
                return far_all[:, k * PAIR : (k + 1) * PAIR]

            for k in range(3):
                qkv_ref[at, k * width : k * width + PAIR] = near(k).astype(BF16)
                qkv_ref[at, k * width + PAIR : k * width + 2 * PAIR] = far(k).astype(BF16)

            def both(one, two):
                return jnp.where(low_lanes, one, two).astype(BF16)

            qkv_ref[at, 2 * PAIR : 3 * PAIR] = both(near(3), pltpu.roll(far(3), HEAD, 1))
            qkv_ref[at, width + 2 * PAIR : width + 3 * PAIR] = both(pltpu.roll(near(3), HEAD, 1), far(3))
            qkv_ref[at, 2 * width + 2 * PAIR : 2 * width + 3 * PAIR] = both(near(4), pltpu.roll(far(4), HEAD, 1))
            rel_ref[at, :] = jnp.where(low_lanes, pltpu.roll(near(4), HEAD, 1), far(4)) + bias_ref[...]
        rows = lax.broadcasted_iota(jnp.int32, (quarter, quarter), 0)
        cols = lax.broadcasted_iota(jnp.int32, (quarter, quarter), 1)
        lower = (cols <= rows).astype(F32)
        carry = jnp.zeros((1, PAIR), F32)
        for a in range(count):
            logit = rel_ref[block_of(pos_ref, a, quarter), :]
            here = slice(a * quarter, (a + 1) * quarter)
            logit_ref[here, :] = logit
            logsig = jnp.minimum(logit, 0.0) - jnp.log1p(jnp.exp(-jnp.abs(logit)))
            cum = jnp.dot(lower, logsig, precision=lax.Precision.HIGHEST, preferred_element_type=F32) + carry
            carry = cum[quarter - 1 :, :]
            cum_ref[here, :] = cum
            cumr_ref[:, here] = cum.T
        lse_ref[...] = jnp.zeros(lse_ref.shape, F32)

    def columns(part):
        return pl.ds(pl.multiple_of(part * width + pair * PAIR, PAIR), PAIR)

    diag_rows = lax.broadcasted_iota(jnp.int32, (quarter, quarter), 0)
    diag_cols = lax.broadcasted_iota(jnp.int32, (quarter, quarter), 1)
    for a in range(count):
        query = (qkv_ref[block_of(pos_ref, a, quarter), columns(0)] * 0.125).astype(BF16)
        seg_q = segc_ref[a * quarter : (a + 1) * quarter, :]
        spans = range(max(0, a - 512 // quarter), a + 1)
        outs = []
        for h in range(2):
            head = lane_of(pair, h)
            mine = (lane >= HEAD) if h else low_lanes
            query_h = jnp.where(mine, query, jnp.zeros_like(query))
            scores = []
            for b in spans:
                keys = qkv_ref[block_of(pos_ref, b, quarter), columns(1)]
                s = nt(query_h, keys) - cumr_ref[pl.ds(head, 1), b * quarter : (b + 1) * quarter]
                allowed = seg_q == segr_ref[:, b * quarter : (b + 1) * quarter]
                if a == b:
                    allowed &= diag_cols <= diag_rows
                scores.append(jnp.where(allowed, s, -jnp.inf))
            top = functools.reduce(jnp.maximum, [jnp.max(s, axis=1, keepdims=True) for s in scores])
            expd = [jnp.exp(s - top) for s in scores]
            total = functools.reduce(jnp.add, [jnp.sum(e, axis=1, keepdims=True) for e in expd])
            scale = 1.0 / total
            out = None
            for e, b in zip(expd, spans):
                values = qkv_ref[block_of(pos_ref, b, quarter), columns(2)]
                part = nn((e * scale).astype(BF16), values)
                out = part if out is None else out + part
            outs.append(out)
            lse = top + jnp.log(total)
            at = pl.ds(a * quarter, quarter)
            lse_ref[at, :] = jnp.where(lane == head, lse, lse_ref[at, :])
        mixed_ref[block_of(pos_ref, a, quarter), columns(0)] = jnp.where(low_lanes, outs[0], outs[1]).astype(BF16)


def backward_kernel(
    quarter, pos_ref, qkv_ref, logit_ref, segr_ref, segc_ref, lse_ref, cum_ref, gmix_ref,
    gnear_ref, gfar_ref, gbias_ref, lser_ref, gcol_ref, grow_ref, grad_ref, gk_ref, gv_ref,
):
    pair = pl.program_id(0)
    pairs = pl.num_programs(0)
    width = 3 * PAIR
    lane = lax.broadcasted_iota(jnp.int32, (quarter, PAIR), 1)
    low_lanes = lane < HEAD
    count = segr_ref.shape[1] // quarter

    @pl.when(pair == 0)
    def _():
        for a in range(count):
            at = slice(a * quarter, (a + 1) * quarter)
            lser_ref[:, at] = lse_ref[at, :].T
        gcol_ref[...] = jnp.zeros(gcol_ref.shape, F32)
        grow_ref[...] = jnp.zeros(grow_ref.shape, F32)

    def columns(part):
        return pl.ds(pl.multiple_of(part * width + pair * PAIR, PAIR), PAIR)

    diag_rows = lax.broadcasted_iota(jnp.int32, (quarter, quarter), 0)
    diag_cols = lax.broadcasted_iota(jnp.int32, (quarter, quarter), 1)
    gk_ref[...] = jnp.zeros(gk_ref.shape, F32)
    gv_ref[...] = jnp.zeros(gv_ref.shape, F32)
    for a in range(count):
        here = slice(a * quarter, (a + 1) * quarter)
        query = (qkv_ref[block_of(pos_ref, a, quarter), columns(0)] * 0.125).astype(BF16)
        gout = gmix_ref[block_of(pos_ref, a, quarter), columns(0)]
        seg_q = segr_ref[:, here]
        spans = range(max(0, a - 512 // quarter), a + 1)
        grad_query = None
        for h in range(2):
            head = lane_of(pair, h)
            mine = (lane >= HEAD) if h else low_lanes
            query_h = jnp.where(mine, query, jnp.zeros_like(query))
            gout_h = jnp.where(mine, gout, jnp.zeros_like(gout))
            lse = lser_ref[pl.ds(head, 1), here]
            probs, gprobs = [], []
            inner = None
            for b in spans:
                there = slice(b * quarter, (b + 1) * quarter)
                keys = qkv_ref[block_of(pos_ref, b, quarter), columns(1)]
                values = qkv_ref[block_of(pos_ref, b, quarter), columns(2)]
                cum_k = jnp.sum(jnp.where(lane == head, cum_ref[there, :], 0.0), axis=1, keepdims=True)
                s = nt(keys, query_h) - cum_k
                allowed = segc_ref[there, :] == seg_q
                if a == b:
                    allowed &= diag_rows <= diag_cols
                p = jnp.where(allowed, jnp.exp(s - lse), 0.0)
                g = nt(values, gout_h)
                probs.append(p)
                gprobs.append(g)
                part = jnp.sum(p * g, axis=0, keepdims=True)
                inner = part if inner is None else inner + part
            row_sum = None
            for p, g, b in zip(probs, gprobs, spans):
                there = slice(b * quarter, (b + 1) * quarter)
                keys = (qkv_ref[block_of(pos_ref, b, quarter), columns(1)] * 0.125).astype(BF16)
                keys_h = jnp.where(mine, keys, jnp.zeros_like(keys))
                gs = p * (g - inner)
                part = jnp.sum(gs, axis=0, keepdims=True)
                row_sum = part if row_sum is None else row_sum + part
                col_sum = jnp.sum(gs, axis=1, keepdims=True)
                gcol_ref[there, :] += jnp.where(lane == head, col_sum, 0.0)
                low = gs.astype(BF16)
                gk_ref[there, :] += nn(low, query_h)
                gv_ref[there, :] += nn(p.astype(BF16), gout_h)
                part = tn(low, keys_h)
                grad_query = part if grad_query is None else grad_query + part
            grow_ref[pl.ds(head, 1), here] = row_sum
        grad_ref[block_of(pos_ref, a, quarter), columns(0)] = grad_query
    for a in range(count):
        here = slice(a * quarter, (a + 1) * quarter)
        grad_ref[block_of(pos_ref, a, quarter), columns(1)] = gk_ref[here, :]
        grad_ref[block_of(pos_ref, a, quarter), columns(2)] = gv_ref[here, :]

    @pl.when(pair == pairs - 1)
    def _():
        upper = (diag_cols >= diag_rows).astype(F32)
        carry = jnp.zeros((1, PAIR), F32)
        bias = jnp.zeros((1, PAIR), F32)
        real = (lane % HEAD) < pairs
        for a in reversed(range(count)):
            here = slice(a * quarter, (a + 1) * quarter)
            at = block_of(pos_ref, a, quarter)
            logit = logit_ref[here, :]
            gcum = jnp.where(real, grow_ref[:, here].T - gcol_ref[here, :], 0.0)
            back = jnp.dot(upper, gcum, precision=lax.Precision.HIGHEST, preferred_element_type=F32) + carry
            carry = back[:1, :]
            glogit = jnp.where(real, back * (1.0 / (1.0 + jnp.exp(logit))), 0.0)
            bias = bias + jnp.sum(glogit, axis=0, keepdims=True)

            def grad(part, k):
                return grad_ref[at, part * width + k * PAIR : part * width + (k + 1) * PAIR]

            for k in range(3):
                gnear_ref[at, k * PAIR : (k + 1) * PAIR] = grad(k, 0).astype(BF16)
                gfar_ref[at, k * PAIR : (k + 1) * PAIR] = grad(k, 1).astype(BF16)
            q_last, k_last, v_last = grad(0, 2), grad(1, 2), grad(2, 2)
            k_roll = pltpu.roll(k_last, HEAD, 1)
            gnear_ref[at, 3 * PAIR : 4 * PAIR] = jnp.where(low_lanes, q_last, k_roll).astype(BF16)
            gnear_ref[at, 4 * PAIR :] = jnp.where(low_lanes, v_last, pltpu.roll(glogit, HEAD, 1)).astype(BF16)
            gfar_ref[at, 3 * PAIR : 4 * PAIR] = jnp.where(low_lanes, pltpu.roll(q_last, HEAD, 1), k_last).astype(BF16)
            gfar_ref[at, 4 * PAIR :] = jnp.where(low_lanes, pltpu.roll(v_last, HEAD, 1), glogit).astype(BF16)
        gbias_ref[...] = bias


def full_spec(shape):
    return pl.BlockSpec(shape, lambda *_: (0,) * len(shape))


NO_COST = pl.CostEstimate(flops=0, bytes_accessed=0, transcendentals=0)


def params():
    return pltpu.CompilerParams(vmem_limit_bytes=56 * 2**20, dimension_semantics=("arbitrary",))


def pack_one(core, query, keys, values, forget, gain, bias):
    share = gain.shape[1]
    out = jax.ShapeDtypeStruct((share, 5 * PAIR), BF16)
    return pl.pallas_call(
        pack_kernel,
        grid=(1,),
        out_shape=(out, out),
        in_specs=[
            pl.BlockSpec(memory_space=pltpu.SMEM),
            *(full_spec(w.shape) for w in (query, keys, values, forget, gain, bias)),
        ],
        out_specs=(full_spec(out.shape), full_spec(out.shape)),
        compiler_params=params(),
        cost_estimate=NO_COST,
    )(core, query, keys, values, forget, gain, bias)


def attend(pos, blocks, wa, wb, bias, seg_row, seg_col):
    quarter, wide = blocks[0].shape
    length = 4 * quarter
    width = 3 * PAIR
    small = jax.ShapeDtypeStruct((length, PAIR), F32)
    outs = (
        jax.ShapeDtypeStruct((length, width), BF16),
        jax.ShapeDtypeStruct((length, wide), BF16),
        jax.ShapeDtypeStruct((length, 3 * width), BF16),
        small,
        small,
        small,
    )
    operands = (*blocks, wa, wb, bias, seg_row, seg_col)
    return pl.pallas_call(
        functools.partial(forward_kernel, quarter),
        grid=(3,),
        out_shape=outs,
        in_specs=[pl.BlockSpec(memory_space=pltpu.SMEM), *(full_spec(o.shape) for o in operands)],
        out_specs=tuple(full_spec(o.shape) for o in outs),
        scratch_shapes=[pltpu.VMEM((PAIR, length), F32), pltpu.VMEM((length, PAIR), F32)],
        compiler_params=params(),
        cost_estimate=NO_COST,
    )(pos, *operands)


def feed_kernel(s0_ref, s1_ref, c0_ref, c1_ref, ga_ref, gb_ref, da_ref, db_ref, *refs):
    hidden_ref, grada_ref, gradb_ref, second_ref, cot_ref, back_ref, gain_ref = refs[-7:]
    cut = da_ref.shape[1]
    block = s0_ref.shape[0]
    gain = None
    for i, (s_ref, c_ref) in enumerate(((s0_ref, c0_ref), (s1_ref, c1_ref))):
        at = slice(i * block, (i + 1) * block)
        second_ref[at, :] = s_ref[...]
        cot_ref[at, :] = c_ref[...]
        back = None
        for k, (w_ref, d_ref, grad_ref) in enumerate(((ga_ref, da_ref, grada_ref), (gb_ref, db_ref, gradb_ref))):
            both = nn(s_ref[...], w_ref[...])
            grad_hidden = nn(c_ref[...], d_ref[...]).astype(BF16).astype(F32)
            gate, upper = both[:, :cut], both[:, cut:]
            sigma = 1.0 / (1.0 + jnp.exp(-gate))
            swish = gate * sigma
            hidden_ref[at, k * cut : (k + 1) * cut] = (swish * upper).astype(BF16)
            grad_gate = (grad_hidden * upper * sigma * (1.0 + gate * (1.0 - sigma))).astype(BF16)
            grad_up = (grad_hidden * swish).astype(BF16)
            grad_ref[at, :cut] = grad_gate
            grad_ref[at, cut:] = grad_up
            part = nt(grad_gate, w_ref[:, :cut]) + nt(grad_up, w_ref[:, cut:])
            back = part if back is None else back + part
        back_ref[at, :] = back
        part = jnp.sum(s_ref[...].astype(F32) * back, axis=0, keepdims=True)
        gain = part if gain is None else gain + part
    gain_ref[...] = gain


def feed_tokens(second, cot, weights, which, before=()):
    block, wide = second[0].shape
    cut = weights[2].shape[1]
    operands = (*second, *cot, *weights)
    widths = (2 * cut, 2 * cut, 2 * cut, wide, wide)
    outs = tuple(jax.ShapeDtypeStruct((4 * block, w), BF16) for w in widths)
    outs += (jax.ShapeDtypeStruct((2 * block, wide), F32), jax.ShapeDtypeStruct((1, wide), F32))
    return pl.pallas_call(
        feed_kernel,
        grid=(1,),
        out_shape=outs,
        in_specs=[*(full_spec(o.shape) for o in operands)] + [pl.BlockSpec(memory_space=pl.ANY)] * len(before),
        out_specs=(
            *(pl.BlockSpec((2 * block, w), lambda i: (which, 0)) for w in widths),
            full_spec((2 * block, wide)),
            full_spec((1, wide)),
        ),
        input_output_aliases={len(operands) + k: k for k in range(len(before))},
        compiler_params=params(),
        cost_estimate=NO_COST,
    )(*operands, *before)


def feed_grads_kernel(
    chip_ref, second_ref, cot_ref, hidden_ref, ga_ref, gb_ref, da_ref, db_ref, outb_ref, outd_ref, outa_ref, part_ref,
):
    cut = da_ref.shape[1]
    second, cot = second_ref[...], cot_ref[...]
    outb_ref[...] = tn(second, gb_ref[...]).astype(BF16)
    outd_ref[...] = tn(cot, hidden_ref[:, cut:]).astype(BF16)
    outa_ref[:, : 2 * cut] = tn(second, ga_ref[...]).astype(BF16)
    outa_ref[:, 2 * cut :] = tn(cot, hidden_ref[:, :cut]).astype(BF16)
    part = nt(hidden_ref[:, :cut], da_ref[...]) + nt(hidden_ref[:, cut:], db_ref[...])
    part_ref[...] = part.astype(BF16)


def pairs_apart(rows, chips):
    block = rows.shape[0] // chips
    return rows_of([rows[r * block : (r + 1) * block] for r in (*range(0, chips, 2), *range(1, chips, 2))])


def feed_grads(chip, second, cot, hidden, ga, gb, da, db, chips):
    length, wide = second.shape
    block = wide // chips
    cut = da.shape[1]
    half_of = chips // 2
    if block % PAIR:
        down = tn(cot, hidden).astype(BF16)
        part = nt(hidden[:, :cut], da) + nt(hidden[:, cut:], db)
        own = jnp.concatenate([tn(second, ga).astype(BF16), down[:, :cut]], axis=1)
        own = [lax.dynamic_slice_in_dim(own, (chip[0] ^ r) * block, block, 0) for r in range(chips)]
        return tn(second, gb).astype(BF16), pairs_apart(down[:, cut:], chips), rows_of(own), part.astype(BF16)
    cols = pl.BlockSpec((length, block), lambda r, chip: (0, r))
    rows = pl.BlockSpec((block, cut), lambda r, chip: (r, 0))
    return pl.pallas_call(
        feed_grads_kernel,
        out_shape=(
            jax.ShapeDtypeStruct((wide, 2 * cut), BF16),
            jax.ShapeDtypeStruct((wide, cut), BF16),
            jax.ShapeDtypeStruct((wide, 3 * cut), BF16),
            jax.ShapeDtypeStruct((length, wide), BF16),
        ),
        grid_spec=pltpu.PrefetchScalarGridSpec(
            num_scalar_prefetch=1,
            grid=(chips,),
            in_specs=[cols, cols, *(full_spec(o.shape) for o in (hidden, ga, gb)), rows, rows],
            out_specs=(
                pl.BlockSpec((block, 2 * cut), lambda r, chip: (r, 0)),
                pl.BlockSpec((block, cut), lambda r, chip: ((r % 2) * half_of + r // 2, 0)),
                pl.BlockSpec((block, 3 * cut), lambda r, chip: (r ^ chip[0], 0)),
                pl.BlockSpec((length, block), lambda r, chip: (0, r)),
            ),
        ),
        compiler_params=params(),
        cost_estimate=NO_COST,
    )(chip, second, cot, hidden, ga, gb, da, db)


def first_grads_kernel(x_ref, near_ref, far_ref, outn_ref, outf_ref, gate_ref):
    x = x_ref[...]
    near, far = tn(x, near_ref[...]), tn(x, far_ref[...])
    outn_ref[...] = near.astype(BF16)
    outf_ref[...] = far.astype(BF16)
    gate_ref[:, :PAIR] = near[:, 4 * PAIR :]
    gate_ref[:, PAIR:] = far[:, 4 * PAIR :]


def first_grads(x_hat, near, far, chips):
    length, wide = x_hat.shape
    block = wide // chips
    cols = near.shape[1]
    half_of = chips // 2
    if block % PAIR:
        near, far = tn(x_hat, near), tn(x_hat, far)
        gate = jnp.concatenate([near[:, 4 * PAIR :], far[:, 4 * PAIR :]], axis=1)
        return near.astype(BF16), pairs_apart(far.astype(BF16), chips), gate
    return pl.pallas_call(
        first_grads_kernel,
        grid=(chips,),
        out_shape=(
            jax.ShapeDtypeStruct((wide, cols), BF16),
            jax.ShapeDtypeStruct((wide, cols), BF16),
            jax.ShapeDtypeStruct((wide, 2 * PAIR), F32),
        ),
        in_specs=[pl.BlockSpec((length, block), lambda r: (0, r)), full_spec(near.shape), full_spec(far.shape)],
        out_specs=(
            pl.BlockSpec((block, cols), lambda r: (r, 0)),
            pl.BlockSpec((block, cols), lambda r: ((r % 2) * half_of + r // 2, 0)),
            pl.BlockSpec((block, 2 * PAIR), lambda r: (r, 0)),
        ),
        compiler_params=params(),
        cost_estimate=NO_COST,
    )(x_hat, near, far)


def attend_back(pos, qkv, logit, seg_row, seg_col, lse, cum, grad_mixed, cols, quarter):
    length = qkv.shape[0]
    grads = jax.ShapeDtypeStruct((length, cols), BF16)
    return pl.pallas_call(
        functools.partial(backward_kernel, quarter),
        grid=(3,),
        out_shape=(grads, grads, jax.ShapeDtypeStruct((1, PAIR), F32)),
        in_specs=[
            pl.BlockSpec(memory_space=pltpu.SMEM),
            full_spec(qkv.shape),
            full_spec(logit.shape),
            full_spec(seg_row.shape),
            full_spec(seg_col.shape),
            full_spec(lse.shape),
            full_spec(cum.shape),
            full_spec(grad_mixed.shape),
        ],
        out_specs=(full_spec((length, cols)), full_spec((length, cols)), full_spec((1, PAIR))),
        scratch_shapes=[
            pltpu.VMEM((PAIR, length), F32),
            pltpu.VMEM((length, PAIR), F32),
            pltpu.VMEM((PAIR, length), F32),
            pltpu.VMEM((length, 9 * PAIR), F32),
            pltpu.VMEM((length, PAIR), F32),
            pltpu.VMEM((length, PAIR), F32),
        ],
        compiler_params=params(),
        cost_estimate=NO_COST,
    )(pos, qkv, logit, seg_row, seg_col, lse, cum, grad_mixed)


def unit_rows(value):
    scale = lax.rsqrt(jnp.mean(value * value, axis=-1, keepdims=True) + EPS)
    return value * scale, scale


def unit_back(value, scale, weighted):
    inner = jnp.mean(weighted * value, axis=-1, keepdims=True)
    return scale * weighted - value * (scale * scale * scale) * inner


def per_device(
    block_input, attn_gain, w_query, w_key, w_value, w_forget, forget_bias, w_output,
    mlp_gain, w_gate, w_up, w_down, segment_ids, cotangent,
):
    width = block_input.shape[1]
    quarter = block_input.shape[0]
    heads = w_forget.shape[1]
    share = w_query.shape[0]
    inner = w_output.shape[0]
    hidden_width = w_gate.shape[1]
    chips = lax.axis_size("dp") // 2
    bits = chips.bit_length() - 1
    d = lax.axis_index("dp")
    t = lax.axis_index("tensor")
    core, chip = d & 1, d >> 1
    first = core == 0
    at_home = core == t >> 1
    wide = width // chips
    half_heads = heads // 2

    def pick(one, two):
        return jnp.where(first, val(one), val(two))

    def pick_home(one, two):
        return jnp.where(at_home, val(one), val(two))

    def by_parity(mine, other):
        return pick(rows_of([mine, other]), rows_of([other, mine]))

    def reorder(rows):
        return jnp.concatenate(
            [lax.dynamic_slice_in_dim(rows, (chip ^ r) * wide, wide, 1) for r in range(chips)], axis=1
        )

    def reorder_rows(rows):
        return rows_of([lax.dynamic_slice_in_dim(rows, (chip ^ r) * wide, wide, 0) for r in range(chips)])

    planes = [[2 * k + c for k in range(chips)] for c in (0, 1)]
    up_order, down_order = list(range(bits)), list(reversed(range(bits)))

    class Pack:
        def __init__(self, mine, other):
            self.mine, self.other = mine, other

        def near(self, *others):
            self.near_other = send(hold(self.other, *others) if others else self.other, over_core)
            return self.near_other

        def cross(self, *others):
            mine, other = hold((self.mine, self.other), *others) if others else (self.mine, self.other)
            self.crossed = (send(mine, over_half), send(other, over_core_half))
            return self.crossed

        def near_rows(self):
            return by_parity(self.mine, self.near_other)

        def far_rows(self):
            return by_parity(*self.crossed)

    class Spread:
        def __init__(self, rows, order):
            self.pieces, self.order = {0: rows}, order

        def early(self):
            for bit in self.order:
                self.pieces[1 << bit] = send(self.pieces[0], over_chip(bit))
            return [self.pieces[1 << bit] for bit in self.order]

        def late(self):
            before = set(self.pieces)
            for i, bit in enumerate(self.order):
                passed = sum(1 << b for b in self.order[:i])
                for at in range(1, 1 << bits):
                    if not at & ~passed:
                        self.pieces[at | (1 << bit)] = send(self.pieces[at], over_chip(bit))
            return [v for k, v in self.pieces.items() if k not in before]

        def direct(self):
            for at in range(1, chips):
                self.pieces[at] = send(self.pieces[0], lambda d, t, at=at: (d ^ (2 * at), t))
            return [self.pieces[at] for at in range(1, chips)]

        def whole(self):
            return rows_of([self.pieces[r] for r in range(chips)])

    class Sum:
        def __init__(self, rows, order):
            cut = rows.shape[0] // 2
            self.order = order
            self.keep, self.give = Box(rows[:cut]), Box(rows[cut:])

        def made(self):
            return self.keep, self.give

        def out(self):
            self.got = send(self.give, over_chip(self.order[0]))
            return self.got

        def rest(self):
            rows = self.keep.v.astype(F32) + self.got.v.astype(F32)
            for bit in self.order[1:]:
                if self.order == down_order:
                    cut = rows.shape[0] // 2
                    self.keep, give = Box(rows[:cut]), rows[cut:]
                else:
                    blocks = [rows[k : k + wide] for k in range(0, rows.shape[0], wide)]
                    self.keep, give = Box(rows_of(blocks[0::2])), rows_of(blocks[1::2])
                self.last = send(give.astype(BF16), over_chip(bit))
                if bit != self.order[-1]:
                    rows = self.keep.v + self.last.v.astype(F32)
            return self.last

        def own(self):
            return (self.keep.v + self.last.v.astype(F32)).astype(BF16)

    class Finish:
        def near(self, rows):
            self.mine_near, other = pick(rows[:share], rows[share:]), pick(rows[share:], rows[:share])
            self.here = send(other, over_core)
            return self.here

        def far_one(self, rows):
            mine, other = pick(rows[:share], rows[share:]), pick(rows[share:], rows[:share])
            self.other = Box(other)
            self.same = send(mine, over_half)
            return self.same

        def far_two(self):
            self.cross = send(self.other, over_core_half)
            return self.cross

        def land(self):
            mine = self.mine_near.astype(F32) + self.same.v.astype(F32)
            rest = self.here.v.astype(F32) + self.cross.v.astype(F32)
            return pick(mine, rest), pick(rest, mine)

    gain_one = attn_gain.astype(F32)[:, None]
    gain_two = mlp_gain.astype(F32)[:, None]
    part, fpart = inner // 2, half_heads
    fcut = hidden_width // 2
    lanes = ((0, 0), (0, PAIR - heads))
    forget_own = jnp.pad(lax.dynamic_slice_in_dim(w_forget, d * share, share, 0), lanes)
    one = Pack(
        *pack_one(
            core.astype(jnp.int32)[None], w_query, w_key, w_value, forget_own, attn_gain[None, :],
            jnp.pad(forget_bias[None, :], lanes),
        )
    )
    out_t, down_t = w_output.T, w_down.T
    gate_scaled, up_scaled = ((w.astype(F32) * gain_two).astype(BF16) for w in (w_gate, w_up))

    def halves_of(arrays, size):
        halves = [jnp.concatenate([w[:, h * size : (h + 1) * size] for w in arrays], axis=1) for h in (0, 1)]
        return pick(*halves), pick(*halves[::-1])

    def stay(d, t):
        return (d, t ^ 1) if (d & 1) == (t >> 1) else None

    def move(d, t):
        return (d, t ^ 1) if (d & 1) != (t >> 1) else None

    one_far = one.cross()
    one.near()
    near_one = Spread(one.near_rows(), up_order)
    near_early = near_one.early()
    x_own, cot_own = Box(reorder(block_input)), Box(reorder(cotangent))

    hold(x_own, one_far, near_early)
    x_home = send(x_own, to_home)
    x_stay = send(x_own, stay)
    far_one = Spread(one.far_rows(), down_order)
    far_early = far_one.early()
    near_late = near_one.late()
    wo = Pack(*halves_of([out_t], part))
    feed_pack = Pack(*halves_of([gate_scaled, up_scaled, down_t], fcut))
    gate_pack, down_pack = Pack(*halves_of([gate_scaled, up_scaled], fcut)), Pack(*halves_of([down_t], fcut))

    hold(x_home, x_stay, far_early, near_late)
    x_move = send(x_home, move)
    x_core = send(x_home, over_core)
    far_late = far_one.late()
    wo_far = wo.cross(x_home)
    wo.near(x_home)
    seg_other = send(hold(segment_ids, x_home), over_core)
    feed_pack.near(x_home)
    near_all = Box(
        lax.all_gather(feed_pack.near_rows(), "dp", axis=0, tiled=True, axis_index_groups=planes)
    )
    seg_row = Box(pick_home(segment_ids, seg_other))
    far_bias = far_one.pieces[0][0, 4 * PAIR + HEAD + fpart + 1 :].astype(F32)
    bias_far = far_bias[:fpart] + far_bias[fpart : 2 * fpart] + far_bias[2 * fpart : 3 * fpart]
    spare = jnp.zeros((HEAD - fpart,), F32)
    bias = Box(jnp.concatenate([pick(forget_bias[:fpart], forget_bias[fpart:]), spare, bias_far, spare])[None, :])
    place = (t & 1) + 2 * core
    pos = jnp.stack([((a ^ place) >> 1) | (((a ^ place) & 1) << 1) for a in range(4)]).astype(jnp.int32)
    wa = Box(near_one.whole())

    hold(x_move, wa, bias, seg_row)
    hold(x_move, far_late)
    x_z = Box(pick_home(x_stay, x_move))
    x_both = send(x_z, over_core)
    wb = Box(far_one.whole())
    hold(x_both, wb, x_core)
    hold(x_both, wo_far)
    wo_a, wo_b = wo.near_rows(), wo.far_rows()
    wo_rows = jnp.concatenate([wo_a[:, :PAIR], wo_b[:, :PAIR], wo_a[:, PAIR:], wo_b[:, PAIR:]], axis=1)
    wo_spread = Spread(wo_rows, up_order)
    wo_sent = wo_spread.direct()
    gate_far = gate_pack.cross(x_both)
    qcols = wa.v.shape[1]

    resid = x_home.v.astype(F32)
    first_scale = unit_rows(resid)[1]
    seg_col = seg_row.v.reshape(-1, 1)
    mixed, x_hat, qkv, logit, lse, cum = attend(
        pos, [x_home.v, x_core.v, x_z.v, x_both.v], wa.v, wb.v, bias.v, seg_row.v, seg_col
    )
    mixed = hold(mixed, wo_sent, gate_far)
    wo_t = wo_spread.whole()

    def half(array, which):
        rows = array.shape[0] // 2
        return array[which * rows : (which + 1) * rows]

    order = {}

    def scatter_group(far, near, at_far=lambda far_sum: None, at_near=lambda near_sum: None, late_core=False):
        rows = far()
        far_in = send(rows[quarter:].astype(BF16), over_core)
        far_sum = Box((rows[:quarter].astype(F32) + far_in.v.astype(F32)).astype(BF16))
        at_far(far_sum)
        far_got = send(far_sum, over_z)
        rows = Box(near())
        if late_core:
            hold(rows, far_got)
        near_in = send(rows.v[quarter:].astype(BF16), over_core)
        near_sum = Box(rows.v[:quarter].astype(F32) + near_in.v.astype(F32))
        at_near(near_sum)
        hold(far_got, near_sum)
        return near_sum.v + far_got.v.astype(F32)

    sent = {}

    def weights_on(near_sum):
        sent["gate"] = Spread(gate_pack.far_rows(), up_order)
        sent["gate_sent"] = sent["gate"].direct()

    mixed = Box(mixed)
    hidden_res = Box(
        resid
        + scatter_group(
            lambda: nt(half(mixed.v, 1), wo_t),
            lambda: nt(half(mixed.v, 0), wo_t),
            lambda far_sum: hold(far_sum, mixed),
            weights_on,
        )
    )
    far_gate = sent["gate"]
    second, second_scale = unit_rows(hidden_res.v)
    second_low = Box(second.astype(BF16))
    second_z = send(second_low, over_z)
    down_far = down_pack.cross(second_low)
    second_core = send(second_low, over_core)
    hold(second_core, sent["gate_sent"])
    cot_stay = send(hold(cot_own, second_core), stay)
    hold(second_core, down_far)
    far_down = Spread(down_pack.far_rows(), down_order)
    down_sent = far_down.direct()
    cot_home = send(hold(cot_own, second_core), to_home)
    hold(near_all, second_core)
    gates_a = Box(reorder_rows(near_all.v[:, : 2 * fcut]))
    downs_a = Box(reorder_rows(near_all.v[:, 2 * fcut :]))
    hold(second_z, gates_a, downs_a)
    hold(second_z, cot_home, down_sent, cot_stay)
    second_both = send(second_z, over_core)
    cot_move = send(cot_home, move)
    cot_core = send(cot_home, over_core)
    gates_b, downs_b = Box(far_gate.whole()), Box(far_down.whole())
    hold(cot_move, second_both, gates_b, downs_b)
    cot_z = Box(pick_home(cot_stay, cot_move))
    cot_both = send(cot_z, over_core)
    hold(cot_both, cot_core)

    feed_weights = (gates_a.v, gates_b.v, downs_a.v, downs_b.v)
    made = {}

    def feed_far():
        made["far"] = feed_tokens((second_z.v, second_both.v), (cot_z.v, cot_both.v), feed_weights, 1)
        return made["far"][5]

    def feed_near():
        made["near"] = feed_tokens(
            (second_low.v, second_core.v), (cot_home.v, cot_core.v), feed_weights, 0, made["far"][:5]
        )
        return made["near"][5]

    grad_second = scatter_group(feed_far, feed_near, lambda far_sum: hold(far_sum, second_low, second_core), late_core=True)
    gain_two_part = made["far"][6] + made["near"][6]
    grad_res = Box(cot_home.v.astype(F32) + unit_back(hidden_res.v, second_scale, grad_second))
    branch = Box(grad_res.v.astype(BF16))
    laid = [Box(m) for m in made["near"][:5]]
    hold(branch, laid)
    branch_z = send(branch, over_z)
    hidden, grads_a, grads_b, second_all, cot_all = (m.v for m in laid)
    gb_rows, db_rows, a_rows, mlp_rows = feed_grads(
        chip.astype(jnp.int32)[None], second_all, cot_all, hidden, grads_a, grads_b, downs_a.v, downs_b.v, chips
    )
    gb_rows, db_rows, a_part, mlp_rows = (Box(m) for m in (gb_rows, db_rows, a_rows, mlp_rows))
    hold(branch_z, gb_rows, db_rows, a_part, mlp_rows)
    hold(branch, branch_z)
    branch_both = send(branch_z, over_core)
    branch_core = send(branch, over_core)
    gb, db = Sum(gb_rows.v, down_order), Sum(db_rows.v, up_order)
    b_out = [gb.out(), db.out()]
    branch_all = Box(rows_of([branch, branch_core, branch_z, branch_both]))

    grad_mixed = Box(nn(branch_all.v, wo_t).astype(BF16))
    mlp_out = Box(scatter_group(lambda: half(mlp_rows.v, 1), lambda: half(mlp_rows.v, 0)))
    hold(branch_all, grad_mixed)
    o_sum = Sum(tn(branch_all.v, mixed.v).astype(BF16), down_order)
    o_out = o_sum.out()
    hold(grad_mixed, o_sum.keep)
    grad_near, grad_far, grad_bias = attend_back(
        pos, qkv, logit, seg_row.v, seg_col, lse, cum, grad_mixed.v, qcols, quarter
    )
    grad_near, grad_far = Box(grad_near), Box(grad_far)
    hold(grad_near, grad_far, b_out, mlp_out)
    out_home = (hidden_res.v + mlp_out.v).astype(BF16)
    out_sent = send(out_home, to_home)
    b_late = [gb.rest(), db.rest()]
    hold(a_part, mlp_out)
    a_own = Box(
        lax.psum_scatter(a_part.v, "dp", scatter_dimension=0, tiled=True, axis_index_groups=planes)
    )
    first_parts = {}

    def first_part(which):
        first_parts[which] = nt(half(grad_near.v, which), wa.v) + nt(half(grad_far.v, which), wb.v)
        return first_parts[which]

    x_hat = Box(x_hat)

    def first_rest(near_sum):
        hold(near_sum, x_hat)
        grads = [Box(g) for g in first_grads(x_hat.v, grad_near.v, grad_far.v, chips)]
        made["qa"], made["qb"] = Sum(grads[0].v, down_order), Sum(grads[1].v, up_order)
        made["q_out"] = [made["qa"].out(), made["qb"].out()]
        made["gate"] = grads[2]
        hold(near_sum, grads[2])

    grad_first = scatter_group(
        lambda: first_part(1), lambda: first_part(0), lambda far_sum: hold(far_sum, grad_near, grad_far, x_hat), first_rest
    )
    qa, qb, gate_cols = made["qa"], made["qb"], made["gate"]
    back_home = Box((grad_res.v + unit_back(resid, first_scale, grad_first)).astype(BF16))
    hold(back_home, b_late, out_sent)
    back_sent = send(back_home, to_home)
    feed_end = Finish()
    b_same = feed_end.far_one(jnp.concatenate([gb.own(), db.own()], axis=1))
    hold(gate_cols, back_home)
    forget = jnp.concatenate([gate_cols.v[:, k * PAIR + HEAD : k * PAIR + HEAD + fpart] for k in (0, 1)], axis=1).T
    gain_part = functools.reduce(
        jnp.add, [jnp.sum(half(x_hat.v, w).astype(F32) * first_parts[w], axis=0) for w in (0, 1)]
    )
    gain_row = wa.v[:, 3 * part + fpart].astype(F32)
    small = reorder(jnp.concatenate([forget * gain_row[None, :], gain_part[None], gain_two_part], axis=0))
    small = Box(jnp.concatenate([small, jnp.pad(grad_bias, ((0, 0), (0, width - PAIR)))], axis=0))
    small_there = send(small, over_chip(0))
    hold(small, made["q_out"], small_there, o_out)
    q_late = [qa.rest(), qb.rest()]
    o_late = o_sum.rest()
    hold(feed_end.other, small)
    b_cross = feed_end.far_two()
    small = Box(small.v + small_there.v)
    hold(small, q_late, o_late)
    for bit in range(1, bits):
        small = Box(small.v + send(small, over_chip(bit)).v)
    near, far = small.v[:fpart], small.v[fpart:heads]
    gains, bias_sum = small.v[heads : heads + 2], small.v[heads + 2 :]
    spread_out = ((0, 0), (0, width - fpart))
    bias_near, bias_far = (jnp.pad(bias_sum[:, k * HEAD : k * HEAD + fpart], spread_out) for k in (0, 1))
    got = send(jnp.concatenate([far, bias_far, gains], axis=0), over_half)
    hold(a_own, q_late)
    feed_end.near(a_own.v)

    own_out = o_sum.own()
    out_halves = [
        jnp.concatenate(
            [own_out[:, h * PAIR : (h + 1) * PAIR], own_out[:, 2 * PAIR + h * HEAD : 2 * PAIR + (h + 1) * HEAD]], axis=1
        )
        for h in (0, 1)
    ]
    q_end = Finish()
    q_same = q_end.far_one(jnp.concatenate([qb.own(), out_halves[1]], axis=1))
    q_cross = q_end.far_two()
    q_here = q_end.near(jnp.concatenate([qa.own(), out_halves[0]], axis=1))
    hold(got, q_here, back_sent, b_same, b_cross)
    mine = jnp.concatenate(
        [near + got.v[:fpart], bias_near + got.v[fpart : fpart + 1], gains + got.v[fpart + 1 :]], axis=0
    )
    rest = send(mine, over_core).v
    grad_forget = pick(rows_of([mine[:fpart], rest[:fpart]]), rows_of([rest[:fpart], mine[:fpart]])).T
    bias_mine, bias_rest = mine[fpart, :fpart], rest[fpart, :fpart]
    grad_bias_out = pick(jnp.concatenate([bias_mine, bias_rest]), jnp.concatenate([bias_rest, bias_mine]))
    gains = mine[fpart + 1 :] + rest[fpart + 1 :]
    gains = lax.dynamic_slice_in_dim(gains, d * share, share, 1)
    gains = Box(gains + send(gains, over_z).v)
    hold(gains, q_same, q_cross)
    gains = gains.v
    grad_gain_one = gains[0] / attn_gain.astype(F32)
    grad_gain_two = gains[1] / mlp_gain.astype(F32)
    f_zero, f_one = feed_end.land()
    gate_sum, up_sum, down_sum = (
        jnp.concatenate([f[:, k * fcut : (k + 1) * fcut] for f in (f_zero, f_one)], axis=1) for k in range(3)
    )
    input_grad = reorder(back_sent.v).astype(F32)
    output = reorder(out_sent.v)
    q_zero, q_one = q_end.land()

    def joined(k):
        if k == 3:
            return jnp.concatenate([q_zero[:, qcols:], q_one[:, qcols:]], axis=1)
        lone = slice(3 * PAIR + k * HEAD, 3 * PAIR + (k + 1) * HEAD)
        pair = slice(k * PAIR, (k + 1) * PAIR)
        return jnp.concatenate([q_zero[:, pair], q_zero[:, lone], q_one[:, pair], q_one[:, lone]], axis=1)

    q_sums = [joined(k) for k in range(4)]

    return (
        output,
        input_grad,
        grad_gain_one,
        q_sums[0] * gain_one,
        q_sums[1] * gain_one,
        q_sums[2] * gain_one,
        grad_forget,
        grad_bias_out,
        q_sums[3].T,
        grad_gain_two,
        gate_sum * gain_two,
        up_sum * gain_two,
        down_sum.T,
    )


def solution(mesh):
    return jax.shard_map(
        per_device,
        mesh=mesh,
        in_specs=(
            P(("dp", "tensor"), None),
            P("dp"),
            P("dp", "tensor"),
            P("dp", "tensor"),
            P("dp", "tensor"),
            P(None, "tensor"),
            P("tensor"),
            P("tensor", "dp"),
            P("dp"),
            P("dp", "tensor"),
            P("dp", "tensor"),
            P("tensor", "dp"),
            P("dp", None),
            P(("dp", "tensor"), None),
        ),
        out_specs=(
            P(("dp", "tensor"), None),
            P(("dp", "tensor"), None),
            P("dp"),
            P("dp", "tensor"),
            P("dp", "tensor"),
            P("dp", "tensor"),
            P(None, "tensor"),
            P("tensor"),
            P("tensor", "dp"),
            P("dp"),
            P("dp", "tensor"),
            P("dp", "tensor"),
            P("tensor", "dp"),
        ),
        check_vma=False,
    )
```

time: 653 us -> 564 us (0.86)
  waiting for transfers between devices: 350 us -> 211 us
  matrix products: 97.5 us -> 16.2 us
  Pallas kernels: 36.7 us -> 113 us
  other arithmetic: 30.7 us -> 68.7 us
  local copies, waits for them, and re-layouts: 19.3 us -> 37.4 us
  starting transfers between devices: 110 us -> 92 us
  between operations: 2.59 us -> 16 us
    ppermute x95 -> x78, waiting for transfers between devices: 350 us -> 211 us  [send(): return Box(lax.ppermute(val(value), AXES, pairs))]
    pallas_call x2 -> x7, Pallas kernels: 36.7 us -> 113 us  [the longest x2 33.1 us: feed_tokens(): pl.pallas_call(feed_kernel, grid=(1,), out_shape=outs, in_specs=[*(full_s...]
    dot_general x29 -> x1, matrix products: 36.5 us -> 1.86 us  [tn(): return lax.dot_general(a, b, TN, preferred_element_type=F32)]
    dot_general x5 -> x1, matrix products: 31.1 us -> 2.74 us  [nn(): return jnp.dot(a, b, preferred_element_type=F32)]
    dot_general x8 -> x6, matrix products: 30 us -> 11.6 us  [nt(): return lax.dot_general(a, b, NT, preferred_element_type=F32)]
    ppermute x95 -> x78, starting transfers between devices: 110 us -> 91.7 us  [send(): return Box(lax.ppermute(val(value), AXES, pairs))]
    slice x10 -> x44, local copies, waits for them, and re-layouts: 1.81 us -> 18.2 us  [the longest x3 4.41 us: per_device(): gate_cols.v[:, k * PAIR + HEAD:k * PAIR + HEAD + fpart]]
    concatenate x6 -> x13, other arithmetic: 1.76 us -> 14 us  [the longest x6 13.1 us: rows_of(): return jnp.concatenate([val(p) for p in pieces], axis=0)]
  transfers between devices with their start and end apart: 95 -> 80, of which waited for: 39 -> 29; matrix products, arithmetic and copies ran while one was open for 14% -> 15% of each run, Pallas kernels for 6% -> 17%
where the time goes in v2:
time: 564 us; the launch traced here: 555 us
  waiting for transfers between devices  211 us (37%)
  Pallas kernels  113 us (20%)
  starting transfers between devices  92 us (16%)
  other arithmetic  68.7 us (12%)
  local copies, waits for them, and re-layouts  37.4 us (7%)
  matrix products  16.2 us (3%)
  between operations  16 us (3%)
    ppermute x78, waiting for transfers between devices, send(): return Box(lax.ppermute(val(value), AXES, pairs))  211 us
    ppermute x78, starting transfers between devices, send(): return Box(lax.ppermute(val(value), AXES, pairs))  91.7 us
    pallas_call x2, Pallas kernels, feed_tokens(): pl.pallas_call(feed_kernel, grid=(1,), out_shape=outs, in_specs=[*(full_s...  33.1 us
    pallas_call x1, Pallas kernels, attend(): pl.pallas_call(functools.partial(forward_kernel, quarter), grid=(3,), out...  25.1 us
    pallas_call x1, Pallas kernels, attend_back(): pl.pallas_call(functools.partial(backward_kernel, quarter), grid=(3,), ou...  23.6 us
    pallas_call x1, Pallas kernels, feed_grads(): pl.pallas_call(feed_grads_kernel, out_shape=(jax.ShapeDtypeStruct((wide,...  20.3 us
    concatenate x6, other arithmetic, rows_of(): return jnp.concatenate([val(p) for p in pieces], axis=0)  13.1 us
    unnamed x196, local copies, waits for them, and re-layouts  12.2 us
  transfers between devices with their start and end apart: 80, of which 29 were waited for; matrix products, arithmetic and copies ran while one was open for 15% of the time, Pallas kernels for 17%

profile of v2, /device:TPU:0, one launch (start us, length us, event | category | flops | bytes accessed | tf_op | source)
XLA Modules:
  0.0 554.6 jit_solution(17999689535638203845)
XLA Ops:
  11.2 2.2 shard_map.237
  13.9 3.7 collective-permute-start.1
  27.1 13.1 %collective-permute-done = bf16[192,640]{1,0:T(8,128)(2,1)} collective-permute-done((bf16[192,640]{1,0:T(8,128)(2,1)}, bf16[192,640]{1,0:T(8,128)(2,1)}, u32[]{:S(2)}, u32[]{:S(2)}) %collective-permute-start) | collective-permute-done | bytes 245792 | tf_op jit(solution)/shard_map/ppermute | solution.py:56
  42.0 2.5 collective-permute-start.6
  49.8 10.5 %collective-permute-done.7 = bf16[384,640]{1,0:T(8,128)(2,1)} collective-permute-done((bf16[384,640]{1,0:T(8,128)(2,1)S(1)}, bf16[384,640]{1,0:T(8,128)(2,1)}, u32[]{:S(2)}, u32[]{:S(2)}) %collective-permute-start.7) | collective-permute-done | bytes 491552 | tf_op jit(solution)/shard_map/ppermute | solution.py:56
  60.3 8.6 %collective-permute-done.9 = bf16[384,640]{1,0:T(8,128)(2,1)} collective-permute-done((bf16[384,640]{1,0:T(8,128)(2,1)}, bf16[384,640]{1,0:T(8,128)(2,1)}, u32[]{:S(2)}, u32[]{:S(2)}) %collective-permute-start.9) | collective-permute-done | bytes 491552 | tf_op jit(solution)/shard_map/ppermute | solution.py:56
  70.5 3.2 collective-permute-start.27
  76.3 2.8 pad_maximum_fusion.2.wa_ref
  80.8 7.5 %collective-permute-done.12 = bf16[384,640]{1,0:T(8,128)(2,1)} collective-permute-done((bf16[384,640]{1,0:T(8,128)(2,1)}, bf16[384,640]{1,0:T(8,128)(2,1)}, u32[]{:S(2)}, u32[]{:S(2)}) %collective-permute-start.12) | collective-permute-done | bytes 491552 | tf_op jit(solution)/shard_map/ppermute | solution.py:56
  93.6 2.9 pad_maximum_fusion.3.wb_ref
  97.3 3.5 collective-permute-done.15
  103.0 2.4 collective-permute-start.22
  110.6 25.1 %shard_map.238 = (bf16[1024,384]{1,0:T(8,128)(2,1)}, bf16[1024,1536]{1,0:T(8,128)(2,1)}, bf16[1024,1152]{1,0:T(8,128)(2,1)}, f32[1024,128]{1,0:T(8,128)}, f32[1024,128]{1,0:T(8,128)}, /*index=5*/f32[1024,128]{1,0:T(8,128)}) custom-call(s32[4]{0:T(128)} %pad_add_fusion.pos_ref, bf16[256,1536]{1,0:T(8,128)(2,1)} %copy-done.5, ...), custom_call_target="tpu_custom_call" | custom-call | tf_op jit(solution)/shard_map/pallas_call | solution.py:386
  135.8 4.3 collective-permute-done.22
  150.2 15.7 %collective-permute-done.24 = bf16[256,1536]{1,0:T(8,128)(2,1)S(1)} collective-permute-done((bf16[256,1536]{1,0:T(8,128)(2,1)S(1)}, bf16[256,1536]{1,0:T(8,128)(2,1)S(1)}, u32[]{:S(2)}, u32[]{:S(2)}) %collective-permute-start.24) | collective-permute-done | bytes 786464 | tf_op jit(solution)/shard_map/ppermute | solution.py:56
  169.1 14.6 %collective-permute-done.30 = bf16[384,1024]{1,0:T(8,128)(2,1)S(1)} collective-permute-done((bf16[384,1024]{1,0:T(8,128)(2,1)S(1)}, bf16[384,1024]{1,0:T(8,128)(2,1)S(1)}, u32[]{:S(2)}, u32[]{:S(2)}) %collective-permute-start.30) | collective-permute-done | bytes 786464 | tf_op jit(solution)/shard_map/ppermute | solution.py:56
  184.9 4.2 collective-permute-done.32
  189.1 10.0 %collective-permute-done.33 = bf16[192,512]{1,0:T(8,128)(2,1)S(1)} collective-permute-done((bf16[192,512]{1,0:T(8,128)(2,1)S(1)}, bf16[192,512]{1,0:T(8,128)(2,1)S(1)}, u32[]{:S(2)}, u32[]{:S(2)}) %collective-permute-start.33) | collective-permute-done | bytes 196640 | tf_op jit(solution)/shard_map/ppermute | solution.py:56
  199.9 2.2 collective-permute-start.36
  212.1 6.8 %collective-permute-done.36 = bf16[384,512]{1,0:T(8,128)(2,1)} collective-permute-done((bf16[384,512]{1,0:T(8,128)(2,1)S(1)}, bf16[384,512]{1,0:T(8,128)(2,1)}, u32[]{:S(2)}, u32[]{:S(2)}) %collective-permute-start.36) | collective-permute-done | bytes 393248 | tf_op jit(solution)/shard_map/ppermute | solution.py:56
  222.5 5.5 collective-permute-start.40
  229.9 2.4 pad_maximum_fusion.5.db_ref
  233.8 5.0 collective-permute-start.41
  241.6 16.5 %shard_map.239 = (bf16[1024,1024]{1,0:T(8,128)(2,1)}, bf16[1024,1024]{1,0:T(8,128)(2,1)}, bf16[1024,1024]{1,0:T(8,128)(2,1)}, bf16[1024,1536]{1,0:T(8,128)(2,1)}...) custom-call(bf16[256,1536]{1,0:T(8,128)(2,1)} %collective-permute-done.26.s0_ref, ...), custom_call_target="tpu_custom_call" | custom-call | tf_op jit(solution)/shard_map/pallas_call | solution.py:434
  263.9 16.6 %shard_map.240 = (bf16[1024,1024]{1,0:T(8,128)(2,1)}, bf16[1024,1024]{1,0:T(8,128)(2,1)}, bf16[1024,1024]{1,0:T(8,128)(2,1)}, bf16[1024,1536]{1,0:T(8,128)(2,1)}...) custom-call(bf16[256,1536]{1,0:T(8,128)(2,1)} %copy-done.20, ...), custom_call_target="tpu_custom_call", output_to_operand_aliasing={{0}: (8, {}), {1}: (9, {}), {2}: (10, {}), {3}: (11, {}), {... | custom-call | tf_op jit(solution)/shard_map/pallas_call | solution.py:434
  280.6 2.9 collective-permute-done.44
  285.0 2.3 collective-permute-done.45
  292.1 20.3 %shard_map.241 = (bf16[1536,1024]{1,0:T(8,128)(2,1)}, bf16[1536,512]{1,0:T(8,128)(2,1)}, bf16[1536,1536]{1,0:T(8,128)(2,1)}, bf16[1024,1536]{1,0:T(8,128)(2,1)}) custom-call(s32[1]{0:T(128)} %bitcast.11.chip_ref, bf16[1024,1536]{1,0:T(8,128)(2,1)} %get-tuple-element.291.second_ref, bf16[1024,1536]{1,0:T(8,128)(2,1)} %get-tuple-element.292.cot_ref, ...), custom_call_target="tpu_custom_call" | custom-call | tf_op jit(solution)/shard_map/pallas_call | solution.py:481
  323.2 2.7 convolution_convert_fusion.1.gmix_ref
  329.0 23.6 %shard_map.242 = (bf16[1024,640]{1,0:T(8,128)(2,1)}, bf16[1024,640]{1,0:T(8,128)(2,1)}, f32[1,128]{1,0:T(1,128)}) custom-call(s32[4]{0:T(128)} %pad_add_fusion.pos_ref, bf16[1024,1152]{1,0:T(8,128)(2,1)} %get-tuple-element.281.qkv_ref, f32[1024,128]{1,0:T(8,128)} %get-tuple-element.282.logit_ref, s32[1,1024]{1,0:T(1,128)} %copy-done.76, ...), custom_call_target="tpu_custom_call" | custom-call | tf_op jit(solution)/shard_map/pallas_call | solution.py:545
  356.9 3.1 convolution_add_fusion.1
  360.0 2.4 slice.686
  367.0 2.6 fusion.14
  371.5 2.2 copy-done.13
  381.9 8.8 %shard_map.243 = (bf16[1536,640]{1,0:T(8,128)(2,1)}, bf16[1536,640]{1,0:T(8,128)(2,1)}, f32[1536,256]{1,0:T(8,128)}) custom-call(bf16[1024,1536]{1,0:T(8,128)(2,1)} %get-tuple-element.321.x_ref, bf16[1024,640]{1,0:T(8,128)(2,1)} %get-tuple-element.317.near_ref, bf16[1024,640]{1,0:T(8,128)(2,1)} %get-tuple-element.318.far_ref), custom_call_target="tpu_custom_call" | custom-call | tf_op jit(solution)/shard_map/pallas_call | solution.py:523
  390.7 13.8 %collective-permute-done.55 = bf16[256,1536]{1,0:T(8,128)(2,1)S(1)} collective-permute-done((bf16[256,1536]{1,0:T(8,128)(2,1)S(1)}, bf16[256,1536]{1,0:T(8,128)(2,1)S(1)}, u32[]{:S(2)}, u32[]{:S(2)}) %collective-permute-start.55) | collective-permute-done | bytes 786464 | tf_op jit(solution)/shard_map/ppermute | solution.py:56
  406.3 7.7 %collective-permute-done.57 = bf16[384,1024]{1,0:T(8,128)(2,1)S(1)} collective-permute-done((bf16[384,1024]{1,0:T(8,128)(2,1)S(1)}, bf16[384,1024]{1,0:T(8,128)(2,1)S(1)}, u32[]{:S(2)}, u32[]{:S(2)}) %collective-permute-start.57) | collective-permute-done | bytes 786464 | tf_op jit(solution)/shard_map/ppermute | solution.py:56
  414.9 7.6 %collective-permute-start.70 = (bf16[256,1536]{1,0:T(8,128)(2,1)}, bf16[256,1536]{1,0:T(8,128)(2,1)}, u32[]{:S(2)}, u32[]{:S(2)}) collective-permute-start(bf16[256,1536]{1,0:T(8,128)(2,1)} %fusion.4), channel_id=1, source_target_pairs={{0,0},{1,1},{2,4},{3,5},{4,2},{5,3},{6,6},{7,7},{8,8},{9,9},{10,12... | collective-permute-start | bytes 2359304 | tf_op jit(solution)/shard_map/ppermute | solution.py:56
  427.0 4.0 multiply_reduce_fusion
  436.8 21.7 %collective-permute-done.62 = f32[9,1536]{1,0:T(8,128)S(1)} collective-permute-done((f32[9,1536]{1,0:T(8,128)S(1)}, f32[9,1536]{1,0:T(8,128)S(1)}, u32[]{:S(2)}, u32[]{:S(2)}) %collective-permute-start.62) | collective-permute-done | bytes 55328 | tf_op jit(solution)/shard_map/ppermute | solution.py:56
  465.0 14.0 %collective-permute-done.66 = bf16[384,384]{1,0:T(8,128)(2,1)S(1)} collective-permute-done((bf16[384,384]{1,0:T(8,128)(2,1)S(1)}, bf16[384,384]{1,0:T(8,128)(2,1)S(1)}, u32[]{:S(2)}, u32[]{:S(2)}) %collective-permute-start.66) | collective-permute-done | bytes 294944 | tf_op jit(solution)/shard_map/ppermute | solution.py:56
  479.1 2.4 collective-permute-start.72
  482.3 4.6 collective-permute-done.67
  491.5 3.0 collective-permute-start.75
  494.5 23.9 %collective-permute-done.68 = f32[6,1536]{1,0:T(8,128)} collective-permute-done((f32[6,1536]{1,0:T(8,128)}, f32[6,1536]{1,0:T(8,128)}, u32[]{:S(2)}, u32[]{:S(2)}) %collective-permute-start.68) | collective-permute-done | bytes 36896 | tf_op jit(solution)/shard_map/ppermute | solution.py:56
  523.7 4.0 collective-permute-start.74
  529.3 3.7 collective-permute-done.75
  533.0 6.2 %collective-permute-done.76 = bf16[192,832]{1,0:T(8,128)(2,1)S(1)} collective-permute-done((bf16[192,832]{1,0:T(8,128)(2,1)S(1)}, bf16[192,832]{1,0:T(8,128)(2,1)S(1)}, u32[]{:S(2)}, u32[]{:S(2)}) %collective-permute-start.76) | collective-permute-done | bytes 319520 | tf_op jit(solution)/shard_map/ppermute | solution.py:56
  (480 shorter events, 159.5 us)
Async XLA Ops:
  7.2 198.6 %all-gather.2.cloned.1.call-start = ((), (), s32[]{:S(2)}) async-start(), calls=%async_computation.1 | async-start | bytes 5898240 | tf_op jit(solution)/shard_map/all_gather | solution.py:769
  13.9 26.3 %collective-permute-start.1 = (bf16[192,640]{1,0:T(8,128)(2,1)}, bf16[192,640]{1,0:T(8,128)(2,1)}, u32[]{:S(2)}, u32[]{:S(2)}) collective-permute-start(bf16[192,640]{1,0:T(8,128)(2,1)} %get-tuple-element.190), channel_id=1, source_target_pairs={{0,6},{1,7},{2,4},{3,5},{4,2},{5,3},{6,0},{7,1},{8,14},{9,15},{10,... | collective-permute-start | bytes 737288 | tf_op jit(solution)/shard_map/ppermute | solution.py:56
  17.6 22.6 %collective-permute-start = (bf16[192,640]{1,0:T(8,128)(2,1)}, bf16[192,640]{1,0:T(8,128)(2,1)}, u32[]{:S(2)}, u32[]{:S(2)}) collective-permute-start(bf16[192,640]{1,0:T(8,128)(2,1)} %get-tuple-element.189), channel_id=1, source_target_pairs={{0,2},{1,3},{2,0},{3,1},{4,6},{5,7},{6,4},{7,5},{8,10},{9,11},{10,... | collective-permute-start | bytes 737288 | tf_op jit(solution)/shard_map/ppermute | solution.py:56
  21.7 18.5 %collective-permute-start.3 = (bf16[384,640]{1,0:T(8,128)(2,1)S(1)}, bf16[384,640]{1,0:T(8,128)(2,1)}, u32[]{:S(2)}, u32[]{:S(2)}) collective-permute-start(bf16[384,640]{1,0:T(8,128)(2,1)S(1)} %maximum_select_fusion.2), channel_id=1, source_target_pairs={{0,8},{1,9},{2,10},{3,11},{4,12},{5,13},{6,14},{7,15},{8,0},{9,1},... | collective-permute-start | bytes 1474568 | tf_op jit(solution)/shard_map/ppermute | solution.py:56
  23.6 16.6 %collective-permute-start.4 = (bf16[384,640]{1,0:T(8,128)(2,1)S(1)}, bf16[384,640]{1,0:T(8,128)(2,1)S(1)}, u32[]{:S(2)}, u32[]{:S(2)}) collective-permute-start(bf16[384,640]{1,0:T(8,128)(2,1)S(1)} %maximum_select_fusion.2), channel_id=1, source_target_pairs={{0,16},{1,17},{2,18},{3,19},{4,20},{5,21},{6,22},{7,23},{8,24},{9,... | collective-permute-start | bytes 1474568 | tf_op jit(solution)/shard_map/ppermute | solution.py:56
  40.2 28.7 %collective-permute-start.5 = (bf16[256,1536]{1,0:T(8,128)(2,1)}, bf16[256,1536]{1,0:T(8,128)(2,1)S(1)}, u32[]{:S(2)}, u32[]{:S(2)}) collective-permute-start(bf16[256,1536]{1,0:T(8,128)(2,1)} %pad_maximum_fusion.7), channel_id=1, source_target_pairs={{0,0},{1,1},{2,4},{3,5},{4,2},{5,3},{6,6},{7,7},{8,8},{9,9},{10,12... | collective-permute-start | bytes 2359304 | tf_op jit(solution)/shard_map/ppermute | solution.py:56
  42.0 26.9 %collective-permute-start.6 = (bf16[256,1536]{1,0:T(8,128)(2,1)}, bf16[256,1536]{1,0:T(8,128)(2,1)}, u32[]{:S(2)}, u32[]{:S(2)}) collective-permute-start(bf16[256,1536]{1,0:T(8,128)(2,1)} %pad_maximum_fusion.7), channel_id=1, source_target_pairs={{0,1},{1,0},{6,7},{7,6},{8,9},{9,8},{14,15},{15,14},{16,17},{17,16... | collective-permute-start | bytes 2359304 | tf_op jit(solution)/shard_map/ppermute | solution.py:56
  49.1 19.9 %collective-permute-start.9 = (bf16[384,640]{1,0:T(8,128)(2,1)}, bf16[384,640]{1,0:T(8,128)(2,1)}, u32[]{:S(2)}, u32[]{:S(2)}) collective-permute-start(bf16[384,640]{1,0:T(8,128)(2,1)} %collective-permute-done.3), channel_id=1, source_target_pairs={{0,16},{1,17},{2,18},{3,19},{4,20},{5,21},{6,22},{7,23},{8,24},{9,... | collective-permute-start | bytes 1474568 | tf_op jit(solution)/shard_map/ppermute | solution.py:56
  74.3 22.1 %collective-permute-start.14 = (bf16[256,1536]{1,0:T(8,128)(2,1)S(1)}, bf16[256,1536]{1,0:T(8,128)(2,1)}, u32[]{:S(2)}, u32[]{:S(2)}) collective-permute-start(bf16[256,1536]{1,0:T(8,128)(2,1)S(1)} %collective-permute-done.5.x0_ref), channel_id=1, source_target_pairs={{0,4},{1,5},{2,6},{3,7},{4,0},{5,1},{6,2},{7,3},{8,12},{9,13},{10,... | collective-permute-start | bytes 2359304 | tf_op jit(solution)/shard_map/ppermute | solution.py:56
  80.5 407.8 %reduce-scatter.2.cloned.1.call-start = ((), (), s32[]{:S(2)}) async-start(), calls=%async_computation.2 | async-start | bytes 5898240 | tf_op jit(solution)/shard_map/reduce_scatter | solution.py:915
  102.9 32.9 %collective-permute-start.21 = (bf16[192,1024]{1,0:T(8,128)(2,1)}, bf16[192,1024]{1,0:T(8,128)(2,1)S(1)}, u32[]{:S(2)}, u32[]{:S(2)}) collective-permute-start(bf16[192,1024]{1,0:T(8,128)(2,1)} %get-tuple-element.223), channel_id=1, source_target_pairs={{0,2},{1,3},{2,0},{3,1},{4,6},{5,7},{6,4},{7,5},{8,10},{9,11},{10,... | collective-permute-start | bytes 1179656 | tf_op jit(solution)/shard_map/ppermute | solution.py:56
  103.0 37.1 %collective-permute-start.22 = (bf16[192,1024]{1,0:T(8,128)(2,1)S(1)}, bf16[192,1024]{1,0:T(8,128)(2,1)S(1)}, u32[]{:S(2)}, u32[]{:S(2)}) collective-permute-start(bf16[192,1024]{1,0:T(8,128)(2,1)S(1)} %get-tuple-element.224), channel_id=1, source_target_pairs={{0,6},{1,7},{2,4},{3,5},{4,2},{5,3},{6,0},{7,1},{8,14},{9,15},{10,... | collective-permute-start | bytes 1179656 | tf_op jit(solution)/shard_map/ppermute | solution.py:56
  105.4 30.3 %collective-permute-start.18 = (bf16[384,384]{1,0:T(8,128)(2,1)S(1)}, bf16[384,384]{1,0:T(8,128)(2,1)S(1)}, u32[]{:S(2)}, u32[]{:S(2)}) collective-permute-start(bf16[384,384]{1,0:T(8,128)(2,1)S(1)} %pad_maximum_fusion.17), channel_id=1, source_target_pairs={{0,8},{1,9},{2,10},{3,11},{4,12},{5,13},{6,14},{7,15},{8,0},{9,1},... | collective-permute-start | bytes 884744 | tf_op jit(solution)/shard_map/ppermute | solution.py:56
  107.0 28.7 %collective-permute-start.19 = (bf16[384,384]{1,0:T(8,128)(2,1)S(1)}, bf16[384,384]{1,0:T(8,128)(2,1)S(1)}, u32[]{:S(2)}, u32[]{:S(2)}) collective-permute-start(bf16[384,384]{1,0:T(8,128)(2,1)S(1)} %pad_maximum_fusion.17), channel_id=1, source_target_pairs={{0,16},{1,17},{2,18},{3,19},{4,20},{5,21},{6,22},{7,23},{8,24},{9,... | collective-permute-start | bytes 884744 | tf_op jit(solution)/shard_map/ppermute | solution.py:56
  108.5 27.2 %collective-permute-start.20 = (bf16[384,384]{1,0:T(8,128)(2,1)S(1)}, bf16[384,384]{1,0:T(8,128)(2,1)S(1)}, u32[]{:S(2)}, u32[]{:S(2)}) collective-permute-start(bf16[384,384]{1,0:T(8,128)(2,1)S(1)} %pad_maximum_fusion.17), channel_id=1, source_target_pairs={{0,24},{1,25},{2,26},{3,27},{4,28},{5,29},{6,30},{7,31},{8,16},{9,... | collective-permute-start | bytes 884744 | tf_op jit(solution)/shard_map/ppermute | solution.py:56
  146.1 19.8 %collective-permute-start.24 = (bf16[256,1536]{1,0:T(8,128)(2,1)S(1)}, bf16[256,1536]{1,0:T(8,128)(2,1)S(1)}, u32[]{:S(2)}, u32[]{:S(2)}) collective-permute-start(bf16[256,1536]{1,0:T(8,128)(2,1)S(1)} %fusion.8), channel_id=1, source_target_pairs={{0,1},{1,0},{2,3},{3,2},{4,5},{5,4},{6,7},{7,6},{8,9},{9,8},{10,11... | collective-permute-start | bytes 2359304 | tf_op jit(solution)/shard_map/ppermute | solution.py:56
  146.4 20.5 %collective-permute-start.29 = (bf16[384,1024]{1,0:T(8,128)(2,1)S(1)}, bf16[384,1024]{1,0:T(8,128)(2,1)S(1)}, u32[]{:S(2)}, u32[]{:S(2)}) collective-permute-start(bf16[384,1024]{1,0:T(8,128)(2,1)S(1)} %maximum_select_fusion.1), channel_id=1, source_target_pairs={{0,8},{1,9},{2,10},{3,11},{4,12},{5,13},{6,14},{7,15},{8,0},{9,1},... | collective-permute-start | bytes 2359304 | tf_op jit(solution)/shard_map/ppermute | solution.py:56
  147.3 36.4 %collective-permute-start.30 = (bf16[384,1024]{1,0:T(8,128)(2,1)S(1)}, bf16[384,1024]{1,0:T(8,128)(2,1)S(1)}, u32[]{:S(2)}, u32[]{:S(2)}) collective-permute-start(bf16[384,1024]{1,0:T(8,128)(2,1)S(1)} %maximum_select_fusion.1), channel_id=1, source_target_pairs={{0,16},{1,17},{2,18},{3,19},{4,20},{5,21},{6,22},{7,23},{8,24},{9,... | collective-permute-start | bytes 2359304 | tf_op jit(solution)/shard_map/ppermute | solution.py:56
  148.9 36.0 %collective-permute-start.31 = (bf16[384,1024]{1,0:T(8,128)(2,1)S(1)}, bf16[384,1024]{1,0:T(8,128)(2,1)S(1)}, u32[]{:S(2)}, u32[]{:S(2)}) collective-permute-start(bf16[384,1024]{1,0:T(8,128)(2,1)S(1)} %maximum_select_fusion.1), channel_id=1, source_target_pairs={{0,24},{1,25},{2,26},{3,27},{4,28},{5,29},{6,30},{7,31},{8,16},{9,... | collective-permute-start | bytes 2359304 | tf_op jit(solution)/shard_map/ppermute | solution.py:56
  166.5 18.3 %collective-permute-start.28 = (bf16[256,1536]{1,0:T(8,128)(2,1)S(1)}, bf16[256,1536]{1,0:T(8,128)(2,1)S(1)}, u32[]{:S(2)}, u32[]{:S(2)}) collective-permute-start(bf16[256,1536]{1,0:T(8,128)(2,1)S(1)} %multiply_convert_fusion.s0_ref), channel_id=1, source_target_pairs={{0,4},{1,5},{2,6},{3,7},{4,0},{5,1},{6,2},{7,3},{8,12},{9,13},{10,... | collective-permute-start | bytes 2359304 | tf_op jit(solution)/shard_map/ppermute | solution.py:56
  166.6 42.0 %collective-permute-start.26 = (bf16[256,1536]{1,0:T(8,128)(2,1)S(1)}, bf16[256,1536]{1,0:T(8,128)(2,1)}, u32[]{:S(2)}, u32[]{:S(2)}) collective-permute-start(bf16[256,1536]{1,0:T(8,128)(2,1)S(1)} %multiply_convert_fusion.s0_ref), channel_id=1, source_target_pairs={{0,1},{1,0},{2,3},{3,2},{4,5},{5,4},{6,7},{7,6},{8,9},{9,8},{10,11... | collective-permute-start | bytes 2359304 | tf_op jit(solution)/shard_map/ppermute | solution.py:56
  167.2 21.9 %collective-permute-start.32 = (bf16[192,512]{1,0:T(8,128)(2,1)S(1)}, bf16[192,512]{1,0:T(8,128)(2,1)S(1)}, u32[]{:S(2)}, u32[]{:S(2)}) collective-permute-start(bf16[192,512]{1,0:T(8,128)(2,1)S(1)} %copy-done.75), channel_id=1, source_target_pairs={{0,2},{1,3},{2,0},{3,1},{4,6},{5,7},{6,4},{7,5},{8,10},{9,11},{10,... | collective-permute-start | bytes 589832 | tf_op jit(solution)/shard_map/ppermute | solution.py:56
  199.9 19.0 %collective-permute-start.36 = (bf16[384,512]{1,0:T(8,128)(2,1)S(1)}, bf16[384,512]{1,0:T(8,128)(2,1)}, u32[]{:S(2)}, u32[]{:S(2)}) collective-permute-start(bf16[384,512]{1,0:T(8,128)(2,1)S(1)} %maximum_select_fusion.4), channel_id=1, source_target_pairs={{0,16},{1,17},{2,18},{3,19},{4,20},{5,21},{6,22},{7,23},{8,24},{9,... | collective-permute-start | bytes 1179656 | tf_op jit(solution)/shard_map/ppermute | solution.py:56
  202.1 19.7 %collective-permute-start.38 = (bf16[256,1536]{1,0:T(8,128)(2,1)}, bf16[256,1536]{1,0:T(8,128)(2,1)}, u32[]{:S(2)}, u32[]{:S(2)}) collective-permute-start(bf16[256,1536]{1,0:T(8,128)(2,1)} %pad_maximum_fusion.8), channel_id=1, source_target_pairs={{0,1},{1,0},{6,7},{7,6},{8,9},{9,8},{14,15},{15,14},{16,17},{17,16... | collective-permute-start | bytes 2359304 | tf_op jit(solution)/shard_map/ppermute | solution.py:56
  263.6 19.9 %collective-permute-start.44 = (bf16[256,1536]{1,0:T(8,128)(2,1)S(1)}, bf16[256,1536]{1,0:T(8,128)(2,1)S(1)}, u32[]{:S(2)}, u32[]{:S(2)}) collective-permute-start(bf16[256,1536]{1,0:T(8,128)(2,1)S(1)} %add_convert_fusion.2), channel_id=1, source_target_pairs={{0,1},{1,0},{2,3},{3,2},{4,5},{5,4},{6,7},{7,6},{8,9},{9,8},{10,11... | collective-permute-start | bytes 2359304 | tf_op jit(solution)/shard_map/ppermute | solution.py:56
  291.8 20.6 %collective-permute-start.46 = (bf16[256,1536]{1,0:T(8,128)(2,1)S(1)}, bf16[256,1536]{1,0:T(8,128)(2,1)S(1)}, u32[]{:S(2)}, u32[]{:S(2)}) collective-permute-start(bf16[256,1536]{1,0:T(8,128)(2,1)S(1)} %get-tuple-element.301), channel_id=1, source_target_pairs={{0,1},{1,0},{2,3},{3,2},{4,5},{5,4},{6,7},{7,6},{8,9},{9,8},{10,11... | collective-permute-start | bytes 2359304 | tf_op jit(solution)/shard_map/ppermute | solution.py:56
  316.4 37.6 %collective-permute-start.49 = (bf16[768,1024]{1,0:T(8,128)(2,1)}, bf16[768,1024]{1,0:T(8,128)(2,1)}, u32[]{:S(2)}, u32[]{:S(2)}) collective-permute-start(bf16[768,1024]{1,0:T(8,128)(2,1)} %slice.408), channel_id=1, source_target_pairs={{0,16},{1,17},{2,18},{3,19},{4,20},{5,21},{6,22},{7,23},{8,24},{9,... | collective-permute-start | bytes 4718600 | tf_op jit(solution)/shard_map/ppermute | solution.py:56
  317.6 36.4 %collective-permute-start.50 = (bf16[768,512]{1,0:T(8,128)(2,1)}, bf16[768,512]{1,0:T(8,128)(2,1)}, u32[]{:S(2)}, u32[]{:S(2)}) collective-permute-start(bf16[768,512]{1,0:T(8,128)(2,1)} %slice.409), channel_id=1, source_target_pairs={{0,8},{1,9},{2,10},{3,11},{4,12},{5,13},{6,14},{7,15},{8,0},{9,1},... | collective-permute-start | bytes 2359304 | tf_op jit(solution)/shard_map/ppermute | solution.py:56
  320.1 32.5 %collective-permute-start.52 = (bf16[256,1536]{1,0:T(8,128)(2,1)}, bf16[256,1536]{1,0:T(8,128)(2,1)S(1)}, u32[]{:S(2)}, u32[]{:S(2)}) collective-permute-start(bf16[256,1536]{1,0:T(8,128)(2,1)} %get-tuple-element.400), channel_id=1, source_target_pairs={{0,1},{1,0},{2,3},{3,2},{4,5},{5,4},{6,7},{7,6},{8,9},{9,8},{10,11... | collective-permute-start | bytes 2359304 | tf_op jit(solution)/shard_map/ppermute | solution.py:56
  363.4 73.3 %collective-permute-start.63 = (bf16[768,384]{1,0:T(8,128)(2,1)}, bf16[768,384]{1,0:T(8,128)(2,1)}, u32[]{:S(2)}, u32[]{:S(2)}) collective-permute-start(bf16[768,384]{1,0:T(8,128)(2,1)} %get-tuple-element.425), channel_id=1, source_target_pairs={{0,16},{1,17},{2,18},{3,19},{4,20},{5,21},{6,22},{7,23},{8,24},{9,... | collective-permute-start | bytes 1769480 | tf_op jit(solution)/shard_map/ppermute | solution.py:56
  374.0 32.4 %collective-permute-start.59 = (bf16[256,1536]{1,0:T(8,128)(2,1)S(1)}, bf16[256,1536]{1,0:T(8,128)(2,1)S(1)}, u32[]{:S(2)}, u32[]{:S(2)}) collective-permute-start(bf16[256,1536]{1,0:T(8,128)(2,1)S(1)} %add_convert_fusion), channel_id=1, source_target_pairs={{0,0},{1,1},{2,4},{3,5},{4,2},{5,3},{6,6},{7,7},{8,8},{9,9},{10,12... | collective-permute-start | bytes 2359304 | tf_op jit(solution)/shard_map/ppermute | solution.py:56
  376.4 30.0 %collective-permute-start.58 = (bf16[384,512]{1,0:T(8,128)(2,1)S(1)}, bf16[384,512]{1,0:T(8,128)(2,1)}, u32[]{:S(2)}, u32[]{:S(2)}) collective-permute-start(bf16[384,512]{1,0:T(8,128)(2,1)S(1)} %slice.693), channel_id=1, source_target_pairs={{0,16},{1,17},{2,18},{3,19},{4,20},{5,21},{6,22},{7,23},{8,24},{9,... | collective-permute-start | bytes 1179656 | tf_op jit(solution)/shard_map/ppermute | solution.py:56
  377.6 26.8 %collective-permute-start.55 = (bf16[256,1536]{1,0:T(8,128)(2,1)S(1)}, bf16[256,1536]{1,0:T(8,128)(2,1)S(1)}, u32[]{:S(2)}, u32[]{:S(2)}) collective-permute-start(bf16[256,1536]{1,0:T(8,128)(2,1)S(1)} %fusion.7), channel_id=1, source_target_pairs={{0,1},{1,0},{2,3},{3,2},{4,5},{5,4},{6,7},{7,6},{8,9},{9,8},{10,11... | collective-permute-start | bytes 2359304 | tf_op jit(solution)/shard_map/ppermute | solution.py:56
  380.1 33.9 %collective-permute-start.57 = (bf16[384,1024]{1,0:T(8,128)(2,1)S(1)}, bf16[384,1024]{1,0:T(8,128)(2,1)S(1)}, u32[]{:S(2)}, u32[]{:S(2)}) collective-permute-start(bf16[384,1024]{1,0:T(8,128)(2,1)S(1)} %slice.684), channel_id=1, source_target_pairs={{0,8},{1,9},{2,10},{3,11},{4,12},{5,13},{6,14},{7,15},{8,0},{9,1},... | collective-permute-start | bytes 2359304 | tf_op jit(solution)/shard_map/ppermute | solution.py:56
  414.9 76.6 %collective-permute-start.70 = (bf16[256,1536]{1,0:T(8,128)(2,1)}, bf16[256,1536]{1,0:T(8,128)(2,1)}, u32[]{:S(2)}, u32[]{:S(2)}) collective-permute-start(bf16[256,1536]{1,0:T(8,128)(2,1)} %fusion.4), channel_id=1, source_target_pairs={{0,0},{1,1},{2,4},{3,5},{4,2},{5,3},{6,6},{7,7},{8,8},{9,9},{10,12... | collective-permute-start | bytes 2359304 | tf_op jit(solution)/shard_map/ppermute | solution.py:56
  431.1 27.3 %collective-permute-start.60 = (bf16[768,640]{1,0:T(8,128)(2,1)S(1)}, bf16[768,640]{1,0:T(8,128)(2,1)S(1)}, u32[]{:S(2)}, u32[]{:S(2)}) collective-permute-start(bf16[768,640]{1,0:T(8,128)(2,1)S(1)} %slice.435), channel_id=1, source_target_pairs={{0,16},{1,17},{2,18},{3,19},{4,20},{5,21},{6,22},{7,23},{8,24},{9,... | collective-permute-start | bytes 2949128 | tf_op jit(solution)/shard_map/ppermute | solution.py:56
  432.8 25.7 %collective-permute-start.61 = (bf16[768,640]{1,0:T(8,128)(2,1)S(1)}, bf16[768,640]{1,0:T(8,128)(2,1)S(1)}, u32[]{:S(2)}, u32[]{:S(2)}) collective-permute-start(bf16[768,640]{1,0:T(8,128)(2,1)S(1)} %slice.436), channel_id=1, source_target_pairs={{0,8},{1,9},{2,10},{3,11},{4,12},{5,13},{6,14},{7,15},{8,0},{9,1},... | collective-permute-start | bytes 2949128 | tf_op jit(solution)/shard_map/ppermute | solution.py:56
  433.5 25.0 %collective-permute-start.62 = (f32[9,1536]{1,0:T(8,128)S(1)}, f32[9,1536]{1,0:T(8,128)S(1)}, u32[]{:S(2)}, u32[]{:S(2)}) collective-permute-start(f32[9,1536]{1,0:T(8,128)S(1)} %select_maximum_fusion), channel_id=1, source_target_pairs={{0,8},{1,9},{2,10},{3,11},{4,12},{5,13},{6,14},{7,15},{8,0},{9,1},... | collective-permute-start | bytes 165896 | tf_op jit(solution)/shard_map/ppermute | solution.py:56
  436.7 54.7 %collective-permute-start.71 = (bf16[192,1536]{1,0:T(8,128)(2,1)S(1)}, bf16[192,1536]{1,0:T(8,128)(2,1)}, u32[]{:S(2)}, u32[]{:S(2)}) collective-permute-start(bf16[192,1536]{1,0:T(8,128)(2,1)S(1)} %get-tuple-element.423), channel_id=1, source_target_pairs={{0,2},{1,3},{2,0},{3,1},{4,6},{5,7},{6,4},{7,5},{8,10},{9,11},{10,... | collective-permute-start | bytes 1769480 | tf_op jit(solution)/shard_map/ppermute | solution.py:56
  458.7 22.7 %collective-permute-start.65 = (bf16[384,640]{1,0:T(8,128)(2,1)S(1)}, bf16[384,640]{1,0:T(8,128)(2,1)S(1)}, u32[]{:S(2)}, u32[]{:S(2)}) collective-permute-start(bf16[384,640]{1,0:T(8,128)(2,1)S(1)} %slice.691), channel_id=1, source_target_pairs={{0,16},{1,17},{2,18},{3,19},{4,20},{5,21},{6,22},{7,23},{8,24},{9,... | collective-permute-start | bytes 1474568 | tf_op jit(solution)/shard_map/ppermute | solution.py:56
  460.6 20.9 %collective-permute-start.64 = (bf16[384,640]{1,0:T(8,128)(2,1)S(1)}, bf16[384,640]{1,0:T(8,128)(2,1)S(1)}, u32[]{:S(2)}, u32[]{:S(2)}) collective-permute-start(bf16[384,640]{1,0:T(8,128)(2,1)S(1)} %slice.692), channel_id=1, source_target_pairs={{0,8},{1,9},{2,10},{3,11},{4,12},{5,13},{6,14},{7,15},{8,0},{9,1},... | collective-permute-start | bytes 1474568 | tf_op jit(solution)/shard_map/ppermute | solution.py:56
  462.7 16.4 %collective-permute-start.66 = (bf16[384,384]{1,0:T(8,128)(2,1)S(1)}, bf16[384,384]{1,0:T(8,128)(2,1)S(1)}, u32[]{:S(2)}, u32[]{:S(2)}) collective-permute-start(bf16[384,384]{1,0:T(8,128)(2,1)S(1)} %slice.694), channel_id=1, source_target_pairs={{0,8},{1,9},{2,10},{3,11},{4,12},{5,13},{6,14},{7,15},{8,0},{9,1},... | collective-permute-start | bytes 884744 | tf_op jit(solution)/shard_map/ppermute | solution.py:56
  479.1 39.3 %collective-permute-start.72 = (bf16[192,1536]{1,0:T(8,128)(2,1)S(1)}, bf16[192,1536]{1,0:T(8,128)(2,1)}, u32[]{:S(2)}, u32[]{:S(2)}) collective-permute-start(bf16[192,1536]{1,0:T(8,128)(2,1)S(1)} %get-tuple-element.354), channel_id=1, source_target_pairs={{0,6},{1,7},{2,4},{3,5},{4,2},{5,3},{6,0},{7,1},{8,14},{9,15},{10,... | collective-permute-start | bytes 1769480 | tf_op jit(solution)/shard_map/ppermute | solution.py:56
  488.3 30.1 %collective-permute-start.68 = (f32[6,1536]{1,0:T(8,128)}, f32[6,1536]{1,0:T(8,128)}, u32[]{:S(2)}, u32[]{:S(2)}) collective-permute-start(f32[6,1536]{1,0:T(8,128)} %fusion.31), channel_id=1, source_target_pairs={{0,2},{1,3},{2,0},{3,1},{4,6},{5,7},{6,4},{7,5},{8,10},{9,11},{10,... | collective-permute-start | bytes 110600 | tf_op jit(solution)/shard_map/ppermute | solution.py:56
  489.9 28.5 %collective-permute-start.69 = (bf16[192,832]{1,0:T(8,128)(2,1)S(1)}, bf16[192,832]{1,0:T(8,128)(2,1)S(1)}, u32[]{:S(2)}, u32[]{:S(2)}) collective-permute-start(bf16[192,832]{1,0:T(8,128)(2,1)S(1)} %broadcast_select_fusion.13), channel_id=1, source_target_pairs={{0,4},{1,5},{2,6},{3,7},{4,0},{5,1},{6,2},{7,3},{8,12},{9,13},{10,... | collective-permute-start | bytes 958472 | tf_op jit(solution)/shard_map/ppermute | solution.py:56
  491.4 52.0 %collective-permute-start.77 = (bf16[192,1536]{1,0:T(8,128)(2,1)S(1)}, bf16[192,1536]{1,0:T(8,128)(2,1)S(1)}, u32[]{:S(2)}, u32[]{:S(2)}) collective-permute-start(bf16[192,1536]{1,0:T(8,128)(2,1)S(1)} %broadcast_select_fusion.2), channel_id=1, source_target_pairs={{0,4},{1,5},{2,6},{3,7},{4,0},{5,1},{6,2},{7,3},{8,12},{9,13},{10,... | collective-permute-start | bytes 1769480 | tf_op jit(solution)/shard_map/ppermute | solution.py:56
  491.5 41.5 %collective-permute-start.75 = (bf16[192,832]{1,0:T(8,128)(2,1)S(1)}, bf16[192,832]{1,0:T(8,128)(2,1)S(1)}, u32[]{:S(2)}, u32[]{:S(2)}) collective-permute-start(bf16[192,832]{1,0:T(8,128)(2,1)S(1)} %get-tuple-element.460), channel_id=1, source_target_pairs={{0,2},{1,3},{2,0},{3,1},{4,6},{5,7},{6,4},{7,5},{8,10},{9,11},{10,... | collective-permute-start | bytes 958472 | tf_op jit(solution)/shard_map/ppermute | solution.py:56
  518.4 20.9 %collective-permute-start.76 = (bf16[192,832]{1,0:T(8,128)(2,1)S(1)}, bf16[192,832]{1,0:T(8,128)(2,1)S(1)}, u32[]{:S(2)}, u32[]{:S(2)}) collective-permute-start(bf16[192,832]{1,0:T(8,128)(2,1)S(1)} %get-tuple-element.459), channel_id=1, source_target_pairs={{0,6},{1,7},{2,4},{3,5},{4,2},{5,3},{6,0},{7,1},{8,14},{9,15},{10,... | collective-permute-start | bytes 958472 | tf_op jit(solution)/shard_map/ppermute | solution.py:56
  (130 other events, 1160.8 us)
Sparse Core Ops, SparseCore 0:
  80.7 67.5 all-gather.1
  364.9 74.4 reduce-scatter.1

commit v3 on v2

--- a/solution.py
+++ b/solution.py
@@ -58,6 +58,10 @@
 
 def to_home(d, t):
     return (d ^ 1, t ^ 2) if (d & 1) != (t >> 1) else (d, t)
+
+
+def swap_home(d, t):
+    return (d ^ 1, t ^ 2) if (d & 1) != (t >> 1) else None
 
 
 def over_core(d, t):
@@ -447,13 +451,49 @@
     )(*operands, *before)
 
 
+def put_half(rows, keep_ref, give_ref):
+    first = pl.program_id(0) < pl.num_programs(0) // 2
+
+    @pl.when(first)
+    def _():
+        keep_ref[...] = rows.astype(BF16)
+
+    @pl.when(jnp.logical_not(first))
+    def _():
+        give_ref[...] = rows.astype(BF16)
+
+
+def put_pair(rows, keep_ref, give_ref):
+    even = pl.program_id(0) % 2 == 0
+
+    @pl.when(even)
+    def _():
+        keep_ref[...] = rows.astype(BF16)
+
+    @pl.when(jnp.logical_not(even))
+    def _():
+        give_ref[...] = rows.astype(BF16)
+
+
+def half_specs(block, cols, half_of):
+    return (
+        pl.BlockSpec((block, cols), lambda r, *_: (jnp.minimum(r, half_of - 1), 0)),
+        pl.BlockSpec((block, cols), lambda r, *_: (jnp.maximum(r - half_of, 0), 0)),
+    )
+
+
+def pair_specs(block, cols):
+    return (pl.BlockSpec((block, cols), lambda r, *_: (r // 2, 0)),) * 2
+
+
 def feed_grads_kernel(
-    chip_ref, second_ref, cot_ref, hidden_ref, ga_ref, gb_ref, da_ref, db_ref, outb_ref, outd_ref, outa_ref, part_ref,
+    chip_ref, second_ref, cot_ref, hidden_ref, ga_ref, gb_ref, da_ref, db_ref,
+    keepb_ref, giveb_ref, keepd_ref, gived_ref, outa_ref, part_ref,
 ):
     cut = da_ref.shape[1]
     second, cot = second_ref[...], cot_ref[...]
-    outb_ref[...] = tn(second, gb_ref[...]).astype(BF16)
-    outd_ref[...] = tn(cot, hidden_ref[:, cut:]).astype(BF16)
+    put_half(tn(second, gb_ref[...]), keepb_ref, giveb_ref)
+    put_pair(tn(cot, hidden_ref[:, cut:]), keepd_ref, gived_ref)
     outa_ref[:, : 2 * cut] = tn(second, ga_ref[...]).astype(BF16)
     outa_ref[:, 2 * cut :] = tn(cot, hidden_ref[:, :cut]).astype(BF16)
     part = nt(hidden_ref[:, :cut], da_ref[...]) + nt(hidden_ref[:, cut:], db_ref[...])
@@ -463,6 +503,11 @@
 def pairs_apart(rows, chips):
     block = rows.shape[0] // chips
     return rows_of([rows[r * block : (r + 1) * block] for r in (*range(0, chips, 2), *range(1, chips, 2))])
+
+
+def halves_apart(rows):
+    cut = rows.shape[0] // 2
+    return rows[:cut], rows[cut:]
 
 
 def feed_grads(chip, second, cot, hidden, ga, gb, da, db, chips):
@@ -475,14 +520,15 @@
         part = nt(hidden[:, :cut], da) + nt(hidden[:, cut:], db)
         own = jnp.concatenate([tn(second, ga).astype(BF16), down[:, :cut]], axis=1)
         own = [lax.dynamic_slice_in_dim(own, (chip[0] ^ r) * block, block, 0) for r in range(chips)]
-        return tn(second, gb).astype(BF16), pairs_apart(down[:, cut:], chips), rows_of(own), part.astype(BF16)
+        halves = halves_apart(tn(second, gb).astype(BF16)) + halves_apart(pairs_apart(down[:, cut:], chips))
+        return *halves, rows_of(own), part.astype(BF16)
     cols = pl.BlockSpec((length, block), lambda r, chip: (0, r))
     rows = pl.BlockSpec((block, cut), lambda r, chip: (r, 0))
     return pl.pallas_call(
         feed_grads_kernel,
         out_shape=(
-            jax.ShapeDtypeStruct((wide, 2 * cut), BF16),
-            jax.ShapeDtypeStruct((wide, cut), BF16),
+            *(jax.ShapeDtypeStruct((wide // 2, 2 * cut), BF16),) * 2,
+            *(jax.ShapeDtypeStruct((wide // 2, cut), BF16),) * 2,
             jax.ShapeDtypeStruct((wide, 3 * cut), BF16),
             jax.ShapeDtypeStruct((length, wide), BF16),
         ),
@@ -491,8 +537,8 @@
             grid=(chips,),
             in_specs=[cols, cols, *(full_spec(o.shape) for o in (hidden, ga, gb)), rows, rows],
             out_specs=(
-                pl.BlockSpec((block, 2 * cut), lambda r, chip: (r, 0)),
-                pl.BlockSpec((block, cut), lambda r, chip: ((r % 2) * half_of + r // 2, 0)),
+                *half_specs(block, 2 * cut, half_of),
+                *pair_specs(block, cut),
                 pl.BlockSpec((block, 3 * cut), lambda r, chip: (r ^ chip[0], 0)),
                 pl.BlockSpec((length, block), lambda r, chip: (0, r)),
             ),
@@ -502,11 +548,11 @@
     )(chip, second, cot, hidden, ga, gb, da, db)
 
 
-def first_grads_kernel(x_ref, near_ref, far_ref, outn_ref, outf_ref, gate_ref):
+def first_grads_kernel(x_ref, near_ref, far_ref, keepn_ref, given_ref, keepf_ref, givef_ref, gate_ref):
     x = x_ref[...]
     near, far = tn(x, near_ref[...]), tn(x, far_ref[...])
-    outn_ref[...] = near.astype(BF16)
-    outf_ref[...] = far.astype(BF16)
+    put_half(near, keepn_ref, given_ref)
+    put_pair(far, keepf_ref, givef_ref)
     gate_ref[:, :PAIR] = near[:, 4 * PAIR :]
     gate_ref[:, PAIR:] = far[:, 4 * PAIR :]
 
@@ -519,19 +565,18 @@
     if block % PAIR:
         near, far = tn(x_hat, near), tn(x_hat, far)
         gate = jnp.concatenate([near[:, 4 * PAIR :], far[:, 4 * PAIR :]], axis=1)
-        return near.astype(BF16), pairs_apart(far.astype(BF16), chips), gate
+        return *halves_apart(near.astype(BF16)), *halves_apart(pairs_apart(far.astype(BF16), chips)), gate
     return pl.pallas_call(
         first_grads_kernel,
         grid=(chips,),
         out_shape=(
-            jax.ShapeDtypeStruct((wide, cols), BF16),
-            jax.ShapeDtypeStruct((wide, cols), BF16),
+            *(jax.ShapeDtypeStruct((wide // 2, cols), BF16),) * 4,
             jax.ShapeDtypeStruct((wide, 2 * PAIR), F32),
         ),
         in_specs=[pl.BlockSpec((length, block), lambda r: (0, r)), full_spec(near.shape), full_spec(far.shape)],
         out_specs=(
-            pl.BlockSpec((block, cols), lambda r: (r, 0)),
-            pl.BlockSpec((block, cols), lambda r: ((r % 2) * half_of + r // 2, 0)),
+            *half_specs(block, cols, half_of),
+            *pair_specs(block, cols),
             pl.BlockSpec((block, 2 * PAIR), lambda r: (r, 0)),
         ),
         compiler_params=params(),
@@ -666,10 +711,9 @@
             return rows_of([self.pieces[r] for r in range(chips)])
 
     class Sum:
-        def __init__(self, rows, order):
-            cut = rows.shape[0] // 2
+        def __init__(self, keep, give, order):
             self.order = order
-            self.keep, self.give = Box(rows[:cut]), Box(rows[cut:])
+            self.keep, self.give = Box(val(keep)), Box(val(give))
 
         def made(self):
             return self.keep, self.give
@@ -747,9 +791,11 @@
     near_early = near_one.early()
     x_own, cot_own = Box(reorder(block_input)), Box(reorder(cotangent))
 
-    hold(x_own, one_far, near_early)
+    x_stay = send(x_own, stay)
+
+    hold(x_own, one_far, near_early, x_stay)
     x_home = send(x_own, to_home)
-    x_stay = send(x_own, stay)
+    cot_stay = send(hold(cot_own, x_own), stay)
     far_one = Spread(one.far_rows(), down_order)
     far_early = far_one.early()
     near_late = near_one.late()
@@ -757,7 +803,7 @@
     feed_pack = Pack(*halves_of([gate_scaled, up_scaled, down_t], fcut))
     gate_pack, down_pack = Pack(*halves_of([gate_scaled, up_scaled], fcut)), Pack(*halves_of([down_t], fcut))
 
-    hold(x_home, x_stay, far_early, near_late)
+    hold(x_home, far_early, near_late, cot_stay)
     x_move = send(x_home, move)
     x_core = send(x_home, over_core)
     far_late = far_one.late()
@@ -778,12 +824,11 @@
     wa = Box(near_one.whole())
 
     hold(x_move, wa, bias, seg_row)
-    hold(x_move, far_late)
+    hold(x_move, far_late, wo_far)
     x_z = Box(pick_home(x_stay, x_move))
     x_both = send(x_z, over_core)
     wb = Box(far_one.whole())
     hold(x_both, wb, x_core)
-    hold(x_both, wo_far)
     wo_a, wo_b = wo.near_rows(), wo.far_rows()
     wo_rows = jnp.concatenate([wo_a[:, :PAIR], wo_b[:, :PAIR], wo_a[:, PAIR:], wo_b[:, PAIR:]], axis=1)
     wo_spread = Spread(wo_rows, up_order)
@@ -806,7 +851,7 @@
 
     order = {}
 
-    def scatter_group(far, near, at_far=lambda far_sum: None, at_near=lambda near_sum: None, late_core=False):
+    def scatter_group(far, near, at_far=lambda far_sum: None, at_near=lambda near_sum: None, at_end=lambda: (), after_far=None, late_core=False):
         rows = far()
         far_in = send(rows[quarter:].astype(BF16), over_core)
         far_sum = Box((rows[:quarter].astype(F32) + far_in.v.astype(F32)).astype(BF16))
@@ -814,18 +859,24 @@
         far_got = send(far_sum, over_z)
         rows = Box(near())
         if late_core:
+            hold(far_got, rows)
+            if after_far:
+                after_far(far_got)
             hold(rows, far_got)
         near_in = send(rows.v[quarter:].astype(BF16), over_core)
         near_sum = Box(rows.v[:quarter].astype(F32) + near_in.v.astype(F32))
         at_near(near_sum)
         hold(far_got, near_sum)
+        if at_end():
+            hold(far_got, at_end())
         return near_sum.v + far_got.v.astype(F32)
 
     sent = {}
 
     def weights_on(near_sum):
         sent["gate"] = Spread(gate_pack.far_rows(), up_order)
-        sent["gate_sent"] = sent["gate"].direct()
+        sent["early"] = sent["gate"].early()
+        sent["down"] = down_pack.cross(near_sum)
 
     mixed = Box(mixed)
     hidden_res = Box(
@@ -835,30 +886,31 @@
             lambda: nt(half(mixed.v, 0), wo_t),
             lambda far_sum: hold(far_sum, mixed),
             weights_on,
+            lambda: (sent["early"], sent["down"]),
         )
     )
     far_gate = sent["gate"]
     second, second_scale = unit_rows(hidden_res.v)
     second_low = Box(second.astype(BF16))
     second_z = send(second_low, over_z)
-    down_far = down_pack.cross(second_low)
     second_core = send(second_low, over_core)
-    hold(second_core, sent["gate_sent"])
-    cot_stay = send(hold(cot_own, second_core), stay)
-    hold(second_core, down_far)
+    gate_late = far_gate.late()
     far_down = Spread(down_pack.far_rows(), down_order)
-    down_sent = far_down.direct()
+    down_early = far_down.early()
     cot_home = send(hold(cot_own, second_core), to_home)
     hold(near_all, second_core)
     gates_a = Box(reorder_rows(near_all.v[:, : 2 * fcut]))
     downs_a = Box(reorder_rows(near_all.v[:, 2 * fcut :]))
     hold(second_z, gates_a, downs_a)
-    hold(second_z, cot_home, down_sent, cot_stay)
+    hold(second_z, cot_home, gate_late, down_early)
     second_both = send(second_z, over_core)
     cot_move = send(cot_home, move)
+    down_late = far_down.late()
     cot_core = send(cot_home, over_core)
-    gates_b, downs_b = Box(far_gate.whole()), Box(far_down.whole())
-    hold(cot_move, second_both, gates_b, downs_b)
+    gates_b = Box(far_gate.whole())
+    hold(cot_move, second_both, gates_b)
+    hold(cot_move, down_late)
+    downs_b = Box(far_down.whole())
     cot_z = Box(pick_home(cot_stay, cot_move))
     cot_both = send(cot_z, over_core)
     hold(cot_both, cot_core)
@@ -884,61 +936,67 @@
     hold(branch, laid)
     branch_z = send(branch, over_z)
     hidden, grads_a, grads_b, second_all, cot_all = (m.v for m in laid)
-    gb_rows, db_rows, a_rows, mlp_rows = feed_grads(
-        chip.astype(jnp.int32)[None], second_all, cot_all, hidden, grads_a, grads_b, downs_a.v, downs_b.v, chips
-    )
-    gb_rows, db_rows, a_part, mlp_rows = (Box(m) for m in (gb_rows, db_rows, a_rows, mlp_rows))
-    hold(branch_z, gb_rows, db_rows, a_part, mlp_rows)
+    *b_rows, a_part, mlp_rows = (
+        Box(m)
+        for m in feed_grads(
+            chip.astype(jnp.int32)[None], second_all, cot_all, hidden, grads_a, grads_b, downs_a.v, downs_b.v, chips
+        )
+    )
+    hold(branch_z, b_rows, a_part, mlp_rows)
     hold(branch, branch_z)
     branch_both = send(branch_z, over_core)
     branch_core = send(branch, over_core)
-    gb, db = Sum(gb_rows.v, down_order), Sum(db_rows.v, up_order)
+    gb, db = Sum(*b_rows[:2], down_order), Sum(*b_rows[2:], up_order)
     b_out = [gb.out(), db.out()]
     branch_all = Box(rows_of([branch, branch_core, branch_z, branch_both]))
 
     grad_mixed = Box(nn(branch_all.v, wo_t).astype(BF16))
     mlp_out = Box(scatter_group(lambda: half(mlp_rows.v, 1), lambda: half(mlp_rows.v, 0)))
     hold(branch_all, grad_mixed)
-    o_sum = Sum(tn(branch_all.v, mixed.v).astype(BF16), down_order)
+    o_sum = Sum(*halves_apart(tn(branch_all.v, mixed.v).astype(BF16)), down_order)
     o_out = o_sum.out()
     hold(grad_mixed, o_sum.keep)
     grad_near, grad_far, grad_bias = attend_back(
         pos, qkv, logit, seg_row.v, seg_col, lse, cum, grad_mixed.v, qcols, quarter
     )
-    grad_near, grad_far = Box(grad_near), Box(grad_far)
+    grad_near, grad_far, x_hat = Box(grad_near), Box(grad_far), Box(x_hat)
     hold(grad_near, grad_far, b_out, mlp_out)
     out_home = (hidden_res.v + mlp_out.v).astype(BF16)
-    out_sent = send(out_home, to_home)
+    out_sent = send(out_home, swap_home)
     b_late = [gb.rest(), db.rest()]
     hold(a_part, mlp_out)
     a_own = Box(
         lax.psum_scatter(a_part.v, "dp", scatter_dimension=0, tiled=True, axis_index_groups=planes)
     )
     first_parts = {}
+    feed_end = Finish()
 
     def first_part(which):
         first_parts[which] = nt(half(grad_near.v, which), wa.v) + nt(half(grad_far.v, which), wb.v)
         return first_parts[which]
 
-    x_hat = Box(x_hat)
-
-    def first_rest(near_sum):
-        hold(near_sum, x_hat)
-        grads = [Box(g) for g in first_grads(x_hat.v, grad_near.v, grad_far.v, chips)]
-        made["qa"], made["qb"] = Sum(grads[0].v, down_order), Sum(grads[1].v, up_order)
-        made["q_out"] = [made["qa"].out(), made["qb"].out()]
-        made["gate"] = grads[2]
-        hold(near_sum, grads[2])
-
-    grad_first = scatter_group(
-        lambda: first_part(1), lambda: first_part(0), lambda far_sum: hold(far_sum, grad_near, grad_far, x_hat), first_rest
-    )
-    qa, qb, gate_cols = made["qa"], made["qb"], made["gate"]
-    back_home = Box((grad_res.v + unit_back(resid, first_scale, grad_first)).astype(BF16))
-    hold(back_home, b_late, out_sent)
-    back_sent = send(back_home, to_home)
-    feed_end = Finish()
+    def first_near():
+        rows = Box(first_part(0))
+        hold(x_hat, rows)
+        made["grads"] = [Box(g) for g in first_grads(x_hat.v, grad_near.v, grad_far.v, chips)]
+        return rows.v
+
+    grad_first = Box(
+        scatter_group(
+            lambda: first_part(1),
+            first_near,
+            lambda far_sum: hold(far_sum, grad_near, grad_far, x_hat),
+            after_far=lambda far_got: hold(far_got, b_late, out_sent, made["grads"]),
+            late_core=True,
+        )
+    )
+    grads = made["grads"]
+    qa, qb, gate_cols = Sum(*grads[:2], down_order), Sum(*grads[2:4], up_order), grads[4]
     b_same = feed_end.far_one(jnp.concatenate([gb.own(), db.own()], axis=1))
+    q_out = [qa.out(), qb.out()]
+    back_home = Box((grad_res.v + unit_back(resid, first_scale, grad_first.v)).astype(BF16))
+    back_sent = send(back_home, swap_home)
+
     hold(gate_cols, back_home)
     forget = jnp.concatenate([gate_cols.v[:, k * PAIR + HEAD : k * PAIR + HEAD + fpart] for k in (0, 1)], axis=1).T
     gain_part = functools.reduce(
@@ -948,21 +1006,24 @@
     small = reorder(jnp.concatenate([forget * gain_row[None, :], gain_part[None], gain_two_part], axis=0))
     small = Box(jnp.concatenate([small, jnp.pad(grad_bias, ((0, 0), (0, width - PAIR)))], axis=0))
     small_there = send(small, over_chip(0))
-    hold(small, made["q_out"], small_there, o_out)
+
+    hold(small, q_out, small_there, o_out, b_same)
     q_late = [qa.rest(), qb.rest()]
     o_late = o_sum.rest()
     hold(feed_end.other, small)
     b_cross = feed_end.far_two()
     small = Box(small.v + small_there.v)
-    hold(small, q_late, o_late)
+    hold(small, q_late, o_late, back_sent)
     for bit in range(1, bits):
         small = Box(small.v + send(small, over_chip(bit)).v)
     near, far = small.v[:fpart], small.v[fpart:heads]
     gains, bias_sum = small.v[heads : heads + 2], small.v[heads + 2 :]
     spread_out = ((0, 0), (0, width - fpart))
     bias_near, bias_far = (jnp.pad(bias_sum[:, k * HEAD : k * HEAD + fpart], spread_out) for k in (0, 1))
-    got = send(jnp.concatenate([far, bias_far, gains], axis=0), over_half)
-    hold(a_own, q_late)
+    far_small = Box(jnp.concatenate([far, bias_far, gains], axis=0))
+    hold(far_small, q_late, o_late)
+    got = send(far_small, over_half)
+    hold(a_own, o_late)
     feed_end.near(a_own.v)
 
     own_out = o_sum.own()
@@ -976,7 +1037,7 @@
     q_same = q_end.far_one(jnp.concatenate([qb.own(), out_halves[1]], axis=1))
     q_cross = q_end.far_two()
     q_here = q_end.near(jnp.concatenate([qa.own(), out_halves[0]], axis=1))
-    hold(got, q_here, back_sent, b_same, b_cross)
+    hold(got, q_here, b_cross)
     mine = jnp.concatenate(
         [near + got.v[:fpart], bias_near + got.v[fpart : fpart + 1], gains + got.v[fpart + 1 :]], axis=0
     )
@@ -995,8 +1056,8 @@
     gate_sum, up_sum, down_sum = (
         jnp.concatenate([f[:, k * fcut : (k + 1) * fcut] for f in (f_zero, f_one)], axis=1) for k in range(3)
     )
-    input_grad = reorder(back_sent.v).astype(F32)
-    output = reorder(out_sent.v)
+    input_grad = reorder(pick_home(back_home, back_sent)).astype(F32)
+    output = reorder(pick_home(out_home, out_sent))
     q_zero, q_one = q_end.land()
 
     def joined(k):

time: 564 us -> 518 us (0.918)
  waiting for transfers between devices: 211 us -> 182 us
  starting transfers between devices: 92 us -> 72.5 us
  other arithmetic: 68.7 us -> 74.8 us
    ppermute x78, waiting for transfers between devices: 211 us -> 182 us  [send(): return Box(lax.ppermute(val(value), AXES, pairs))]
    ppermute x78, starting transfers between devices: 91.7 us -> 72.2 us  [send(): return Box(lax.ppermute(val(value), AXES, pairs))]
    unnamed x196 -> x184, local copies, waits for them, and re-layouts: 12.2 us -> 13.2 us
  transfers between devices with their start and end apart: 80 -> 80, of which waited for: 29 -> 26; matrix products, arithmetic and copies ran while one was open for 15% -> 18% of each run, Pallas kernels for 17% -> 19%
where the time goes in v3:
time: 518 us; the launch traced here: 509 us
  waiting for transfers between devices  182 us (35%)
  Pallas kernels  116 us (22%)
  other arithmetic  74.8 us (14%)
  starting transfers between devices  72.5 us (14%)
  local copies, waits for them, and re-layouts  33.7 us (7%)
  between operations  16 us (3%)
  matrix products  13.4 us (3%)
    ppermute x78, waiting for transfers between devices, send(): return Box(lax.ppermute(val(value), AXES, pairs))  182 us
    ppermute x78, starting transfers between devices, send(): return Box(lax.ppermute(val(value), AXES, pairs))  72.2 us
    pallas_call x2, Pallas kernels, feed_tokens(): pl.pallas_call(feed_kernel, grid=(1,), out_shape=outs, in_specs=[*(full_s...  33 us
    pallas_call x1, Pallas kernels, attend(): pl.pallas_call(functools.partial(forward_kernel, quarter), grid=(3,), out...  25.1 us
    pallas_call x1, Pallas kernels, attend_back(): pl.pallas_call(functools.partial(backward_kernel, quarter), grid=(3,), ou...  23.4 us
    pallas_call x1, Pallas kernels, feed_grads(): pl.pallas_call(feed_grads_kernel, out_shape=(*(jax.ShapeDtypeStruct((wide...  22.7 us
    concatenate x6, other arithmetic, rows_of(): return jnp.concatenate([val(p) for p in pieces], axis=0)  14.4 us
    unnamed x184, local copies, waits for them, and re-layouts  13.2 us
  transfers between devices with their start and end apart: 80, of which 26 were waited for; matrix products, arithmetic and copies ran while one was open for 18% of the time, Pallas kernels for 19%

profile of v3, /device:TPU:0, one launch (start us, length us, event | category | flops | bytes accessed | tf_op | source)
XLA Modules:
  0.0 508.7 jit_solution(17907032778168139576)
XLA Ops:
  11.2 2.2 shard_map.237
  13.4 3.5 collective-permute-start.1
  17.6 2.4 constant_dynamic-slice_fusion.25
  20.9 3.8 collective-permute-start.5
  33.1 6.5 %collective-permute-done = bf16[192,640]{1,0:T(8,128)(2,1)} collective-permute-done((bf16[192,640]{1,0:T(8,128)(2,1)}, bf16[192,640]{1,0:T(8,128)(2,1)}, u32[]{:S(2)}, u32[]{:S(2)}) %collective-permute-start) | collective-permute-done | bytes 245792 | tf_op jit(solution)/shard_map/ppermute | solution.py:56
  40.1 3.8 collective-permute-done.5
  45.7 1.9 collective-permute-start.10
  49.0 2.5 collective-permute-start.7
  53.8 10.0 %collective-permute-done.7 = bf16[384,640]{1,0:T(8,128)(2,1)} collective-permute-done((bf16[384,640]{1,0:T(8,128)(2,1)S(1)}, bf16[384,640]{1,0:T(8,128)(2,1)}, u32[]{:S(2)}, u32[]{:S(2)}) %collective-permute-start.7) | collective-permute-done | bytes 491552 | tf_op jit(solution)/shard_map/ppermute | solution.py:56
  63.8 9.0 %collective-permute-done.9 = bf16[384,640]{1,0:T(8,128)(2,1)} collective-permute-done((bf16[384,640]{1,0:T(8,128)(2,1)}, bf16[384,640]{1,0:T(8,128)(2,1)}, u32[]{:S(2)}, u32[]{:S(2)}) %collective-permute-start.9) | collective-permute-done | bytes 491552 | tf_op jit(solution)/shard_map/ppermute | solution.py:56
  76.1 2.8 pad_maximum_fusion.2.wa_ref
  79.6 1.9 collective-permute-start.15
  83.1 6.5 %collective-permute-done.14 = bf16[192,192]{1,0:T(8,128)(2,1)S(1)} collective-permute-done((bf16[192,192]{1,0:T(8,128)(2,1)S(1)}, bf16[192,192]{1,0:T(8,128)(2,1)S(1)}, u32[]{:S(2)}, u32[]{:S(2)}) %collective-permute-start.14) | collective-permute-done | bytes 73760 | tf_op jit(solution)/shard_map/ppermute | solution.py:56
  94.7 2.8 pad_maximum_fusion.3.wb_ref
  98.4 2.6 collective-permute-start.23
  106.3 25.1 %shard_map.238 = (bf16[1024,384]{1,0:T(8,128)(2,1)}, bf16[1024,1536]{1,0:T(8,128)(2,1)}, bf16[1024,1152]{1,0:T(8,128)(2,1)}, f32[1024,128]{1,0:T(8,128)}, f32[1024,128]{1,0:T(8,128)}, /*index=5*/f32[1024,128]{1,0:T(8,128)}) custom-call(s32[4]{0:T(128)} %pad_add_fusion.pos_ref, bf16[256,1536]{1,0:T(8,128)(2,1)} %copy-done.5, ...), custom_call_target="tpu_custom_call" | custom-call | tf_op jit(solution)/shard_map/pallas_call | solution.py:390
  131.5 3.6 collective-permute-done.23
  135.1 2.0 fusion.26
  137.4 2.2 collective-permute-done.24
  144.3 2.5 collective-permute-start.29
  146.8 22.6 %collective-permute-done.25 = bf16[256,1536]{1,0:T(8,128)(2,1)S(1)} collective-permute-done((bf16[256,1536]{1,0:T(8,128)(2,1)S(1)}, bf16[256,1536]{1,0:T(8,128)(2,1)S(1)}, u32[]{:S(2)}, u32[]{:S(2)}) %collective-permute-start.25) | collective-permute-done | bytes 786464 | tf_op jit(solution)/shard_map/ppermute | solution.py:56
  180.3 1.9 pad_maximum_fusion.ga_ref
  182.3 17.2 %collective-permute-done.31.s0_ref = bf16[256,1536]{1,0:T(8,128)(2,1)} collective-permute-done((bf16[256,1536]{1,0:T(8,128)(2,1)S(1)}, bf16[256,1536]{1,0:T(8,128)(2,1)}, u32[]{:S(2)}, u32[]{:S(2)}) %collective-permute-start.31) | collective-permute-done | bytes 786464 | tf_op jit(solution)/shard_map/ppermute | solution.py:56
  200.3 2.1 collective-permute-start.39
  203.4 3.0 pad_maximum_fusion.1.gb_ref
  206.4 7.3 %collective-permute-done.40 = bf16[384,512]{1,0:T(8,128)(2,1)S(1)} collective-permute-done((bf16[384,512]{1,0:T(8,128)(2,1)}, bf16[384,512]{1,0:T(8,128)(2,1)S(1)}, u32[]{:S(2)}, u32[]{:S(2)}) %collective-permute-start.40) | collective-permute-done | bytes 393248 | tf_op jit(solution)/shard_map/ppermute | solution.py:56
  215.0 2.6 pad_maximum_fusion.5.db_ref
  218.6 16.5 %shard_map.239 = (bf16[1024,1024]{1,0:T(8,128)(2,1)}, bf16[1024,1024]{1,0:T(8,128)(2,1)}, bf16[1024,1024]{1,0:T(8,128)(2,1)}, bf16[1024,1536]{1,0:T(8,128)(2,1)}...) custom-call(bf16[256,1536]{1,0:T(8,128)(2,1)} %collective-permute-done.31.s0_ref, ...), custom_call_target="tpu_custom_call" | custom-call | tf_op jit(solution)/shard_map/pallas_call | solution.py:438
  236.9 2.0 collective-permute-done.43
  241.1 16.5 %shard_map.240 = (bf16[1024,1024]{1,0:T(8,128)(2,1)}, bf16[1024,1024]{1,0:T(8,128)(2,1)}, bf16[1024,1024]{1,0:T(8,128)(2,1)}, bf16[1024,1536]{1,0:T(8,128)(2,1)}...) custom-call(bf16[256,1536]{1,0:T(8,128)(2,1)} %copy-done.18, ...), custom_call_target="tpu_custom_call", output_to_operand_aliasing={{0}: (8, {}), {1}: (9, {}), {2}: (10, {}), {3}: (11, {}), {... | custom-call | tf_op jit(solution)/shard_map/pallas_call | solution.py:438
  257.7 2.6 collective-permute-done.44
  261.9 2.3 collective-permute-done.45
  269.2 22.7 %shard_map.241 = (bf16[768,1024]{1,0:T(8,128)(2,1)}, bf16[768,1024]{1,0:T(8,128)(2,1)}, bf16[768,512]{1,0:T(8,128)(2,1)}, bf16[768,512]{1,0:T(8,128)(2,1)}, bf16...) custom-call(s32[1]{0:T(128)} %bitcast.11.chip_ref, bf16[1024,1536]{1,0:T(8,128)(2,1)} %get-tuple-element.306.second_ref, ...), custom_call_target="tpu_custom_call" | custom-call | tf_op jit(solution)/shard_map/pallas_call | solution.py:527
  305.1 2.7 convolution_convert_fusion.1.gmix_ref
  307.9 1.8 convolution_convert_fusion
  311.4 23.4 %shard_map.242 = (bf16[1024,640]{1,0:T(8,128)(2,1)}, bf16[1024,640]{1,0:T(8,128)(2,1)}, f32[1,128]{1,0:T(1,128)}) custom-call(s32[4]{0:T(128)} %pad_add_fusion.pos_ref, bf16[1024,1152]{1,0:T(8,128)(2,1)} %get-tuple-element.255.qkv_ref, f32[1024,128]{1,0:T(8,128)} %get-tuple-element.256.logit_ref, s32[1,1024]{1,0:T(1,128)} %copy-done.71, ...), custom_call_target="tpu_custom_call" | custom-call | tf_op jit(solution)/shard_map/pallas_call | solution.py:590
  342.1 2.0 convert_add_fusion
  351.0 1.9 collective-permute-start.58
  353.0 2.8 fusion.7
  359.8 9.9 %shard_map.243 = (bf16[768,640]{1,0:T(8,128)(2,1)}, bf16[768,640]{1,0:T(8,128)(2,1)}, bf16[768,640]{1,0:T(8,128)(2,1)}, bf16[768,640]{1,0:T(8,128)(2,1)}, f32[1536,256]{1,0:T(8,128)}) custom-call(bf16[1024,1536]{1,0:T(8,128)(2,1)} %get-tuple-element.344.x_ref, bf16[1024,640]{1,0:T(8,128)(2,1)} %get-tuple-element.336.near_ref, ...), custom_call_target="tpu_custom_call" | custom-call | tf_op jit(solution)/shard_map/pallas_call | solution.py:569
  369.7 3.0 multiply_reduce_fusion
  372.8 10.5 %collective-permute-done.55 = bf16[256,1536]{1,0:T(8,128)(2,1)} collective-permute-done((bf16[256,1536]{1,0:T(8,128)(2,1)}, bf16[256,1536]{1,0:T(8,128)(2,1)}, u32[]{:S(2)}, u32[]{:S(2)}) %collective-permute-start.55) | collective-permute-done | bytes 786464 | tf_op jit(solution)/shard_map/ppermute | solution.py:56
  399.3 26.8 %collective-permute-done.64 = bf16[192,1536]{1,0:T(8,128)(2,1)} collective-permute-done((bf16[192,1536]{1,0:T(8,128)(2,1)}, bf16[192,1536]{1,0:T(8,128)(2,1)}, u32[]{:S(2)}, u32[]{:S(2)}) %collective-permute-start.64) | collective-permute-done | bytes 589856 | tf_op jit(solution)/shard_map/ppermute | solution.py:56
  433.9 13.2 %collective-permute-done.67 = bf16[384,384]{1,0:T(8,128)(2,1)S(1)} collective-permute-done((bf16[384,384]{1,0:T(8,128)(2,1)S(1)}, bf16[384,384]{1,0:T(8,128)(2,1)S(1)}, u32[]{:S(2)}, u32[]{:S(2)}) %collective-permute-start.67) | collective-permute-done | bytes 294944 | tf_op jit(solution)/shard_map/ppermute | solution.py:56
  454.4 3.0 collective-permute-start.75
  457.6 20.3 %collective-permute-done.72 = bf16[192,1536]{1,0:T(8,128)(2,1)S(1)} collective-permute-done((bf16[192,1536]{1,0:T(8,128)(2,1)S(1)}, bf16[192,1536]{1,0:T(8,128)(2,1)S(1)}, u32[]{:S(2)}, u32[]{:S(2)}) %collective-permute-start.72) | collective-permute-done | bytes 589856 | tf_op jit(solution)/shard_map/ppermute | solution.py:56
  484.1 2.5 collective-permute-done.74
  486.6 7.1 %collective-permute-done.76 = bf16[192,832]{1,0:T(8,128)(2,1)S(1)} collective-permute-done((bf16[192,832]{1,0:T(8,128)(2,1)S(1)}, bf16[192,832]{1,0:T(8,128)(2,1)S(1)}, u32[]{:S(2)}, u32[]{:S(2)}) %collective-permute-start.76) | collective-permute-done | bytes 319520 | tf_op jit(solution)/shard_map/ppermute | solution.py:56
  (466 shorter events, 145.0 us)
Async XLA Ops:
  7.2 168.8 %all-gather.2.cloned.1.call-start = ((), (), s32[]{:S(2)}) async-start(), calls=%async_computation.1 | async-start | bytes 5898240 | tf_op jit(solution)/shard_map/all_gather | solution.py:815
  13.4 26.2 %collective-permute-start.1 = (bf16[192,640]{1,0:T(8,128)(2,1)}, bf16[192,640]{1,0:T(8,128)(2,1)}, u32[]{:S(2)}, u32[]{:S(2)}) collective-permute-start(bf16[192,640]{1,0:T(8,128)(2,1)} %get-tuple-element.206), channel_id=1, source_target_pairs={{0,6},{1,7},{2,4},{3,5},{4,2},{5,3},{6,0},{7,1},{8,14},{9,15},{10,... | collective-permute-start | bytes 737288 | tf_op jit(solution)/shard_map/ppermute | solution.py:56
  17.6 22.1 %collective-permute-start = (bf16[192,640]{1,0:T(8,128)(2,1)}, bf16[192,640]{1,0:T(8,128)(2,1)}, u32[]{:S(2)}, u32[]{:S(2)}) collective-permute-start(bf16[192,640]{1,0:T(8,128)(2,1)} %get-tuple-element.205), channel_id=1, source_target_pairs={{0,2},{1,3},{2,0},{3,1},{4,6},{5,7},{6,4},{7,5},{8,10},{9,11},{10,... | collective-permute-start | bytes 737288 | tf_op jit(solution)/shard_map/ppermute | solution.py:56
  20.9 23.0 %collective-permute-start.5 = (bf16[256,1536]{1,0:T(8,128)(2,1)}, bf16[256,1536]{1,0:T(8,128)(2,1)}, u32[]{:S(2)}, u32[]{:S(2)}) collective-permute-start(bf16[256,1536]{1,0:T(8,128)(2,1)} %pad_maximum_fusion.7), channel_id=1, source_target_pairs={{0,1},{1,0},{6,7},{7,6},{8,9},{9,8},{14,15},{15,14},{16,17},{17,16... | collective-permute-start | bytes 2359304 | tf_op jit(solution)/shard_map/ppermute | solution.py:56
  43.9 28.9 %collective-permute-start.6 = (bf16[256,1536]{1,0:T(8,128)(2,1)}, bf16[256,1536]{1,0:T(8,128)(2,1)S(1)}, u32[]{:S(2)}, u32[]{:S(2)}) collective-permute-start(bf16[256,1536]{1,0:T(8,128)(2,1)} %pad_maximum_fusion.7), channel_id=1, source_target_pairs={{0,0},{1,1},{2,4},{3,5},{4,2},{5,3},{6,6},{7,7},{8,8},{9,9},{10,12... | collective-permute-start | bytes 2359304 | tf_op jit(solution)/shard_map/ppermute | solution.py:56
  45.7 27.1 %collective-permute-start.10 = (bf16[256,1536]{1,0:T(8,128)(2,1)}, bf16[256,1536]{1,0:T(8,128)(2,1)}, u32[]{:S(2)}, u32[]{:S(2)}) collective-permute-start(bf16[256,1536]{1,0:T(8,128)(2,1)} %pad_maximum_fusion.8), channel_id=1, source_target_pairs={{0,1},{1,0},{6,7},{7,6},{8,9},{9,8},{14,15},{15,14},{16,17},{17,16... | collective-permute-start | bytes 2359304 | tf_op jit(solution)/shard_map/ppermute | solution.py:56
  53.1 19.7 %collective-permute-start.9 = (bf16[384,640]{1,0:T(8,128)(2,1)}, bf16[384,640]{1,0:T(8,128)(2,1)}, u32[]{:S(2)}, u32[]{:S(2)}) collective-permute-start(bf16[384,640]{1,0:T(8,128)(2,1)} %collective-permute-done.3), channel_id=1, source_target_pairs={{0,16},{1,17},{2,18},{3,19},{4,20},{5,21},{6,22},{7,23},{8,24},{9,... | collective-permute-start | bytes 1474568 | tf_op jit(solution)/shard_map/ppermute | solution.py:56
  75.0 22.5 %collective-permute-start.17 = (bf16[256,1536]{1,0:T(8,128)(2,1)S(1)}, bf16[256,1536]{1,0:T(8,128)(2,1)}, u32[]{:S(2)}, u32[]{:S(2)}) collective-permute-start(bf16[256,1536]{1,0:T(8,128)(2,1)S(1)} %collective-permute-done.6.x0_ref), channel_id=1, source_target_pairs={{0,4},{1,5},{2,6},{3,7},{4,0},{5,1},{6,2},{7,3},{8,12},{9,13},{10,... | collective-permute-start | bytes 2359304 | tf_op jit(solution)/shard_map/ppermute | solution.py:56
  82.8 370.0 %reduce-scatter.2.cloned.1.call-start = ((), (), s32[]{:S(2)}) async-start(), calls=%async_computation.2 | async-start | bytes 5898240 | tf_op jit(solution)/shard_map/reduce_scatter | solution.py:969
  98.4 33.1 %collective-permute-start.22 = (bf16[192,1024]{1,0:T(8,128)(2,1)}, bf16[192,1024]{1,0:T(8,128)(2,1)S(1)}, u32[]{:S(2)}, u32[]{:S(2)}) collective-permute-start(bf16[192,1024]{1,0:T(8,128)(2,1)} %get-tuple-element.239), channel_id=1, source_target_pairs={{0,2},{1,3},{2,0},{3,1},{4,6},{5,7},{6,4},{7,5},{8,10},{9,11},{10,... | collective-permute-start | bytes 1179656 | tf_op jit(solution)/shard_map/ppermute | solution.py:56
  98.4 36.6 %collective-permute-start.23 = (bf16[192,1024]{1,0:T(8,128)(2,1)S(1)}, bf16[192,1024]{1,0:T(8,128)(2,1)S(1)}, u32[]{:S(2)}, u32[]{:S(2)}) collective-permute-start(bf16[192,1024]{1,0:T(8,128)(2,1)S(1)} %get-tuple-element.240), channel_id=1, source_target_pairs={{0,6},{1,7},{2,4},{3,5},{4,2},{5,3},{6,0},{7,1},{8,14},{9,15},{10,... | collective-permute-start | bytes 1179656 | tf_op jit(solution)/shard_map/ppermute | solution.py:56
  101.1 30.3 %collective-permute-start.19 = (bf16[384,384]{1,0:T(8,128)(2,1)S(1)}, bf16[384,384]{1,0:T(8,128)(2,1)S(1)}, u32[]{:S(2)}, u32[]{:S(2)}) collective-permute-start(bf16[384,384]{1,0:T(8,128)(2,1)S(1)} %pad_maximum_fusion.17), channel_id=1, source_target_pairs={{0,8},{1,9},{2,10},{3,11},{4,12},{5,13},{6,14},{7,15},{8,0},{9,1},... | collective-permute-start | bytes 884744 | tf_op jit(solution)/shard_map/ppermute | solution.py:56
  102.6 28.8 %collective-permute-start.20 = (bf16[384,384]{1,0:T(8,128)(2,1)S(1)}, bf16[384,384]{1,0:T(8,128)(2,1)S(1)}, u32[]{:S(2)}, u32[]{:S(2)}) collective-permute-start(bf16[384,384]{1,0:T(8,128)(2,1)S(1)} %pad_maximum_fusion.17), channel_id=1, source_target_pairs={{0,16},{1,17},{2,18},{3,19},{4,20},{5,21},{6,22},{7,23},{8,24},{9,... | collective-permute-start | bytes 884744 | tf_op jit(solution)/shard_map/ppermute | solution.py:56
  104.1 27.3 %collective-permute-start.21 = (bf16[384,384]{1,0:T(8,128)(2,1)S(1)}, bf16[384,384]{1,0:T(8,128)(2,1)S(1)}, u32[]{:S(2)}, u32[]{:S(2)}) collective-permute-start(bf16[384,384]{1,0:T(8,128)(2,1)S(1)} %pad_maximum_fusion.17), channel_id=1, source_target_pairs={{0,24},{1,25},{2,26},{3,27},{4,28},{5,29},{6,30},{7,31},{8,16},{9,... | collective-permute-start | bytes 884744 | tf_op jit(solution)/shard_map/ppermute | solution.py:56
  141.1 28.2 %collective-permute-start.25 = (bf16[256,1536]{1,0:T(8,128)(2,1)S(1)}, bf16[256,1536]{1,0:T(8,128)(2,1)S(1)}, u32[]{:S(2)}, u32[]{:S(2)}) collective-permute-start(bf16[256,1536]{1,0:T(8,128)(2,1)S(1)} %fusion.8), channel_id=1, source_target_pairs={{0,1},{1,0},{2,3},{3,2},{4,5},{5,4},{6,7},{7,6},{8,9},{9,8},{10,11... | collective-permute-start | bytes 2359304 | tf_op jit(solution)/shard_map/ppermute | solution.py:56
  141.5 27.9 %collective-permute-start.27 = (bf16[384,1024]{1,0:T(8,128)(2,1)S(1)}, bf16[384,1024]{1,0:T(8,128)(2,1)}, u32[]{:S(2)}, u32[]{:S(2)}) collective-permute-start(bf16[384,1024]{1,0:T(8,128)(2,1)S(1)} %maximum_select_fusion.1), channel_id=1, source_target_pairs={{0,8},{1,9},{2,10},{3,11},{4,12},{5,13},{6,14},{7,15},{8,0},{9,1},... | collective-permute-start | bytes 2359304 | tf_op jit(solution)/shard_map/ppermute | solution.py:56
  142.6 26.8 %collective-permute-start.28 = (bf16[384,1024]{1,0:T(8,128)(2,1)S(1)}, bf16[384,1024]{1,0:T(8,128)(2,1)S(1)}, u32[]{:S(2)}, u32[]{:S(2)}) collective-permute-start(bf16[384,1024]{1,0:T(8,128)(2,1)S(1)} %maximum_select_fusion.1), channel_id=1, source_target_pairs={{0,16},{1,17},{2,18},{3,19},{4,20},{5,21},{6,22},{7,23},{8,24},{9,... | collective-permute-start | bytes 2359304 | tf_op jit(solution)/shard_map/ppermute | solution.py:56
  144.3 25.1 %collective-permute-start.29 = (bf16[192,512]{1,0:T(8,128)(2,1)S(1)}, bf16[192,512]{1,0:T(8,128)(2,1)S(1)}, u32[]{:S(2)}, u32[]{:S(2)}) collective-permute-start(bf16[192,512]{1,0:T(8,128)(2,1)S(1)} %copy-done.64), channel_id=1, source_target_pairs={{0,2},{1,3},{2,0},{3,1},{4,6},{5,7},{6,4},{7,5},{8,10},{9,11},{10,... | collective-permute-start | bytes 589832 | tf_op jit(solution)/shard_map/ppermute | solution.py:56
  146.8 23.5 %collective-permute-start.30 = (bf16[192,512]{1,0:T(8,128)(2,1)S(1)}, bf16[192,512]{1,0:T(8,128)(2,1)S(1)}, u32[]{:S(2)}, u32[]{:S(2)}) collective-permute-start(bf16[192,512]{1,0:T(8,128)(2,1)S(1)} %copy-done.63), channel_id=1, source_target_pairs={{0,6},{1,7},{2,4},{3,5},{4,2},{5,3},{6,0},{7,1},{8,14},{9,15},{10,... | collective-permute-start | bytes 589832 | tf_op jit(solution)/shard_map/ppermute | solution.py:56
  170.9 28.5 %collective-permute-start.31 = (bf16[256,1536]{1,0:T(8,128)(2,1)S(1)}, bf16[256,1536]{1,0:T(8,128)(2,1)}, u32[]{:S(2)}, u32[]{:S(2)}) collective-permute-start(bf16[256,1536]{1,0:T(8,128)(2,1)S(1)} %multiply_convert_fusion.s0_ref), channel_id=1, source_target_pairs={{0,1},{1,0},{2,3},{3,2},{4,5},{5,4},{6,7},{7,6},{8,9},{9,8},{10,11... | collective-permute-start | bytes 2359304 | tf_op jit(solution)/shard_map/ppermute | solution.py:56
  171.2 28.3 %collective-permute-start.36 = (bf16[384,512]{1,0:T(8,128)(2,1)S(1)}, bf16[384,512]{1,0:T(8,128)(2,1)}, u32[]{:S(2)}, u32[]{:S(2)}) collective-permute-start(bf16[384,512]{1,0:T(8,128)(2,1)S(1)} %maximum_select_fusion.4), channel_id=1, source_target_pairs={{0,16},{1,17},{2,18},{3,19},{4,20},{5,21},{6,22},{7,23},{8,24},{9,... | collective-permute-start | bytes 1179656 | tf_op jit(solution)/shard_map/ppermute | solution.py:56
  172.7 26.7 %collective-permute-start.37 = (bf16[384,512]{1,0:T(8,128)(2,1)S(1)}, bf16[384,512]{1,0:T(8,128)(2,1)}, u32[]{:S(2)}, u32[]{:S(2)}) collective-permute-start(bf16[384,512]{1,0:T(8,128)(2,1)S(1)} %maximum_select_fusion.4), channel_id=1, source_target_pairs={{0,8},{1,9},{2,10},{3,11},{4,12},{5,13},{6,14},{7,15},{8,0},{9,1},... | collective-permute-start | bytes 1179656 | tf_op jit(solution)/shard_map/ppermute | solution.py:56
  173.7 25.9 %collective-permute-start.35 = (bf16[384,1024]{1,0:T(8,128)(2,1)}, bf16[384,1024]{1,0:T(8,128)(2,1)}, u32[]{:S(2)}, u32[]{:S(2)}) collective-permute-start(bf16[384,1024]{1,0:T(8,128)(2,1)} %collective-permute-done.27), channel_id=1, source_target_pairs={{0,16},{1,17},{2,18},{3,19},{4,20},{5,21},{6,22},{7,23},{8,24},{9,... | collective-permute-start | bytes 2359304 | tf_op jit(solution)/shard_map/ppermute | solution.py:56
  174.2 25.4 %collective-permute-start.34 = (bf16[256,1536]{1,0:T(8,128)(2,1)}, bf16[256,1536]{1,0:T(8,128)(2,1)S(1)}, u32[]{:S(2)}, u32[]{:S(2)}) collective-permute-start(bf16[256,1536]{1,0:T(8,128)(2,1)} %pad_maximum_fusion.8), channel_id=1, source_target_pairs={{0,0},{1,1},{2,4},{3,5},{4,2},{5,3},{6,6},{7,7},{8,8},{9,9},{10,12... | collective-permute-start | bytes 2359304 | tf_op jit(solution)/shard_map/ppermute | solution.py:56
  240.5 19.8 %collective-permute-start.44 = (bf16[256,1536]{1,0:T(8,128)(2,1)S(1)}, bf16[256,1536]{1,0:T(8,128)(2,1)S(1)}, u32[]{:S(2)}, u32[]{:S(2)}) collective-permute-start(bf16[256,1536]{1,0:T(8,128)(2,1)S(1)} %add_convert_fusion.2), channel_id=1, source_target_pairs={{0,1},{1,0},{2,3},{3,2},{4,5},{5,4},{6,7},{7,6},{8,9},{9,8},{10,11... | collective-permute-start | bytes 2359304 | tf_op jit(solution)/shard_map/ppermute | solution.py:56
  268.6 23.3 %collective-permute-start.46 = (bf16[256,1536]{1,0:T(8,128)(2,1)S(1)}, bf16[256,1536]{1,0:T(8,128)(2,1)S(1)}, u32[]{:S(2)}, u32[]{:S(2)}) collective-permute-start(bf16[256,1536]{1,0:T(8,128)(2,1)S(1)} %get-tuple-element.318), channel_id=1, source_target_pairs={{0,1},{1,0},{2,3},{3,2},{4,5},{5,4},{6,7},{7,6},{8,9},{9,8},{10,11... | collective-permute-start | bytes 2359304 | tf_op jit(solution)/shard_map/ppermute | solution.py:56
  297.2 37.7 %collective-permute-start.49 = (bf16[768,1024]{1,0:T(8,128)(2,1)}, bf16[768,1024]{1,0:T(8,128)(2,1)}, u32[]{:S(2)}, u32[]{:S(2)}) collective-permute-start(bf16[768,1024]{1,0:T(8,128)(2,1)} %get-tuple-element.325), channel_id=1, source_target_pairs={{0,16},{1,17},{2,18},{3,19},{4,20},{5,21},{6,22},{7,23},{8,24},{9,... | collective-permute-start | bytes 4718600 | tf_op jit(solution)/shard_map/ppermute | solution.py:56
  299.9 35.0 %collective-permute-start.50 = (bf16[768,512]{1,0:T(8,128)(2,1)}, bf16[768,512]{1,0:T(8,128)(2,1)}, u32[]{:S(2)}, u32[]{:S(2)}) collective-permute-start(bf16[768,512]{1,0:T(8,128)(2,1)} %get-tuple-element.326), channel_id=1, source_target_pairs={{0,8},{1,9},{2,10},{3,11},{4,12},{5,13},{6,14},{7,15},{8,0},{9,1},... | collective-permute-start | bytes 2359304 | tf_op jit(solution)/shard_map/ppermute | solution.py:56
  302.3 32.5 %collective-permute-start.52 = (bf16[256,1536]{1,0:T(8,128)(2,1)}, bf16[256,1536]{1,0:T(8,128)(2,1)S(1)}, u32[]{:S(2)}, u32[]{:S(2)}) collective-permute-start(bf16[256,1536]{1,0:T(8,128)(2,1)} %get-tuple-element.432), channel_id=1, source_target_pairs={{0,1},{1,0},{2,3},{3,2},{4,5},{5,4},{6,7},{7,6},{8,9},{9,8},{10,11... | collective-permute-start | bytes 2359304 | tf_op jit(solution)/shard_map/ppermute | solution.py:56
  310.8 87.4 %collective-permute-start.63 = (bf16[768,384]{1,0:T(8,128)(2,1)}, bf16[768,384]{1,0:T(8,128)(2,1)}, u32[]{:S(2)}, u32[]{:S(2)}) collective-permute-start(bf16[768,384]{1,0:T(8,128)(2,1)} %get-tuple-element.457), channel_id=1, source_target_pairs={{0,16},{1,17},{2,18},{3,19},{4,20},{5,21},{6,22},{7,23},{8,24},{9,... | collective-permute-start | bytes 1769480 | tf_op jit(solution)/shard_map/ppermute | solution.py:56
  345.2 38.1 %collective-permute-start.56 = (bf16[384,1024]{1,0:T(8,128)(2,1)}, bf16[384,1024]{1,0:T(8,128)(2,1)}, u32[]{:S(2)}, u32[]{:S(2)}) collective-permute-start(bf16[384,1024]{1,0:T(8,128)(2,1)} %slice.648), channel_id=1, source_target_pairs={{0,8},{1,9},{2,10},{3,11},{4,12},{5,13},{6,14},{7,15},{8,0},{9,1},... | collective-permute-start | bytes 2359304 | tf_op jit(solution)/shard_map/ppermute | solution.py:56
  348.4 34.9 %collective-permute-start.57 = (bf16[384,512]{1,0:T(8,128)(2,1)}, bf16[384,512]{1,0:T(8,128)(2,1)}, u32[]{:S(2)}, u32[]{:S(2)}) collective-permute-start(bf16[384,512]{1,0:T(8,128)(2,1)} %slice.656), channel_id=1, source_target_pairs={{0,16},{1,17},{2,18},{3,19},{4,20},{5,21},{6,22},{7,23},{8,24},{9,... | collective-permute-start | bytes 1179656 | tf_op jit(solution)/shard_map/ppermute | solution.py:56
  351.0 32.3 %collective-permute-start.58 = (bf16[256,1536]{1,0:T(8,128)(2,1)}, bf16[256,1536]{1,0:T(8,128)(2,1)}, u32[]{:S(2)}, u32[]{:S(2)}) collective-permute-start(bf16[256,1536]{1,0:T(8,128)(2,1)} %add_convert_fusion), channel_id=1, source_target_pairs={{2,4},{3,5},{4,2},{5,3},{10,12},{11,13},{12,10},{13,11},{18,20},{1... | collective-permute-start | bytes 2359304 | tf_op jit(solution)/shard_map/ppermute | solution.py:56
  355.8 27.5 %collective-permute-start.55 = (bf16[256,1536]{1,0:T(8,128)(2,1)}, bf16[256,1536]{1,0:T(8,128)(2,1)}, u32[]{:S(2)}, u32[]{:S(2)}) collective-permute-start(bf16[256,1536]{1,0:T(8,128)(2,1)} %fusion.7), channel_id=1, source_target_pairs={{0,1},{1,0},{2,3},{3,2},{4,5},{5,4},{6,7},{7,6},{8,9},{9,8},{10,11... | collective-permute-start | bytes 2359304 | tf_op jit(solution)/shard_map/ppermute | solution.py:56
  384.7 41.4 %collective-permute-start.60 = (bf16[768,640]{1,0:T(8,128)(2,1)}, bf16[768,640]{1,0:T(8,128)(2,1)}, u32[]{:S(2)}, u32[]{:S(2)}) collective-permute-start(bf16[768,640]{1,0:T(8,128)(2,1)} %get-tuple-element.365), channel_id=1, source_target_pairs={{0,16},{1,17},{2,18},{3,19},{4,20},{5,21},{6,22},{7,23},{8,24},{9,... | collective-permute-start | bytes 2949128 | tf_op jit(solution)/shard_map/ppermute | solution.py:56
  385.2 40.8 %collective-permute-start.61 = (bf16[768,640]{1,0:T(8,128)(2,1)}, bf16[768,640]{1,0:T(8,128)(2,1)S(1)}, u32[]{:S(2)}, u32[]{:S(2)}) collective-permute-start(bf16[768,640]{1,0:T(8,128)(2,1)} %get-tuple-element.366), channel_id=1, source_target_pairs={{0,8},{1,9},{2,10},{3,11},{4,12},{5,13},{6,14},{7,15},{8,0},{9,1},... | collective-permute-start | bytes 2949128 | tf_op jit(solution)/shard_map/ppermute | solution.py:56
  390.0 36.0 %collective-permute-start.64 = (bf16[192,1536]{1,0:T(8,128)(2,1)}, bf16[192,1536]{1,0:T(8,128)(2,1)}, u32[]{:S(2)}, u32[]{:S(2)}) collective-permute-start(bf16[192,1536]{1,0:T(8,128)(2,1)} %get-tuple-element.455), channel_id=1, source_target_pairs={{0,2},{1,3},{2,0},{3,1},{4,6},{5,7},{6,4},{7,5},{8,10},{9,11},{10,... | collective-permute-start | bytes 1769480 | tf_op jit(solution)/shard_map/ppermute | solution.py:56
  395.9 30.2 %collective-permute-start.62 = (f32[9,1536]{1,0:T(8,128)S(1)}, f32[9,1536]{1,0:T(8,128)S(1)}, u32[]{:S(2)}, u32[]{:S(2)}) collective-permute-start(f32[9,1536]{1,0:T(8,128)S(1)} %select_maximum_fusion), channel_id=1, source_target_pairs={{0,8},{1,9},{2,10},{3,11},{4,12},{5,13},{6,14},{7,15},{8,0},{9,1},... | collective-permute-start | bytes 165896 | tf_op jit(solution)/shard_map/ppermute | solution.py:56
  398.2 48.9 %collective-permute-start.68 = (bf16[256,1536]{1,0:T(8,128)(2,1)S(1)}, bf16[256,1536]{1,0:T(8,128)(2,1)S(1)}, u32[]{:S(2)}, u32[]{:S(2)}) collective-permute-start(bf16[256,1536]{1,0:T(8,128)(2,1)S(1)} %fusion.4), channel_id=1, source_target_pairs={{2,4},{3,5},{4,2},{5,3},{10,12},{11,13},{12,10},{13,11},{18,20},{1... | collective-permute-start | bytes 2359304 | tf_op jit(solution)/shard_map/ppermute | solution.py:56
  427.6 19.5 %collective-permute-start.65 = (bf16[384,640]{1,0:T(8,128)(2,1)S(1)}, bf16[384,640]{1,0:T(8,128)(2,1)S(1)}, u32[]{:S(2)}, u32[]{:S(2)}) collective-permute-start(bf16[384,640]{1,0:T(8,128)(2,1)S(1)} %slice.655), channel_id=1, source_target_pairs={{0,8},{1,9},{2,10},{3,11},{4,12},{5,13},{6,14},{7,15},{8,0},{9,1},... | collective-permute-start | bytes 1474568 | tf_op jit(solution)/shard_map/ppermute | solution.py:56
  429.2 18.0 %collective-permute-start.66 = (bf16[384,640]{1,0:T(8,128)(2,1)S(1)}, bf16[384,640]{1,0:T(8,128)(2,1)S(1)}, u32[]{:S(2)}, u32[]{:S(2)}) collective-permute-start(bf16[384,640]{1,0:T(8,128)(2,1)S(1)} %slice.654), channel_id=1, source_target_pairs={{0,16},{1,17},{2,18},{3,19},{4,20},{5,21},{6,22},{7,23},{8,24},{9,... | collective-permute-start | bytes 1474568 | tf_op jit(solution)/shard_map/ppermute | solution.py:56
  431.9 15.2 %collective-permute-start.67 = (bf16[384,384]{1,0:T(8,128)(2,1)S(1)}, bf16[384,384]{1,0:T(8,128)(2,1)S(1)}, u32[]{:S(2)}, u32[]{:S(2)}) collective-permute-start(bf16[384,384]{1,0:T(8,128)(2,1)S(1)} %slice.657), channel_id=1, source_target_pairs={{0,8},{1,9},{2,10},{3,11},{4,12},{5,13},{6,14},{7,15},{8,0},{9,1},... | collective-permute-start | bytes 884744 | tf_op jit(solution)/shard_map/ppermute | solution.py:56
  433.9 44.0 %collective-permute-start.72 = (bf16[192,1536]{1,0:T(8,128)(2,1)S(1)}, bf16[192,1536]{1,0:T(8,128)(2,1)S(1)}, u32[]{:S(2)}, u32[]{:S(2)}) collective-permute-start(bf16[192,1536]{1,0:T(8,128)(2,1)S(1)} %copy-done.46), channel_id=1, source_target_pairs={{0,6},{1,7},{2,4},{3,5},{4,2},{5,3},{6,0},{7,1},{8,14},{9,15},{10,... | collective-permute-start | bytes 1769480 | tf_op jit(solution)/shard_map/ppermute | solution.py:56
  452.6 26.3 %collective-permute-start.70 = (f32[6,1536]{1,0:T(8,128)}, f32[6,1536]{1,0:T(8,128)}, u32[]{:S(2)}, u32[]{:S(2)}) collective-permute-start(f32[6,1536]{1,0:T(8,128)} %fusion.31), channel_id=1, source_target_pairs={{0,2},{1,3},{2,0},{3,1},{4,6},{5,7},{6,4},{7,5},{8,10},{9,11},{10,... | collective-permute-start | bytes 110600 | tf_op jit(solution)/shard_map/ppermute | solution.py:56
  454.2 24.8 %collective-permute-start.71 = (bf16[192,832]{1,0:T(8,128)(2,1)S(1)}, bf16[192,832]{1,0:T(8,128)(2,1)S(1)}, u32[]{:S(2)}, u32[]{:S(2)}) collective-permute-start(bf16[192,832]{1,0:T(8,128)(2,1)S(1)} %broadcast_select_fusion.15), channel_id=1, source_target_pairs={{0,4},{1,5},{2,6},{3,7},{4,0},{5,1},{6,2},{7,3},{8,12},{9,13},{10,... | collective-permute-start | bytes 958472 | tf_op jit(solution)/shard_map/ppermute | solution.py:56
  454.4 32.2 %collective-permute-start.75 = (bf16[192,832]{1,0:T(8,128)(2,1)S(1)}, bf16[192,832]{1,0:T(8,128)(2,1)S(1)}, u32[]{:S(2)}, u32[]{:S(2)}) collective-permute-start(bf16[192,832]{1,0:T(8,128)(2,1)S(1)} %get-tuple-element.492), channel_id=1, source_target_pairs={{0,2},{1,3},{2,0},{3,1},{4,6},{5,7},{6,4},{7,5},{8,10},{9,11},{10,... | collective-permute-start | bytes 958472 | tf_op jit(solution)/shard_map/ppermute | solution.py:56
  457.4 36.3 %collective-permute-start.76 = (bf16[192,832]{1,0:T(8,128)(2,1)S(1)}, bf16[192,832]{1,0:T(8,128)(2,1)S(1)}, u32[]{:S(2)}, u32[]{:S(2)}) collective-permute-start(bf16[192,832]{1,0:T(8,128)(2,1)S(1)} %get-tuple-element.491), channel_id=1, source_target_pairs={{0,6},{1,7},{2,4},{3,5},{4,2},{5,3},{6,0},{7,1},{8,14},{9,15},{10,... | collective-permute-start | bytes 958472 | tf_op jit(solution)/shard_map/ppermute | solution.py:56
  477.9 19.9 %collective-permute-start.77 = (bf16[192,1536]{1,0:T(8,128)(2,1)S(1)}, bf16[192,1536]{1,0:T(8,128)(2,1)S(1)}, u32[]{:S(2)}, u32[]{:S(2)}) collective-permute-start(bf16[192,1536]{1,0:T(8,128)(2,1)S(1)} %broadcast_select_fusion.4), channel_id=1, source_target_pairs={{0,4},{1,5},{2,6},{3,7},{4,0},{5,1},{6,2},{7,3},{8,12},{9,13},{10,... | collective-permute-start | bytes 1769480 | tf_op jit(solution)/shard_map/ppermute | solution.py:56
  (124 other events, 1006.6 us)
Sparse Core Ops, SparseCore 0:
  82.9 61.2 all-gather.1
  353.1 73.2 reduce-scatter.1

commit v4 on v3

--- a/solution.py
+++ b/solution.py
@@ -803,7 +803,7 @@
     feed_pack = Pack(*halves_of([gate_scaled, up_scaled, down_t], fcut))
     gate_pack, down_pack = Pack(*halves_of([gate_scaled, up_scaled], fcut)), Pack(*halves_of([down_t], fcut))
 
-    hold(x_home, far_early, near_late, cot_stay)
+    hold(x_home, far_early, cot_stay)
     x_move = send(x_home, move)
     x_core = send(x_home, over_core)
     far_late = far_one.late()
@@ -964,10 +964,6 @@
     out_home = (hidden_res.v + mlp_out.v).astype(BF16)
     out_sent = send(out_home, swap_home)
     b_late = [gb.rest(), db.rest()]
-    hold(a_part, mlp_out)
-    a_own = Box(
-        lax.psum_scatter(a_part.v, "dp", scatter_dimension=0, tiled=True, axis_index_groups=planes)
-    )
     first_parts = {}
     feed_end = Finish()
 
@@ -992,6 +988,10 @@
     )
     grads = made["grads"]
     qa, qb, gate_cols = Sum(*grads[:2], down_order), Sum(*grads[2:4], up_order), grads[4]
+    hold(a_part, grad_first)
+    a_own = Box(
+        lax.psum_scatter(a_part.v, "dp", scatter_dimension=0, tiled=True, axis_index_groups=planes)
+    )
     b_same = feed_end.far_one(jnp.concatenate([gb.own(), db.own()], axis=1))
     q_out = [qa.out(), qb.out()]
     back_home = Box((grad_res.v + unit_back(resid, first_scale, grad_first.v)).astype(BF16))
@@ -1023,8 +1023,6 @@
     far_small = Box(jnp.concatenate([far, bias_far, gains], axis=0))
     hold(far_small, q_late, o_late)
     got = send(far_small, over_half)
-    hold(a_own, o_late)
-    feed_end.near(a_own.v)
 
     own_out = o_sum.own()
     out_halves = [
@@ -1037,6 +1035,8 @@
     q_same = q_end.far_one(jnp.concatenate([qb.own(), out_halves[1]], axis=1))
     q_cross = q_end.far_two()
     q_here = q_end.near(jnp.concatenate([qa.own(), out_halves[0]], axis=1))
+    hold(a_own, q_same)
+    feed_end.near(a_own.v)
     hold(got, q_here, b_cross)
     mine = jnp.concatenate(
         [near + got.v[:fpart], bias_near + got.v[fpart : fpart + 1], gains + got.v[fpart + 1 :]], axis=0
@@ -1047,15 +1047,17 @@
     grad_bias_out = pick(jnp.concatenate([bias_mine, bias_rest]), jnp.concatenate([bias_rest, bias_mine]))
     gains = mine[fpart + 1 :] + rest[fpart + 1 :]
     gains = lax.dynamic_slice_in_dim(gains, d * share, share, 1)
-    gains = Box(gains + send(gains, over_z).v)
-    hold(gains, q_same, q_cross)
-    gains = gains.v
+    gains = gains + send(gains, over_z).v
     grad_gain_one = gains[0] / attn_gain.astype(F32)
     grad_gain_two = gains[1] / mlp_gain.astype(F32)
     f_zero, f_one = feed_end.land()
     gate_sum, up_sum, down_sum = (
         jnp.concatenate([f[:, k * fcut : (k + 1) * fcut] for f in (f_zero, f_one)], axis=1) for k in range(3)
     )
+    done = [Box(v) for v in (gate_sum * gain_two, up_sum * gain_two, down_sum.T, grad_gain_one, grad_gain_two)]
+    hold(q_same, done)
+    hold(q_cross, q_same)
+    gate_out, up_out, down_out, grad_gain_one, grad_gain_two = (b.v for b in done)
     input_grad = reorder(pick_home(back_home, back_sent)).astype(F32)
     output = reorder(pick_home(out_home, out_sent))
     q_zero, q_one = q_end.land()
@@ -1080,9 +1082,9 @@
         grad_bias_out,
         q_sums[3].T,
         grad_gain_two,
-        gate_sum * gain_two,
-        up_sum * gain_two,
-        down_sum.T,
+        gate_out,
+        up_out,
+        down_out,
     )
 
 

time: 518 us -> 511 us (0.986)
    unnamed x184 -> x166, local copies, waits for them, and re-layouts: 13.2 us -> 12.2 us
  transfers between devices with their start and end apart: 80 -> 80, of which waited for: 26 -> 25; matrix products, arithmetic and copies ran while one was open for 18% -> 18% of each run, Pallas kernels for 19% -> 19%
where the time goes in v4:
time: 511 us; the launch traced here: 502 us
  waiting for transfers between devices  178 us (35%)
  Pallas kernels  116 us (23%)
  starting transfers between devices  75.2 us (15%)
  other arithmetic  70.8 us (14%)
  local copies, waits for them, and re-layouts  31.9 us (6%)
  between operations  16 us (3%)
  matrix products  13.4 us (3%)
    ppermute x78, waiting for transfers between devices, send(): return Box(lax.ppermute(val(value), AXES, pairs))  178 us
    ppermute x78, starting transfers between devices, send(): return Box(lax.ppermute(val(value), AXES, pairs))  74.9 us
    pallas_call x2, Pallas kernels, feed_tokens(): pl.pallas_call(feed_kernel, grid=(1,), out_shape=outs, in_specs=[*(full_s...  33 us
    pallas_call x1, Pallas kernels, attend(): pl.pallas_call(functools.partial(forward_kernel, quarter), grid=(3,), out...  25.1 us
    pallas_call x1, Pallas kernels, attend_back(): pl.pallas_call(functools.partial(backward_kernel, quarter), grid=(3,), ou...  23.4 us
    pallas_call x1, Pallas kernels, feed_grads(): pl.pallas_call(feed_grads_kernel, out_shape=(*(jax.ShapeDtypeStruct((wide...  22.8 us
    concatenate x6, other arithmetic, rows_of(): return jnp.concatenate([val(p) for p in pieces], axis=0)  14.2 us
    select_n x19, other arithmetic, pick(): return jnp.where(first, val(one), val(two))  12.5 us
  transfers between devices with their start and end apart: 80, of which 25 were waited for; matrix products, arithmetic and copies ran while one was open for 18% of the time, Pallas kernels for 19%

profile of v4, /device:TPU:0, one launch (start us, length us, event | category | flops | bytes accessed | tf_op | source)
XLA Modules:
  0.0 501.9 jit_solution(10980845017320950868)
XLA Ops:
  11.2 2.2 shard_map.237
  13.4 3.5 collective-permute-start.1
  17.6 2.4 constant_dynamic-slice_fusion.25
  20.9 3.8 collective-permute-start.5
  33.1 6.6 %collective-permute-done = bf16[192,640]{1,0:T(8,128)(2,1)} collective-permute-done((bf16[192,640]{1,0:T(8,128)(2,1)}, bf16[192,640]{1,0:T(8,128)(2,1)}, u32[]{:S(2)}, u32[]{:S(2)}) %collective-permute-start) | collective-permute-done | bytes 245792 | tf_op jit(solution)/shard_map/ppermute | solution.py:56
  40.1 3.8 collective-permute-done.5
  45.7 1.9 collective-permute-start.9
  49.0 2.5 collective-permute-start.7
  53.8 10.0 %collective-permute-done.7 = bf16[384,640]{1,0:T(8,128)(2,1)} collective-permute-done((bf16[384,640]{1,0:T(8,128)(2,1)S(1)}, bf16[384,640]{1,0:T(8,128)(2,1)}, u32[]{:S(2)}, u32[]{:S(2)}) %collective-permute-start.7) | collective-permute-done | bytes 491552 | tf_op jit(solution)/shard_map/ppermute | solution.py:56
  63.8 4.1 collective-permute-done.9
  70.7 2.2 collective-permute-start.13
  72.8 2.6 pad_maximum_fusion.2.wa_ref
  79.9 6.0 %collective-permute-done.14 = bf16[192,192]{1,0:T(8,128)(2,1)S(1)} collective-permute-done((bf16[192,192]{1,0:T(8,128)(2,1)S(1)}, bf16[192,192]{1,0:T(8,128)(2,1)S(1)}, u32[]{:S(2)}, u32[]{:S(2)}) %collective-permute-start.14) | collective-permute-done | bytes 73760 | tf_op jit(solution)/shard_map/ppermute | solution.py:56
  91.8 2.8 pad_maximum_fusion.3.wb_ref
  95.5 2.4 collective-permute-start.23
  103.3 25.1 %shard_map.238 = (bf16[1024,384]{1,0:T(8,128)(2,1)}, bf16[1024,1536]{1,0:T(8,128)(2,1)}, bf16[1024,1152]{1,0:T(8,128)(2,1)}, f32[1024,128]{1,0:T(8,128)}, f32[1024,128]{1,0:T(8,128)}, /*index=5*/f32[1024,128]{1,0:T(8,128)}) custom-call(s32[4]{0:T(128)} %pad_add_fusion.pos_ref, bf16[256,1536]{1,0:T(8,128)(2,1)} %copy-done.5, ...), custom_call_target="tpu_custom_call" | custom-call | tf_op jit(solution)/shard_map/pallas_call | solution.py:390
  128.4 3.5 collective-permute-done.23
  132.0 2.0 fusion.26
  134.3 2.2 collective-permute-done.24
  140.6 3.1 collective-permute-start.29
  143.7 22.6 %collective-permute-done.25 = bf16[256,1536]{1,0:T(8,128)(2,1)S(1)} collective-permute-done((bf16[256,1536]{1,0:T(8,128)(2,1)S(1)}, bf16[256,1536]{1,0:T(8,128)(2,1)S(1)}, u32[]{:S(2)}, u32[]{:S(2)}) %collective-permute-start.25) | collective-permute-done | bytes 786464 | tf_op jit(solution)/shard_map/ppermute | solution.py:56
  178.4 18.0 %collective-permute-done.31.s0_ref = bf16[256,1536]{1,0:T(8,128)(2,1)} collective-permute-done((bf16[256,1536]{1,0:T(8,128)(2,1)S(1)}, bf16[256,1536]{1,0:T(8,128)(2,1)}, u32[]{:S(2)}, u32[]{:S(2)}) %collective-permute-start.31) | collective-permute-done | bytes 786464 | tf_op jit(solution)/shard_map/ppermute | solution.py:56
  197.3 2.1 collective-permute-start.39
  199.5 3.0 pad_maximum_fusion.1.gb_ref
  202.6 8.1 %collective-permute-done.40 = bf16[384,512]{1,0:T(8,128)(2,1)S(1)} collective-permute-done((bf16[384,512]{1,0:T(8,128)(2,1)}, bf16[384,512]{1,0:T(8,128)(2,1)S(1)}, u32[]{:S(2)}, u32[]{:S(2)}) %collective-permute-start.40) | collective-permute-done | bytes 393248 | tf_op jit(solution)/shard_map/ppermute | solution.py:56
  211.9 2.6 pad_maximum_fusion.5.db_ref
  215.5 16.4 %shard_map.239 = (bf16[1024,1024]{1,0:T(8,128)(2,1)}, bf16[1024,1024]{1,0:T(8,128)(2,1)}, bf16[1024,1024]{1,0:T(8,128)(2,1)}, bf16[1024,1536]{1,0:T(8,128)(2,1)}...) custom-call(bf16[256,1536]{1,0:T(8,128)(2,1)} %collective-permute-done.31.s0_ref, ...), custom_call_target="tpu_custom_call" | custom-call | tf_op jit(solution)/shard_map/pallas_call | solution.py:438
  233.8 2.0 collective-permute-done.43
  238.1 16.6 %shard_map.240 = (bf16[1024,1024]{1,0:T(8,128)(2,1)}, bf16[1024,1024]{1,0:T(8,128)(2,1)}, bf16[1024,1024]{1,0:T(8,128)(2,1)}, bf16[1024,1536]{1,0:T(8,128)(2,1)}...) custom-call(bf16[256,1536]{1,0:T(8,128)(2,1)} %copy-done.15, ...), custom_call_target="tpu_custom_call", output_to_operand_aliasing={{0}: (8, {}), {1}: (9, {}), {2}: (10, {}), {3}: (11, {}), {... | custom-call | tf_op jit(solution)/shard_map/pallas_call | solution.py:438
  254.6 2.6 collective-permute-done.44
  258.8 2.3 collective-permute-done.45
  263.8 1.9 fusion.35
  266.4 22.8 %shard_map.241 = (bf16[768,1024]{1,0:T(8,128)(2,1)}, bf16[768,1024]{1,0:T(8,128)(2,1)}, bf16[768,512]{1,0:T(8,128)(2,1)}, bf16[768,512]{1,0:T(8,128)(2,1)}, bf16...) custom-call(s32[1]{0:T(128)} %bitcast.11.chip_ref, bf16[1024,1536]{1,0:T(8,128)(2,1)} %get-tuple-element.310.second_ref, ...), custom_call_target="tpu_custom_call" | custom-call | tf_op jit(solution)/shard_map/pallas_call | solution.py:527
  299.8 2.7 convolution_convert_fusion.1.gmix_ref
  307.0 23.4 %shard_map.242 = (bf16[1024,640]{1,0:T(8,128)(2,1)}, bf16[1024,640]{1,0:T(8,128)(2,1)}, f32[1,128]{1,0:T(1,128)}) custom-call(s32[4]{0:T(128)} %pad_add_fusion.pos_ref, bf16[1024,1152]{1,0:T(8,128)(2,1)} %get-tuple-element.259.qkv_ref, f32[1024,128]{1,0:T(8,128)} %get-tuple-element.260.logit_ref, s32[1,1024]{1,0:T(1,128)} %copy-done.65, ...), custom_call_target="tpu_custom_call" | custom-call | tf_op jit(solution)/shard_map/pallas_call | solution.py:590
  335.7 2.4 copy-done.25
  338.0 2.0 convert_add_fusion
  346.0 1.9 collective-permute-start.58
  352.5 9.9 %shard_map.243 = (bf16[768,640]{1,0:T(8,128)(2,1)}, bf16[768,640]{1,0:T(8,128)(2,1)}, bf16[768,640]{1,0:T(8,128)(2,1)}, bf16[768,640]{1,0:T(8,128)(2,1)}, f32[1536,256]{1,0:T(8,128)}) custom-call(bf16[1024,1536]{1,0:T(8,128)(2,1)} %get-tuple-element.348.x_ref, bf16[1024,640]{1,0:T(8,128)(2,1)} %get-tuple-element.340.near_ref, ...), custom_call_target="tpu_custom_call" | custom-call | tf_op jit(solution)/shard_map/pallas_call | solution.py:569
  362.5 3.0 multiply_reduce_fusion
  365.5 10.7 %collective-permute-done.55 = bf16[256,1536]{1,0:T(8,128)(2,1)} collective-permute-done((bf16[256,1536]{1,0:T(8,128)(2,1)}, bf16[256,1536]{1,0:T(8,128)(2,1)}, u32[]{:S(2)}, u32[]{:S(2)}) %collective-permute-start.55) | collective-permute-done | bytes 786464 | tf_op jit(solution)/shard_map/ppermute | solution.py:56
  386.4 1.9 fusion.4
  393.5 26.3 %collective-permute-done.64 = bf16[192,1536]{1,0:T(8,128)(2,1)} collective-permute-done((bf16[192,1536]{1,0:T(8,128)(2,1)}, bf16[192,1536]{1,0:T(8,128)(2,1)}, u32[]{:S(2)}, u32[]{:S(2)}) %collective-permute-start.64) | collective-permute-done | bytes 589856 | tf_op jit(solution)/shard_map/ppermute | solution.py:56
  429.0 19.7 %collective-permute-done.67 = bf16[384,384]{1,0:T(8,128)(2,1)S(1)} collective-permute-done((bf16[384,384]{1,0:T(8,128)(2,1)S(1)}, bf16[384,384]{1,0:T(8,128)(2,1)S(1)}, u32[]{:S(2)}, u32[]{:S(2)}) %collective-permute-start.67) | collective-permute-done | bytes 294944 | tf_op jit(solution)/shard_map/ppermute | solution.py:56
  450.3 5.4 %collective-permute-done.69 = f32[9,1536]{1,0:T(8,128)S(1)} collective-permute-done((f32[9,1536]{1,0:T(8,128)S(1)}, f32[9,1536]{1,0:T(8,128)S(1)}, u32[]{:S(2)}, u32[]{:S(2)}) %collective-permute-start.69) | collective-permute-done | bytes 55328 | tf_op jit(solution)/shard_map/ppermute | solution.py:56
  462.6 2.0 collective-permute-start.76
  465.8 9.2 %collective-permute-done.76 = f32[2,192]{1,0:T(2,128)S(1)} collective-permute-done((f32[2,192]{1,0:T(2,128)S(1)}, f32[2,192]{1,0:T(2,128)S(1)}, u32[]{:S(2)}, u32[]{:S(2)}) %collective-permute-start.76) | collective-permute-done | bytes 1568 | tf_op jit(solution)/shard_map/ppermute | solution.py:56
  475.1 9.8 %collective-permute-done.70 = bf16[192,832]{1,0:T(8,128)(2,1)S(1)} collective-permute-done((bf16[192,832]{1,0:T(8,128)(2,1)S(1)}, bf16[192,832]{1,0:T(8,128)(2,1)S(1)}, u32[]{:S(2)}, u32[]{:S(2)}) %collective-permute-start.70) | collective-permute-done | bytes 319520 | tf_op jit(solution)/shard_map/ppermute | solution.py:56
  (449 shorter events, 141.8 us)
Async XLA Ops:
  7.2 165.0 %all-gather.2.cloned.1.call-start = ((), (), s32[]{:S(2)}) async-start(), calls=%async_computation.1 | async-start | bytes 5898240 | tf_op jit(solution)/shard_map/all_gather | solution.py:815
  13.4 26.2 %collective-permute-start.1 = (bf16[192,640]{1,0:T(8,128)(2,1)}, bf16[192,640]{1,0:T(8,128)(2,1)}, u32[]{:S(2)}, u32[]{:S(2)}) collective-permute-start(bf16[192,640]{1,0:T(8,128)(2,1)} %get-tuple-element.211), channel_id=1, source_target_pairs={{0,6},{1,7},{2,4},{3,5},{4,2},{5,3},{6,0},{7,1},{8,14},{9,15},{10,... | collective-permute-start | bytes 737288 | tf_op jit(solution)/shard_map/ppermute | solution.py:56
  17.6 22.1 %collective-permute-start = (bf16[192,640]{1,0:T(8,128)(2,1)}, bf16[192,640]{1,0:T(8,128)(2,1)}, u32[]{:S(2)}, u32[]{:S(2)}) collective-permute-start(bf16[192,640]{1,0:T(8,128)(2,1)} %get-tuple-element.210), channel_id=1, source_target_pairs={{0,2},{1,3},{2,0},{3,1},{4,6},{5,7},{6,4},{7,5},{8,10},{9,11},{10,... | collective-permute-start | bytes 737288 | tf_op jit(solution)/shard_map/ppermute | solution.py:56
  20.9 23.0 %collective-permute-start.5 = (bf16[256,1536]{1,0:T(8,128)(2,1)}, bf16[256,1536]{1,0:T(8,128)(2,1)}, u32[]{:S(2)}, u32[]{:S(2)}) collective-permute-start(bf16[256,1536]{1,0:T(8,128)(2,1)} %pad_maximum_fusion.7), channel_id=1, source_target_pairs={{0,1},{1,0},{6,7},{7,6},{8,9},{9,8},{14,15},{15,14},{16,17},{17,16... | collective-permute-start | bytes 2359304 | tf_op jit(solution)/shard_map/ppermute | solution.py:56
  43.9 19.9 %collective-permute-start.6 = (bf16[256,1536]{1,0:T(8,128)(2,1)}, bf16[256,1536]{1,0:T(8,128)(2,1)S(1)}, u32[]{:S(2)}, u32[]{:S(2)}) collective-permute-start(bf16[256,1536]{1,0:T(8,128)(2,1)} %pad_maximum_fusion.7), channel_id=1, source_target_pairs={{0,0},{1,1},{2,4},{3,5},{4,2},{5,3},{6,6},{7,7},{8,8},{9,9},{10,12... | collective-permute-start | bytes 2359304 | tf_op jit(solution)/shard_map/ppermute | solution.py:56
  45.7 22.3 %collective-permute-start.9 = (bf16[256,1536]{1,0:T(8,128)(2,1)}, bf16[256,1536]{1,0:T(8,128)(2,1)}, u32[]{:S(2)}, u32[]{:S(2)}) collective-permute-start(bf16[256,1536]{1,0:T(8,128)(2,1)} %pad_maximum_fusion.8), channel_id=1, source_target_pairs={{0,1},{1,0},{6,7},{7,6},{8,9},{9,8},{14,15},{15,14},{16,17},{17,16... | collective-permute-start | bytes 2359304 | tf_op jit(solution)/shard_map/ppermute | solution.py:56
  49.0 14.8 %collective-permute-start.7 = (bf16[384,640]{1,0:T(8,128)(2,1)S(1)}, bf16[384,640]{1,0:T(8,128)(2,1)}, u32[]{:S(2)}, u32[]{:S(2)}) collective-permute-start(bf16[384,640]{1,0:T(8,128)(2,1)S(1)} %maximum_select_fusion.3), channel_id=1, source_target_pairs={{0,16},{1,17},{2,18},{3,19},{4,20},{5,21},{6,22},{7,23},{8,24},{9,... | collective-permute-start | bytes 1474568 | tf_op jit(solution)/shard_map/ppermute | solution.py:56
  53.1 19.7 %collective-permute-start.11 = (bf16[384,640]{1,0:T(8,128)(2,1)}, bf16[384,640]{1,0:T(8,128)(2,1)S(1)}, u32[]{:S(2)}, u32[]{:S(2)}) collective-permute-start(bf16[384,640]{1,0:T(8,128)(2,1)} %copy-done.42), channel_id=1, source_target_pairs={{0,16},{1,17},{2,18},{3,19},{4,20},{5,21},{6,22},{7,23},{8,24},{9,... | collective-permute-start | bytes 1474568 | tf_op jit(solution)/shard_map/ppermute | solution.py:56
  70.7 17.0 %collective-permute-start.13 = (bf16[384,640]{1,0:T(8,128)(2,1)}, bf16[384,640]{1,0:T(8,128)(2,1)}, u32[]{:S(2)}, u32[]{:S(2)}) collective-permute-start(bf16[384,640]{1,0:T(8,128)(2,1)} %collective-permute-done.7), channel_id=1, source_target_pairs={{0,8},{1,9},{2,10},{3,11},{4,12},{5,13},{6,14},{7,15},{8,0},{9,1},... | collective-permute-start | bytes 1474568 | tf_op jit(solution)/shard_map/ppermute | solution.py:56
  75.4 19.2 %collective-permute-start.17 = (bf16[256,1536]{1,0:T(8,128)(2,1)S(1)}, bf16[256,1536]{1,0:T(8,128)(2,1)}, u32[]{:S(2)}, u32[]{:S(2)}) collective-permute-start(bf16[256,1536]{1,0:T(8,128)(2,1)S(1)} %collective-permute-done.6.x0_ref), channel_id=1, source_target_pairs={{0,4},{1,5},{2,6},{3,7},{4,0},{5,1},{6,2},{7,3},{8,12},{9,13},{10,... | collective-permute-start | bytes 2359304 | tf_op jit(solution)/shard_map/ppermute | solution.py:56
  79.7 405.2 %reduce-scatter.2.cloned.1.call-start = ((), (), s32[]{:S(2)}) async-start(), calls=%async_computation.2 | async-start | bytes 5898240 | tf_op jit(solution)/shard_map/reduce_scatter | solution.py:993
  95.5 32.9 %collective-permute-start.22 = (bf16[192,1024]{1,0:T(8,128)(2,1)}, bf16[192,1024]{1,0:T(8,128)(2,1)S(1)}, u32[]{:S(2)}, u32[]{:S(2)}) collective-permute-start(bf16[192,1024]{1,0:T(8,128)(2,1)} %get-tuple-element.243), channel_id=1, source_target_pairs={{0,2},{1,3},{2,0},{3,1},{4,6},{5,7},{6,4},{7,5},{8,10},{9,11},{10,... | collective-permute-start | bytes 1179656 | tf_op jit(solution)/shard_map/ppermute | solution.py:56
  95.5 36.4 %collective-permute-start.23 = (bf16[192,1024]{1,0:T(8,128)(2,1)S(1)}, bf16[192,1024]{1,0:T(8,128)(2,1)S(1)}, u32[]{:S(2)}, u32[]{:S(2)}) collective-permute-start(bf16[192,1024]{1,0:T(8,128)(2,1)S(1)} %get-tuple-element.244), channel_id=1, source_target_pairs={{0,6},{1,7},{2,4},{3,5},{4,2},{5,3},{6,0},{7,1},{8,14},{9,15},{10,... | collective-permute-start | bytes 1179656 | tf_op jit(solution)/shard_map/ppermute | solution.py:56
  98.1 30.3 %collective-permute-start.19 = (bf16[384,384]{1,0:T(8,128)(2,1)S(1)}, bf16[384,384]{1,0:T(8,128)(2,1)S(1)}, u32[]{:S(2)}, u32[]{:S(2)}) collective-permute-start(bf16[384,384]{1,0:T(8,128)(2,1)S(1)} %pad_maximum_fusion.17), channel_id=1, source_target_pairs={{0,8},{1,9},{2,10},{3,11},{4,12},{5,13},{6,14},{7,15},{8,0},{9,1},... | collective-permute-start | bytes 884744 | tf_op jit(solution)/shard_map/ppermute | solution.py:56
  98.4 30.0 %collective-permute-start.20 = (bf16[384,384]{1,0:T(8,128)(2,1)S(1)}, bf16[384,384]{1,0:T(8,128)(2,1)S(1)}, u32[]{:S(2)}, u32[]{:S(2)}) collective-permute-start(bf16[384,384]{1,0:T(8,128)(2,1)S(1)} %pad_maximum_fusion.17), channel_id=1, source_target_pairs={{0,16},{1,17},{2,18},{3,19},{4,20},{5,21},{6,22},{7,23},{8,24},{9,... | collective-permute-start | bytes 884744 | tf_op jit(solution)/shard_map/ppermute | solution.py:56
  100.2 28.2 %collective-permute-start.21 = (bf16[384,384]{1,0:T(8,128)(2,1)S(1)}, bf16[384,384]{1,0:T(8,128)(2,1)S(1)}, u32[]{:S(2)}, u32[]{:S(2)}) collective-permute-start(bf16[384,384]{1,0:T(8,128)(2,1)S(1)} %pad_maximum_fusion.17), channel_id=1, source_target_pairs={{0,24},{1,25},{2,26},{3,27},{4,28},{5,29},{6,30},{7,31},{8,16},{9,... | collective-permute-start | bytes 884744 | tf_op jit(solution)/shard_map/ppermute | solution.py:56
  138.0 28.2 %collective-permute-start.25 = (bf16[256,1536]{1,0:T(8,128)(2,1)S(1)}, bf16[256,1536]{1,0:T(8,128)(2,1)S(1)}, u32[]{:S(2)}, u32[]{:S(2)}) collective-permute-start(bf16[256,1536]{1,0:T(8,128)(2,1)S(1)} %fusion.8), channel_id=1, source_target_pairs={{0,1},{1,0},{2,3},{3,2},{4,5},{5,4},{6,7},{7,6},{8,9},{9,8},{10,11... | collective-permute-start | bytes 2359304 | tf_op jit(solution)/shard_map/ppermute | solution.py:56
  138.4 27.9 %collective-permute-start.27 = (bf16[384,1024]{1,0:T(8,128)(2,1)S(1)}, bf16[384,1024]{1,0:T(8,128)(2,1)}, u32[]{:S(2)}, u32[]{:S(2)}) collective-permute-start(bf16[384,1024]{1,0:T(8,128)(2,1)S(1)} %maximum_select_fusion.1), channel_id=1, source_target_pairs={{0,8},{1,9},{2,10},{3,11},{4,12},{5,13},{6,14},{7,15},{8,0},{9,1},... | collective-permute-start | bytes 2359304 | tf_op jit(solution)/shard_map/ppermute | solution.py:56
  138.7 27.6 %collective-permute-start.28 = (bf16[384,1024]{1,0:T(8,128)(2,1)S(1)}, bf16[384,1024]{1,0:T(8,128)(2,1)S(1)}, u32[]{:S(2)}, u32[]{:S(2)}) collective-permute-start(bf16[384,1024]{1,0:T(8,128)(2,1)S(1)} %maximum_select_fusion.1), channel_id=1, source_target_pairs={{0,16},{1,17},{2,18},{3,19},{4,20},{5,21},{6,22},{7,23},{8,24},{9,... | collective-permute-start | bytes 2359304 | tf_op jit(solution)/shard_map/ppermute | solution.py:56
  140.6 25.7 %collective-permute-start.29 = (bf16[192,512]{1,0:T(8,128)(2,1)S(1)}, bf16[192,512]{1,0:T(8,128)(2,1)S(1)}, u32[]{:S(2)}, u32[]{:S(2)}) collective-permute-start(bf16[192,512]{1,0:T(8,128)(2,1)S(1)} %copy-done.58), channel_id=1, source_target_pairs={{0,2},{1,3},{2,0},{3,1},{4,6},{5,7},{6,4},{7,5},{8,10},{9,11},{10,... | collective-permute-start | bytes 589832 | tf_op jit(solution)/shard_map/ppermute | solution.py:56
  143.7 23.5 %collective-permute-start.30 = (bf16[192,512]{1,0:T(8,128)(2,1)S(1)}, bf16[192,512]{1,0:T(8,128)(2,1)S(1)}, u32[]{:S(2)}, u32[]{:S(2)}) collective-permute-start(bf16[192,512]{1,0:T(8,128)(2,1)S(1)} %copy-done.57), channel_id=1, source_target_pairs={{0,6},{1,7},{2,4},{3,5},{4,2},{5,3},{6,0},{7,1},{8,14},{9,15},{10,... | collective-permute-start | bytes 589832 | tf_op jit(solution)/shard_map/ppermute | solution.py:56
  167.9 28.5 %collective-permute-start.31 = (bf16[256,1536]{1,0:T(8,128)(2,1)S(1)}, bf16[256,1536]{1,0:T(8,128)(2,1)}, u32[]{:S(2)}, u32[]{:S(2)}) collective-permute-start(bf16[256,1536]{1,0:T(8,128)(2,1)S(1)} %multiply_convert_fusion.s0_ref), channel_id=1, source_target_pairs={{0,1},{1,0},{2,3},{3,2},{4,5},{5,4},{6,7},{7,6},{8,9},{9,8},{10,11... | collective-permute-start | bytes 2359304 | tf_op jit(solution)/shard_map/ppermute | solution.py:56
  168.1 28.3 %collective-permute-start.36 = (bf16[384,512]{1,0:T(8,128)(2,1)S(1)}, bf16[384,512]{1,0:T(8,128)(2,1)}, u32[]{:S(2)}, u32[]{:S(2)}) collective-permute-start(bf16[384,512]{1,0:T(8,128)(2,1)S(1)} %maximum_select_fusion.4), channel_id=1, source_target_pairs={{0,16},{1,17},{2,18},{3,19},{4,20},{5,21},{6,22},{7,23},{8,24},{9,... | collective-permute-start | bytes 1179656 | tf_op jit(solution)/shard_map/ppermute | solution.py:56
  169.7 26.7 %collective-permute-start.37 = (bf16[384,512]{1,0:T(8,128)(2,1)S(1)}, bf16[384,512]{1,0:T(8,128)(2,1)}, u32[]{:S(2)}, u32[]{:S(2)}) collective-permute-start(bf16[384,512]{1,0:T(8,128)(2,1)S(1)} %maximum_select_fusion.4), channel_id=1, source_target_pairs={{0,8},{1,9},{2,10},{3,11},{4,12},{5,13},{6,14},{7,15},{8,0},{9,1},... | collective-permute-start | bytes 1179656 | tf_op jit(solution)/shard_map/ppermute | solution.py:56
  170.1 26.4 %collective-permute-start.35 = (bf16[384,1024]{1,0:T(8,128)(2,1)}, bf16[384,1024]{1,0:T(8,128)(2,1)}, u32[]{:S(2)}, u32[]{:S(2)}) collective-permute-start(bf16[384,1024]{1,0:T(8,128)(2,1)} %collective-permute-done.27), channel_id=1, source_target_pairs={{0,16},{1,17},{2,18},{3,19},{4,20},{5,21},{6,22},{7,23},{8,24},{9,... | collective-permute-start | bytes 2359304 | tf_op jit(solution)/shard_map/ppermute | solution.py:56
  170.4 26.2 %collective-permute-start.34 = (bf16[256,1536]{1,0:T(8,128)(2,1)}, bf16[256,1536]{1,0:T(8,128)(2,1)S(1)}, u32[]{:S(2)}, u32[]{:S(2)}) collective-permute-start(bf16[256,1536]{1,0:T(8,128)(2,1)} %pad_maximum_fusion.8), channel_id=1, source_target_pairs={{0,0},{1,1},{2,4},{3,5},{4,2},{5,3},{6,6},{7,7},{8,8},{9,9},{10,12... | collective-permute-start | bytes 2359304 | tf_op jit(solution)/shard_map/ppermute | solution.py:56
  199.5 15.0 %collective-permute-start.42 = (bf16[256,1536]{1,0:T(8,128)(2,1)S(1)}, bf16[256,1536]{1,0:T(8,128)(2,1)S(1)}, u32[]{:S(2)}, u32[]{:S(2)}) collective-permute-start(bf16[256,1536]{1,0:T(8,128)(2,1)S(1)} %collective-permute-done.34.c0_ref), channel_id=1, source_target_pairs={{0,4},{1,5},{2,6},{3,7},{4,0},{5,1},{6,2},{7,3},{8,12},{9,13},{10,... | collective-permute-start | bytes 2359304 | tf_op jit(solution)/shard_map/ppermute | solution.py:56
  237.4 19.8 %collective-permute-start.44 = (bf16[256,1536]{1,0:T(8,128)(2,1)S(1)}, bf16[256,1536]{1,0:T(8,128)(2,1)S(1)}, u32[]{:S(2)}, u32[]{:S(2)}) collective-permute-start(bf16[256,1536]{1,0:T(8,128)(2,1)S(1)} %add_convert_fusion.2), channel_id=1, source_target_pairs={{0,1},{1,0},{2,3},{3,2},{4,5},{5,4},{6,7},{7,6},{8,9},{9,8},{10,11... | collective-permute-start | bytes 2359304 | tf_op jit(solution)/shard_map/ppermute | solution.py:56
  265.7 23.4 %collective-permute-start.46 = (bf16[256,1536]{1,0:T(8,128)(2,1)}, bf16[256,1536]{1,0:T(8,128)(2,1)}, u32[]{:S(2)}, u32[]{:S(2)}) collective-permute-start(bf16[256,1536]{1,0:T(8,128)(2,1)} %get-tuple-element.322), channel_id=1, source_target_pairs={{0,1},{1,0},{2,3},{3,2},{4,5},{5,4},{6,7},{7,6},{8,9},{9,8},{10,11... | collective-permute-start | bytes 2359304 | tf_op jit(solution)/shard_map/ppermute | solution.py:56
  292.3 39.6 %collective-permute-start.49 = (bf16[768,1024]{1,0:T(8,128)(2,1)}, bf16[768,1024]{1,0:T(8,128)(2,1)}, u32[]{:S(2)}, u32[]{:S(2)}) collective-permute-start(bf16[768,1024]{1,0:T(8,128)(2,1)} %get-tuple-element.329), channel_id=1, source_target_pairs={{0,16},{1,17},{2,18},{3,19},{4,20},{5,21},{6,22},{7,23},{8,24},{9,... | collective-permute-start | bytes 4718600 | tf_op jit(solution)/shard_map/ppermute | solution.py:56
  295.0 36.9 %collective-permute-start.50 = (bf16[768,512]{1,0:T(8,128)(2,1)}, bf16[768,512]{1,0:T(8,128)(2,1)S(1)}, u32[]{:S(2)}, u32[]{:S(2)}) collective-permute-start(bf16[768,512]{1,0:T(8,128)(2,1)} %get-tuple-element.330), channel_id=1, source_target_pairs={{0,8},{1,9},{2,10},{3,11},{4,12},{5,13},{6,14},{7,15},{8,0},{9,1},... | collective-permute-start | bytes 2359304 | tf_op jit(solution)/shard_map/ppermute | solution.py:56
  296.6 33.7 %collective-permute-start.52 = (bf16[256,1536]{1,0:T(8,128)(2,1)}, bf16[256,1536]{1,0:T(8,128)(2,1)}, u32[]{:S(2)}, u32[]{:S(2)}) collective-permute-start(bf16[256,1536]{1,0:T(8,128)(2,1)} %get-tuple-element.442), channel_id=1, source_target_pairs={{0,1},{1,0},{2,3},{3,2},{4,5},{5,4},{6,7},{7,6},{8,9},{9,8},{10,11... | collective-permute-start | bytes 2359304 | tf_op jit(solution)/shard_map/ppermute | solution.py:56
  305.5 86.9 %collective-permute-start.63 = (bf16[768,384]{1,0:T(8,128)(2,1)}, bf16[768,384]{1,0:T(8,128)(2,1)}, u32[]{:S(2)}, u32[]{:S(2)}) collective-permute-start(bf16[768,384]{1,0:T(8,128)(2,1)} %get-tuple-element.467), channel_id=1, source_target_pairs={{0,16},{1,17},{2,18},{3,19},{4,20},{5,21},{6,22},{7,23},{8,24},{9,... | collective-permute-start | bytes 1769480 | tf_op jit(solution)/shard_map/ppermute | solution.py:56
  341.1 35.0 %collective-permute-start.56 = (bf16[384,1024]{1,0:T(8,128)(2,1)}, bf16[384,1024]{1,0:T(8,128)(2,1)}, u32[]{:S(2)}, u32[]{:S(2)}) collective-permute-start(bf16[384,1024]{1,0:T(8,128)(2,1)} %slice.650), channel_id=1, source_target_pairs={{0,8},{1,9},{2,10},{3,11},{4,12},{5,13},{6,14},{7,15},{8,0},{9,1},... | collective-permute-start | bytes 2359304 | tf_op jit(solution)/shard_map/ppermute | solution.py:56
  344.2 31.9 %collective-permute-start.57 = (bf16[384,512]{1,0:T(8,128)(2,1)}, bf16[384,512]{1,0:T(8,128)(2,1)}, u32[]{:S(2)}, u32[]{:S(2)}) collective-permute-start(bf16[384,512]{1,0:T(8,128)(2,1)} %slice.658), channel_id=1, source_target_pairs={{0,16},{1,17},{2,18},{3,19},{4,20},{5,21},{6,22},{7,23},{8,24},{9,... | collective-permute-start | bytes 1179656 | tf_op jit(solution)/shard_map/ppermute | solution.py:56
  346.0 30.1 %collective-permute-start.58 = (bf16[256,1536]{1,0:T(8,128)(2,1)}, bf16[256,1536]{1,0:T(8,128)(2,1)}, u32[]{:S(2)}, u32[]{:S(2)}) collective-permute-start(bf16[256,1536]{1,0:T(8,128)(2,1)} %add_convert_fusion), channel_id=1, source_target_pairs={{2,4},{3,5},{4,2},{5,3},{10,12},{11,13},{12,10},{13,11},{18,20},{1... | collective-permute-start | bytes 2359304 | tf_op jit(solution)/shard_map/ppermute | solution.py:56
  349.1 27.1 %collective-permute-start.55 = (bf16[256,1536]{1,0:T(8,128)(2,1)}, bf16[256,1536]{1,0:T(8,128)(2,1)}, u32[]{:S(2)}, u32[]{:S(2)}) collective-permute-start(bf16[256,1536]{1,0:T(8,128)(2,1)} %fusion.7), channel_id=1, source_target_pairs={{0,1},{1,0},{2,3},{3,2},{4,5},{5,4},{6,7},{7,6},{8,9},{9,8},{10,11... | collective-permute-start | bytes 2359304 | tf_op jit(solution)/shard_map/ppermute | solution.py:56
  377.0 42.8 %collective-permute-start.60 = (bf16[768,640]{1,0:T(8,128)(2,1)}, bf16[768,640]{1,0:T(8,128)(2,1)}, u32[]{:S(2)}, u32[]{:S(2)}) collective-permute-start(bf16[768,640]{1,0:T(8,128)(2,1)} %get-tuple-element.371), channel_id=1, source_target_pairs={{0,16},{1,17},{2,18},{3,19},{4,20},{5,21},{6,22},{7,23},{8,24},{9,... | collective-permute-start | bytes 2949128 | tf_op jit(solution)/shard_map/ppermute | solution.py:56
  378.3 41.5 %collective-permute-start.61 = (bf16[768,640]{1,0:T(8,128)(2,1)}, bf16[768,640]{1,0:T(8,128)(2,1)}, u32[]{:S(2)}, u32[]{:S(2)}) collective-permute-start(bf16[768,640]{1,0:T(8,128)(2,1)} %get-tuple-element.372), channel_id=1, source_target_pairs={{0,8},{1,9},{2,10},{3,11},{4,12},{5,13},{6,14},{7,15},{8,0},{9,1},... | collective-permute-start | bytes 2949128 | tf_op jit(solution)/shard_map/ppermute | solution.py:56
  382.8 37.0 %collective-permute-start.64 = (bf16[192,1536]{1,0:T(8,128)(2,1)}, bf16[192,1536]{1,0:T(8,128)(2,1)}, u32[]{:S(2)}, u32[]{:S(2)}) collective-permute-start(bf16[192,1536]{1,0:T(8,128)(2,1)} %get-tuple-element.465), channel_id=1, source_target_pairs={{0,2},{1,3},{2,0},{3,1},{4,6},{5,7},{6,4},{7,5},{8,10},{9,11},{10,... | collective-permute-start | bytes 1769480 | tf_op jit(solution)/shard_map/ppermute | solution.py:56
  389.5 30.3 %collective-permute-start.62 = (f32[9,1536]{1,0:T(8,128)S(1)}, f32[9,1536]{1,0:T(8,128)S(1)}, u32[]{:S(2)}, u32[]{:S(2)}) collective-permute-start(f32[9,1536]{1,0:T(8,128)S(1)} %select_maximum_fusion), channel_id=1, source_target_pairs={{0,8},{1,9},{2,10},{3,11},{4,12},{5,13},{6,14},{7,15},{8,0},{9,1},... | collective-permute-start | bytes 165896 | tf_op jit(solution)/shard_map/ppermute | solution.py:56
  392.5 56.2 %collective-permute-start.68 = (bf16[256,1536]{1,0:T(8,128)(2,1)S(1)}, bf16[256,1536]{1,0:T(8,128)(2,1)S(1)}, u32[]{:S(2)}, u32[]{:S(2)}) collective-permute-start(bf16[256,1536]{1,0:T(8,128)(2,1)S(1)} %fusion.4), channel_id=1, source_target_pairs={{2,4},{3,5},{4,2},{5,3},{10,12},{11,13},{12,10},{13,11},{18,20},{1... | collective-permute-start | bytes 2359304 | tf_op jit(solution)/shard_map/ppermute | solution.py:56
  421.3 27.3 %collective-permute-start.65 = (bf16[384,640]{1,0:T(8,128)(2,1)S(1)}, bf16[384,640]{1,0:T(8,128)(2,1)S(1)}, u32[]{:S(2)}, u32[]{:S(2)}) collective-permute-start(bf16[384,640]{1,0:T(8,128)(2,1)S(1)} %slice.657), channel_id=1, source_target_pairs={{0,8},{1,9},{2,10},{3,11},{4,12},{5,13},{6,14},{7,15},{8,0},{9,1},... | collective-permute-start | bytes 1474568 | tf_op jit(solution)/shard_map/ppermute | solution.py:56
  424.3 24.4 %collective-permute-start.66 = (bf16[384,640]{1,0:T(8,128)(2,1)S(1)}, bf16[384,640]{1,0:T(8,128)(2,1)S(1)}, u32[]{:S(2)}, u32[]{:S(2)}) collective-permute-start(bf16[384,640]{1,0:T(8,128)(2,1)S(1)} %slice.656), channel_id=1, source_target_pairs={{0,16},{1,17},{2,18},{3,19},{4,20},{5,21},{6,22},{7,23},{8,24},{9,... | collective-permute-start | bytes 1474568 | tf_op jit(solution)/shard_map/ppermute | solution.py:56
  426.3 22.4 %collective-permute-start.67 = (bf16[384,384]{1,0:T(8,128)(2,1)S(1)}, bf16[384,384]{1,0:T(8,128)(2,1)S(1)}, u32[]{:S(2)}, u32[]{:S(2)}) collective-permute-start(bf16[384,384]{1,0:T(8,128)(2,1)S(1)} %slice.659), channel_id=1, source_target_pairs={{0,8},{1,9},{2,10},{3,11},{4,12},{5,13},{6,14},{7,15},{8,0},{9,1},... | collective-permute-start | bytes 884744 | tf_op jit(solution)/shard_map/ppermute | solution.py:56
  429.0 32.2 %collective-permute-start.74 = (bf16[192,1536]{1,0:T(8,128)(2,1)S(1)}, bf16[192,1536]{1,0:T(8,128)(2,1)S(1)}, u32[]{:S(2)}, u32[]{:S(2)}) collective-permute-start(bf16[192,1536]{1,0:T(8,128)(2,1)S(1)} %copy-done.41), channel_id=1, source_target_pairs={{0,6},{1,7},{2,4},{3,5},{4,2},{5,3},{6,0},{7,1},{8,14},{9,15},{10,... | collective-permute-start | bytes 1769480 | tf_op jit(solution)/shard_map/ppermute | solution.py:56
  458.3 26.6 %collective-permute-start.70 = (bf16[192,832]{1,0:T(8,128)(2,1)S(1)}, bf16[192,832]{1,0:T(8,128)(2,1)S(1)}, u32[]{:S(2)}, u32[]{:S(2)}) collective-permute-start(bf16[192,832]{1,0:T(8,128)(2,1)S(1)} %get-tuple-element.502), channel_id=1, source_target_pairs={{0,2},{1,3},{2,0},{3,1},{4,6},{5,7},{6,4},{7,5},{8,10},{9,11},{10,... | collective-permute-start | bytes 958472 | tf_op jit(solution)/shard_map/ppermute | solution.py:56
  459.6 32.7 %collective-permute-start.77 = (bf16[192,832]{1,0:T(8,128)(2,1)S(1)}, bf16[192,832]{1,0:T(8,128)(2,1)S(1)}, u32[]{:S(2)}, u32[]{:S(2)}) collective-permute-start(bf16[192,832]{1,0:T(8,128)(2,1)S(1)} %get-tuple-element.501), channel_id=1, source_target_pairs={{0,6},{1,7},{2,4},{3,5},{4,2},{5,3},{6,0},{7,1},{8,14},{9,15},{10,... | collective-permute-start | bytes 958472 | tf_op jit(solution)/shard_map/ppermute | solution.py:56
  (115 other events, 1005.8 us)
Sparse Core Ops, SparseCore 0:
  79.8 61.0 all-gather.1
  386.5 73.8 reduce-scatter.1

commit v5 on v4

--- a/solution.py
+++ b/solution.py
@@ -352,8 +352,8 @@
 NO_COST = pl.CostEstimate(flops=0, bytes_accessed=0, transcendentals=0)
 
 
-def params():
-    return pltpu.CompilerParams(vmem_limit_bytes=56 * 2**20, dimension_semantics=("arbitrary",))
+def params(mib):
+    return pltpu.CompilerParams(vmem_limit_bytes=mib * 2**20, dimension_semantics=("arbitrary",))
 
 
 def pack_one(core, query, keys, values, forget, gain, bias):
@@ -368,7 +368,7 @@
             *(full_spec(w.shape) for w in (query, keys, values, forget, gain, bias)),
         ],
         out_specs=(full_spec(out.shape), full_spec(out.shape)),
-        compiler_params=params(),
+        compiler_params=params(6),
         cost_estimate=NO_COST,
     )(core, query, keys, values, forget, gain, bias)
 
@@ -394,7 +394,7 @@
         in_specs=[pl.BlockSpec(memory_space=pltpu.SMEM), *(full_spec(o.shape) for o in operands)],
         out_specs=tuple(full_spec(o.shape) for o in outs),
         scratch_shapes=[pltpu.VMEM((PAIR, length), F32), pltpu.VMEM((length, PAIR), F32)],
-        compiler_params=params(),
+        compiler_params=params(27),
         cost_estimate=NO_COST,
     )(pos, *operands)
 
@@ -446,7 +446,7 @@
             full_spec((1, wide)),
         ),
         input_output_aliases={len(operands) + k: k for k in range(len(before))},
-        compiler_params=params(),
+        compiler_params=params(28),
         cost_estimate=NO_COST,
     )(*operands, *before)
 
@@ -543,7 +543,7 @@
                 pl.BlockSpec((length, block), lambda r, chip: (0, r)),
             ),
         ),
-        compiler_params=params(),
+        compiler_params=params(26),
         cost_estimate=NO_COST,
     )(chip, second, cot, hidden, ga, gb, da, db)
 
@@ -579,7 +579,7 @@
             *pair_specs(block, cols),
             pl.BlockSpec((block, 2 * PAIR), lambda r: (r, 0)),
         ),
-        compiler_params=params(),
+        compiler_params=params(14),
         cost_estimate=NO_COST,
     )(x_hat, near, far)
 
@@ -610,7 +610,7 @@
             pltpu.VMEM((length, PAIR), F32),
             pltpu.VMEM((length, PAIR), F32),
         ],
-        compiler_params=params(),
+        compiler_params=params(28),
         cost_estimate=NO_COST,
     )(pos, qkv, logit, seg_row, seg_col, lse, cum, grad_mixed)
 

time: 511 us -> 496 us (0.971)
  Pallas kernels: 116 us -> 89.2 us
  local copies, waits for them, and re-layouts: 31.9 us -> 45.9 us
  other arithmetic: 70.8 us -> 60 us
  starting transfers between devices: 75.2 us -> 81.4 us
    unnamed x166 -> x208, local copies, waits for them, and re-layouts: 12.2 us -> 31.3 us
    pallas_call x2, Pallas kernels: 33 us -> 23.3 us  [feed_tokens(): pl.pallas_call(feed_kernel, grid=(1,), out_shape=outs, in_specs=[*(full_s...]
    ppermute x78, starting transfers between devices: 74.9 us -> 81.2 us  [send(): return Box(lax.ppermute(val(value), AXES, pairs))]
    pallas_call x1, Pallas kernels: 25.1 us -> 19.7 us  [attend(): pl.pallas_call(functools.partial(forward_kernel, quarter), grid=(3,), out...]
    concatenate x6, other arithmetic: 14.2 us -> 8.9 us  [rows_of(): return jnp.concatenate([val(p) for p in pieces], axis=0)]
    select_n x19, other arithmetic: 12.5 us -> 17.7 us  [pick(): return jnp.where(first, val(one), val(two))]
  transfers between devices with their start and end apart: 80 -> 80, of which waited for: 25 -> 27; matrix products, arithmetic and copies ran while one was open for 18% -> 16% of each run, Pallas kernels for 19% -> 16%
where the time goes in v5:
time: 496 us; the launch traced here: 486 us
  waiting for transfers between devices  178 us (36%)
  Pallas kernels  89.2 us (18%)
  starting transfers between devices  81.4 us (16%)
  other arithmetic  60 us (12%)
  local copies, waits for them, and re-layouts  45.9 us (9%)
  between operations  16.1 us (3%)
  matrix products  15 us (3%)
    ppermute x78, waiting for transfers between devices, send(): return Box(lax.ppermute(val(value), AXES, pairs))  178 us
    ppermute x78, starting transfers between devices, send(): return Box(lax.ppermute(val(value), AXES, pairs))  81.2 us
    unnamed x208, local copies, waits for them, and re-layouts  31.3 us
    pallas_call x2, Pallas kernels, feed_tokens(): pl.pallas_call(feed_kernel, grid=(1,), out_shape=outs, in_specs=[*(full_s...  23.3 us
    pallas_call x1, Pallas kernels, attend_back(): pl.pallas_call(functools.partial(backward_kernel, quarter), grid=(3,), ou...  20 us
    pallas_call x1, Pallas kernels, attend(): pl.pallas_call(functools.partial(forward_kernel, quarter), grid=(3,), out...  19.7 us
    pallas_call x1, Pallas kernels, feed_grads(): pl.pallas_call(feed_grads_kernel, out_shape=(*(jax.ShapeDtypeStruct((wide...  18.2 us
    select_n x19, other arithmetic, pick(): return jnp.where(first, val(one), val(two))  17.7 us
  transfers between devices with their start and end apart: 80, of which 27 were waited for; matrix products, arithmetic and copies ran while one was open for 16% of the time, Pallas kernels for 16%

profile of v5, /device:TPU:0, one launch (start us, length us, event | category | flops | bytes accessed | tf_op | source)
XLA Modules:
  0.0 485.9 jit_solution(16577696273683884975)
XLA Ops:
  12.6 3.5 collective-permute-start.1
  19.5 3.8 collective-permute-start.5
  32.5 6.2 %collective-permute-done = bf16[192,640]{1,0:T(8,128)(2,1)} collective-permute-done((bf16[192,640]{1,0:T(8,128)(2,1)S(1)}, bf16[192,640]{1,0:T(8,128)(2,1)}, u32[]{:S(2)}, u32[]{:S(2)}) %collective-permute-start) | collective-permute-done | bytes 245792 | tf_op jit(solution)/shard_map/ppermute | solution.py:56
  38.7 3.7 collective-permute-done.5
  45.1 1.9 collective-permute-start.9
  48.2 2.5 collective-permute-start.7
  53.0 10.0 %collective-permute-done.7 = bf16[384,640]{1,0:T(8,128)(2,1)} collective-permute-done((bf16[384,640]{1,0:T(8,128)(2,1)S(1)}, bf16[384,640]{1,0:T(8,128)(2,1)}, u32[]{:S(2)}, u32[]{:S(2)}) %collective-permute-start.7) | collective-permute-done | bytes 491552 | tf_op jit(solution)/shard_map/ppermute | solution.py:56
  63.0 2.6 collective-permute-done.9
  67.8 3.1 collective-permute-start.13
  76.9 6.6 %collective-permute-done.14 = bf16[192,192]{1,0:T(8,128)(2,1)} collective-permute-done((bf16[192,192]{1,0:T(8,128)(2,1)}, bf16[192,192]{1,0:T(8,128)(2,1)}, u32[]{:S(2)}, u32[]{:S(2)}) %collective-permute-start.14) | collective-permute-done | bytes 73760 | tf_op jit(solution)/shard_map/ppermute | solution.py:56
  91.0 2.7 pad_maximum_fusion.3.wb_ref
  95.5 2.5 collective-permute-start.23
  99.0 2.0 collective-permute-start.20
  107.9 19.7 %shard_map.238 = (bf16[1024,384]{1,0:T(8,128)(2,1)S(1)}, bf16[1024,1536]{1,0:T(8,128)(2,1)S(1)}, bf16[1024,1152]{1,0:T(8,128)(2,1)S(1)}, f32[1024,128]{1,0:T(8,1...) custom-call(s32[4]{0:T(128)S(1)} %pad_add_fusion.pos_ref, ...), custom_call_target="tpu_custom_call" | custom-call | tf_op jit(solution)/shard_map/pallas_call | solution.py:390
  127.7 5.5 %collective-permute-done.23 = bf16[192,1024]{1,0:T(8,128)(2,1)} collective-permute-done((bf16[192,1024]{1,0:T(8,128)(2,1)}, bf16[192,1024]{1,0:T(8,128)(2,1)}, u32[]{:S(2)}, u32[]{:S(2)}) %collective-permute-start.23) | collective-permute-done | bytes 393248 | tf_op jit(solution)/shard_map/ppermute | solution.py:56
  133.1 2.2 fusion.26
  135.6 2.2 collective-permute-done.24
  138.0 2.2 fusion.24
  142.3 2.1 collective-permute-start.28
  144.7 2.2 collective-permute-start.29
  146.9 21.9 %collective-permute-done.25 = bf16[256,1536]{1,0:T(8,128)(2,1)S(1)} collective-permute-done((bf16[256,1536]{1,0:T(8,128)(2,1)S(1)}, bf16[256,1536]{1,0:T(8,128)(2,1)S(1)}, u32[]{:S(2)}, u32[]{:S(2)}) %collective-permute-start.25) | collective-permute-done | bytes 786464 | tf_op jit(solution)/shard_map/ppermute | solution.py:56
  175.1 7.4 %collective-permute-start.34 = (bf16[256,1536]{1,0:T(8,128)(2,1)}, bf16[256,1536]{1,0:T(8,128)(2,1)}, u32[]{:S(2)}, u32[]{:S(2)}) collective-permute-start(bf16[256,1536]{1,0:T(8,128)(2,1)} %pad_maximum_fusion.8), channel_id=1, source_target_pairs={{0,0},{1,1},{2,4},{3,5},{4,2},{5,3},{6,6},{7,7},{8,8},{9,9},{10,12... | collective-permute-start | bytes 2359304 | tf_op jit(solution)/shard_map/ppermute | solution.py:56
  186.8 13.1 %collective-permute-done.31.s0_ref = bf16[256,1536]{1,0:T(8,128)(2,1)} collective-permute-done((bf16[256,1536]{1,0:T(8,128)(2,1)}, bf16[256,1536]{1,0:T(8,128)(2,1)}, u32[]{:S(2)}, u32[]{:S(2)}) %collective-permute-start.31) | collective-permute-done | bytes 786464 | tf_op jit(solution)/shard_map/ppermute | solution.py:56
  201.5 2.1 collective-permute-start.39
  204.3 3.0 pad_maximum_fusion.1.gb_ref
  207.3 7.6 %collective-permute-done.40 = bf16[384,512]{1,0:T(8,128)(2,1)S(1)} collective-permute-done((bf16[384,512]{1,0:T(8,128)(2,1)}, bf16[384,512]{1,0:T(8,128)(2,1)S(1)}, u32[]{:S(2)}, u32[]{:S(2)}) %collective-permute-start.40) | collective-permute-done | bytes 393248 | tf_op jit(solution)/shard_map/ppermute | solution.py:56
  217.4 11.4 %shard_map.239 = (bf16[1024,1024]{1,0:T(8,128)(2,1)S(1)}, bf16[1024,1024]{1,0:T(8,128)(2,1)S(1)}, bf16[1024,1024]{1,0:T(8,128)(2,1)S(1)}, bf16[1024,1536]{1,0:T(...) custom-call(bf16[256,1536]{1,0:T(8,128)(2,1)} %collective-permute-done.31.s0_ref, ...), custom_call_target="tpu_custom_call" | custom-call | tf_op jit(solution)/shard_map/pallas_call | solution.py:438
  229.1 2.2 collective-permute-done.43
  232.1 11.8 %shard_map.240 = (bf16[1024,1024]{1,0:T(8,128)(2,1)S(1)}, bf16[1024,1024]{1,0:T(8,128)(2,1)S(1)}, bf16[1024,1024]{1,0:T(8,128)(2,1)S(1)}, bf16[1024,1536]{1,0:T(...) custom-call(bf16[256,1536]{1,0:T(8,128)(2,1)} %multiply_convert_fusi, ...), custom_call_target="tpu_custom_call", output_to_operand_aliasing={{0}: (8, {}), {1}: (9, {}), {2}: (10, {}), {3}: (11, {}), {... | custom-call | tf_op jit(solution)/shard_map/pallas_call | solution.py:438
  245.6 5.5 %collective-permute-done.44 = bf16[256,1536]{1,0:T(8,128)(2,1)S(1)} collective-permute-done((bf16[256,1536]{1,0:T(8,128)(2,1)S(1)}, bf16[256,1536]{1,0:T(8,128)(2,1)S(1)}, u32[]{:S(2)}, u32[]{:S(2)}) %collective-permute-start.44) | collective-permute-done | bytes 786464 | tf_op jit(solution)/shard_map/ppermute | solution.py:56
  251.3 2.3 collective-permute-done.45
  254.1 2.9 fusion.35
  259.3 18.2 %shard_map.241 = (bf16[768,1024]{1,0:T(8,128)(2,1)S(1)}, bf16[768,1024]{1,0:T(8,128)(2,1)S(1)}, bf16[768,512]{1,0:T(8,128)(2,1)S(1)}, bf16[768,512]{1,0:T(8,128)...) custom-call(s32[1]{0:T(128)} %bitcast.11.chip_ref, bf16[1024,1536]{1,0:T(8,128)(2,1)S(1)} %copy-done.3, ...), custom_call_target="tpu_custom_call" | custom-call | tf_op jit(solution)/shard_map/pallas_call | solution.py:527
  277.5 2.1 copy-done.12
  295.7 3.1 convolution_convert_fusion.1.gmix_ref
  298.8 1.9 convolution_convert_fusion
  303.1 20.0 %shard_map.242 = (bf16[1024,640]{1,0:T(8,128)(2,1)S(1)}, bf16[1024,640]{1,0:T(8,128)(2,1)S(1)}, f32[1,128]{1,0:T(1,128)S(1)}) custom-call(s32[4]{0:T(128)S(1)} %pad_add_fusion.pos_ref, bf16[1024,1152]{1,0:T(8,128)(2,1)S(1)} %copy-done.18, f32[1024,128]{1,0:T(8,128)S(1)} %copy-done.32, s32[1,1024]{1,0:T(1,128)S(1)} %broadcast_select_fusion.20.segr_ref, ...), custom_call_target="tpu_custom_call" | custom-call | tf_op jit(solution)/shard_map/pallas_call | solution.py:590
  323.3 3.6 collective-permute-done.49
  340.8 7.7 %shard_map.243 = (bf16[768,640]{1,0:T(8,128)(2,1)S(1)}, bf16[768,640]{1,0:T(8,128)(2,1)}, bf16[768,640]{1,0:T(8,128)(2,1)S(1)}, bf16[768,640]{1,0:T(8,128)(2,1)}, f32[1536,256]{1,0:T(8,128)S(1)}) custom-call(bf16[1024,1536]{1,0:T(8,128)(2,1)S(1)} %copy-done.7, bf16[1024,640]{1,0:T(8,128)(2,1)S(1)} %get-tuple-element.340.near_ref, ...), custom_call_target="tpu_custom_call" | custom-call | tf_op jit(solution)/shard_map/pallas_call | solution.py:569
  350.6 12.4 %collective-permute-done.55 = bf16[256,1536]{1,0:T(8,128)(2,1)S(1)} collective-permute-done((bf16[256,1536]{1,0:T(8,128)(2,1)S(1)}, bf16[256,1536]{1,0:T(8,128)(2,1)S(1)}, u32[]{:S(2)}, u32[]{:S(2)}) %collective-permute-start.55) | collective-permute-done | bytes 786464 | tf_op jit(solution)/shard_map/ppermute | solution.py:56
  363.0 2.0 collective-permute-start.59
  372.3 3.2 fusion.4
  380.9 24.5 %collective-permute-done.64 = bf16[192,1536]{1,0:T(8,128)(2,1)} collective-permute-done((bf16[192,1536]{1,0:T(8,128)(2,1)}, bf16[192,1536]{1,0:T(8,128)(2,1)}, u32[]{:S(2)}, u32[]{:S(2)}) %collective-permute-start.64) | collective-permute-done | bytes 589856 | tf_op jit(solution)/shard_map/ppermute | solution.py:56
  414.5 18.9 %collective-permute-done.67 = bf16[384,384]{1,0:T(8,128)(2,1)S(1)} collective-permute-done((bf16[384,384]{1,0:T(8,128)(2,1)S(1)}, bf16[384,384]{1,0:T(8,128)(2,1)S(1)}, u32[]{:S(2)}, u32[]{:S(2)}) %collective-permute-start.67) | collective-permute-done | bytes 294944 | tf_op jit(solution)/shard_map/ppermute | solution.py:56
  436.5 4.2 collective-permute-done.69
  442.7 1.9 collective-permute-start.70
  449.9 10.2 %collective-permute-done.76 = f32[2,192]{1,0:T(2,128)S(1)} collective-permute-done((f32[2,192]{1,0:T(2,128)S(1)}, f32[2,192]{1,0:T(2,128)S(1)}, u32[]{:S(2)}, u32[]{:S(2)}) %collective-permute-start.76) | collective-permute-done | bytes 1568 | tf_op jit(solution)/shard_map/ppermute | solution.py:56
  460.1 8.8 %collective-permute-done.70 = bf16[192,832]{1,0:T(8,128)(2,1)S(1)} collective-permute-done((bf16[192,832]{1,0:T(8,128)(2,1)S(1)}, bf16[192,832]{1,0:T(8,128)(2,1)S(1)}, u32[]{:S(2)}, u32[]{:S(2)}) %collective-permute-start.70) | collective-permute-done | bytes 319520 | tf_op jit(solution)/shard_map/ppermute | solution.py:56
  (491 shorter events, 149.0 us)
Async XLA Ops:
  7.2 175.3 %all-gather.2.cloned.1.call-start = ((), (), s32[]{:S(2)}) async-start(), calls=%async_computation.1 | async-start | bytes 5898240 | tf_op jit(solution)/shard_map/all_gather | solution.py:815
  12.6 26.1 %collective-permute-start.1 = (bf16[192,640]{1,0:T(8,128)(2,1)S(1)}, bf16[192,640]{1,0:T(8,128)(2,1)S(1)}, u32[]{:S(2)}, u32[]{:S(2)}) collective-permute-start(bf16[192,640]{1,0:T(8,128)(2,1)S(1)} %get-tuple-element.211), channel_id=1, source_target_pairs={{0,6},{1,7},{2,4},{3,5},{4,2},{5,3},{6,0},{7,1},{8,14},{9,15},{10,... | collective-permute-start | bytes 737288 | tf_op jit(solution)/shard_map/ppermute | solution.py:56
  16.8 21.8 %collective-permute-start = (bf16[192,640]{1,0:T(8,128)(2,1)S(1)}, bf16[192,640]{1,0:T(8,128)(2,1)}, u32[]{:S(2)}, u32[]{:S(2)}) collective-permute-start(bf16[192,640]{1,0:T(8,128)(2,1)S(1)} %get-tuple-element.210), channel_id=1, source_target_pairs={{0,2},{1,3},{2,0},{3,1},{4,6},{5,7},{6,4},{7,5},{8,10},{9,11},{10,... | collective-permute-start | bytes 737288 | tf_op jit(solution)/shard_map/ppermute | solution.py:56
  19.5 22.9 %collective-permute-start.5 = (bf16[256,1536]{1,0:T(8,128)(2,1)}, bf16[256,1536]{1,0:T(8,128)(2,1)S(1)}, u32[]{:S(2)}, u32[]{:S(2)}) collective-permute-start(bf16[256,1536]{1,0:T(8,128)(2,1)} %pad_maximum_fusion.7), channel_id=1, source_target_pairs={{0,1},{1,0},{6,7},{7,6},{8,9},{9,8},{14,15},{15,14},{16,17},{17,16... | collective-permute-start | bytes 2359304 | tf_op jit(solution)/shard_map/ppermute | solution.py:56
  43.3 19.7 %collective-permute-start.6 = (bf16[256,1536]{1,0:T(8,128)(2,1)}, bf16[256,1536]{1,0:T(8,128)(2,1)S(1)}, u32[]{:S(2)}, u32[]{:S(2)}) collective-permute-start(bf16[256,1536]{1,0:T(8,128)(2,1)} %pad_maximum_fusion.7), channel_id=1, source_target_pairs={{0,0},{1,1},{2,4},{3,5},{4,2},{5,3},{6,6},{7,7},{8,8},{9,9},{10,12... | collective-permute-start | bytes 2359304 | tf_op jit(solution)/shard_map/ppermute | solution.py:56
  45.1 20.5 %collective-permute-start.9 = (bf16[256,1536]{1,0:T(8,128)(2,1)}, bf16[256,1536]{1,0:T(8,128)(2,1)S(1)}, u32[]{:S(2)}, u32[]{:S(2)}) collective-permute-start(bf16[256,1536]{1,0:T(8,128)(2,1)} %pad_maximum_fusion.8), channel_id=1, source_target_pairs={{0,1},{1,0},{6,7},{7,6},{8,9},{9,8},{14,15},{15,14},{16,17},{17,16... | collective-permute-start | bytes 2359304 | tf_op jit(solution)/shard_map/ppermute | solution.py:56
  48.2 14.7 %collective-permute-start.7 = (bf16[384,640]{1,0:T(8,128)(2,1)S(1)}, bf16[384,640]{1,0:T(8,128)(2,1)}, u32[]{:S(2)}, u32[]{:S(2)}) collective-permute-start(bf16[384,640]{1,0:T(8,128)(2,1)S(1)} %maximum_select_fusion.3), channel_id=1, source_target_pairs={{0,16},{1,17},{2,18},{3,19},{4,20},{5,21},{6,22},{7,23},{8,24},{9,... | collective-permute-start | bytes 1474568 | tf_op jit(solution)/shard_map/ppermute | solution.py:56
  52.3 18.6 %collective-permute-start.11 = (bf16[384,640]{1,0:T(8,128)(2,1)}, bf16[384,640]{1,0:T(8,128)(2,1)S(1)}, u32[]{:S(2)}, u32[]{:S(2)}) collective-permute-start(bf16[384,640]{1,0:T(8,128)(2,1)} %copy-done.79), channel_id=1, source_target_pairs={{0,16},{1,17},{2,18},{3,19},{4,20},{5,21},{6,22},{7,23},{8,24},{9,... | collective-permute-start | bytes 1474568 | tf_op jit(solution)/shard_map/ppermute | solution.py:56
  67.8 16.9 %collective-permute-start.13 = (bf16[384,640]{1,0:T(8,128)(2,1)}, bf16[384,640]{1,0:T(8,128)(2,1)}, u32[]{:S(2)}, u32[]{:S(2)}) collective-permute-start(bf16[384,640]{1,0:T(8,128)(2,1)} %collective-permute-done.7), channel_id=1, source_target_pairs={{0,8},{1,9},{2,10},{3,11},{4,12},{5,13},{6,14},{7,15},{8,0},{9,1},... | collective-permute-start | bytes 1474568 | tf_op jit(solution)/shard_map/ppermute | solution.py:56
  72.3 21.4 %collective-permute-start.17 = (bf16[256,1536]{1,0:T(8,128)(2,1)S(1)}, bf16[256,1536]{1,0:T(8,128)(2,1)S(1)}, u32[]{:S(2)}, u32[]{:S(2)}) collective-permute-start(bf16[256,1536]{1,0:T(8,128)(2,1)S(1)} %collective-permute-done.6.x0_ref), channel_id=1, source_target_pairs={{0,4},{1,5},{2,6},{3,7},{4,0},{5,1},{6,2},{7,3},{8,12},{9,13},{10,... | collective-permute-start | bytes 2359304 | tf_op jit(solution)/shard_map/ppermute | solution.py:56
  76.6 392.3 %reduce-scatter.2.cloned.1.call-start = ((), (), s32[]{:S(2)}) async-start(), calls=%async_computation.2 | async-start | bytes 5898240 | tf_op jit(solution)/shard_map/reduce_scatter | solution.py:993
  95.5 32.2 %collective-permute-start.22 = (bf16[192,1024]{1,0:T(8,128)(2,1)}, bf16[192,1024]{1,0:T(8,128)(2,1)}, u32[]{:S(2)}, u32[]{:S(2)}) collective-permute-start(bf16[192,1024]{1,0:T(8,128)(2,1)} %get-tuple-element.243), channel_id=1, source_target_pairs={{0,2},{1,3},{2,0},{3,1},{4,6},{5,7},{6,4},{7,5},{8,10},{9,11},{10,... | collective-permute-start | bytes 1179656 | tf_op jit(solution)/shard_map/ppermute | solution.py:56
  95.5 37.6 %collective-permute-start.23 = (bf16[192,1024]{1,0:T(8,128)(2,1)}, bf16[192,1024]{1,0:T(8,128)(2,1)}, u32[]{:S(2)}, u32[]{:S(2)}) collective-permute-start(bf16[192,1024]{1,0:T(8,128)(2,1)} %get-tuple-element.244), channel_id=1, source_target_pairs={{0,6},{1,7},{2,4},{3,5},{4,2},{5,3},{6,0},{7,1},{8,14},{9,15},{10,... | collective-permute-start | bytes 1179656 | tf_op jit(solution)/shard_map/ppermute | solution.py:56
  98.8 28.8 %collective-permute-start.19 = (bf16[384,384]{1,0:T(8,128)(2,1)}, bf16[384,384]{1,0:T(8,128)(2,1)}, u32[]{:S(2)}, u32[]{:S(2)}) collective-permute-start(bf16[384,384]{1,0:T(8,128)(2,1)} %pad_maximum_fusion.17), channel_id=1, source_target_pairs={{0,8},{1,9},{2,10},{3,11},{4,12},{5,13},{6,14},{7,15},{8,0},{9,1},... | collective-permute-start | bytes 884744 | tf_op jit(solution)/shard_map/ppermute | solution.py:56
  99.0 28.6 %collective-permute-start.20 = (bf16[384,384]{1,0:T(8,128)(2,1)}, bf16[384,384]{1,0:T(8,128)(2,1)}, u32[]{:S(2)}, u32[]{:S(2)}) collective-permute-start(bf16[384,384]{1,0:T(8,128)(2,1)} %pad_maximum_fusion.17), channel_id=1, source_target_pairs={{0,16},{1,17},{2,18},{3,19},{4,20},{5,21},{6,22},{7,23},{8,24},{9,... | collective-permute-start | bytes 884744 | tf_op jit(solution)/shard_map/ppermute | solution.py:56
  101.0 26.7 %collective-permute-start.21 = (bf16[384,384]{1,0:T(8,128)(2,1)}, bf16[384,384]{1,0:T(8,128)(2,1)}, u32[]{:S(2)}, u32[]{:S(2)}) collective-permute-start(bf16[384,384]{1,0:T(8,128)(2,1)} %pad_maximum_fusion.17), channel_id=1, source_target_pairs={{0,24},{1,25},{2,26},{3,27},{4,28},{5,29},{6,30},{7,31},{8,16},{9,... | collective-permute-start | bytes 884744 | tf_op jit(solution)/shard_map/ppermute | solution.py:56
  140.5 28.2 %collective-permute-start.25 = (bf16[256,1536]{1,0:T(8,128)(2,1)S(1)}, bf16[256,1536]{1,0:T(8,128)(2,1)S(1)}, u32[]{:S(2)}, u32[]{:S(2)}) collective-permute-start(bf16[256,1536]{1,0:T(8,128)(2,1)S(1)} %fusion.8), channel_id=1, source_target_pairs={{0,1},{1,0},{2,3},{3,2},{4,5},{5,4},{6,7},{7,6},{8,9},{9,8},{10,11... | collective-permute-start | bytes 2359304 | tf_op jit(solution)/shard_map/ppermute | solution.py:56
  142.2 26.5 %collective-permute-start.27 = (bf16[384,1024]{1,0:T(8,128)(2,1)S(1)}, bf16[384,1024]{1,0:T(8,128)(2,1)}, u32[]{:S(2)}, u32[]{:S(2)}) collective-permute-start(bf16[384,1024]{1,0:T(8,128)(2,1)S(1)} %maximum_select_fusion.1), channel_id=1, source_target_pairs={{0,8},{1,9},{2,10},{3,11},{4,12},{5,13},{6,14},{7,15},{8,0},{9,1},... | collective-permute-start | bytes 2359304 | tf_op jit(solution)/shard_map/ppermute | solution.py:56
  142.3 26.4 %collective-permute-start.28 = (bf16[384,1024]{1,0:T(8,128)(2,1)S(1)}, bf16[384,1024]{1,0:T(8,128)(2,1)S(1)}, u32[]{:S(2)}, u32[]{:S(2)}) collective-permute-start(bf16[384,1024]{1,0:T(8,128)(2,1)S(1)} %maximum_select_fusion.1), channel_id=1, source_target_pairs={{0,16},{1,17},{2,18},{3,19},{4,20},{5,21},{6,22},{7,23},{8,24},{9,... | collective-permute-start | bytes 2359304 | tf_op jit(solution)/shard_map/ppermute | solution.py:56
  144.7 24.1 %collective-permute-start.29 = (bf16[192,512]{1,0:T(8,128)(2,1)S(1)}, bf16[192,512]{1,0:T(8,128)(2,1)S(1)}, u32[]{:S(2)}, u32[]{:S(2)}) collective-permute-start(bf16[192,512]{1,0:T(8,128)(2,1)S(1)} %copy-done.96), channel_id=1, source_target_pairs={{0,2},{1,3},{2,0},{3,1},{4,6},{5,7},{6,4},{7,5},{8,10},{9,11},{10,... | collective-permute-start | bytes 589832 | tf_op jit(solution)/shard_map/ppermute | solution.py:56
  146.9 22.7 %collective-permute-start.30 = (bf16[192,512]{1,0:T(8,128)(2,1)S(1)}, bf16[192,512]{1,0:T(8,128)(2,1)S(1)}, u32[]{:S(2)}, u32[]{:S(2)}) collective-permute-start(bf16[192,512]{1,0:T(8,128)(2,1)S(1)} %copy-done.95), channel_id=1, source_target_pairs={{0,6},{1,7},{2,4},{3,5},{4,2},{5,3},{6,0},{7,1},{8,14},{9,15},{10,... | collective-permute-start | bytes 589832 | tf_op jit(solution)/shard_map/ppermute | solution.py:56
  171.2 28.7 %collective-permute-start.31 = (bf16[256,1536]{1,0:T(8,128)(2,1)}, bf16[256,1536]{1,0:T(8,128)(2,1)}, u32[]{:S(2)}, u32[]{:S(2)}) collective-permute-start(bf16[256,1536]{1,0:T(8,128)(2,1)} %multiply_convert_fusion.s0_ref), channel_id=1, source_target_pairs={{0,1},{1,0},{2,3},{3,2},{4,5},{5,4},{6,7},{7,6},{8,9},{9,8},{10,11... | collective-permute-start | bytes 2359304 | tf_op jit(solution)/shard_map/ppermute | solution.py:56
  172.1 27.8 %collective-permute-start.36 = (bf16[384,512]{1,0:T(8,128)(2,1)}, bf16[384,512]{1,0:T(8,128)(2,1)}, u32[]{:S(2)}, u32[]{:S(2)}) collective-permute-start(bf16[384,512]{1,0:T(8,128)(2,1)} %maximum_select_fusion.4), channel_id=1, source_target_pairs={{0,16},{1,17},{2,18},{3,19},{4,20},{5,21},{6,22},{7,23},{8,24},{9,... | collective-permute-start | bytes 1179656 | tf_op jit(solution)/shard_map/ppermute | solution.py:56
  173.6 26.3 %collective-permute-start.37 = (bf16[384,512]{1,0:T(8,128)(2,1)}, bf16[384,512]{1,0:T(8,128)(2,1)}, u32[]{:S(2)}, u32[]{:S(2)}) collective-permute-start(bf16[384,512]{1,0:T(8,128)(2,1)} %maximum_select_fusion.4), channel_id=1, source_target_pairs={{0,8},{1,9},{2,10},{3,11},{4,12},{5,13},{6,14},{7,15},{8,0},{9,1},... | collective-permute-start | bytes 1179656 | tf_op jit(solution)/shard_map/ppermute | solution.py:56
  174.2 26.5 %collective-permute-start.35 = (bf16[384,1024]{1,0:T(8,128)(2,1)}, bf16[384,1024]{1,0:T(8,128)(2,1)}, u32[]{:S(2)}, u32[]{:S(2)}) collective-permute-start(bf16[384,1024]{1,0:T(8,128)(2,1)} %collective-permute-done.27), channel_id=1, source_target_pairs={{0,16},{1,17},{2,18},{3,19},{4,20},{5,21},{6,22},{7,23},{8,24},{9,... | collective-permute-start | bytes 2359304 | tf_op jit(solution)/shard_map/ppermute | solution.py:56
  175.1 25.7 %collective-permute-start.34 = (bf16[256,1536]{1,0:T(8,128)(2,1)}, bf16[256,1536]{1,0:T(8,128)(2,1)}, u32[]{:S(2)}, u32[]{:S(2)}) collective-permute-start(bf16[256,1536]{1,0:T(8,128)(2,1)} %pad_maximum_fusion.8), channel_id=1, source_target_pairs={{0,0},{1,1},{2,4},{3,5},{4,2},{5,3},{6,6},{7,7},{8,8},{9,9},{10,12... | collective-permute-start | bytes 2359304 | tf_op jit(solution)/shard_map/ppermute | solution.py:56
  231.4 19.6 %collective-permute-start.44 = (bf16[256,1536]{1,0:T(8,128)(2,1)S(1)}, bf16[256,1536]{1,0:T(8,128)(2,1)S(1)}, u32[]{:S(2)}, u32[]{:S(2)}) collective-permute-start(bf16[256,1536]{1,0:T(8,128)(2,1)S(1)} %add_convert_fusion.2), channel_id=1, source_target_pairs={{0,1},{1,0},{2,3},{3,2},{4,5},{5,4},{6,7},{7,6},{8,9},{9,8},{10,11... | collective-permute-start | bytes 2359304 | tf_op jit(solution)/shard_map/ppermute | solution.py:56
  257.0 28.5 %collective-permute-start.46 = (bf16[256,1536]{1,0:T(8,128)(2,1)S(1)}, bf16[256,1536]{1,0:T(8,128)(2,1)S(1)}, u32[]{:S(2)}, u32[]{:S(2)}) collective-permute-start(bf16[256,1536]{1,0:T(8,128)(2,1)S(1)} %get-tuple-element.322), channel_id=1, source_target_pairs={{0,1},{1,0},{2,3},{3,2},{4,5},{5,4},{6,7},{7,6},{8,9},{9,8},{10,11... | collective-permute-start | bytes 2359304 | tf_op jit(solution)/shard_map/ppermute | solution.py:56
  289.5 37.5 %collective-permute-start.49 = (bf16[768,1024]{1,0:T(8,128)(2,1)}, bf16[768,1024]{1,0:T(8,128)(2,1)S(1)}, u32[]{:S(2)}, u32[]{:S(2)}) collective-permute-start(bf16[768,1024]{1,0:T(8,128)(2,1)} %copy-done.40), channel_id=1, source_target_pairs={{0,16},{1,17},{2,18},{3,19},{4,20},{5,21},{6,22},{7,23},{8,24},{9,... | collective-permute-start | bytes 4718600 | tf_op jit(solution)/shard_map/ppermute | solution.py:56
  292.2 31.1 %collective-permute-start.50 = (bf16[768,512]{1,0:T(8,128)(2,1)S(1)}, bf16[768,512]{1,0:T(8,128)(2,1)S(1)}, u32[]{:S(2)}, u32[]{:S(2)}) collective-permute-start(bf16[768,512]{1,0:T(8,128)(2,1)S(1)} %copy-done.44), channel_id=1, source_target_pairs={{0,8},{1,9},{2,10},{3,11},{4,12},{5,13},{6,14},{7,15},{8,0},{9,1},... | collective-permute-start | bytes 2359304 | tf_op jit(solution)/shard_map/ppermute | solution.py:56
  293.3 29.8 %collective-permute-start.52 = (bf16[256,1536]{1,0:T(8,128)(2,1)S(1)}, bf16[256,1536]{1,0:T(8,128)(2,1)S(1)}, u32[]{:S(2)}, u32[]{:S(2)}) collective-permute-start(bf16[256,1536]{1,0:T(8,128)(2,1)S(1)} %get-tuple-element.442), channel_id=1, source_target_pairs={{0,1},{1,0},{2,3},{3,2},{4,5},{5,4},{6,7},{7,6},{8,9},{9,8},{10,11... | collective-permute-start | bytes 2359304 | tf_op jit(solution)/shard_map/ppermute | solution.py:56
  301.9 78.1 %collective-permute-start.63 = (bf16[768,384]{1,0:T(8,128)(2,1)}, bf16[768,384]{1,0:T(8,128)(2,1)}, u32[]{:S(2)}, u32[]{:S(2)}) collective-permute-start(bf16[768,384]{1,0:T(8,128)(2,1)} %get-tuple-element.467), channel_id=1, source_target_pairs={{0,16},{1,17},{2,18},{3,19},{4,20},{5,21},{6,22},{7,23},{8,24},{9,... | collective-permute-start | bytes 1769480 | tf_op jit(solution)/shard_map/ppermute | solution.py:56
  332.0 30.9 %collective-permute-start.56 = (bf16[384,1024]{1,0:T(8,128)(2,1)S(1)}, bf16[384,1024]{1,0:T(8,128)(2,1)S(1)}, u32[]{:S(2)}, u32[]{:S(2)}) collective-permute-start(bf16[384,1024]{1,0:T(8,128)(2,1)S(1)} %slice.650), channel_id=1, source_target_pairs={{0,8},{1,9},{2,10},{3,11},{4,12},{5,13},{6,14},{7,15},{8,0},{9,1},... | collective-permute-start | bytes 2359304 | tf_op jit(solution)/shard_map/ppermute | solution.py:56
  333.3 29.6 %collective-permute-start.57 = (bf16[384,512]{1,0:T(8,128)(2,1)S(1)}, bf16[384,512]{1,0:T(8,128)(2,1)S(1)}, u32[]{:S(2)}, u32[]{:S(2)}) collective-permute-start(bf16[384,512]{1,0:T(8,128)(2,1)S(1)} %slice.658), channel_id=1, source_target_pairs={{0,16},{1,17},{2,18},{3,19},{4,20},{5,21},{6,22},{7,23},{8,24},{9,... | collective-permute-start | bytes 1179656 | tf_op jit(solution)/shard_map/ppermute | solution.py:56
  335.1 27.8 %collective-permute-start.58 = (bf16[256,1536]{1,0:T(8,128)(2,1)S(1)}, bf16[256,1536]{1,0:T(8,128)(2,1)S(1)}, u32[]{:S(2)}, u32[]{:S(2)}) collective-permute-start(bf16[256,1536]{1,0:T(8,128)(2,1)S(1)} %add_convert_fusion), channel_id=1, source_target_pairs={{2,4},{3,5},{4,2},{5,3},{10,12},{11,13},{12,10},{13,11},{18,20},{1... | collective-permute-start | bytes 2359304 | tf_op jit(solution)/shard_map/ppermute | solution.py:56
  336.1 26.8 %collective-permute-start.55 = (bf16[256,1536]{1,0:T(8,128)(2,1)S(1)}, bf16[256,1536]{1,0:T(8,128)(2,1)S(1)}, u32[]{:S(2)}, u32[]{:S(2)}) collective-permute-start(bf16[256,1536]{1,0:T(8,128)(2,1)S(1)} %fusion.7), channel_id=1, source_target_pairs={{0,1},{1,0},{2,3},{3,2},{4,5},{5,4},{6,7},{7,6},{8,9},{9,8},{10,11... | collective-permute-start | bytes 2359304 | tf_op jit(solution)/shard_map/ppermute | solution.py:56
  365.0 40.4 %collective-permute-start.60 = (bf16[768,640]{1,0:T(8,128)(2,1)}, bf16[768,640]{1,0:T(8,128)(2,1)}, u32[]{:S(2)}, u32[]{:S(2)}) collective-permute-start(bf16[768,640]{1,0:T(8,128)(2,1)} %get-tuple-element.371), channel_id=1, source_target_pairs={{0,16},{1,17},{2,18},{3,19},{4,20},{5,21},{6,22},{7,23},{8,24},{9,... | collective-permute-start | bytes 2949128 | tf_op jit(solution)/shard_map/ppermute | solution.py:56
  365.5 39.9 %collective-permute-start.61 = (bf16[768,640]{1,0:T(8,128)(2,1)}, bf16[768,640]{1,0:T(8,128)(2,1)}, u32[]{:S(2)}, u32[]{:S(2)}) collective-permute-start(bf16[768,640]{1,0:T(8,128)(2,1)} %get-tuple-element.372), channel_id=1, source_target_pairs={{0,8},{1,9},{2,10},{3,11},{4,12},{5,13},{6,14},{7,15},{8,0},{9,1},... | collective-permute-start | bytes 2949128 | tf_op jit(solution)/shard_map/ppermute | solution.py:56
  368.4 37.0 %collective-permute-start.64 = (bf16[192,1536]{1,0:T(8,128)(2,1)}, bf16[192,1536]{1,0:T(8,128)(2,1)}, u32[]{:S(2)}, u32[]{:S(2)}) collective-permute-start(bf16[192,1536]{1,0:T(8,128)(2,1)} %get-tuple-element.465), channel_id=1, source_target_pairs={{0,2},{1,3},{2,0},{3,1},{4,6},{5,7},{6,4},{7,5},{8,10},{9,11},{10,... | collective-permute-start | bytes 1769480 | tf_op jit(solution)/shard_map/ppermute | solution.py:56
  378.8 26.6 %collective-permute-start.62 = (f32[9,1536]{1,0:T(8,128)S(1)}, f32[9,1536]{1,0:T(8,128)S(1)}, u32[]{:S(2)}, u32[]{:S(2)}) collective-permute-start(f32[9,1536]{1,0:T(8,128)S(1)} %select_maximum_fusion), channel_id=1, source_target_pairs={{0,8},{1,9},{2,10},{3,11},{4,12},{5,13},{6,14},{7,15},{8,0},{9,1},... | collective-permute-start | bytes 165896 | tf_op jit(solution)/shard_map/ppermute | solution.py:56
  380.0 53.4 %collective-permute-start.68 = (bf16[256,1536]{1,0:T(8,128)(2,1)S(1)}, bf16[256,1536]{1,0:T(8,128)(2,1)S(1)}, u32[]{:S(2)}, u32[]{:S(2)}) collective-permute-start(bf16[256,1536]{1,0:T(8,128)(2,1)S(1)} %copy-done.49), channel_id=1, source_target_pairs={{2,4},{3,5},{4,2},{5,3},{10,12},{11,13},{12,10},{13,11},{18,20},{1... | collective-permute-start | bytes 2359304 | tf_op jit(solution)/shard_map/ppermute | solution.py:56
  407.0 26.4 %collective-permute-start.65 = (bf16[384,640]{1,0:T(8,128)(2,1)S(1)}, bf16[384,640]{1,0:T(8,128)(2,1)S(1)}, u32[]{:S(2)}, u32[]{:S(2)}) collective-permute-start(bf16[384,640]{1,0:T(8,128)(2,1)S(1)} %slice.657), channel_id=1, source_target_pairs={{0,8},{1,9},{2,10},{3,11},{4,12},{5,13},{6,14},{7,15},{8,0},{9,1},... | collective-permute-start | bytes 1474568 | tf_op jit(solution)/shard_map/ppermute | solution.py:56
  409.5 23.9 %collective-permute-start.66 = (bf16[384,640]{1,0:T(8,128)(2,1)S(1)}, bf16[384,640]{1,0:T(8,128)(2,1)S(1)}, u32[]{:S(2)}, u32[]{:S(2)}) collective-permute-start(bf16[384,640]{1,0:T(8,128)(2,1)S(1)} %slice.656), channel_id=1, source_target_pairs={{0,16},{1,17},{2,18},{3,19},{4,20},{5,21},{6,22},{7,23},{8,24},{9,... | collective-permute-start | bytes 1474568 | tf_op jit(solution)/shard_map/ppermute | solution.py:56
  412.3 21.1 %collective-permute-start.67 = (bf16[384,384]{1,0:T(8,128)(2,1)S(1)}, bf16[384,384]{1,0:T(8,128)(2,1)S(1)}, u32[]{:S(2)}, u32[]{:S(2)}) collective-permute-start(bf16[384,384]{1,0:T(8,128)(2,1)S(1)} %slice.659), channel_id=1, source_target_pairs={{0,8},{1,9},{2,10},{3,11},{4,12},{5,13},{6,14},{7,15},{8,0},{9,1},... | collective-permute-start | bytes 884744 | tf_op jit(solution)/shard_map/ppermute | solution.py:56
  414.5 31.1 %collective-permute-start.74 = (bf16[192,1536]{1,0:T(8,128)(2,1)S(1)}, bf16[192,1536]{1,0:T(8,128)(2,1)S(1)}, u32[]{:S(2)}, u32[]{:S(2)}) collective-permute-start(bf16[192,1536]{1,0:T(8,128)(2,1)S(1)} %copy-done.76), channel_id=1, source_target_pairs={{0,6},{1,7},{2,4},{3,5},{4,2},{5,3},{6,0},{7,1},{8,14},{9,15},{10,... | collective-permute-start | bytes 1769480 | tf_op jit(solution)/shard_map/ppermute | solution.py:56
  442.7 26.2 %collective-permute-start.70 = (bf16[192,832]{1,0:T(8,128)(2,1)S(1)}, bf16[192,832]{1,0:T(8,128)(2,1)S(1)}, u32[]{:S(2)}, u32[]{:S(2)}) collective-permute-start(bf16[192,832]{1,0:T(8,128)(2,1)S(1)} %get-tuple-element.502), channel_id=1, source_target_pairs={{0,2},{1,3},{2,0},{3,1},{4,6},{5,7},{6,4},{7,5},{8,10},{9,11},{10,... | collective-permute-start | bytes 958472 | tf_op jit(solution)/shard_map/ppermute | solution.py:56
  444.7 31.6 %collective-permute-start.77 = (bf16[192,832]{1,0:T(8,128)(2,1)S(1)}, bf16[192,832]{1,0:T(8,128)(2,1)S(1)}, u32[]{:S(2)}, u32[]{:S(2)}) collective-permute-start(bf16[192,832]{1,0:T(8,128)(2,1)S(1)} %get-tuple-element.501), channel_id=1, source_target_pairs={{0,6},{1,7},{2,4},{3,5},{4,2},{5,3},{6,0},{7,1},{8,14},{9,15},{10,... | collective-permute-start | bytes 958472 | tf_op jit(solution)/shard_map/ppermute | solution.py:56
  447.4 12.8 %collective-permute-start.76 = (f32[2,192]{1,0:T(2,128)S(1)}, f32[2,192]{1,0:T(2,128)S(1)}, u32[]{:S(2)}, u32[]{:S(2)}) collective-permute-start(f32[2,192]{1,0:T(2,128)S(1)} %fusion.34), channel_id=1, source_target_pairs={{0,1},{1,0},{2,3},{3,2},{4,5},{5,4},{6,7},{7,6},{8,9},{9,8},{10,11... | collective-permute-start | bytes 4616 | tf_op jit(solution)/shard_map/ppermute | solution.py:56
  (136 other events, 891.5 us)
Sparse Core Ops, SparseCore 0:
  76.7 63.7 all-gather.1
  372.5 77.9 reduce-scatter.1

commit v6 on v5

--- a/solution.py
+++ b/solution.py
@@ -368,7 +368,7 @@
             *(full_spec(w.shape) for w in (query, keys, values, forget, gain, bias)),
         ],
         out_specs=(full_spec(out.shape), full_spec(out.shape)),
-        compiler_params=params(6),
+        compiler_params=params(4),
         cost_estimate=NO_COST,
     )(core, query, keys, values, forget, gain, bias)
 
@@ -394,7 +394,7 @@
         in_specs=[pl.BlockSpec(memory_space=pltpu.SMEM), *(full_spec(o.shape) for o in operands)],
         out_specs=tuple(full_spec(o.shape) for o in outs),
         scratch_shapes=[pltpu.VMEM((PAIR, length), F32), pltpu.VMEM((length, PAIR), F32)],
-        compiler_params=params(27),
+        compiler_params=params(24),
         cost_estimate=NO_COST,
     )(pos, *operands)
 
@@ -446,7 +446,7 @@
             full_spec((1, wide)),
         ),
         input_output_aliases={len(operands) + k: k for k in range(len(before))},
-        compiler_params=params(28),
+        compiler_params=params(25),
         cost_estimate=NO_COST,
     )(*operands, *before)
 
@@ -543,7 +543,7 @@
                 pl.BlockSpec((length, block), lambda r, chip: (0, r)),
             ),
         ),
-        compiler_params=params(26),
+        compiler_params=params(23),
         cost_estimate=NO_COST,
     )(chip, second, cot, hidden, ga, gb, da, db)
 
@@ -579,7 +579,7 @@
             *pair_specs(block, cols),
             pl.BlockSpec((block, 2 * PAIR), lambda r: (r, 0)),
         ),
-        compiler_params=params(14),
+        compiler_params=params(12),
         cost_estimate=NO_COST,
     )(x_hat, near, far)
 
@@ -610,7 +610,7 @@
             pltpu.VMEM((length, PAIR), F32),
             pltpu.VMEM((length, PAIR), F32),
         ],
-        compiler_params=params(28),
+        compiler_params=params(25),
         cost_estimate=NO_COST,
     )(pos, qkv, logit, seg_row, seg_col, lse, cum, grad_mixed)
 

time: 496 us -> 491 us (0.990)
  other arithmetic: 60 us -> 52.3 us
  waiting for transfers between devices: 178 us -> 185 us
  starting transfers between devices: 81.4 us -> 76.2 us
    ppermute x78, waiting for transfers between devices: 178 us -> 185 us  [send(): return Box(lax.ppermute(val(value), AXES, pairs))]
    ppermute x78, starting transfers between devices: 81.2 us -> 75.9 us  [send(): return Box(lax.ppermute(val(value), AXES, pairs))]
    unnamed x208 -> x214, local copies, waits for them, and re-layouts: 31.3 us -> 33.5 us
  transfers between devices with their start and end apart: 80 -> 80, of which waited for: 27 -> 27; matrix products, arithmetic and copies ran while one was open for 16% -> 15% of each run, Pallas kernels for 16% -> 16%
where the time goes in v6:
time: 491 us; the launch traced here: 482 us
  waiting for transfers between devices  185 us (38%)
  Pallas kernels  88.3 us (18%)
  starting transfers between devices  76.2 us (16%)
  other arithmetic  52.3 us (11%)
  local copies, waits for them, and re-layouts  48.9 us (10%)
  between operations  16.1 us (3%)
  matrix products  15 us (3%)
    ppermute x78, waiting for transfers between devices, send(): return Box(lax.ppermute(val(value), AXES, pairs))  185 us
    ppermute x78, starting transfers between devices, send(): return Box(lax.ppermute(val(value), AXES, pairs))  75.9 us
    unnamed x214, local copies, waits for them, and re-layouts  33.5 us
    pallas_call x2, Pallas kernels, feed_tokens(): pl.pallas_call(feed_kernel, grid=(1,), out_shape=outs, in_specs=[*(full_s...  21.2 us
    pallas_call x1, Pallas kernels, attend(): pl.pallas_call(functools.partial(forward_kernel, quarter), grid=(3,), out...  20.8 us
    pallas_call x1, Pallas kernels, attend_back(): pl.pallas_call(functools.partial(backward_kernel, quarter), grid=(3,), ou...  20.1 us
    pallas_call x1, Pallas kernels, feed_grads(): pl.pallas_call(feed_grads_kernel, out_shape=(*(jax.ShapeDtypeStruct((wide...  18.1 us
    select_n x19, other arithmetic, pick(): return jnp.where(first, val(one), val(two))  15.6 us
  transfers between devices with their start and end apart: 80, of which 27 were waited for; matrix products, arithmetic and copies ran while one was open for 15% of the time, Pallas kernels for 16%

profile of v6, /device:TPU:0, one launch (start us, length us, event | category | flops | bytes accessed | tf_op | source)
XLA Modules:
  0.0 481.7 jit_solution(8561365883019060114)
XLA Ops:
  12.6 3.5 collective-permute-start.1
  16.9 2.4 constant_dynamic-slice_fusion.25
  19.4 3.9 collective-permute-start.5
  31.2 7.5 %collective-permute-done = bf16[192,640]{1,0:T(8,128)(2,1)} collective-permute-done((bf16[192,640]{1,0:T(8,128)(2,1)S(1)}, bf16[192,640]{1,0:T(8,128)(2,1)}, u32[]{:S(2)}, u32[]{:S(2)}) %collective-permute-start) | collective-permute-done | bytes 245792 | tf_op jit(solution)/shard_map/ppermute | solution.py:56
  38.7 3.6 collective-permute-done.5
  44.1 1.9 collective-permute-start.9
  47.5 2.5 collective-permute-start.7
  52.2 10.0 %collective-permute-done.7 = bf16[384,640]{1,0:T(8,128)(2,1)} collective-permute-done((bf16[384,640]{1,0:T(8,128)(2,1)S(1)}, bf16[384,640]{1,0:T(8,128)(2,1)}, u32[]{:S(2)}, u32[]{:S(2)}) %collective-permute-start.7) | collective-permute-done | bytes 491552 | tf_op jit(solution)/shard_map/ppermute | solution.py:56
  62.3 3.1 collective-permute-done.9
  67.5 2.4 collective-permute-start.13
  76.1 6.4 %collective-permute-done.14 = bf16[192,192]{1,0:T(8,128)(2,1)} collective-permute-done((bf16[192,192]{1,0:T(8,128)(2,1)S(1)}, bf16[192,192]{1,0:T(8,128)(2,1)}, u32[]{:S(2)}, u32[]{:S(2)}) %collective-permute-start.14) | collective-permute-done | bytes 73760 | tf_op jit(solution)/shard_map/ppermute | solution.py:56
  85.5 2.0 broadcast_select_fusion.10
  88.9 2.7 pad_maximum_fusion.3.wb_ref
  92.6 2.5 collective-permute-start.23
  103.5 20.8 %shard_map.238 = (bf16[1024,384]{1,0:T(8,128)(2,1)S(1)}, bf16[1024,1536]{1,0:T(8,128)(2,1)S(1)}, bf16[1024,1152]{1,0:T(8,128)(2,1)S(1)}, f32[1024,128]{1,0:T(8,1...) custom-call(s32[4]{0:T(128)S(1)} %pad_add_fusion.pos_ref, ...), custom_call_target="tpu_custom_call" | custom-call | tf_op jit(solution)/shard_map/pallas_call | solution.py:390
  124.4 5.6 %collective-permute-done.23 = bf16[192,1024]{1,0:T(8,128)(2,1)} collective-permute-done((bf16[192,1024]{1,0:T(8,128)(2,1)}, bf16[192,1024]{1,0:T(8,128)(2,1)}, u32[]{:S(2)}, u32[]{:S(2)}) %collective-permute-start.23) | collective-permute-done | bytes 393248 | tf_op jit(solution)/shard_map/ppermute | solution.py:56
  130.0 2.2 fusion.26
  132.5 2.2 collective-permute-done.24
  134.9 2.2 fusion.24
  139.8 1.8 collective-permute-start.28
  141.8 2.0 collective-permute-start.29
  143.9 21.6 %collective-permute-done.25 = bf16[256,1536]{1,0:T(8,128)(2,1)S(1)} collective-permute-done((bf16[256,1536]{1,0:T(8,128)(2,1)S(1)}, bf16[256,1536]{1,0:T(8,128)(2,1)S(1)}, u32[]{:S(2)}, u32[]{:S(2)}) %collective-permute-start.25) | collective-permute-done | bytes 786464 | tf_op jit(solution)/shard_map/ppermute | solution.py:56
  171.6 7.4 %collective-permute-start.34 = (bf16[256,1536]{1,0:T(8,128)(2,1)}, bf16[256,1536]{1,0:T(8,128)(2,1)}, u32[]{:S(2)}, u32[]{:S(2)}) collective-permute-start(bf16[256,1536]{1,0:T(8,128)(2,1)} %pad_maximum_fusion.8), channel_id=1, source_target_pairs={{0,0},{1,1},{2,4},{3,5},{4,2},{5,3},{6,6},{7,7},{8,8},{9,9},{10,12... | collective-permute-start | bytes 2359304 | tf_op jit(solution)/shard_map/ppermute | solution.py:56
  183.2 12.4 %collective-permute-done.31.s0_ref = bf16[256,1536]{1,0:T(8,128)(2,1)} collective-permute-done((bf16[256,1536]{1,0:T(8,128)(2,1)S(1)}, bf16[256,1536]{1,0:T(8,128)(2,1)}, u32[]{:S(2)}, u32[]{:S(2)}) %collective-permute-start.31) | collective-permute-done | bytes 786464 | tf_op jit(solution)/shard_map/ppermute | solution.py:56
  196.5 2.1 collective-permute-start.39
  201.1 8.8 %collective-permute-done.40 = bf16[384,512]{1,0:T(8,128)(2,1)S(1)} collective-permute-done((bf16[384,512]{1,0:T(8,128)(2,1)}, bf16[384,512]{1,0:T(8,128)(2,1)S(1)}, u32[]{:S(2)}, u32[]{:S(2)}) %collective-permute-start.40) | collective-permute-done | bytes 393248 | tf_op jit(solution)/shard_map/ppermute | solution.py:56
  212.4 10.5 %shard_map.239 = (bf16[1024,1024]{1,0:T(8,128)(2,1)S(1)}, bf16[1024,1024]{1,0:T(8,128)(2,1)S(1)}, bf16[1024,1024]{1,0:T(8,128)(2,1)S(1)}, bf16[1024,1536]{1,0:T(...) custom-call(bf16[256,1536]{1,0:T(8,128)(2,1)} %collective-permute-done.31.s0_ref, ...), custom_call_target="tpu_custom_call" | custom-call | tf_op jit(solution)/shard_map/pallas_call | solution.py:438
  223.2 2.2 collective-permute-done.43
  226.1 10.7 %shard_map.240 = (bf16[1024,1024]{1,0:T(8,128)(2,1)S(1)}, bf16[1024,1024]{1,0:T(8,128)(2,1)S(1)}, bf16[1024,1024]{1,0:T(8,128)(2,1)S(1)}, bf16[1024,1536]{1,0:T(...) custom-call(bf16[256,1536]{1,0:T(8,128)(2,1)S(1)} %multiply_convert_, ...), custom_call_target="tpu_custom_call", output_to_operand_aliasing={{0}: (8, {}), {1}: (9, {}), {2}: (10, {}), {3}: (11, {}), {... | custom-call | tf_op jit(solution)/shard_map/pallas_call | solution.py:438
  241.1 4.1 collective-permute-done.44
  245.4 2.3 collective-permute-done.45
  248.2 3.1 fusion.35
  254.7 18.1 %shard_map.241 = (bf16[768,1024]{1,0:T(8,128)(2,1)S(1)}, bf16[768,1024]{1,0:T(8,128)(2,1)S(1)}, bf16[768,512]{1,0:T(8,128)(2,1)S(1)}, bf16[768,512]{1,0:T(8,128)...) custom-call(s32[1]{0:T(128)} %bitcast.11.chip_ref, bf16[1024,1536]{1,0:T(8,128)(2,1)S(1)} %copy-done.5, ...), custom_call_target="tpu_custom_call" | custom-call | tf_op jit(solution)/shard_map/pallas_call | solution.py:527
  272.9 2.1 copy-done.20
  290.1 3.1 convolution_convert_fusion.1.gmix_ref
  293.2 1.9 convolution_convert_fusion
  297.2 20.1 %shard_map.242 = (bf16[1024,640]{1,0:T(8,128)(2,1)S(1)}, bf16[1024,640]{1,0:T(8,128)(2,1)S(1)}, f32[1,128]{1,0:T(1,128)S(1)}) custom-call(s32[4]{0:T(128)S(1)} %pad_add_fusion.pos_ref, bf16[1024,1152]{1,0:T(8,128)(2,1)S(1)} %copy-done.26, f32[1024,128]{1,0:T(8,128)S(1)} %copy-done.36, s32[1,1024]{1,0:T(1,128)S(1)} %broadcast_select_fusion.20.segr_ref, ...), custom_call_target="tpu_custom_call" | custom-call | tf_op jit(solution)/shard_map/pallas_call | solution.py:590
  317.5 3.9 collective-permute-done.49
  334.7 7.7 %shard_map.243 = (bf16[768,640]{1,0:T(8,128)(2,1)S(1)}, bf16[768,640]{1,0:T(8,128)(2,1)}, bf16[768,640]{1,0:T(8,128)(2,1)S(1)}, bf16[768,640]{1,0:T(8,128)(2,1)}, f32[1536,256]{1,0:T(8,128)S(1)}) custom-call(bf16[1024,1536]{1,0:T(8,128)(2,1)S(1)} %copy-done.9, bf16[1024,640]{1,0:T(8,128)(2,1)S(1)} %get-tuple-element.340.near_ref, ...), custom_call_target="tpu_custom_call" | custom-call | tf_op jit(solution)/shard_map/pallas_call | solution.py:569
  344.4 14.8 %collective-permute-done.55 = bf16[256,1536]{1,0:T(8,128)(2,1)S(1)} collective-permute-done((bf16[256,1536]{1,0:T(8,128)(2,1)S(1)}, bf16[256,1536]{1,0:T(8,128)(2,1)S(1)}, u32[]{:S(2)}, u32[]{:S(2)}) %collective-permute-start.55) | collective-permute-done | bytes 786464 | tf_op jit(solution)/shard_map/ppermute | solution.py:56
  365.1 3.2 fusion.4
  373.7 26.3 %collective-permute-done.64 = bf16[192,1536]{1,0:T(8,128)(2,1)} collective-permute-done((bf16[192,1536]{1,0:T(8,128)(2,1)}, bf16[192,1536]{1,0:T(8,128)(2,1)}, u32[]{:S(2)}, u32[]{:S(2)}) %collective-permute-start.64) | collective-permute-done | bytes 589856 | tf_op jit(solution)/shard_map/ppermute | solution.py:56
  409.1 20.7 %collective-permute-done.67 = bf16[384,384]{1,0:T(8,128)(2,1)S(1)} collective-permute-done((bf16[384,384]{1,0:T(8,128)(2,1)S(1)}, bf16[384,384]{1,0:T(8,128)(2,1)S(1)}, u32[]{:S(2)}, u32[]{:S(2)}) %collective-permute-start.67) | collective-permute-done | bytes 294944 | tf_op jit(solution)/shard_map/ppermute | solution.py:56
  433.2 3.9 collective-permute-done.69
  438.1 3.0 collective-permute-start.70
  441.2 16.1 %collective-permute-done.72 = f32[6,1536]{1,0:T(8,128)S(1)} collective-permute-done((f32[6,1536]{1,0:T(8,128)S(1)}, f32[6,1536]{1,0:T(8,128)S(1)}, u32[]{:S(2)}, u32[]{:S(2)}) %collective-permute-start.72) | collective-permute-done | bytes 36896 | tf_op jit(solution)/shard_map/ppermute | solution.py:56
  460.0 2.5 collective-permute-done.76
  462.5 2.2 collective-permute-done.70
  (497 shorter events, 139.7 us)
Async XLA Ops:
  7.2 171.8 %all-gather.2.cloned.1.call-start = ((), (), s32[]{:S(2)}) async-start(), calls=%async_computation.1 | async-start | bytes 5898240 | tf_op jit(solution)/shard_map/all_gather | solution.py:815
  12.6 26.1 %collective-permute-start.1 = (bf16[192,640]{1,0:T(8,128)(2,1)S(1)}, bf16[192,640]{1,0:T(8,128)(2,1)}, u32[]{:S(2)}, u32[]{:S(2)}) collective-permute-start(bf16[192,640]{1,0:T(8,128)(2,1)S(1)} %get-tuple-element.211), channel_id=1, source_target_pairs={{0,6},{1,7},{2,4},{3,5},{4,2},{5,3},{6,0},{7,1},{8,14},{9,15},{10,... | collective-permute-start | bytes 737288 | tf_op jit(solution)/shard_map/ppermute | solution.py:56
  16.8 21.9 %collective-permute-start = (bf16[192,640]{1,0:T(8,128)(2,1)S(1)}, bf16[192,640]{1,0:T(8,128)(2,1)}, u32[]{:S(2)}, u32[]{:S(2)}) collective-permute-start(bf16[192,640]{1,0:T(8,128)(2,1)S(1)} %get-tuple-element.210), channel_id=1, source_target_pairs={{0,2},{1,3},{2,0},{3,1},{4,6},{5,7},{6,4},{7,5},{8,10},{9,11},{10,... | collective-permute-start | bytes 737288 | tf_op jit(solution)/shard_map/ppermute | solution.py:56
  19.4 22.9 %collective-permute-start.5 = (bf16[256,1536]{1,0:T(8,128)(2,1)S(1)}, bf16[256,1536]{1,0:T(8,128)(2,1)}, u32[]{:S(2)}, u32[]{:S(2)}) collective-permute-start(bf16[256,1536]{1,0:T(8,128)(2,1)S(1)} %pad_maximum_fusion.7), channel_id=1, source_target_pairs={{0,1},{1,0},{6,7},{7,6},{8,9},{9,8},{14,15},{15,14},{16,17},{17,16... | collective-permute-start | bytes 2359304 | tf_op jit(solution)/shard_map/ppermute | solution.py:56
  42.4 19.9 %collective-permute-start.6 = (bf16[256,1536]{1,0:T(8,128)(2,1)}, bf16[256,1536]{1,0:T(8,128)(2,1)S(1)}, u32[]{:S(2)}, u32[]{:S(2)}) collective-permute-start(bf16[256,1536]{1,0:T(8,128)(2,1)} %copy-done.77), channel_id=1, source_target_pairs={{0,0},{1,1},{2,4},{3,5},{4,2},{5,3},{6,6},{7,7},{8,8},{9,9},{10,12... | collective-permute-start | bytes 2359304 | tf_op jit(solution)/shard_map/ppermute | solution.py:56
  44.1 21.2 %collective-permute-start.9 = (bf16[256,1536]{1,0:T(8,128)(2,1)}, bf16[256,1536]{1,0:T(8,128)(2,1)S(1)}, u32[]{:S(2)}, u32[]{:S(2)}) collective-permute-start(bf16[256,1536]{1,0:T(8,128)(2,1)} %pad_maximum_fusion.8), channel_id=1, source_target_pairs={{0,1},{1,0},{6,7},{7,6},{8,9},{9,8},{14,15},{15,14},{16,17},{17,16... | collective-permute-start | bytes 2359304 | tf_op jit(solution)/shard_map/ppermute | solution.py:56
  51.6 18.4 %collective-permute-start.11 = (bf16[384,640]{1,0:T(8,128)(2,1)}, bf16[384,640]{1,0:T(8,128)(2,1)S(1)}, u32[]{:S(2)}, u32[]{:S(2)}) collective-permute-start(bf16[384,640]{1,0:T(8,128)(2,1)} %copy-done.87), channel_id=1, source_target_pairs={{0,16},{1,17},{2,18},{3,19},{4,20},{5,21},{6,22},{7,23},{8,24},{9,... | collective-permute-start | bytes 1474568 | tf_op jit(solution)/shard_map/ppermute | solution.py:56
  67.5 16.1 %collective-permute-start.13 = (bf16[384,640]{1,0:T(8,128)(2,1)}, bf16[384,640]{1,0:T(8,128)(2,1)}, u32[]{:S(2)}, u32[]{:S(2)}) collective-permute-start(bf16[384,640]{1,0:T(8,128)(2,1)} %collective-permute-done.7), channel_id=1, source_target_pairs={{0,8},{1,9},{2,10},{3,11},{4,12},{5,13},{6,14},{7,15},{8,0},{9,1},... | collective-permute-start | bytes 1474568 | tf_op jit(solution)/shard_map/ppermute | solution.py:56
  71.5 20.1 %collective-permute-start.17 = (bf16[256,1536]{1,0:T(8,128)(2,1)S(1)}, bf16[256,1536]{1,0:T(8,128)(2,1)}, u32[]{:S(2)}, u32[]{:S(2)}) collective-permute-start(bf16[256,1536]{1,0:T(8,128)(2,1)S(1)} %collective-permute-done.6.x0_ref), channel_id=1, source_target_pairs={{0,4},{1,5},{2,6},{3,7},{4,0},{5,1},{6,2},{7,3},{8,12},{9,13},{10,... | collective-permute-start | bytes 2359304 | tf_op jit(solution)/shard_map/ppermute | solution.py:56
  75.8 388.9 %reduce-scatter.2.cloned.1.call-start = ((), (), s32[]{:S(2)}) async-start(), calls=%async_computation.2 | async-start | bytes 5898240 | tf_op jit(solution)/shard_map/reduce_scatter | solution.py:993
  92.5 31.9 %collective-permute-start.22 = (bf16[192,1024]{1,0:T(8,128)(2,1)}, bf16[192,1024]{1,0:T(8,128)(2,1)}, u32[]{:S(2)}, u32[]{:S(2)}) collective-permute-start(bf16[192,1024]{1,0:T(8,128)(2,1)} %get-tuple-element.243), channel_id=1, source_target_pairs={{0,2},{1,3},{2,0},{3,1},{4,6},{5,7},{6,4},{7,5},{8,10},{9,11},{10,... | collective-permute-start | bytes 1179656 | tf_op jit(solution)/shard_map/ppermute | solution.py:56
  92.6 37.4 %collective-permute-start.23 = (bf16[192,1024]{1,0:T(8,128)(2,1)}, bf16[192,1024]{1,0:T(8,128)(2,1)}, u32[]{:S(2)}, u32[]{:S(2)}) collective-permute-start(bf16[192,1024]{1,0:T(8,128)(2,1)} %get-tuple-element.244), channel_id=1, source_target_pairs={{0,6},{1,7},{2,4},{3,5},{4,2},{5,3},{6,0},{7,1},{8,14},{9,15},{10,... | collective-permute-start | bytes 1179656 | tf_op jit(solution)/shard_map/ppermute | solution.py:56
  95.9 28.5 %collective-permute-start.19 = (bf16[384,384]{1,0:T(8,128)(2,1)}, bf16[384,384]{1,0:T(8,128)(2,1)}, u32[]{:S(2)}, u32[]{:S(2)}) collective-permute-start(bf16[384,384]{1,0:T(8,128)(2,1)} %pad_maximum_fusion.17), channel_id=1, source_target_pairs={{0,8},{1,9},{2,10},{3,11},{4,12},{5,13},{6,14},{7,15},{8,0},{9,1},... | collective-permute-start | bytes 884744 | tf_op jit(solution)/shard_map/ppermute | solution.py:56
  96.5 27.9 %collective-permute-start.20 = (bf16[384,384]{1,0:T(8,128)(2,1)}, bf16[384,384]{1,0:T(8,128)(2,1)}, u32[]{:S(2)}, u32[]{:S(2)}) collective-permute-start(bf16[384,384]{1,0:T(8,128)(2,1)} %pad_maximum_fusion.17), channel_id=1, source_target_pairs={{0,16},{1,17},{2,18},{3,19},{4,20},{5,21},{6,22},{7,23},{8,24},{9,... | collective-permute-start | bytes 884744 | tf_op jit(solution)/shard_map/ppermute | solution.py:56
  98.1 26.2 %collective-permute-start.21 = (bf16[384,384]{1,0:T(8,128)(2,1)}, bf16[384,384]{1,0:T(8,128)(2,1)}, u32[]{:S(2)}, u32[]{:S(2)}) collective-permute-start(bf16[384,384]{1,0:T(8,128)(2,1)} %pad_maximum_fusion.17), channel_id=1, source_target_pairs={{0,24},{1,25},{2,26},{3,27},{4,28},{5,29},{6,30},{7,31},{8,16},{9,... | collective-permute-start | bytes 884744 | tf_op jit(solution)/shard_map/ppermute | solution.py:56
  137.3 28.2 %collective-permute-start.25 = (bf16[256,1536]{1,0:T(8,128)(2,1)S(1)}, bf16[256,1536]{1,0:T(8,128)(2,1)S(1)}, u32[]{:S(2)}, u32[]{:S(2)}) collective-permute-start(bf16[256,1536]{1,0:T(8,128)(2,1)S(1)} %fusion.8), channel_id=1, source_target_pairs={{0,1},{1,0},{2,3},{3,2},{4,5},{5,4},{6,7},{7,6},{8,9},{9,8},{10,11... | collective-permute-start | bytes 2359304 | tf_op jit(solution)/shard_map/ppermute | solution.py:56
  139.0 26.6 %collective-permute-start.27 = (bf16[384,1024]{1,0:T(8,128)(2,1)S(1)}, bf16[384,1024]{1,0:T(8,128)(2,1)}, u32[]{:S(2)}, u32[]{:S(2)}) collective-permute-start(bf16[384,1024]{1,0:T(8,128)(2,1)S(1)} %maximum_select_fusion.1), channel_id=1, source_target_pairs={{0,8},{1,9},{2,10},{3,11},{4,12},{5,13},{6,14},{7,15},{8,0},{9,1},... | collective-permute-start | bytes 2359304 | tf_op jit(solution)/shard_map/ppermute | solution.py:56
  139.8 25.8 %collective-permute-start.28 = (bf16[384,1024]{1,0:T(8,128)(2,1)S(1)}, bf16[384,1024]{1,0:T(8,128)(2,1)S(1)}, u32[]{:S(2)}, u32[]{:S(2)}) collective-permute-start(bf16[384,1024]{1,0:T(8,128)(2,1)S(1)} %maximum_select_fusion.1), channel_id=1, source_target_pairs={{0,16},{1,17},{2,18},{3,19},{4,20},{5,21},{6,22},{7,23},{8,24},{9,... | collective-permute-start | bytes 2359304 | tf_op jit(solution)/shard_map/ppermute | solution.py:56
  141.8 23.8 %collective-permute-start.29 = (bf16[192,512]{1,0:T(8,128)(2,1)S(1)}, bf16[192,512]{1,0:T(8,128)(2,1)S(1)}, u32[]{:S(2)}, u32[]{:S(2)}) collective-permute-start(bf16[192,512]{1,0:T(8,128)(2,1)S(1)} %copy-done.100), channel_id=1, source_target_pairs={{0,2},{1,3},{2,0},{3,1},{4,6},{5,7},{6,4},{7,5},{8,10},{9,11},{10,... | collective-permute-start | bytes 589832 | tf_op jit(solution)/shard_map/ppermute | solution.py:56
  143.8 22.6 %collective-permute-start.30 = (bf16[192,512]{1,0:T(8,128)(2,1)S(1)}, bf16[192,512]{1,0:T(8,128)(2,1)S(1)}, u32[]{:S(2)}, u32[]{:S(2)}) collective-permute-start(bf16[192,512]{1,0:T(8,128)(2,1)S(1)} %copy-done.99), channel_id=1, source_target_pairs={{0,6},{1,7},{2,4},{3,5},{4,2},{5,3},{6,0},{7,1},{8,14},{9,15},{10,... | collective-permute-start | bytes 589832 | tf_op jit(solution)/shard_map/ppermute | solution.py:56
  167.1 28.5 %collective-permute-start.31 = (bf16[256,1536]{1,0:T(8,128)(2,1)S(1)}, bf16[256,1536]{1,0:T(8,128)(2,1)}, u32[]{:S(2)}, u32[]{:S(2)}) collective-permute-start(bf16[256,1536]{1,0:T(8,128)(2,1)S(1)} %multiply_convert_fusion.s0_ref), channel_id=1, source_target_pairs={{0,1},{1,0},{2,3},{3,2},{4,5},{5,4},{6,7},{7,6},{8,9},{9,8},{10,11... | collective-permute-start | bytes 2359304 | tf_op jit(solution)/shard_map/ppermute | solution.py:56
  168.0 27.6 %collective-permute-start.36 = (bf16[384,512]{1,0:T(8,128)(2,1)S(1)}, bf16[384,512]{1,0:T(8,128)(2,1)}, u32[]{:S(2)}, u32[]{:S(2)}) collective-permute-start(bf16[384,512]{1,0:T(8,128)(2,1)S(1)} %maximum_select_fusion.4), channel_id=1, source_target_pairs={{0,16},{1,17},{2,18},{3,19},{4,20},{5,21},{6,22},{7,23},{8,24},{9,... | collective-permute-start | bytes 1179656 | tf_op jit(solution)/shard_map/ppermute | solution.py:56
  169.5 26.1 %collective-permute-start.37 = (bf16[384,512]{1,0:T(8,128)(2,1)S(1)}, bf16[384,512]{1,0:T(8,128)(2,1)}, u32[]{:S(2)}, u32[]{:S(2)}) collective-permute-start(bf16[384,512]{1,0:T(8,128)(2,1)S(1)} %maximum_select_fusion.4), channel_id=1, source_target_pairs={{0,8},{1,9},{2,10},{3,11},{4,12},{5,13},{6,14},{7,15},{8,0},{9,1},... | collective-permute-start | bytes 1179656 | tf_op jit(solution)/shard_map/ppermute | solution.py:56
  170.5 25.3 %collective-permute-start.35 = (bf16[384,1024]{1,0:T(8,128)(2,1)}, bf16[384,1024]{1,0:T(8,128)(2,1)}, u32[]{:S(2)}, u32[]{:S(2)}) collective-permute-start(bf16[384,1024]{1,0:T(8,128)(2,1)} %collective-permute-done.27), channel_id=1, source_target_pairs={{0,16},{1,17},{2,18},{3,19},{4,20},{5,21},{6,22},{7,23},{8,24},{9,... | collective-permute-start | bytes 2359304 | tf_op jit(solution)/shard_map/ppermute | solution.py:56
  171.6 24.2 %collective-permute-start.34 = (bf16[256,1536]{1,0:T(8,128)(2,1)}, bf16[256,1536]{1,0:T(8,128)(2,1)}, u32[]{:S(2)}, u32[]{:S(2)}) collective-permute-start(bf16[256,1536]{1,0:T(8,128)(2,1)} %pad_maximum_fusion.8), channel_id=1, source_target_pairs={{0,0},{1,1},{2,4},{3,5},{4,2},{5,3},{6,6},{7,7},{8,8},{9,9},{10,12... | collective-permute-start | bytes 2359304 | tf_op jit(solution)/shard_map/ppermute | solution.py:56
  225.6 19.6 %collective-permute-start.44 = (bf16[256,1536]{1,0:T(8,128)(2,1)S(1)}, bf16[256,1536]{1,0:T(8,128)(2,1)S(1)}, u32[]{:S(2)}, u32[]{:S(2)}) collective-permute-start(bf16[256,1536]{1,0:T(8,128)(2,1)S(1)} %add_convert_fusion.2), channel_id=1, source_target_pairs={{0,1},{1,0},{2,3},{3,2},{4,5},{5,4},{6,7},{7,6},{8,9},{9,8},{10,11... | collective-permute-start | bytes 2359304 | tf_op jit(solution)/shard_map/ppermute | solution.py:56
  251.3 28.6 %collective-permute-start.46 = (bf16[256,1536]{1,0:T(8,128)(2,1)S(1)}, bf16[256,1536]{1,0:T(8,128)(2,1)S(1)}, u32[]{:S(2)}, u32[]{:S(2)}) collective-permute-start(bf16[256,1536]{1,0:T(8,128)(2,1)S(1)} %get-tuple-element.322), channel_id=1, source_target_pairs={{0,1},{1,0},{2,3},{3,2},{4,5},{5,4},{6,7},{7,6},{8,9},{9,8},{10,11... | collective-permute-start | bytes 2359304 | tf_op jit(solution)/shard_map/ppermute | solution.py:56
  283.9 37.4 %collective-permute-start.49 = (bf16[768,1024]{1,0:T(8,128)(2,1)}, bf16[768,1024]{1,0:T(8,128)(2,1)S(1)}, u32[]{:S(2)}, u32[]{:S(2)}) collective-permute-start(bf16[768,1024]{1,0:T(8,128)(2,1)} %copy-done.44), channel_id=1, source_target_pairs={{0,16},{1,17},{2,18},{3,19},{4,20},{5,21},{6,22},{7,23},{8,24},{9,... | collective-permute-start | bytes 4718600 | tf_op jit(solution)/shard_map/ppermute | solution.py:56
  286.6 30.9 %collective-permute-start.50 = (bf16[768,512]{1,0:T(8,128)(2,1)S(1)}, bf16[768,512]{1,0:T(8,128)(2,1)S(1)}, u32[]{:S(2)}, u32[]{:S(2)}) collective-permute-start(bf16[768,512]{1,0:T(8,128)(2,1)S(1)} %copy-done.48), channel_id=1, source_target_pairs={{0,8},{1,9},{2,10},{3,11},{4,12},{5,13},{6,14},{7,15},{8,0},{9,1},... | collective-permute-start | bytes 2359304 | tf_op jit(solution)/shard_map/ppermute | solution.py:56
  288.1 29.2 %collective-permute-start.52 = (bf16[256,1536]{1,0:T(8,128)(2,1)S(1)}, bf16[256,1536]{1,0:T(8,128)(2,1)S(1)}, u32[]{:S(2)}, u32[]{:S(2)}) collective-permute-start(bf16[256,1536]{1,0:T(8,128)(2,1)S(1)} %get-tuple-element.442), channel_id=1, source_target_pairs={{0,1},{1,0},{2,3},{3,2},{4,5},{5,4},{6,7},{7,6},{8,9},{9,8},{10,11... | collective-permute-start | bytes 2359304 | tf_op jit(solution)/shard_map/ppermute | solution.py:56
  296.3 76.3 %collective-permute-start.63 = (bf16[768,384]{1,0:T(8,128)(2,1)}, bf16[768,384]{1,0:T(8,128)(2,1)}, u32[]{:S(2)}, u32[]{:S(2)}) collective-permute-start(bf16[768,384]{1,0:T(8,128)(2,1)} %get-tuple-element.467), channel_id=1, source_target_pairs={{0,16},{1,17},{2,18},{3,19},{4,20},{5,21},{6,22},{7,23},{8,24},{9,... | collective-permute-start | bytes 1769480 | tf_op jit(solution)/shard_map/ppermute | solution.py:56
  326.4 32.8 %collective-permute-start.56 = (bf16[384,1024]{1,0:T(8,128)(2,1)S(1)}, bf16[384,1024]{1,0:T(8,128)(2,1)S(1)}, u32[]{:S(2)}, u32[]{:S(2)}) collective-permute-start(bf16[384,1024]{1,0:T(8,128)(2,1)S(1)} %slice.650), channel_id=1, source_target_pairs={{0,8},{1,9},{2,10},{3,11},{4,12},{5,13},{6,14},{7,15},{8,0},{9,1},... | collective-permute-start | bytes 2359304 | tf_op jit(solution)/shard_map/ppermute | solution.py:56
  327.6 31.6 %collective-permute-start.57 = (bf16[384,512]{1,0:T(8,128)(2,1)S(1)}, bf16[384,512]{1,0:T(8,128)(2,1)S(1)}, u32[]{:S(2)}, u32[]{:S(2)}) collective-permute-start(bf16[384,512]{1,0:T(8,128)(2,1)S(1)} %slice.658), channel_id=1, source_target_pairs={{0,16},{1,17},{2,18},{3,19},{4,20},{5,21},{6,22},{7,23},{8,24},{9,... | collective-permute-start | bytes 1179656 | tf_op jit(solution)/shard_map/ppermute | solution.py:56
  329.6 29.6 %collective-permute-start.58 = (bf16[256,1536]{1,0:T(8,128)(2,1)S(1)}, bf16[256,1536]{1,0:T(8,128)(2,1)S(1)}, u32[]{:S(2)}, u32[]{:S(2)}) collective-permute-start(bf16[256,1536]{1,0:T(8,128)(2,1)S(1)} %add_convert_fusion), channel_id=1, source_target_pairs={{2,4},{3,5},{4,2},{5,3},{10,12},{11,13},{12,10},{13,11},{18,20},{1... | collective-permute-start | bytes 2359304 | tf_op jit(solution)/shard_map/ppermute | solution.py:56
  330.9 28.3 %collective-permute-start.55 = (bf16[256,1536]{1,0:T(8,128)(2,1)S(1)}, bf16[256,1536]{1,0:T(8,128)(2,1)S(1)}, u32[]{:S(2)}, u32[]{:S(2)}) collective-permute-start(bf16[256,1536]{1,0:T(8,128)(2,1)S(1)} %fusion.7), channel_id=1, source_target_pairs={{0,1},{1,0},{2,3},{3,2},{4,5},{5,4},{6,7},{7,6},{8,9},{9,8},{10,11... | collective-permute-start | bytes 2359304 | tf_op jit(solution)/shard_map/ppermute | solution.py:56
  359.8 40.2 %collective-permute-start.60 = (bf16[768,640]{1,0:T(8,128)(2,1)}, bf16[768,640]{1,0:T(8,128)(2,1)}, u32[]{:S(2)}, u32[]{:S(2)}) collective-permute-start(bf16[768,640]{1,0:T(8,128)(2,1)} %get-tuple-element.371), channel_id=1, source_target_pairs={{0,16},{1,17},{2,18},{3,19},{4,20},{5,21},{6,22},{7,23},{8,24},{9,... | collective-permute-start | bytes 2949128 | tf_op jit(solution)/shard_map/ppermute | solution.py:56
  360.2 39.8 %collective-permute-start.61 = (bf16[768,640]{1,0:T(8,128)(2,1)}, bf16[768,640]{1,0:T(8,128)(2,1)}, u32[]{:S(2)}, u32[]{:S(2)}) collective-permute-start(bf16[768,640]{1,0:T(8,128)(2,1)} %get-tuple-element.372), channel_id=1, source_target_pairs={{0,8},{1,9},{2,10},{3,11},{4,12},{5,13},{6,14},{7,15},{8,0},{9,1},... | collective-permute-start | bytes 2949128 | tf_op jit(solution)/shard_map/ppermute | solution.py:56
  363.1 36.9 %collective-permute-start.64 = (bf16[192,1536]{1,0:T(8,128)(2,1)}, bf16[192,1536]{1,0:T(8,128)(2,1)}, u32[]{:S(2)}, u32[]{:S(2)}) collective-permute-start(bf16[192,1536]{1,0:T(8,128)(2,1)} %get-tuple-element.465), channel_id=1, source_target_pairs={{0,2},{1,3},{2,0},{3,1},{4,6},{5,7},{6,4},{7,5},{8,10},{9,11},{10,... | collective-permute-start | bytes 1769480 | tf_op jit(solution)/shard_map/ppermute | solution.py:56
  371.5 28.5 %collective-permute-start.62 = (f32[9,1536]{1,0:T(8,128)S(1)}, f32[9,1536]{1,0:T(8,128)S(1)}, u32[]{:S(2)}, u32[]{:S(2)}) collective-permute-start(f32[9,1536]{1,0:T(8,128)S(1)} %select_maximum_fusion), channel_id=1, source_target_pairs={{0,8},{1,9},{2,10},{3,11},{4,12},{5,13},{6,14},{7,15},{8,0},{9,1},... | collective-permute-start | bytes 165896 | tf_op jit(solution)/shard_map/ppermute | solution.py:56
  372.8 57.0 %collective-permute-start.68 = (bf16[256,1536]{1,0:T(8,128)(2,1)S(1)}, bf16[256,1536]{1,0:T(8,128)(2,1)S(1)}, u32[]{:S(2)}, u32[]{:S(2)}) collective-permute-start(bf16[256,1536]{1,0:T(8,128)(2,1)S(1)} %copy-done.54), channel_id=1, source_target_pairs={{2,4},{3,5},{4,2},{5,3},{10,12},{11,13},{12,10},{13,11},{18,20},{1... | collective-permute-start | bytes 2359304 | tf_op jit(solution)/shard_map/ppermute | solution.py:56
  401.5 28.3 %collective-permute-start.65 = (bf16[384,640]{1,0:T(8,128)(2,1)S(1)}, bf16[384,640]{1,0:T(8,128)(2,1)S(1)}, u32[]{:S(2)}, u32[]{:S(2)}) collective-permute-start(bf16[384,640]{1,0:T(8,128)(2,1)S(1)} %slice.657), channel_id=1, source_target_pairs={{0,8},{1,9},{2,10},{3,11},{4,12},{5,13},{6,14},{7,15},{8,0},{9,1},... | collective-permute-start | bytes 1474568 | tf_op jit(solution)/shard_map/ppermute | solution.py:56
  404.3 25.5 %collective-permute-start.66 = (bf16[384,640]{1,0:T(8,128)(2,1)S(1)}, bf16[384,640]{1,0:T(8,128)(2,1)S(1)}, u32[]{:S(2)}, u32[]{:S(2)}) collective-permute-start(bf16[384,640]{1,0:T(8,128)(2,1)S(1)} %slice.656), channel_id=1, source_target_pairs={{0,16},{1,17},{2,18},{3,19},{4,20},{5,21},{6,22},{7,23},{8,24},{9,... | collective-permute-start | bytes 1474568 | tf_op jit(solution)/shard_map/ppermute | solution.py:56
  407.0 22.9 %collective-permute-start.67 = (bf16[384,384]{1,0:T(8,128)(2,1)S(1)}, bf16[384,384]{1,0:T(8,128)(2,1)S(1)}, u32[]{:S(2)}, u32[]{:S(2)}) collective-permute-start(bf16[384,384]{1,0:T(8,128)(2,1)S(1)} %slice.659), channel_id=1, source_target_pairs={{0,8},{1,9},{2,10},{3,11},{4,12},{5,13},{6,14},{7,15},{8,0},{9,1},... | collective-permute-start | bytes 884744 | tf_op jit(solution)/shard_map/ppermute | solution.py:56
  409.1 32.1 %collective-permute-start.74 = (bf16[192,1536]{1,0:T(8,128)(2,1)S(1)}, bf16[192,1536]{1,0:T(8,128)(2,1)S(1)}, u32[]{:S(2)}, u32[]{:S(2)}) collective-permute-start(bf16[192,1536]{1,0:T(8,128)(2,1)S(1)} %copy-done.84), channel_id=1, source_target_pairs={{0,6},{1,7},{2,4},{3,5},{4,2},{5,3},{6,0},{7,1},{8,14},{9,15},{10,... | collective-permute-start | bytes 1769480 | tf_op jit(solution)/shard_map/ppermute | solution.py:56
  437.2 20.1 %collective-permute-start.72 = (f32[6,1536]{1,0:T(8,128)S(1)}, f32[6,1536]{1,0:T(8,128)S(1)}, u32[]{:S(2)}, u32[]{:S(2)}) collective-permute-start(f32[6,1536]{1,0:T(8,128)S(1)} %fusion.31), channel_id=1, source_target_pairs={{0,2},{1,3},{2,0},{3,1},{4,6},{5,7},{6,4},{7,5},{8,10},{9,11},{10,... | collective-permute-start | bytes 110600 | tf_op jit(solution)/shard_map/ppermute | solution.py:56
  437.7 19.6 %collective-permute-start.73 = (bf16[192,832]{1,0:T(8,128)(2,1)S(1)}, bf16[192,832]{1,0:T(8,128)(2,1)S(1)}, u32[]{:S(2)}, u32[]{:S(2)}) collective-permute-start(bf16[192,832]{1,0:T(8,128)(2,1)S(1)} %broadcast_select_fusion.14), channel_id=1, source_target_pairs={{0,4},{1,5},{2,6},{3,7},{4,0},{5,1},{6,2},{7,3},{8,12},{9,13},{10,... | collective-permute-start | bytes 958472 | tf_op jit(solution)/shard_map/ppermute | solution.py:56
  438.1 26.6 %collective-permute-start.70 = (bf16[192,832]{1,0:T(8,128)(2,1)S(1)}, bf16[192,832]{1,0:T(8,128)(2,1)S(1)}, u32[]{:S(2)}, u32[]{:S(2)}) collective-permute-start(bf16[192,832]{1,0:T(8,128)(2,1)S(1)} %get-tuple-element.502), channel_id=1, source_target_pairs={{0,2},{1,3},{2,0},{3,1},{4,6},{5,7},{6,4},{7,5},{8,10},{9,11},{10,... | collective-permute-start | bytes 958472 | tf_op jit(solution)/shard_map/ppermute | solution.py:56
  441.0 31.1 %collective-permute-start.77 = (bf16[192,832]{1,0:T(8,128)(2,1)S(1)}, bf16[192,832]{1,0:T(8,128)(2,1)S(1)}, u32[]{:S(2)}, u32[]{:S(2)}) collective-permute-start(bf16[192,832]{1,0:T(8,128)(2,1)S(1)} %get-tuple-element.501), channel_id=1, source_target_pairs={{0,6},{1,7},{2,4},{3,5},{4,2},{5,3},{6,0},{7,1},{8,14},{9,15},{10,... | collective-permute-start | bytes 958472 | tf_op jit(solution)/shard_map/ppermute | solution.py:56
  (139 other events, 934.2 us)
Sparse Core Ops, SparseCore 0:
  76.0 62.4 all-gather.1
  365.3 77.6 reduce-scatter.1

commit v7 on v6

--- a/solution.py
+++ b/solution.py
@@ -897,13 +897,15 @@
     gate_late = far_gate.late()
     far_down = Spread(down_pack.far_rows(), down_order)
     down_early = far_down.early()
-    cot_home = send(hold(cot_own, second_core), to_home)
+    hold(cot_own, second_core)
+    cot_home = send(cot_own, swap_home)
     hold(near_all, second_core)
     gates_a = Box(reorder_rows(near_all.v[:, : 2 * fcut]))
     downs_a = Box(reorder_rows(near_all.v[:, 2 * fcut :]))
     hold(second_z, gates_a, downs_a)
     hold(second_z, cot_home, gate_late, down_early)
     second_both = send(second_z, over_core)
+    cot_home = Box(pick_home(cot_own, cot_home))
     cot_move = send(cot_home, move)
     down_late = far_down.late()
     cot_core = send(cot_home, over_core)

time: 491 us -> 491 us (level)
  waiting for transfers between devices: 185 us -> 192 us
  starting transfers between devices: 76.2 us -> 70.6 us
    ppermute x78, waiting for transfers between devices: 185 us -> 192 us  [send(): return Box(lax.ppermute(val(value), AXES, pairs))]
    ppermute x78, starting transfers between devices: 75.9 us -> 70.4 us  [send(): return Box(lax.ppermute(val(value), AXES, pairs))]
where the time goes in v7:
time: 491 us; the launch traced here: 483 us
  waiting for transfers between devices  192 us (39%)
  Pallas kernels  87.1 us (18%)
  starting transfers between devices  70.6 us (14%)
  other arithmetic  52.2 us (11%)
  local copies, waits for them, and re-layouts  50 us (10%)
  between operations  16.1 us (3%)
  matrix products  15 us (3%)
    ppermute x78, waiting for transfers between devices, send(): return Box(lax.ppermute(val(value), AXES, pairs))  192 us
    ppermute x78, starting transfers between devices, send(): return Box(lax.ppermute(val(value), AXES, pairs))  70.4 us
    unnamed x214, local copies, waits for them, and re-layouts  34.6 us
    pallas_call x1, Pallas kernels, attend(): pl.pallas_call(functools.partial(forward_kernel, quarter), grid=(3,), out...  20.8 us
    pallas_call x1, Pallas kernels, attend_back(): pl.pallas_call(functools.partial(backward_kernel, quarter), grid=(3,), ou...  20.1 us
    pallas_call x2, Pallas kernels, feed_tokens(): pl.pallas_call(feed_kernel, grid=(1,), out_shape=outs, in_specs=[*(full_s...  20 us
    pallas_call x1, Pallas kernels, feed_grads(): pl.pallas_call(feed_grads_kernel, out_shape=(*(jax.ShapeDtypeStruct((wide...  18.1 us
    select_n x19, other arithmetic, pick(): return jnp.where(first, val(one), val(two))  15.6 us
  transfers between devices with their start and end apart: 80, of which 27 were waited for; matrix products, arithmetic and copies ran while one was open for 15% of the time, Pallas kernels for 16%

profile of v7, /device:TPU:0, one launch (start us, length us, event | category | flops | bytes accessed | tf_op | source)
XLA Modules:
  0.0 482.8 jit_solution(16926868399019248083)
XLA Ops:
  12.6 3.5 collective-permute-start.1
  16.9 2.4 constant_dynamic-slice_fusion.25
  19.4 3.9 collective-permute-start.5
  31.2 7.5 %collective-permute-done = bf16[192,640]{1,0:T(8,128)(2,1)} collective-permute-done((bf16[192,640]{1,0:T(8,128)(2,1)S(1)}, bf16[192,640]{1,0:T(8,128)(2,1)}, u32[]{:S(2)}, u32[]{:S(2)}) %collective-permute-start) | collective-permute-done | bytes 245792 | tf_op jit(solution)/shard_map/ppermute | solution.py:56
  38.7 3.6 collective-permute-done.5
  42.4 1.8 collective-permute-start.6
  44.1 1.9 collective-permute-start.9
  47.5 2.5 collective-permute-start.7
  52.2 10.0 %collective-permute-done.7 = bf16[384,640]{1,0:T(8,128)(2,1)} collective-permute-done((bf16[384,640]{1,0:T(8,128)(2,1)S(1)}, bf16[384,640]{1,0:T(8,128)(2,1)}, u32[]{:S(2)}, u32[]{:S(2)}) %collective-permute-start.7) | collective-permute-done | bytes 491552 | tf_op jit(solution)/shard_map/ppermute | solution.py:56
  62.3 3.1 collective-permute-done.9
  67.5 2.4 collective-permute-start.13
  76.1 6.4 %collective-permute-done.14 = bf16[192,192]{1,0:T(8,128)(2,1)} collective-permute-done((bf16[192,192]{1,0:T(8,128)(2,1)S(1)}, bf16[192,192]{1,0:T(8,128)(2,1)}, u32[]{:S(2)}, u32[]{:S(2)}) %collective-permute-start.14) | collective-permute-done | bytes 73760 | tf_op jit(solution)/shard_map/ppermute | solution.py:56
  85.5 2.0 broadcast_select_fusion.11
  88.9 2.7 pad_maximum_fusion.3.wb_ref
  92.6 2.5 collective-permute-start.23
  103.5 20.8 %shard_map.238 = (bf16[1024,384]{1,0:T(8,128)(2,1)S(1)}, bf16[1024,1536]{1,0:T(8,128)(2,1)S(1)}, bf16[1024,1152]{1,0:T(8,128)(2,1)S(1)}, f32[1024,128]{1,0:T(8,1...) custom-call(s32[4]{0:T(128)S(1)} %pad_add_fusion.pos_ref, ...), custom_call_target="tpu_custom_call" | custom-call | tf_op jit(solution)/shard_map/pallas_call | solution.py:390
  124.4 5.6 %collective-permute-done.23 = bf16[192,1024]{1,0:T(8,128)(2,1)} collective-permute-done((bf16[192,1024]{1,0:T(8,128)(2,1)}, bf16[192,1024]{1,0:T(8,128)(2,1)}, u32[]{:S(2)}, u32[]{:S(2)}) %collective-permute-start.23) | collective-permute-done | bytes 393248 | tf_op jit(solution)/shard_map/ppermute | solution.py:56
  130.0 2.2 fusion.26
  132.5 2.2 collective-permute-done.24
  134.9 2.2 fusion.24
  139.8 1.8 collective-permute-start.28
  141.8 2.0 collective-permute-start.29
  143.9 21.6 %collective-permute-done.25 = bf16[256,1536]{1,0:T(8,128)(2,1)S(1)} collective-permute-done((bf16[256,1536]{1,0:T(8,128)(2,1)S(1)}, bf16[256,1536]{1,0:T(8,128)(2,1)S(1)}, u32[]{:S(2)}, u32[]{:S(2)}) %collective-permute-start.25) | collective-permute-done | bytes 786464 | tf_op jit(solution)/shard_map/ppermute | solution.py:56
  177.3 18.3 %collective-permute-done.32.s0_ref = bf16[256,1536]{1,0:T(8,128)(2,1)} collective-permute-done((bf16[256,1536]{1,0:T(8,128)(2,1)S(1)}, bf16[256,1536]{1,0:T(8,128)(2,1)}, u32[]{:S(2)}, u32[]{:S(2)}) %collective-permute-start.32) | collective-permute-done | bytes 786464 | tf_op jit(solution)/shard_map/ppermute | solution.py:56
  197.9 2.1 collective-permute-start.39
  202.5 8.8 %collective-permute-done.40 = bf16[384,512]{1,0:T(8,128)(2,1)S(1)} collective-permute-done((bf16[384,512]{1,0:T(8,128)(2,1)}, bf16[384,512]{1,0:T(8,128)(2,1)S(1)}, u32[]{:S(2)}, u32[]{:S(2)}) %collective-permute-start.40) | collective-permute-done | bytes 393248 | tf_op jit(solution)/shard_map/ppermute | solution.py:56
  213.8 10.5 %shard_map.239 = (bf16[1024,1024]{1,0:T(8,128)(2,1)S(1)}, bf16[1024,1024]{1,0:T(8,128)(2,1)S(1)}, bf16[1024,1024]{1,0:T(8,128)(2,1)S(1)}, bf16[1024,1536]{1,0:T(...) custom-call(bf16[256,1536]{1,0:T(8,128)(2,1)} %collective-permute-done.32.s0_ref, ...), custom_call_target="tpu_custom_call" | custom-call | tf_op jit(solution)/shard_map/pallas_call | solution.py:438
  224.6 2.2 collective-permute-done.43
  227.4 9.5 %shard_map.240 = (bf16[1024,1024]{1,0:T(8,128)(2,1)S(1)}, bf16[1024,1024]{1,0:T(8,128)(2,1)S(1)}, bf16[1024,1024]{1,0:T(8,128)(2,1)S(1)}, bf16[1024,1536]{1,0:T(...) custom-call(bf16[256,1536]{1,0:T(8,128)(2,1)S(1)} %multiply_convert_, ...), custom_call_target="tpu_custom_call", output_to_operand_aliasing={{0}: (8, {}), {1}: (9, {}), {2}: (10, {}), {3}: (11, {}), {... | custom-call | tf_op jit(solution)/shard_map/pallas_call | solution.py:438
  241.2 5.4 %collective-permute-done.44 = bf16[256,1536]{1,0:T(8,128)(2,1)S(1)} collective-permute-done((bf16[256,1536]{1,0:T(8,128)(2,1)S(1)}, bf16[256,1536]{1,0:T(8,128)(2,1)S(1)}, u32[]{:S(2)}, u32[]{:S(2)}) %collective-permute-start.44) | collective-permute-done | bytes 786464 | tf_op jit(solution)/shard_map/ppermute | solution.py:56
  246.8 2.3 collective-permute-done.45
  255.8 18.1 %shard_map.241 = (bf16[768,1024]{1,0:T(8,128)(2,1)S(1)}, bf16[768,1024]{1,0:T(8,128)(2,1)S(1)}, bf16[768,512]{1,0:T(8,128)(2,1)S(1)}, bf16[768,512]{1,0:T(8,128)...) custom-call(s32[1]{0:T(128)} %bitcast.11.chip_ref, bf16[1024,1536]{1,0:T(8,128)(2,1)S(1)} %copy-done.5, ...), custom_call_target="tpu_custom_call" | custom-call | tf_op jit(solution)/shard_map/pallas_call | solution.py:527
  274.0 2.1 copy-done.20
  291.3 3.1 convolution_convert_fusion.1.gmix_ref
  294.4 1.9 convolution_convert_fusion
  298.3 20.1 %shard_map.242 = (bf16[1024,640]{1,0:T(8,128)(2,1)S(1)}, bf16[1024,640]{1,0:T(8,128)(2,1)S(1)}, f32[1,128]{1,0:T(1,128)S(1)}) custom-call(s32[4]{0:T(128)S(1)} %pad_add_fusion.pos_ref, bf16[1024,1152]{1,0:T(8,128)(2,1)S(1)} %copy-done.26, f32[1024,128]{1,0:T(8,128)S(1)} %copy-done.36, s32[1,1024]{1,0:T(1,128)S(1)} %broadcast_select_fusion.21.segr_ref, ...), custom_call_target="tpu_custom_call" | custom-call | tf_op jit(solution)/shard_map/pallas_call | solution.py:590
  318.6 3.9 collective-permute-done.49
  335.9 7.7 %shard_map.243 = (bf16[768,640]{1,0:T(8,128)(2,1)S(1)}, bf16[768,640]{1,0:T(8,128)(2,1)}, bf16[768,640]{1,0:T(8,128)(2,1)S(1)}, bf16[768,640]{1,0:T(8,128)(2,1)}, f32[1536,256]{1,0:T(8,128)S(1)}) custom-call(bf16[1024,1536]{1,0:T(8,128)(2,1)S(1)} %copy-done.9, bf16[1024,640]{1,0:T(8,128)(2,1)S(1)} %get-tuple-element.340.near_ref, ...), custom_call_target="tpu_custom_call" | custom-call | tf_op jit(solution)/shard_map/pallas_call | solution.py:569
  345.5 15.0 %collective-permute-done.55 = bf16[256,1536]{1,0:T(8,128)(2,1)S(1)} collective-permute-done((bf16[256,1536]{1,0:T(8,128)(2,1)S(1)}, bf16[256,1536]{1,0:T(8,128)(2,1)S(1)}, u32[]{:S(2)}, u32[]{:S(2)}) %collective-permute-start.55) | collective-permute-done | bytes 786464 | tf_op jit(solution)/shard_map/ppermute | solution.py:56
  366.3 3.2 fusion.4
  374.8 26.3 %collective-permute-done.64 = bf16[192,1536]{1,0:T(8,128)(2,1)} collective-permute-done((bf16[192,1536]{1,0:T(8,128)(2,1)}, bf16[192,1536]{1,0:T(8,128)(2,1)}, u32[]{:S(2)}, u32[]{:S(2)}) %collective-permute-start.64) | collective-permute-done | bytes 589856 | tf_op jit(solution)/shard_map/ppermute | solution.py:56
  410.3 20.6 %collective-permute-done.67 = bf16[384,384]{1,0:T(8,128)(2,1)S(1)} collective-permute-done((bf16[384,384]{1,0:T(8,128)(2,1)S(1)}, bf16[384,384]{1,0:T(8,128)(2,1)S(1)}, u32[]{:S(2)}, u32[]{:S(2)}) %collective-permute-start.67) | collective-permute-done | bytes 294944 | tf_op jit(solution)/shard_map/ppermute | solution.py:56
  430.9 2.1 collective-permute-start.69
  434.5 3.7 collective-permute-done.69
  439.2 3.0 collective-permute-start.70
  442.3 16.1 %collective-permute-done.72 = f32[6,1536]{1,0:T(8,128)S(1)} collective-permute-done((f32[6,1536]{1,0:T(8,128)S(1)}, f32[6,1536]{1,0:T(8,128)S(1)}, u32[]{:S(2)}, u32[]{:S(2)}) %collective-permute-start.72) | collective-permute-done | bytes 36896 | tf_op jit(solution)/shard_map/ppermute | solution.py:56
  461.2 2.5 collective-permute-done.76
  463.6 2.2 collective-permute-done.70
  (498 shorter events, 141.8 us)
Async XLA Ops:
  7.2 166.0 %all-gather.2.cloned.1.call-start = ((), (), s32[]{:S(2)}) async-start(), calls=%async_computation.1 | async-start | bytes 5898240 | tf_op jit(solution)/shard_map/all_gather | solution.py:815
  12.6 26.1 %collective-permute-start.1 = (bf16[192,640]{1,0:T(8,128)(2,1)S(1)}, bf16[192,640]{1,0:T(8,128)(2,1)}, u32[]{:S(2)}, u32[]{:S(2)}) collective-permute-start(bf16[192,640]{1,0:T(8,128)(2,1)S(1)} %get-tuple-element.211), channel_id=1, source_target_pairs={{0,6},{1,7},{2,4},{3,5},{4,2},{5,3},{6,0},{7,1},{8,14},{9,15},{10,... | collective-permute-start | bytes 737288 | tf_op jit(solution)/shard_map/ppermute | solution.py:56
  16.8 21.9 %collective-permute-start = (bf16[192,640]{1,0:T(8,128)(2,1)S(1)}, bf16[192,640]{1,0:T(8,128)(2,1)}, u32[]{:S(2)}, u32[]{:S(2)}) collective-permute-start(bf16[192,640]{1,0:T(8,128)(2,1)S(1)} %get-tuple-element.210), channel_id=1, source_target_pairs={{0,2},{1,3},{2,0},{3,1},{4,6},{5,7},{6,4},{7,5},{8,10},{9,11},{10,... | collective-permute-start | bytes 737288 | tf_op jit(solution)/shard_map/ppermute | solution.py:56
  19.4 22.9 %collective-permute-start.5 = (bf16[256,1536]{1,0:T(8,128)(2,1)S(1)}, bf16[256,1536]{1,0:T(8,128)(2,1)}, u32[]{:S(2)}, u32[]{:S(2)}) collective-permute-start(bf16[256,1536]{1,0:T(8,128)(2,1)S(1)} %pad_maximum_fusion.7), channel_id=1, source_target_pairs={{0,1},{1,0},{6,7},{7,6},{8,9},{9,8},{14,15},{15,14},{16,17},{17,16... | collective-permute-start | bytes 2359304 | tf_op jit(solution)/shard_map/ppermute | solution.py:56
  42.4 19.9 %collective-permute-start.6 = (bf16[256,1536]{1,0:T(8,128)(2,1)}, bf16[256,1536]{1,0:T(8,128)(2,1)S(1)}, u32[]{:S(2)}, u32[]{:S(2)}) collective-permute-start(bf16[256,1536]{1,0:T(8,128)(2,1)} %copy-done.77), channel_id=1, source_target_pairs={{0,0},{1,1},{2,4},{3,5},{4,2},{5,3},{6,6},{7,7},{8,8},{9,9},{10,12... | collective-permute-start | bytes 2359304 | tf_op jit(solution)/shard_map/ppermute | solution.py:56
  44.1 21.2 %collective-permute-start.9 = (bf16[256,1536]{1,0:T(8,128)(2,1)}, bf16[256,1536]{1,0:T(8,128)(2,1)S(1)}, u32[]{:S(2)}, u32[]{:S(2)}) collective-permute-start(bf16[256,1536]{1,0:T(8,128)(2,1)} %pad_maximum_fusion.8), channel_id=1, source_target_pairs={{0,1},{1,0},{6,7},{7,6},{8,9},{9,8},{14,15},{15,14},{16,17},{17,16... | collective-permute-start | bytes 2359304 | tf_op jit(solution)/shard_map/ppermute | solution.py:56
  51.6 18.4 %collective-permute-start.11 = (bf16[384,640]{1,0:T(8,128)(2,1)}, bf16[384,640]{1,0:T(8,128)(2,1)S(1)}, u32[]{:S(2)}, u32[]{:S(2)}) collective-permute-start(bf16[384,640]{1,0:T(8,128)(2,1)} %copy-done.87), channel_id=1, source_target_pairs={{0,16},{1,17},{2,18},{3,19},{4,20},{5,21},{6,22},{7,23},{8,24},{9,... | collective-permute-start | bytes 1474568 | tf_op jit(solution)/shard_map/ppermute | solution.py:56
  67.5 16.1 %collective-permute-start.13 = (bf16[384,640]{1,0:T(8,128)(2,1)}, bf16[384,640]{1,0:T(8,128)(2,1)}, u32[]{:S(2)}, u32[]{:S(2)}) collective-permute-start(bf16[384,640]{1,0:T(8,128)(2,1)} %collective-permute-done.7), channel_id=1, source_target_pairs={{0,8},{1,9},{2,10},{3,11},{4,12},{5,13},{6,14},{7,15},{8,0},{9,1},... | collective-permute-start | bytes 1474568 | tf_op jit(solution)/shard_map/ppermute | solution.py:56
  71.5 20.1 %collective-permute-start.17 = (bf16[256,1536]{1,0:T(8,128)(2,1)S(1)}, bf16[256,1536]{1,0:T(8,128)(2,1)}, u32[]{:S(2)}, u32[]{:S(2)}) collective-permute-start(bf16[256,1536]{1,0:T(8,128)(2,1)S(1)} %collective-permute-done.6.x0_ref), channel_id=1, source_target_pairs={{0,4},{1,5},{2,6},{3,7},{4,0},{5,1},{6,2},{7,3},{8,12},{9,13},{10,... | collective-permute-start | bytes 2359304 | tf_op jit(solution)/shard_map/ppermute | solution.py:56
  75.8 390.0 %reduce-scatter.2.cloned.1.call-start = ((), (), s32[]{:S(2)}) async-start(), calls=%async_computation.2 | async-start | bytes 5898240 | tf_op jit(solution)/shard_map/reduce_scatter | solution.py:995
  92.5 31.9 %collective-permute-start.22 = (bf16[192,1024]{1,0:T(8,128)(2,1)}, bf16[192,1024]{1,0:T(8,128)(2,1)}, u32[]{:S(2)}, u32[]{:S(2)}) collective-permute-start(bf16[192,1024]{1,0:T(8,128)(2,1)} %get-tuple-element.243), channel_id=1, source_target_pairs={{0,2},{1,3},{2,0},{3,1},{4,6},{5,7},{6,4},{7,5},{8,10},{9,11},{10,... | collective-permute-start | bytes 1179656 | tf_op jit(solution)/shard_map/ppermute | solution.py:56
  92.6 37.4 %collective-permute-start.23 = (bf16[192,1024]{1,0:T(8,128)(2,1)}, bf16[192,1024]{1,0:T(8,128)(2,1)}, u32[]{:S(2)}, u32[]{:S(2)}) collective-permute-start(bf16[192,1024]{1,0:T(8,128)(2,1)} %get-tuple-element.244), channel_id=1, source_target_pairs={{0,6},{1,7},{2,4},{3,5},{4,2},{5,3},{6,0},{7,1},{8,14},{9,15},{10,... | collective-permute-start | bytes 1179656 | tf_op jit(solution)/shard_map/ppermute | solution.py:56
  95.9 28.5 %collective-permute-start.19 = (bf16[384,384]{1,0:T(8,128)(2,1)}, bf16[384,384]{1,0:T(8,128)(2,1)}, u32[]{:S(2)}, u32[]{:S(2)}) collective-permute-start(bf16[384,384]{1,0:T(8,128)(2,1)} %pad_maximum_fusion.17), channel_id=1, source_target_pairs={{0,8},{1,9},{2,10},{3,11},{4,12},{5,13},{6,14},{7,15},{8,0},{9,1},... | collective-permute-start | bytes 884744 | tf_op jit(solution)/shard_map/ppermute | solution.py:56
  96.5 27.9 %collective-permute-start.20 = (bf16[384,384]{1,0:T(8,128)(2,1)}, bf16[384,384]{1,0:T(8,128)(2,1)}, u32[]{:S(2)}, u32[]{:S(2)}) collective-permute-start(bf16[384,384]{1,0:T(8,128)(2,1)} %pad_maximum_fusion.17), channel_id=1, source_target_pairs={{0,16},{1,17},{2,18},{3,19},{4,20},{5,21},{6,22},{7,23},{8,24},{9,... | collective-permute-start | bytes 884744 | tf_op jit(solution)/shard_map/ppermute | solution.py:56
  98.1 26.2 %collective-permute-start.21 = (bf16[384,384]{1,0:T(8,128)(2,1)}, bf16[384,384]{1,0:T(8,128)(2,1)}, u32[]{:S(2)}, u32[]{:S(2)}) collective-permute-start(bf16[384,384]{1,0:T(8,128)(2,1)} %pad_maximum_fusion.17), channel_id=1, source_target_pairs={{0,24},{1,25},{2,26},{3,27},{4,28},{5,29},{6,30},{7,31},{8,16},{9,... | collective-permute-start | bytes 884744 | tf_op jit(solution)/shard_map/ppermute | solution.py:56
  137.3 28.2 %collective-permute-start.25 = (bf16[256,1536]{1,0:T(8,128)(2,1)S(1)}, bf16[256,1536]{1,0:T(8,128)(2,1)S(1)}, u32[]{:S(2)}, u32[]{:S(2)}) collective-permute-start(bf16[256,1536]{1,0:T(8,128)(2,1)S(1)} %fusion.8), channel_id=1, source_target_pairs={{0,1},{1,0},{2,3},{3,2},{4,5},{5,4},{6,7},{7,6},{8,9},{9,8},{10,11... | collective-permute-start | bytes 2359304 | tf_op jit(solution)/shard_map/ppermute | solution.py:56
  139.0 26.6 %collective-permute-start.27 = (bf16[384,1024]{1,0:T(8,128)(2,1)S(1)}, bf16[384,1024]{1,0:T(8,128)(2,1)}, u32[]{:S(2)}, u32[]{:S(2)}) collective-permute-start(bf16[384,1024]{1,0:T(8,128)(2,1)S(1)} %maximum_select_fusion.1), channel_id=1, source_target_pairs={{0,8},{1,9},{2,10},{3,11},{4,12},{5,13},{6,14},{7,15},{8,0},{9,1},... | collective-permute-start | bytes 2359304 | tf_op jit(solution)/shard_map/ppermute | solution.py:56
  139.8 25.8 %collective-permute-start.28 = (bf16[384,1024]{1,0:T(8,128)(2,1)S(1)}, bf16[384,1024]{1,0:T(8,128)(2,1)S(1)}, u32[]{:S(2)}, u32[]{:S(2)}) collective-permute-start(bf16[384,1024]{1,0:T(8,128)(2,1)S(1)} %maximum_select_fusion.1), channel_id=1, source_target_pairs={{0,16},{1,17},{2,18},{3,19},{4,20},{5,21},{6,22},{7,23},{8,24},{9,... | collective-permute-start | bytes 2359304 | tf_op jit(solution)/shard_map/ppermute | solution.py:56
  141.8 23.8 %collective-permute-start.29 = (bf16[192,512]{1,0:T(8,128)(2,1)S(1)}, bf16[192,512]{1,0:T(8,128)(2,1)S(1)}, u32[]{:S(2)}, u32[]{:S(2)}) collective-permute-start(bf16[192,512]{1,0:T(8,128)(2,1)S(1)} %copy-done.100), channel_id=1, source_target_pairs={{0,2},{1,3},{2,0},{3,1},{4,6},{5,7},{6,4},{7,5},{8,10},{9,11},{10,... | collective-permute-start | bytes 589832 | tf_op jit(solution)/shard_map/ppermute | solution.py:56
  143.8 22.6 %collective-permute-start.30 = (bf16[192,512]{1,0:T(8,128)(2,1)S(1)}, bf16[192,512]{1,0:T(8,128)(2,1)S(1)}, u32[]{:S(2)}, u32[]{:S(2)}) collective-permute-start(bf16[192,512]{1,0:T(8,128)(2,1)S(1)} %copy-done.99), channel_id=1, source_target_pairs={{0,6},{1,7},{2,4},{3,5},{4,2},{5,3},{6,0},{7,1},{8,14},{9,15},{10,... | collective-permute-start | bytes 589832 | tf_op jit(solution)/shard_map/ppermute | solution.py:56
  167.1 28.5 %collective-permute-start.32 = (bf16[256,1536]{1,0:T(8,128)(2,1)S(1)}, bf16[256,1536]{1,0:T(8,128)(2,1)}, u32[]{:S(2)}, u32[]{:S(2)}) collective-permute-start(bf16[256,1536]{1,0:T(8,128)(2,1)S(1)} %multiply_convert_fusion.s0_ref), channel_id=1, source_target_pairs={{0,1},{1,0},{2,3},{3,2},{4,5},{5,4},{6,7},{7,6},{8,9},{9,8},{10,11... | collective-permute-start | bytes 2359304 | tf_op jit(solution)/shard_map/ppermute | solution.py:56
  168.0 27.6 %collective-permute-start.36 = (bf16[384,512]{1,0:T(8,128)(2,1)S(1)}, bf16[384,512]{1,0:T(8,128)(2,1)}, u32[]{:S(2)}, u32[]{:S(2)}) collective-permute-start(bf16[384,512]{1,0:T(8,128)(2,1)S(1)} %maximum_select_fusion.4), channel_id=1, source_target_pairs={{0,16},{1,17},{2,18},{3,19},{4,20},{5,21},{6,22},{7,23},{8,24},{9,... | collective-permute-start | bytes 1179656 | tf_op jit(solution)/shard_map/ppermute | solution.py:56
  169.5 26.1 %collective-permute-start.37 = (bf16[384,512]{1,0:T(8,128)(2,1)S(1)}, bf16[384,512]{1,0:T(8,128)(2,1)}, u32[]{:S(2)}, u32[]{:S(2)}) collective-permute-start(bf16[384,512]{1,0:T(8,128)(2,1)S(1)} %maximum_select_fusion.4), channel_id=1, source_target_pairs={{0,8},{1,9},{2,10},{3,11},{4,12},{5,13},{6,14},{7,15},{8,0},{9,1},... | collective-permute-start | bytes 1179656 | tf_op jit(solution)/shard_map/ppermute | solution.py:56
  170.5 25.3 %collective-permute-start.35 = (bf16[384,1024]{1,0:T(8,128)(2,1)}, bf16[384,1024]{1,0:T(8,128)(2,1)}, u32[]{:S(2)}, u32[]{:S(2)}) collective-permute-start(bf16[384,1024]{1,0:T(8,128)(2,1)} %collective-permute-done.27), channel_id=1, source_target_pairs={{0,16},{1,17},{2,18},{3,19},{4,20},{5,21},{6,22},{7,23},{8,24},{9,... | collective-permute-start | bytes 2359304 | tf_op jit(solution)/shard_map/ppermute | solution.py:56
  171.6 24.2 %collective-permute-start.34 = (bf16[256,1536]{1,0:T(8,128)(2,1)}, bf16[256,1536]{1,0:T(8,128)(2,1)}, u32[]{:S(2)}, u32[]{:S(2)}) collective-permute-start(bf16[256,1536]{1,0:T(8,128)(2,1)} %pad_maximum_fusion.8), channel_id=1, source_target_pairs={{2,4},{3,5},{4,2},{5,3},{10,12},{11,13},{12,10},{13,11},{18,20},{1... | collective-permute-start | bytes 2359304 | tf_op jit(solution)/shard_map/ppermute | solution.py:56
  226.9 19.6 %collective-permute-start.44 = (bf16[256,1536]{1,0:T(8,128)(2,1)S(1)}, bf16[256,1536]{1,0:T(8,128)(2,1)S(1)}, u32[]{:S(2)}, u32[]{:S(2)}) collective-permute-start(bf16[256,1536]{1,0:T(8,128)(2,1)S(1)} %add_convert_fusion.2), channel_id=1, source_target_pairs={{0,1},{1,0},{2,3},{3,2},{4,5},{5,4},{6,7},{7,6},{8,9},{9,8},{10,11... | collective-permute-start | bytes 2359304 | tf_op jit(solution)/shard_map/ppermute | solution.py:56
  251.4 29.7 %collective-permute-start.46 = (bf16[256,1536]{1,0:T(8,128)(2,1)S(1)}, bf16[256,1536]{1,0:T(8,128)(2,1)S(1)}, u32[]{:S(2)}, u32[]{:S(2)}) collective-permute-start(bf16[256,1536]{1,0:T(8,128)(2,1)S(1)} %get-tuple-element.322), channel_id=1, source_target_pairs={{0,1},{1,0},{2,3},{3,2},{4,5},{5,4},{6,7},{7,6},{8,9},{9,8},{10,11... | collective-permute-start | bytes 2359304 | tf_op jit(solution)/shard_map/ppermute | solution.py:56
  285.1 37.5 %collective-permute-start.49 = (bf16[768,1024]{1,0:T(8,128)(2,1)}, bf16[768,1024]{1,0:T(8,128)(2,1)S(1)}, u32[]{:S(2)}, u32[]{:S(2)}) collective-permute-start(bf16[768,1024]{1,0:T(8,128)(2,1)} %copy-done.44), channel_id=1, source_target_pairs={{0,16},{1,17},{2,18},{3,19},{4,20},{5,21},{6,22},{7,23},{8,24},{9,... | collective-permute-start | bytes 4718600 | tf_op jit(solution)/shard_map/ppermute | solution.py:56
  287.8 30.9 %collective-permute-start.50 = (bf16[768,512]{1,0:T(8,128)(2,1)S(1)}, bf16[768,512]{1,0:T(8,128)(2,1)S(1)}, u32[]{:S(2)}, u32[]{:S(2)}) collective-permute-start(bf16[768,512]{1,0:T(8,128)(2,1)S(1)} %copy-done.48), channel_id=1, source_target_pairs={{0,8},{1,9},{2,10},{3,11},{4,12},{5,13},{6,14},{7,15},{8,0},{9,1},... | collective-permute-start | bytes 2359304 | tf_op jit(solution)/shard_map/ppermute | solution.py:56
  289.2 29.2 %collective-permute-start.52 = (bf16[256,1536]{1,0:T(8,128)(2,1)S(1)}, bf16[256,1536]{1,0:T(8,128)(2,1)S(1)}, u32[]{:S(2)}, u32[]{:S(2)}) collective-permute-start(bf16[256,1536]{1,0:T(8,128)(2,1)S(1)} %get-tuple-element.442), channel_id=1, source_target_pairs={{0,1},{1,0},{2,3},{3,2},{4,5},{5,4},{6,7},{7,6},{8,9},{9,8},{10,11... | collective-permute-start | bytes 2359304 | tf_op jit(solution)/shard_map/ppermute | solution.py:56
  297.4 76.3 %collective-permute-start.63 = (bf16[768,384]{1,0:T(8,128)(2,1)}, bf16[768,384]{1,0:T(8,128)(2,1)}, u32[]{:S(2)}, u32[]{:S(2)}) collective-permute-start(bf16[768,384]{1,0:T(8,128)(2,1)} %get-tuple-element.467), channel_id=1, source_target_pairs={{0,16},{1,17},{2,18},{3,19},{4,20},{5,21},{6,22},{7,23},{8,24},{9,... | collective-permute-start | bytes 1769480 | tf_op jit(solution)/shard_map/ppermute | solution.py:56
  327.5 32.9 %collective-permute-start.56 = (bf16[384,1024]{1,0:T(8,128)(2,1)S(1)}, bf16[384,1024]{1,0:T(8,128)(2,1)S(1)}, u32[]{:S(2)}, u32[]{:S(2)}) collective-permute-start(bf16[384,1024]{1,0:T(8,128)(2,1)S(1)} %slice.650), channel_id=1, source_target_pairs={{0,8},{1,9},{2,10},{3,11},{4,12},{5,13},{6,14},{7,15},{8,0},{9,1},... | collective-permute-start | bytes 2359304 | tf_op jit(solution)/shard_map/ppermute | solution.py:56
  328.8 31.7 %collective-permute-start.57 = (bf16[384,512]{1,0:T(8,128)(2,1)S(1)}, bf16[384,512]{1,0:T(8,128)(2,1)S(1)}, u32[]{:S(2)}, u32[]{:S(2)}) collective-permute-start(bf16[384,512]{1,0:T(8,128)(2,1)S(1)} %slice.658), channel_id=1, source_target_pairs={{0,16},{1,17},{2,18},{3,19},{4,20},{5,21},{6,22},{7,23},{8,24},{9,... | collective-permute-start | bytes 1179656 | tf_op jit(solution)/shard_map/ppermute | solution.py:56
  330.7 29.8 %collective-permute-start.58 = (bf16[256,1536]{1,0:T(8,128)(2,1)S(1)}, bf16[256,1536]{1,0:T(8,128)(2,1)S(1)}, u32[]{:S(2)}, u32[]{:S(2)}) collective-permute-start(bf16[256,1536]{1,0:T(8,128)(2,1)S(1)} %add_convert_fusion), channel_id=1, source_target_pairs={{2,4},{3,5},{4,2},{5,3},{10,12},{11,13},{12,10},{13,11},{18,20},{1... | collective-permute-start | bytes 2359304 | tf_op jit(solution)/shard_map/ppermute | solution.py:56
  332.1 28.4 %collective-permute-start.55 = (bf16[256,1536]{1,0:T(8,128)(2,1)S(1)}, bf16[256,1536]{1,0:T(8,128)(2,1)S(1)}, u32[]{:S(2)}, u32[]{:S(2)}) collective-permute-start(bf16[256,1536]{1,0:T(8,128)(2,1)S(1)} %fusion.7), channel_id=1, source_target_pairs={{0,1},{1,0},{2,3},{3,2},{4,5},{5,4},{6,7},{7,6},{8,9},{9,8},{10,11... | collective-permute-start | bytes 2359304 | tf_op jit(solution)/shard_map/ppermute | solution.py:56
  361.0 40.2 %collective-permute-start.60 = (bf16[768,640]{1,0:T(8,128)(2,1)}, bf16[768,640]{1,0:T(8,128)(2,1)}, u32[]{:S(2)}, u32[]{:S(2)}) collective-permute-start(bf16[768,640]{1,0:T(8,128)(2,1)} %get-tuple-element.371), channel_id=1, source_target_pairs={{0,16},{1,17},{2,18},{3,19},{4,20},{5,21},{6,22},{7,23},{8,24},{9,... | collective-permute-start | bytes 2949128 | tf_op jit(solution)/shard_map/ppermute | solution.py:56
  361.4 39.8 %collective-permute-start.61 = (bf16[768,640]{1,0:T(8,128)(2,1)}, bf16[768,640]{1,0:T(8,128)(2,1)}, u32[]{:S(2)}, u32[]{:S(2)}) collective-permute-start(bf16[768,640]{1,0:T(8,128)(2,1)} %get-tuple-element.372), channel_id=1, source_target_pairs={{0,8},{1,9},{2,10},{3,11},{4,12},{5,13},{6,14},{7,15},{8,0},{9,1},... | collective-permute-start | bytes 2949128 | tf_op jit(solution)/shard_map/ppermute | solution.py:56
  364.2 36.9 %collective-permute-start.64 = (bf16[192,1536]{1,0:T(8,128)(2,1)}, bf16[192,1536]{1,0:T(8,128)(2,1)}, u32[]{:S(2)}, u32[]{:S(2)}) collective-permute-start(bf16[192,1536]{1,0:T(8,128)(2,1)} %get-tuple-element.465), channel_id=1, source_target_pairs={{0,2},{1,3},{2,0},{3,1},{4,6},{5,7},{6,4},{7,5},{8,10},{9,11},{10,... | collective-permute-start | bytes 1769480 | tf_op jit(solution)/shard_map/ppermute | solution.py:56
  372.7 28.5 %collective-permute-start.62 = (f32[9,1536]{1,0:T(8,128)S(1)}, f32[9,1536]{1,0:T(8,128)S(1)}, u32[]{:S(2)}, u32[]{:S(2)}) collective-permute-start(f32[9,1536]{1,0:T(8,128)S(1)} %select_maximum_fusion), channel_id=1, source_target_pairs={{0,8},{1,9},{2,10},{3,11},{4,12},{5,13},{6,14},{7,15},{8,0},{9,1},... | collective-permute-start | bytes 165896 | tf_op jit(solution)/shard_map/ppermute | solution.py:56
  374.0 56.9 %collective-permute-start.68 = (bf16[256,1536]{1,0:T(8,128)(2,1)S(1)}, bf16[256,1536]{1,0:T(8,128)(2,1)S(1)}, u32[]{:S(2)}, u32[]{:S(2)}) collective-permute-start(bf16[256,1536]{1,0:T(8,128)(2,1)S(1)} %copy-done.54), channel_id=1, source_target_pairs={{2,4},{3,5},{4,2},{5,3},{10,12},{11,13},{12,10},{13,11},{18,20},{1... | collective-permute-start | bytes 2359304 | tf_op jit(solution)/shard_map/ppermute | solution.py:56
  402.7 28.2 %collective-permute-start.65 = (bf16[384,640]{1,0:T(8,128)(2,1)S(1)}, bf16[384,640]{1,0:T(8,128)(2,1)S(1)}, u32[]{:S(2)}, u32[]{:S(2)}) collective-permute-start(bf16[384,640]{1,0:T(8,128)(2,1)S(1)} %slice.657), channel_id=1, source_target_pairs={{0,8},{1,9},{2,10},{3,11},{4,12},{5,13},{6,14},{7,15},{8,0},{9,1},... | collective-permute-start | bytes 1474568 | tf_op jit(solution)/shard_map/ppermute | solution.py:56
  405.5 25.4 %collective-permute-start.66 = (bf16[384,640]{1,0:T(8,128)(2,1)S(1)}, bf16[384,640]{1,0:T(8,128)(2,1)S(1)}, u32[]{:S(2)}, u32[]{:S(2)}) collective-permute-start(bf16[384,640]{1,0:T(8,128)(2,1)S(1)} %slice.656), channel_id=1, source_target_pairs={{0,16},{1,17},{2,18},{3,19},{4,20},{5,21},{6,22},{7,23},{8,24},{9,... | collective-permute-start | bytes 1474568 | tf_op jit(solution)/shard_map/ppermute | solution.py:56
  408.1 22.7 %collective-permute-start.67 = (bf16[384,384]{1,0:T(8,128)(2,1)S(1)}, bf16[384,384]{1,0:T(8,128)(2,1)S(1)}, u32[]{:S(2)}, u32[]{:S(2)}) collective-permute-start(bf16[384,384]{1,0:T(8,128)(2,1)S(1)} %slice.659), channel_id=1, source_target_pairs={{0,8},{1,9},{2,10},{3,11},{4,12},{5,13},{6,14},{7,15},{8,0},{9,1},... | collective-permute-start | bytes 884744 | tf_op jit(solution)/shard_map/ppermute | solution.py:56
  410.3 32.1 %collective-permute-start.74 = (bf16[192,1536]{1,0:T(8,128)(2,1)S(1)}, bf16[192,1536]{1,0:T(8,128)(2,1)S(1)}, u32[]{:S(2)}, u32[]{:S(2)}) collective-permute-start(bf16[192,1536]{1,0:T(8,128)(2,1)S(1)} %copy-done.84), channel_id=1, source_target_pairs={{0,6},{1,7},{2,4},{3,5},{4,2},{5,3},{6,0},{7,1},{8,14},{9,15},{10,... | collective-permute-start | bytes 1769480 | tf_op jit(solution)/shard_map/ppermute | solution.py:56
  438.4 20.1 %collective-permute-start.72 = (f32[6,1536]{1,0:T(8,128)S(1)}, f32[6,1536]{1,0:T(8,128)S(1)}, u32[]{:S(2)}, u32[]{:S(2)}) collective-permute-start(f32[6,1536]{1,0:T(8,128)S(1)} %fusion.31), channel_id=1, source_target_pairs={{0,2},{1,3},{2,0},{3,1},{4,6},{5,7},{6,4},{7,5},{8,10},{9,11},{10,... | collective-permute-start | bytes 110600 | tf_op jit(solution)/shard_map/ppermute | solution.py:56
  438.8 19.6 %collective-permute-start.73 = (bf16[192,832]{1,0:T(8,128)(2,1)S(1)}, bf16[192,832]{1,0:T(8,128)(2,1)S(1)}, u32[]{:S(2)}, u32[]{:S(2)}) collective-permute-start(bf16[192,832]{1,0:T(8,128)(2,1)S(1)} %broadcast_select_fusion.15), channel_id=1, source_target_pairs={{0,4},{1,5},{2,6},{3,7},{4,0},{5,1},{6,2},{7,3},{8,12},{9,13},{10,... | collective-permute-start | bytes 958472 | tf_op jit(solution)/shard_map/ppermute | solution.py:56
  439.2 26.6 %collective-permute-start.70 = (bf16[192,832]{1,0:T(8,128)(2,1)S(1)}, bf16[192,832]{1,0:T(8,128)(2,1)S(1)}, u32[]{:S(2)}, u32[]{:S(2)}) collective-permute-start(bf16[192,832]{1,0:T(8,128)(2,1)S(1)} %get-tuple-element.502), channel_id=1, source_target_pairs={{0,2},{1,3},{2,0},{3,1},{4,6},{5,7},{6,4},{7,5},{8,10},{9,11},{10,... | collective-permute-start | bytes 958472 | tf_op jit(solution)/shard_map/ppermute | solution.py:56
  442.2 31.1 %collective-permute-start.77 = (bf16[192,832]{1,0:T(8,128)(2,1)S(1)}, bf16[192,832]{1,0:T(8,128)(2,1)S(1)}, u32[]{:S(2)}, u32[]{:S(2)}) collective-permute-start(bf16[192,832]{1,0:T(8,128)(2,1)S(1)} %get-tuple-element.501), channel_id=1, source_target_pairs={{0,6},{1,7},{2,4},{3,5},{4,2},{5,3},{6,0},{7,1},{8,14},{9,15},{10,... | collective-permute-start | bytes 958472 | tf_op jit(solution)/shard_map/ppermute | solution.py:56
  (139 other events, 936.5 us)
Sparse Core Ops, SparseCore 0:
  76.0 62.4 all-gather.1
  366.4 77.6 reduce-scatter.1
